TPU v7x, 32 devices: a whole 2x2x4 slice. The times are simulated.
32 devices in a mesh: groups: 2 (over x), dp: 8 (over z, y), tensor: 2 (over core).
Axes of the slice: x: 2, y: 2, z: 4, core: 2. Of those that a mesh axis runs over, the one named last changes fastest.
Arguments:
- tokens: bfloat16 [12288, 8192], P(('groups', 'dp'), 'tensor'), parts along dimension 0, may hold values from -6 to 6
- key_projection_weight: bfloat16 [8192, 1024], P('tensor'), may hold values from -0.0625 to 0.0625
- adapter_down_weight: bfloat16 [8, 64, 8192], P('dp', None, 'tensor'), may hold values from -0.0625 to 0.0625
- adapter_up_weight: bfloat16 [8, 64, 1024], P('dp', None, 'tensor'), may hold values from -0.75 to 0.75
- adapter_pool_index: int32 [8], replicated, may hold values from 0 to 7, each once
- block_adapter_index: int32 [96, 1], P('groups'), parts along dimension 0, may hold values from 0 to 7
- block_live_tokens: int32 [96], P('groups'), parts along dimension 0, may hold values from 1 to 128
Outputs:
- keys: bfloat16 [12288, 1024], P(('groups', 'dp'), 'tensor'), parts along dimension 0
There are 2 independent parts, one for each index of `groups`. A program takes and returns all parts, laid end to end along the dimension named above; an argument that names none is the same for every part. Nothing has to cross between parts.
Inputs may be any that keep to these rules, and one draw needn't show every extreme that they name: `block_adapter_index`: every adapter is named by some block. `adapter_pool_index`: a permutation of the pool indices.
All inputs are finite; a program needn't handle non-finite values.
Results may differ from a plain program's by a relative error of at most 0.001.
Values may be sent and summed in bfloat16 or wider, within the bound.
No kernel may reach another device: no remote copies, remote signals or barrier semaphores. Data moves between devices by JAX's collectives and lax.ppermute only.
A program may use at most 128 MiB of HBM per device.

v0:
```python
import jax
import jax.numpy as jnp
from jax import lax
from jax.sharding import PartitionSpec as P

ADAPTER_RANK = 64
BLK = 128


def per_device(
    tokens,
    key_projection_weight,
    adapter_down_weight,
    adapter_up_weight,
    adapter_pool_index,
    block_adapter_index,
    block_live_tokens,
):
    count_of_rows = tokens.shape[0]
    count_of_blocks = count_of_rows // BLK
    block_pool_index = adapter_pool_index[block_adapter_index[:, 0]]
    first_block = lax.axis_index("dp") * count_of_blocks
    own_slots = lax.dynamic_slice_in_dim(block_pool_index, first_block, count_of_blocks)
    own_fill = lax.dynamic_slice_in_dim(block_live_tokens, first_block, count_of_blocks)
    base_part = jnp.dot(tokens, key_projection_weight, preferred_element_type=jnp.float32)
    token_blocks = tokens.reshape(count_of_blocks, BLK, tokens.shape[1])
    blank_down_matrix = jnp.zeros(
        (count_of_blocks, ADAPTER_RANK, adapter_down_weight.shape[2]), jnp.bfloat16
    )
    blank_up_matrix = jnp.zeros(
        (count_of_blocks, ADAPTER_RANK, adapter_up_weight.shape[2]), jnp.bfloat16
    )
    down_matrix_block = lax.all_gather(adapter_down_weight, "dp", axis=0, tiled=True)
    up_matrix_block = lax.all_gather(adapter_up_weight, "dp", axis=0, tiled=True)
    piece_count = down_matrix_block.shape[0]
    inside = (own_slots >= 0) & (own_slots < piece_count)
    pick_index = jnp.clip(own_slots, 0, piece_count - 1)
    new_down = jnp.where(
        inside[:, None, None], jnp.take(down_matrix_block, pick_index, axis=0), blank_down_matrix
    )
    new_up = jnp.where(
        inside[:, None, None], jnp.take(up_matrix_block, pick_index, axis=0), blank_up_matrix
    )
    shrink = jnp.einsum("nrd,nbd->rnb", new_down, token_blocks, preferred_element_type=jnp.float32)
    shrink = shrink.reshape(ADAPTER_RANK, count_of_rows)
    shrink_total = lax.psum(shrink, "tensor")
    adapter_output_delta = jnp.einsum(
        "rnb,nrc->nbc",
        shrink_total.reshape(ADAPTER_RANK, count_of_blocks, BLK),
        new_up.astype(jnp.float32),
        precision=lax.Precision.HIGHEST,
        preferred_element_type=jnp.float32,
    )
    base_output = lax.psum_scatter(base_part, "tensor", scatter_dimension=1, tiled=True)
    live_row_mask = jnp.arange(BLK, dtype=jnp.int32)[None, :] < own_fill[:, None]
    live_row_mask = live_row_mask.reshape(count_of_rows, 1)
    summed_output = base_output + adapter_output_delta.reshape(count_of_rows, base_output.shape[1])
    return jnp.where(live_row_mask, summed_output, 0.0).astype(jnp.bfloat16)


def solution(mesh):
    in_specs = (
        P(("groups", "dp"), "tensor"),
        P("tensor", None),
        P("dp", None, "tensor"),
        P("dp", None, "tensor"),
        P(),
        P("groups", None),
        P("groups"),
    )
    out_specs = P(("groups", "dp"), "tensor")
    return jax.shard_map(
        per_device, mesh=mesh, in_specs=in_specs, out_specs=out_specs, check_vma=False
    )
```

profile of v0, /device:TPU:0, one launch (start us, length us, event | category | flops | bytes accessed | tf_op | source)
XLA Modules:
  0.0 150.3 jit_solution(1581435673275003701)
XLA Ops:
  6.5 0.0 all-gather.2.cloned.1.call-start
  6.5 0.7 all-gather.2.cloned.1.call-update
  7.3 0.0 all-reduce.2.cloned.1.call-start
  7.3 1.6 %fusion.25 = (s32[1]{0:T(128)}, s32[1]{0:T(128)}, s32[1]{0:T(128)}, s32[1]{0:T(128)}, s32[1]{0:T(128)}, /*index=5*/s32[1]{0:T(128)}, s32[1]{0:T(128)}, s32[1]{0:T(128)}) fusion(s32[8]{0:T(128)} %param.11), kind=kLoop, calls=%fused_computation.39 | loop fusion | bytes 64 | tf_op jit(solution)/shard_map/gather | solution.py:21
  8.9 5.7 %bitcast_select_fusion = s32[48]{0:T(128)S(1)} fusion(s32[48,1]{0,1:T(1,128)} %param.12, s32[]{:T(128)} %bitcast.3, s32[]{:T(128)} %bitcast.4, s32[]{:T(128)} %bitcast.5, s32[]{:T(128)} %bitcast.6, s32[]{:T(128)} %bitcast.7, s32[]{:T(128)} %bitcast.9, s32[]{:T(128)} %bitcast.8, s32[]{:T(128)} %bitcast.2), kind=kLoop, calls=%fused_computation.25 | loop fusion | flops 816 | bytes 416 | tf_op jit(solution)/shard_map/gather | solution.py:21
  14.6 0.1 compare_and_fusion
  14.7 70.9 %all-gather.2.cloned.1.call-done = bf16[8,64,4096]{2,1,0:T(8,128)(2,1)} async-done(((bf16[1,64,4096]{2,1,0:T(8,128)(2,1)}), bf16[8,64,4096]{2,1,0:T(8,128)(2,1)}) %all-gather.2.cloned.1.call-update) | async-done | bytes 4194320 | tf_op jit(solution)/shard_map/all_gather | solution.py:33
  85.6 2.9 %gather_fusion = bf16[6,64,4096]{2,1,0:T(8,128)(2,1)S(1)} fusion(bf16[8,64,4096]{2,1,0:T(8,128)(2,1)} %all-gather.2.cloned.1.call-done, s32[1024]{0:T(1024)S(1)} %pad_clamp_fusion), kind=kCustom, calls=%fused_computation | custom fusion | bytes 6291480 | tf_op jit(solution)/shard_map/jit(_take)/gather | solution.py:39
  88.6 5.8 %fusion.9 = f32[64,6,128]{2,0,1:T(8,128)} fusion(bf16[6,128,4096]{2,1,0:T(8,128)(2,1)} %bitcast.29, bf16[6,64,4096]{2,1,0:T(8,128)(2,1)S(1)} %gather_fusion, pred[6]{0:T(512)(128)(4,1)S(1)} %get-tuple-element.5, pred[6]{0:T(512)(128)(4,1)S(1)} %get-tuple-element.7), kind=kOutput, calls=%fused_computation.12 | convolution fusion | flops 405798912 | bytes 9633804 | tf_op jit(solution)/shard_map/nrd,nbd->rnb/dot_general | solution.py:44
  94.4 0.0 all-reduce.2.cloned.1.call-update
  94.4 0.0 reduce-scatter.2.cloned.1.call-start
  94.5 12.1 %fusion.26 = f32[768,1024]{1,0:T(8,128)} fusion(bf16[768,4096]{1,0:T(8,128)(2,1)} %param.7, bf16[4096,1024]{1,0:T(8,128)(2,1)} %param.8), kind=kOutput, calls=%fused_computation.40 | convolution fusion | flops 6442450944 | bytes 17825792 | tf_op jit(solution)/shard_map/dot_general | solution.py:25
  106.6 0.0 copy-start
  106.6 0.0 copy-start.1
  106.6 0.0 reduce-scatter.2.cloned.1.call-update
  106.6 0.8 copy-done
  107.4 31.3 %all_gather.7 = bf16[8,64,512]{2,1,0:T(8,128)(2,1)S(1)} all-gather(bf16[1,64,512]{2,1,0:T(8,128)(2,1)S(1)} %copy-done), channel_id=1, replica_groups=mesh['groups'=2,'dp'=8,'tensor'=2] {'dp'}, dimensions={0}, use_global_device_ids=true | all-gather | bytes 589824 | tf_op jit(solution)/shard_map/all_gather | solution.py:34
  138.7 0.6 gather_fusion.1
  139.2 0.0 copy-done.1
  139.2 0.1 dynamic_slice.6
  139.3 0.1 fusion.19
  139.4 0.0 all-reduce.2.cloned.1.call-done
  139.4 1.8 %fusion.12 = f32[6,128,512]{2,1,0:T(8,128)S(1)} fusion(f32[64,6,128]{2,0,1:T(8,128)} %all-reduce.2.cloned.1.call-done, bf16[6,64,512]{2,1,0:T(8,128)(2,1)S(1)} %gather_fusion.1, pred[6]{0:T(512)(128)(4,1)S(1)} %get-tuple-element.5, pred[6]{0:T(512)(128)(4,1)S(1)} %get-tuple-element.7), kind=kOutput, calls=%fused_computation.13 | convolution fusion | flops 302383104 | bytes 2162700 | tf_op jit(solution)/shard_map/rnb,nrc->nbc/dot_general | solution.py:47
  141.2 0.0 reduce-scatter.2.cloned.1.call-done
  141.2 2.5 %fusion.6 = bf16[768,512]{1,0:T(8,128)(2,1)} fusion(f32[768,512]{1,0:T(8,128)} %reduce-scatter.2.cloned.1.call-done, f32[6,128,512]{2,1,0:T(8,128)S(1)} %fusion.12, pred[768]{0:T(1024)(128)(4,1)S(1)} %fusion.19), kind=kLoop, calls=%fused_computation.9 | loop fusion | flops 1179648 | bytes 3932928 | tf_op jit(solution)/shard_map/convert_element_type | solution.py:58
  (1 shorter events, 0.0 us)
Async XLA Ops:
  6.5 79.1 %all-gather.2.cloned.1.call-start = ((), (), s32[]{:S(2)}) async-start(), calls=%async_computation.2 | async-start | bytes 4718592 | tf_op jit(solution)/shard_map/all_gather | solution.py:33
  7.3 132.2 %all-reduce.2.cloned.1.call-start = ((), (), s32[]{:S(2)}) async-start(), calls=%async_computation.3 | async-start | bytes 393216 | tf_op jit(solution)/shard_map/psum | solution.py:46
  94.4 46.8 %reduce-scatter.2.cloned.1.call-start = ((), (), s32[]{:S(2)}) async-start(), calls=%async_computation.1 | async-start | bytes 4718592 | tf_op jit(solution)/shard_map/reduce_scatter | solution.py:54
  106.6 0.8 copy-start
  106.6 32.7 %copy-start.1 = (s32[48]{0:T(128)S(1)}, s32[48]{0:T(128)}, u32[]{:S(2)}) copy-start(s32[48]{0:T(128)} %param.13) | copy-start | bytes 580
Sparse Core Ops, SparseCore 0:
  9.5 76.0 all-gather.1
  94.5 16.3 all-reduce.1
  113.1 12.0 reduce-scatter.1
where the time goes:
time: 151 us; the launch traced here: 150 us
  waiting for transfers between devices  71.7 us (47%)
  blocking collectives  31.3 us (21%)
  matrix products  19.7 us (13%)
  between operations  13.2 us (9%)
  other arithmetic  8.4 us (6%)
  local copies, waits for them, and re-layouts  6.03 us (4%)
    all_gather x1, waiting for transfers between devices, per_device(): lax.all_gather(adapter_down_weight, 'dp', axis=0, tiled=True)  70.9 us
    all_gather x1, blocking collectives, per_device(): lax.all_gather(adapter_up_weight, 'dp', axis=0, tiled=True)  31.3 us
    dot_general x1, matrix products, per_device(): jnp.dot(tokens, key_projection_weight, preferred_element_type=jnp.float32)  12.1 us
    dot_general x1, matrix products, per_device(): jnp.einsum('nrd,nbd->rnb', new_down, token_blocks, preferred_element_type...  5.82 us
    gather x1, other arithmetic, per_device(): block_pool_index = adapter_pool_index[block_adapter_index[:, 0]]  5.7 us
  transfers between devices with their start and end apart: 3, of which 1 were waited for; matrix products, arithmetic and copies ran while one was open for 15% of the time, Pallas kernels for 0%

commit v1 on v0

v1 whole, which is shorter than its diff:
```python
import functools

import jax
import jax.numpy as jnp
from jax import lax
from jax.experimental import pallas as pl
from jax.experimental.pallas import tpu as pltpu
from jax.sharding import PartitionSpec as P

ADAPTER_RANK = 64
BLK = 128
VMEM_LIMIT = 48 * 1024 * 1024
SWAP = [(0, 1), (1, 0)]
NT = (((1,), (1,)), ((), ()))
TN = (((0,), (0,)), ((), ()))


def params():
    return pltpu.CompilerParams(
        dimension_semantics=("arbitrary",), vmem_limit_bytes=VMEM_LIMIT
    )


def base_kernel(place, tokens_ref, weight_ref, out_ref):
    @pl.when(pl.program_id(0) == 0)
    def _():
        out_ref[...] = jnp.zeros_like(out_ref)

    out_ref[...] += jnp.dot(
        tokens_ref[...], weight_ref[...], preferred_element_type=jnp.float32
    )


def base_half(place, tokens, weight, other):
    rows, width = tokens.shape
    half = weight.shape[1] // 2
    depth = 1024
    return pl.pallas_call(
        base_kernel,
        grid_spec=pltpu.PrefetchScalarGridSpec(
            num_scalar_prefetch=1,
            grid=(width // depth,),
            in_specs=[
                pl.BlockSpec((rows, depth), lambda k, place: (0, k)),
                pl.BlockSpec(
                    (depth, half), lambda k, place: (k, 1 - place[2] if other else place[2])
                ),
            ],
            out_specs=pl.BlockSpec((rows, half), lambda k, place: (0, 0)),
        ),
        out_shape=jax.ShapeDtypeStruct((rows, half), jnp.float32),
        compiler_params=params(),
        cost_estimate=pl.CostEstimate(
            flops=2 * rows * width * half,
            bytes_accessed=2 * rows * width + 2 * width * half + 4 * rows * half,
            transcendentals=0,
        ),
    )(place, tokens, weight)


def own_slot(place, pool_index, adapter_index):
    blocks = pl.num_programs(0)
    return pool_index[adapter_index[place[1] * blocks + pl.program_id(0)]]


def pool_of(place, step, other):
    depth = place[1] // 2
    column = place[1] - 2 * depth
    level = lax.rem(depth + 4 - step, 4)
    return 2 * level + (1 - column if other else column)


def half_of(place, kind):
    return {"a": 0, "b": 1, "own": place[0], "far": 1 - place[0]}[kind]


def shrink_kernel(pieces, has_prior, place, pool_index, adapter_index, tokens_ref, *refs):
    piece_refs, out_ref = refs[: len(pieces)], refs[-1]
    width = tokens_ref.shape[1] // 2
    slot = own_slot(place, pool_index, adapter_index)
    out_ref[...] = refs[-2][...] if has_prior else jnp.zeros_like(out_ref)
    for (step, other, kind), piece_ref in zip(pieces, piece_refs):

        @pl.when(slot == pool_of(place, step, other))
        def _(kind=kind, piece_ref=piece_ref):
            start = pl.multiple_of(half_of(place, kind) * width, width)
            out_ref[...] += lax.dot_general(
                piece_ref[:, :width],
                tokens_ref[:, pl.ds(start, width)],
                NT,
                preferred_element_type=jnp.float32,
            )


def shrink_sums(scalars, tokens, pieces, prior=None):
    rows, width = tokens.shape
    blocks = rows // BLK
    rank = ADAPTER_RANK
    block = pl.BlockSpec((rank, BLK), lambda b, *_: (0, b))
    specs = [
        pl.BlockSpec((rank, wide), functools.partial(lambda at, b, *_: (0, at), at))
        for _, at, wide, _ in pieces
    ]
    has_prior = prior is not None
    return pl.pallas_call(
        functools.partial(shrink_kernel, [name for name, *_ in pieces], has_prior),
        grid_spec=pltpu.PrefetchScalarGridSpec(
            num_scalar_prefetch=len(scalars),
            grid=(blocks,),
            in_specs=[pl.BlockSpec((BLK, width), lambda b, *_: (b, 0))]
            + specs
            + ([block] if has_prior else []),
            out_specs=block,
        ),
        out_shape=jax.ShapeDtypeStruct((rank, rows), jnp.float32),
        compiler_params=params(),
        cost_estimate=pl.CostEstimate(
            flops=8 * rows * width * rank,
            bytes_accessed=2 * rows * width + len(pieces) * rank * width,
            transcendentals=0,
        ),
    )(*scalars, tokens, *[piece[-1] for piece in pieces], *([prior] if has_prior else []))


def final_kernel(
    pieces, place, pool_index, adapter_index, live, mine_ref, far_ref, sum_ref, far_sum_ref, *refs
):
    piece_refs, out_ref, up_ref = refs[: len(pieces)], refs[-2], refs[-1]
    rank, half = piece_refs[0].shape
    slot = own_slot(place, pool_index, adapter_index)
    for (step, other, kind), piece_ref in zip(pieces, piece_refs):

        @pl.when(slot == pool_of(place, step, other))
        def _(kind=kind, piece_ref=piece_ref):
            start = pl.multiple_of(half_of(place, kind) * half, half)
            for part in range(3):
                up_ref[part * rank : (part + 1) * rank, pl.ds(start, half)] = piece_ref[...]

    total = sum_ref[...] + far_sum_ref[...]
    high = total.astype(jnp.bfloat16)
    rest = total - high.astype(jnp.float32)
    middle = rest.astype(jnp.bfloat16)
    low = (rest - middle.astype(jnp.float32)).astype(jnp.bfloat16)
    delta = lax.dot_general(
        jnp.concatenate([high, middle, low], axis=0),
        up_ref[...],
        TN,
        preferred_element_type=jnp.float32,
    )
    blocks = pl.num_programs(0)
    fill = live[place[1] * blocks + pl.program_id(0)]
    row = lax.broadcasted_iota(jnp.int32, out_ref.shape, 0)
    keys = mine_ref[...] + far_ref[...] + delta
    out_ref[...] = jnp.where(row < fill, keys, 0.0).astype(out_ref.dtype)


def final_keys(scalars, mine, far, sums, far_sums, pieces):
    rows, half = mine.shape
    rank = ADAPTER_RANK
    tile = pl.BlockSpec((BLK, half), lambda b, *_: (b, 0))
    block = pl.BlockSpec((rank, BLK), lambda b, *_: (0, b))
    specs = [
        pl.BlockSpec((rank, half // 2), functools.partial(lambda at, b, *_: (0, at), at))
        for _, at, _ in pieces
    ]
    return pl.pallas_call(
        functools.partial(final_kernel, [name for name, _, _ in pieces]),
        grid_spec=pltpu.PrefetchScalarGridSpec(
            num_scalar_prefetch=len(scalars),
            grid=(rows // BLK,),
            in_specs=[tile, tile, block, block] + specs,
            out_specs=tile,
            scratch_shapes=[pltpu.VMEM((3 * rank, half), jnp.bfloat16)],
        ),
        out_shape=jax.ShapeDtypeStruct((rows, half), jnp.bfloat16),
        compiler_params=params(),
        cost_estimate=pl.CostEstimate(
            flops=6 * rows * half * rank, bytes_accessed=10 * rows * half, transcendentals=0
        ),
    )(*scalars, mine, far, sums, far_sums, *[array for _, _, array in pieces])


def per_device_planes(
    tokens,
    key_projection_weight,
    adapter_down_weight,
    adapter_up_weight,
    adapter_pool_index,
    block_adapter_index,
    block_live_tokens,
):
    place = jnp.stack(
        [lax.axis_index("groups"), lax.axis_index("dp"), lax.axis_index("tensor")]
    ).astype(jnp.int32)
    down, up = adapter_down_weight[0], adapter_up_weight[0]
    width, half = down.shape[1] // 2, up.shape[1] // 2
    piece = width + half
    own = jnp.concatenate([down[:, :width], up[:, :half], down[:, width:], up[:, half:]], axis=1)
    first = lax.axis_index("groups") == 0
    own_half = jnp.where(first, own[:, :piece], own[:, piece:])

    def ring(array, step):
        pairs = [(2 * z + y, 2 * ((z + step) % 4) + y) for z in range(4) for y in range(2)]
        return lax.ppermute(array, "dp", pairs)

    def over_y(array):
        return lax.ppermute(array, "dp", [(i, i ^ 1) for i in range(8)])

    def over_x(array):
        return lax.ppermute(array, "groups", SWAP)

    def over_cores(array):
        return lax.ppermute(array, "tensor", SWAP)

    z1 = ring(own_half, 1)
    y0 = over_y(own)
    z3 = ring(own_half, -1)
    x1 = over_x(z1)
    y1 = over_y(z1)
    z2a = ring(z1, 1)
    x3 = over_x(z3)
    y3 = over_y(z3)
    z2b = ring(x1, 1)
    y2a = over_y(z2a)
    x1y = over_x(y1)
    x3y = over_x(y3)
    y2b = over_y(z2b)

    early = [
        ((0, False, "a"), 0, width, down),
        ((0, False, "b"), 1, width, down),
        ((0, True, "a"), 0, piece, y0),
        ((0, True, "b"), 1, piece, y0),
        ((1, False, "own"), 0, piece, z1),
        ((1, False, "far"), 0, piece, x1),
        ((3, False, "own"), 0, piece, z3),
        ((3, False, "far"), 0, piece, x3),
        ((2, False, "own"), 0, piece, z2a),
        ((1, True, "own"), 0, piece, y1),
        ((3, True, "own"), 0, piece, y3),
    ]
    late = [
        ((2, False, "far"), 0, piece, z2b),
        ((1, True, "far"), 0, piece, x1y),
        ((3, True, "far"), 0, piece, x3y),
        ((2, True, "own"), 0, piece, y2a),
        ((2, True, "far"), 0, piece, y2b),
    ]
    at_up = width // half
    ups = [
        ((0, False, "a"), 0, up),
        ((0, False, "b"), 1, up),
        ((0, True, "a"), at_up, y0),
        ((0, True, "b"), 2 * at_up + 1, y0),
    ] + [(name, at_up, array) for name, _, _, array in (early + late)[4:]]

    adapter_index = block_adapter_index[:, 0]
    scalars = (place, adapter_pool_index, adapter_index)
    base_far = over_cores(base_half(place, tokens, key_projection_weight, True))
    base_mine = base_half(place, tokens, key_projection_weight, False)
    sums = shrink_sums(scalars, tokens, early)
    sums = shrink_sums(scalars, tokens, late, sums)
    far_sums = over_cores(sums)
    return final_keys(
        (*scalars, block_live_tokens), base_mine, base_far, sums, far_sums, ups
    )


def per_device_gathered(
    tokens,
    key_projection_weight,
    adapter_down_weight,
    adapter_up_weight,
    adapter_pool_index,
    block_adapter_index,
    block_live_tokens,
):
    rows = tokens.shape[0]
    blocks = rows // BLK
    first_block = lax.axis_index("dp") * blocks
    slots = lax.dynamic_slice_in_dim(
        adapter_pool_index[block_adapter_index[:, 0]], first_block, blocks
    )
    fill = lax.dynamic_slice_in_dim(block_live_tokens, first_block, blocks)
    base_part = jnp.dot(tokens, key_projection_weight, preferred_element_type=jnp.float32)
    down = lax.all_gather(adapter_down_weight, "dp", axis=0, tiled=True)
    up = lax.all_gather(adapter_up_weight, "dp", axis=0, tiled=True)
    token_blocks = tokens.reshape(blocks, BLK, tokens.shape[1])
    shrink = jnp.einsum(
        "nrd,nbd->rnb",
        jnp.take(down, slots, axis=0),
        token_blocks,
        preferred_element_type=jnp.float32,
    )
    shrink = lax.psum(shrink.reshape(ADAPTER_RANK, rows), "tensor")
    delta = jnp.einsum(
        "rnb,nrc->nbc",
        shrink.reshape(ADAPTER_RANK, blocks, BLK),
        jnp.take(up, slots, axis=0).astype(jnp.float32),
        precision=lax.Precision.HIGHEST,
        preferred_element_type=jnp.float32,
    )
    base = lax.psum_scatter(base_part, "tensor", scatter_dimension=1, tiled=True)
    mask = jnp.arange(BLK, dtype=jnp.int32)[None, :] < fill[:, None]
    keys = base + delta.reshape(rows, base.shape[1])
    return jnp.where(mask.reshape(rows, 1), keys, 0.0).astype(jnp.bfloat16)


def solution(mesh):
    in_specs = (
        P(("groups", "dp"), "tensor"),
        P("tensor", None),
        P("dp", None, "tensor"),
        P("dp", None, "tensor"),
        P(),
        P("groups", None),
        P("groups"),
    )
    out_specs = P(("groups", "dp"), "tensor")
    planes = dict(mesh.shape) == {"groups": 2, "dp": 8, "tensor": 2}
    return jax.shard_map(
        per_device_planes if planes else per_device_gathered,
        mesh=mesh,
        in_specs=in_specs,
        out_specs=out_specs,
        check_vma=False,
    )
```

time: 151 us -> 80.6 us (0.53)
  waiting for transfers between devices: 71.7 us -> 27.4 us
  Pallas kernels: 0 us -> 32.9 us
  blocking collectives: 31.3 us -> 0 us
  matrix products: 19.7 us -> 0 us
  starting transfers between devices: 0.08 us -> 16.6 us
  between operations: 13.2 us -> 0.15 us
  other arithmetic: 8.4 us -> 0.18 us
  local copies, waits for them, and re-layouts: 6.03 us -> 3.04 us
    all_gather x1 -> x0, waiting for transfers between devices: 70.9 us -> none  [per_device(): lax.all_gather(adapter_down_weight, 'dp', axis=0, tiled=True)]
    pallas_call x0 -> x5, Pallas kernels: none -> 32.9 us  [the longest x2 14.5 us: base_half(): pl.pallas_call(base_kernel, grid_spec=pltpu.PrefetchScalarGridSpec(num_sc...]
    all_gather x1 -> x0, blocking collectives: 31.3 us -> none  [per_device(): lax.all_gather(adapter_up_weight, 'dp', axis=0, tiled=True)]
    ppermute x0 -> x15, waiting for transfers between devices: none -> 27.4 us  [the longest x5 14.8 us: over_y(): return lax.ppermute(array, 'dp', [(i, i ^ 1) for i in range(8)])]
    dot_general x3 -> x0, matrix products: 19.7 us -> none  [the longest x1 12.1 us: per_device(): jnp.dot(tokens, key_projection_weight, preferred_element_type=jnp.float32)]
    ppermute x0 -> x15, starting transfers between devices: none -> 16.6 us  [the longest x4 6.3 us: ring(): return lax.ppermute(array, 'dp', pairs)]
    gather x2 -> x0, other arithmetic: 5.71 us -> none  [the longest x1 5.7 us: per_device(): block_pool_index = adapter_pool_index[block_adapter_index[:, 0]]]
    gather x3 -> x0, local copies, waits for them, and re-layouts: 5.13 us -> none  [the longest x1 2.93 us: per_device(): jnp.take(down_matrix_block, pick_index, axis=0)]
  transfers between devices with their start and end apart: 3 -> 15, of which waited for: 1 -> 8; matrix products, arithmetic and copies ran while one was open for 15% -> 0% of each run, Pallas kernels for 0% -> 34%
where the time goes in v1:
time: 80.6 us; the launch traced here: 80.2 us
  Pallas kernels  32.9 us (41%)
  waiting for transfers between devices  27.4 us (34%)
  starting transfers between devices  16.6 us (21%)
  local copies, waits for them, and re-layouts  3.04 us (4%)
    ppermute x5, waiting for transfers between devices, over_y(): return lax.ppermute(array, 'dp', [(i, i ^ 1) for i in range(8)])  14.8 us
    pallas_call x2, Pallas kernels, base_half(): pl.pallas_call(base_kernel, grid_spec=pltpu.PrefetchScalarGridSpec(num_sc...  14.5 us
    pallas_call x2, Pallas kernels, shrink_sums(): pl.pallas_call(functools.partial(shrink_kernel, [name for name, *_ in pie...  12.4 us
    ppermute x4, waiting for transfers between devices, over_x(): return lax.ppermute(array, 'groups', SWAP)  7.89 us
    ppermute x4, starting transfers between devices, ring(): return lax.ppermute(array, 'dp', pairs)  6.3 us
    pallas_call x1, Pallas kernels, final_keys(): pl.pallas_call(functools.partial(final_kernel, [name for name, _, _ in pi...  5.98 us
    ppermute x5, starting transfers between devices, over_y(): return lax.ppermute(array, 'dp', [(i, i ^ 1) for i in range(8)])  5.79 us
    ppermute x4, waiting for transfers between devices, ring(): return lax.ppermute(array, 'dp', pairs)  4.71 us
  transfers between devices with their start and end apart: 15, of which 8 were waited for; matrix products, arithmetic and copies ran while one was open for 0% of the time, Pallas kernels for 34%

profile of v1, /device:TPU:0, one launch (start us, length us, event | category | flops | bytes accessed | tf_op | source)
XLA Modules:
  0.0 80.2 jit_solution(947427930412115550)
XLA Ops:
  0.0 1.1 %fusion = (bf16[64,2048]{1,0:T(8,128)(2,1)S(1)}, bf16[64,2048]{1,0:T(8,128)(2,1)S(1)}) fusion(bf16[64,4096]{1,0:T(8,128)(2,1)} %bitcast.6), kind=kLoop, calls=%fused_computation.3 | loop fusion | bytes 1048576 | tf_op jit(solution)/shard_map/slice | solution.py:198
  1.1 0.8 fusion.1
  1.9 0.1 maximum_select_fusion
  1.9 3.1 %collective-permute-start.1 = (bf16[64,2304]{1,0:T(8,128)(2,1)S(1)}, bf16[64,2304]{1,0:T(8,128)(2,1)S(1)}, u32[]{:S(2)}, u32[]{:S(2)}) collective-permute-start(bf16[64,2304]{1,0:T(8,128)(2,1)S(1)} %maximum_select_fusion), channel_id=1, source_target_pairs={{0,4},{2,6},{4,8},{6,10},{8,12},{10,14},{12,0},{14,2},{1,5},{3,7},... | collective-permute-start | bytes 884744 | tf_op jit(solution)/shard_map/ppermute | solution.py:204
  5.0 2.1 %collective-permute-start.6 = (bf16[64,2304]{1,0:T(8,128)(2,1)S(1)}, bf16[64,2304]{1,0:T(8,128)(2,1)S(1)}, u32[]{:S(2)}, u32[]{:S(2)}) collective-permute-start(bf16[64,2304]{1,0:T(8,128)(2,1)S(1)} %maximum_select_fusion), channel_id=1, source_target_pairs={{0,12},{2,14},{4,0},{6,2},{8,4},{10,6},{12,8},{14,10},{1,13},{3,15... | collective-permute-start | bytes 884744 | tf_op jit(solution)/shard_map/ppermute | solution.py:204
  7.1 0.1 pad_add_fusion.place
  7.2 7.2 %shard_map.74 = f32[768,512]{1,0:T(8,128)S(1)} custom-call(s32[3]{0:T(128)S(1)} %pad_add_fusion.place, bf16[768,4096]{1,0:T(8,128)(2,1)} %tokens_ref.7, bf16[4096,1024]{1,0:T(8,128)(2,1)} %weight_ref.3), custom_call_target="tpu_custom_call" | custom-call | flops 3221225472 | bytes 12058624 | tf_op jit(solution)/shard_map/pallas_call | solution.py:38
  14.4 0.0 copy-start
  14.4 0.0 copy-start.2
  14.4 0.0 copy-start.3
  14.4 0.1 collective-permute-start
  14.5 0.4 collective-permute-done.1.refs_4_
  14.9 1.7 %collective-permute-start.2 = (bf16[64,2304]{1,0:T(8,128)(2,1)S(1)}, bf16[64,2304]{1,0:T(8,128)(2,1)S(1)}, u32[]{:S(2)}, u32[]{:S(2)}) collective-permute-start(bf16[64,2304]{1,0:T(8,128)(2,1)S(1)} %collective-permute-done.1.refs_4_), channel_id=1, source_target_pairs={{0,16},{16,0},{1,17},{17,1},{2,18},{18,2},{3,19},{19,3},{4,20},{20... | collective-permute-start | bytes 884744 | tf_op jit(solution)/shard_map/ppermute | solution.py:210
  16.6 1.5 %collective-permute-start.4 = (bf16[64,2304]{1,0:T(8,128)(2,1)S(1)}, bf16[64,2304]{1,0:T(8,128)(2,1)S(1)}, u32[]{:S(2)}, u32[]{:S(2)}) collective-permute-start(bf16[64,2304]{1,0:T(8,128)(2,1)S(1)} %collective-permute-done.1.refs_4_), channel_id=1, source_target_pairs={{0,2},{2,0},{4,6},{6,4},{8,10},{10,8},{12,14},{14,12},{1,3},{3,1},... | collective-permute-start | bytes 884744 | tf_op jit(solution)/shard_map/ppermute | solution.py:207
  18.2 0.6 collective-permute-start.12
  18.8 1.0 %collective-permute-done.6.refs_6_ = bf16[64,2304]{1,0:T(8,128)(2,1)S(1)} collective-permute-done((bf16[64,2304]{1,0:T(8,128)(2,1)S(1)}, bf16[64,2304]{1,0:T(8,128)(2,1)S(1)}, u32[]{:S(2)}, u32[]{:S(2)}) %collective-permute-start.6) | collective-permute-done | bytes 294944 | tf_op jit(solution)/shard_map/ppermute | solution.py:204
  19.8 1.1 %collective-permute-start.9 = (bf16[64,2304]{1,0:T(8,128)(2,1)S(1)}, bf16[64,2304]{1,0:T(8,128)(2,1)S(1)}, u32[]{:S(2)}, u32[]{:S(2)}) collective-permute-start(bf16[64,2304]{1,0:T(8,128)(2,1)S(1)} %collective-permute-done.1.refs_4_), channel_id=1, source_target_pairs={{0,4},{2,6},{4,8},{6,10},{8,12},{10,14},{12,0},{14,2},{1,5},{3,7},... | collective-permute-start | bytes 884744 | tf_op jit(solution)/shard_map/ppermute | solution.py:204
  20.9 3.0 %collective-permute-done.2.refs_5_ = bf16[64,2304]{1,0:T(8,128)(2,1)S(1)} collective-permute-done((bf16[64,2304]{1,0:T(8,128)(2,1)S(1)}, bf16[64,2304]{1,0:T(8,128)(2,1)S(1)}, u32[]{:S(2)}, u32[]{:S(2)}) %collective-permute-start.2) | collective-permute-done | bytes 294944 | tf_op jit(solution)/shard_map/ppermute | solution.py:210
  23.9 1.7 %collective-permute-start.7 = (bf16[64,2304]{1,0:T(8,128)(2,1)S(1)}, bf16[64,2304]{1,0:T(8,128)(2,1)S(1)}, u32[]{:S(2)}, u32[]{:S(2)}) collective-permute-start(bf16[64,2304]{1,0:T(8,128)(2,1)S(1)} %collective-permute-done.6.refs_6_), channel_id=1, source_target_pairs={{0,2},{2,0},{4,6},{6,4},{8,10},{10,8},{12,14},{14,12},{1,3},{3,1},... | collective-permute-start | bytes 884744 | tf_op jit(solution)/shard_map/ppermute | solution.py:207
  25.6 0.9 %collective-permute-done.4.refs_9_ = bf16[64,2304]{1,0:T(8,128)(2,1)S(1)} collective-permute-done((bf16[64,2304]{1,0:T(8,128)(2,1)S(1)}, bf16[64,2304]{1,0:T(8,128)(2,1)S(1)}, u32[]{:S(2)}, u32[]{:S(2)}) %collective-permute-start.4) | collective-permute-done | bytes 294944 | tf_op jit(solution)/shard_map/ppermute | solution.py:207
  26.6 0.6 collective-permute-start.13
  27.1 3.3 %collective-permute-done.9.refs_8_ = bf16[64,2304]{1,0:T(8,128)(2,1)S(1)} collective-permute-done((bf16[64,2304]{1,0:T(8,128)(2,1)S(1)}, bf16[64,2304]{1,0:T(8,128)(2,1)S(1)}, u32[]{:S(2)}, u32[]{:S(2)}) %collective-permute-start.9) | collective-permute-done | bytes 294944 | tf_op jit(solution)/shard_map/ppermute | solution.py:204
  30.4 0.0 collective-permute-start.3
  30.4 13.8 %collective-permute-done.7.refs_10_ = bf16[64,2304]{1,0:T(8,128)(2,1)S(1)} collective-permute-done((bf16[64,2304]{1,0:T(8,128)(2,1)S(1)}, bf16[64,2304]{1,0:T(8,128)(2,1)S(1)}, u32[]{:S(2)}, u32[]{:S(2)}) %collective-permute-start.7) | collective-permute-done | bytes 294944 | tf_op jit(solution)/shard_map/ppermute | solution.py:207
  44.3 1.5 %collective-permute-start.10 = (bf16[64,2304]{1,0:T(8,128)(2,1)S(1)}, bf16[64,2304]{1,0:T(8,128)(2,1)S(1)}, u32[]{:S(2)}, u32[]{:S(2)}) collective-permute-start(bf16[64,2304]{1,0:T(8,128)(2,1)S(1)} %collective-permute-done.9.refs_8_), channel_id=1, source_target_pairs={{0,2},{2,0},{4,6},{6,4},{8,10},{10,8},{12,14},{14,12},{1,3},{3,1},... | collective-permute-start | bytes 884744 | tf_op jit(solution)/shard_map/ppermute | solution.py:207
  45.8 0.0 collective-permute-done.13.refs_7_
  45.8 0.5 collective-permute-start.5
  46.3 0.0 collective-permute-done.12.refs_2_.refs_3_
  46.3 1.5 %collective-permute-start.8 = (bf16[64,2304]{1,0:T(8,128)(2,1)S(1)}, bf16[64,2304]{1,0:T(8,128)(2,1)S(1)}, u32[]{:S(2)}, u32[]{:S(2)}) collective-permute-start(bf16[64,2304]{1,0:T(8,128)(2,1)S(1)} %collective-permute-done.7.refs_10_), channel_id=1, source_target_pairs={{0,16},{16,0},{1,17},{17,1},{2,18},{18,2},{3,19},{19,3},{4,20},{20... | collective-permute-start | bytes 884744 | tf_op jit(solution)/shard_map/ppermute | solution.py:210
  47.8 0.0 collective-permute-done.3.refs_0_.refs_11_
  47.8 0.5 collective-permute-start.11
  48.3 0.0 copy-done.2
  48.3 6.4 %shard_map.75.refs_5_ = f32[64,768]{1,0:T(8,128)S(1)} custom-call(s32[3]{0:T(128)S(1)} %pad_add_fusion.place, s32[8]{0:T(128)S(1)} %copy-done.2, s32[48]{0:T(128)S(1)} %bitcast.12, bf16[768,4096]{1,0:T(8,128)(2,1)} %tokens_ref.7, bf16[64,4096]{1,0:T(8,128)(2,1)S(1)} %bitcast.7, bf16[64,4096]{1,0:T(8,128)(2,1)S(1)} %bitcast.8, ...), custom_call_target="tpu_custom_call" | custom-call | flops 1610612736 | bytes 9175040 | tf_op jit(solution)/shard_map/pallas_call | solution.py:105
  54.7 0.0 collective-permute-done.10.refs_3_.refs_14_
  54.7 1.0 %collective-permute-done.5.refs_1_.refs_12_ = bf16[64,2304]{1,0:T(8,128)(2,1)S(1)} collective-permute-done((bf16[64,2304]{1,0:T(8,128)(2,1)S(1)}, bf16[64,2304]{1,0:T(8,128)(2,1)S(1)}, u32[]{:S(2)}, u32[]{:S(2)}) %collective-permute-start.5) | collective-permute-done | bytes 294944 | tf_op jit(solution)/shard_map/ppermute | solution.py:210
  55.7 3.9 %collective-permute-done.8.refs_2_.refs_13_ = bf16[64,2304]{1,0:T(8,128)(2,1)S(1)} collective-permute-done((bf16[64,2304]{1,0:T(8,128)(2,1)S(1)}, bf16[64,2304]{1,0:T(8,128)(2,1)S(1)}, u32[]{:S(2)}, u32[]{:S(2)}) %collective-permute-start.8) | collective-permute-done | bytes 294944 | tf_op jit(solution)/shard_map/ppermute | solution.py:210
  59.6 0.0 collective-permute-done.11.refs_4_.refs_15_
  59.6 6.1 %shard_map.76.sum_ref = f32[64,768]{1,0:T(8,128)S(1)} custom-call(s32[3]{0:T(128)S(1)} %pad_add_fusion.place, s32[8]{0:T(128)S(1)} %copy-done.2, s32[48]{0:T(128)S(1)} %bitcast.13, bf16[768,4096]{1,0:T(8,128)(2,1)} %tokens_ref.7, bf16[64,2304]{1,0:T(8,128)(2,1)S(1)} %collective-permute-done.3.refs_0_.refs_11_, ...), custom_call_target="tpu_custom_call" | custom-call | flops 1610612736 | bytes 7602176 | tf_op jit(solution)/shard_map/pallas_call | solution.py:105
  65.7 0.0 copy-start.1
  65.7 0.0 copy-start.4
  65.7 0.1 collective-permute-start.14
  65.8 7.2 %shard_map.73.mine_ref = f32[768,512]{1,0:T(8,128)S(1)} custom-call(s32[3]{0:T(128)S(1)} %pad_add_fusion.place, bf16[768,4096]{1,0:T(8,128)(2,1)} %tokens_ref.7, bf16[4096,1024]{1,0:T(8,128)(2,1)} %weight_ref.3), custom_call_target="tpu_custom_call" | custom-call | flops 3221225472 | bytes 12058624 | tf_op jit(solution)/shard_map/pallas_call | solution.py:38
  73.0 0.0 collective-permute-done.14.far_sum_ref
  73.0 0.0 collective-permute-done.far_ref
  73.1 0.0 copy-start.5
  73.1 1.2 %copy-done.5 = f32[768,512]{1,0:T(8,128)} copy-done((f32[768,512]{1,0:T(8,128)}, f32[768,512]{1,0:T(8,128)S(1)}, u32[]{:S(2)}) %copy-start.5) | copy-done | bytes 1572888
  74.2 0.0 copy-done.1
  74.2 6.0 %shard_map.77 = bf16[768,512]{1,0:T(8,128)(2,1)} custom-call(s32[3]{0:T(128)S(1)} %pad_add_fusion.place, s32[8]{0:T(128)S(1)} %copy-done.2, s32[48]{0:T(128)S(1)} %bitcast.14, s32[48]{0:T(128)S(1)} %copy-done.4, f32[768,512]{1,0:T(8,128)S(1)} %shard_map.73.mine_ref, f32[768,512]{1,0:T(8,128)} %copy-done.5, f32[64,768]{1,0:T(8,128)S(1)} %shard_map.76.sum_ref, ...), custom_call_target="tpu_custom_call" | custom-call | flops 150994944 | bytes 3932160 | tf_op jit(solution)/shard_map/pallas_call | solution.py:166
  (4 shorter events, 0.0 us)
Async XLA Ops:
  1.9 13.0 %collective-permute-start.1 = (bf16[64,2304]{1,0:T(8,128)(2,1)S(1)}, bf16[64,2304]{1,0:T(8,128)(2,1)S(1)}, u32[]{:S(2)}, u32[]{:S(2)}) collective-permute-start(bf16[64,2304]{1,0:T(8,128)(2,1)S(1)} %maximum_select_fusion), channel_id=1, source_target_pairs={{0,4},{2,6},{4,8},{6,10},{8,12},{10,14},{12,0},{14,2},{1,5},{3,7},... | collective-permute-start | bytes 884744 | tf_op jit(solution)/shard_map/ppermute | solution.py:204
  5.0 14.8 %collective-permute-start.6 = (bf16[64,2304]{1,0:T(8,128)(2,1)S(1)}, bf16[64,2304]{1,0:T(8,128)(2,1)S(1)}, u32[]{:S(2)}, u32[]{:S(2)}) collective-permute-start(bf16[64,2304]{1,0:T(8,128)(2,1)S(1)} %maximum_select_fusion), channel_id=1, source_target_pairs={{0,12},{2,14},{4,0},{6,2},{8,4},{10,6},{12,8},{14,10},{1,13},{3,15... | collective-permute-start | bytes 884744 | tf_op jit(solution)/shard_map/ppermute | solution.py:204
  14.4 33.9 %copy-start = (bf16[1,64,4096]{2,1,0:T(8,128)(2,1)S(1)}, bf16[1,64,4096]{2,1,0:T(8,128)(2,1)}, u32[]{:S(2)}) copy-start(bf16[1,64,4096]{2,1,0:T(8,128)(2,1)} %param.9) | copy-start | bytes 1572868
  14.4 33.9 %copy-start.2 = (s32[8]{0:T(128)S(1)}, s32[8]{0:T(128)}, u32[]{:S(2)}) copy-start(s32[8]{0:T(128)} %pool_index.5) | copy-start | bytes 100
  14.4 33.9 %copy-start.3 = (s32[48,1]{0,1:T(1,128)S(1)}, s32[48,1]{0,1:T(1,128)}, u32[]{:S(2)}) copy-start(s32[48,1]{0,1:T(1,128)} %param.12) | copy-start | bytes 580
  14.4 58.6 %collective-permute-start = (f32[768,512]{1,0:T(8,128)S(1)}, f32[768,512]{1,0:T(8,128)S(1)}, u32[]{:S(2)}, u32[]{:S(2)}) collective-permute-start(f32[768,512]{1,0:T(8,128)S(1)} %shard_map.74), channel_id=1, source_target_pairs={{0,1},{1,0},{2,3},{3,2},{4,5},{5,4},{6,7},{7,6},{8,9},{9,8},{10,11... | collective-permute-start | bytes 4718600 | tf_op jit(solution)/shard_map/ppermute | solution.py:213
  14.9 9.0 %collective-permute-start.2 = (bf16[64,2304]{1,0:T(8,128)(2,1)S(1)}, bf16[64,2304]{1,0:T(8,128)(2,1)S(1)}, u32[]{:S(2)}, u32[]{:S(2)}) collective-permute-start(bf16[64,2304]{1,0:T(8,128)(2,1)S(1)} %collective-permute-done.1.refs_4_), channel_id=1, source_target_pairs={{0,16},{16,0},{1,17},{17,1},{2,18},{18,2},{3,19},{19,3},{4,20},{20... | collective-permute-start | bytes 884744 | tf_op jit(solution)/shard_map/ppermute | solution.py:210
  16.6 9.9 %collective-permute-start.4 = (bf16[64,2304]{1,0:T(8,128)(2,1)S(1)}, bf16[64,2304]{1,0:T(8,128)(2,1)S(1)}, u32[]{:S(2)}, u32[]{:S(2)}) collective-permute-start(bf16[64,2304]{1,0:T(8,128)(2,1)S(1)} %collective-permute-done.1.refs_4_), channel_id=1, source_target_pairs={{0,2},{2,0},{4,6},{6,4},{8,10},{10,8},{12,14},{14,12},{1,3},{3,1},... | collective-permute-start | bytes 884744 | tf_op jit(solution)/shard_map/ppermute | solution.py:207
  18.2 28.1 %collective-permute-start.12 = (bf16[64,4608]{1,0:T(8,128)(2,1)S(1)}, bf16[64,4608]{1,0:T(8,128)(2,1)S(1)}, u32[]{:S(2)}, u32[]{:S(2)}) collective-permute-start(bf16[64,4608]{1,0:T(8,128)(2,1)S(1)} %pad_maximum_fusion), channel_id=1, source_target_pairs={{0,2},{2,0},{4,6},{6,4},{8,10},{10,8},{12,14},{14,12},{1,3},{3,1},... | collective-permute-start | bytes 1769480 | tf_op jit(solution)/shard_map/ppermute | solution.py:207
  19.8 10.6 %collective-permute-start.9 = (bf16[64,2304]{1,0:T(8,128)(2,1)S(1)}, bf16[64,2304]{1,0:T(8,128)(2,1)S(1)}, u32[]{:S(2)}, u32[]{:S(2)}) collective-permute-start(bf16[64,2304]{1,0:T(8,128)(2,1)S(1)} %collective-permute-done.1.refs_4_), channel_id=1, source_target_pairs={{0,4},{2,6},{4,8},{6,10},{8,12},{10,14},{12,0},{14,2},{1,5},{3,7},... | collective-permute-start | bytes 884744 | tf_op jit(solution)/shard_map/ppermute | solution.py:204
  23.9 20.3 %collective-permute-start.7 = (bf16[64,2304]{1,0:T(8,128)(2,1)S(1)}, bf16[64,2304]{1,0:T(8,128)(2,1)S(1)}, u32[]{:S(2)}, u32[]{:S(2)}) collective-permute-start(bf16[64,2304]{1,0:T(8,128)(2,1)S(1)} %collective-permute-done.6.refs_6_), channel_id=1, source_target_pairs={{0,2},{2,0},{4,6},{6,4},{8,10},{10,8},{12,14},{14,12},{1,3},{3,1},... | collective-permute-start | bytes 884744 | tf_op jit(solution)/shard_map/ppermute | solution.py:207
  26.6 19.2 %collective-permute-start.13 = (bf16[64,2304]{1,0:T(8,128)(2,1)S(1)}, bf16[64,2304]{1,0:T(8,128)(2,1)S(1)}, u32[]{:S(2)}, u32[]{:S(2)}) collective-permute-start(bf16[64,2304]{1,0:T(8,128)(2,1)S(1)} %collective-permute-done.6.refs_6_), channel_id=1, source_target_pairs={{0,16},{16,0},{1,17},{17,1},{2,18},{18,2},{3,19},{19,3},{4,20},{20... | collective-permute-start | bytes 884744 | tf_op jit(solution)/shard_map/ppermute | solution.py:210
  30.4 17.4 %collective-permute-start.3 = (bf16[64,2304]{1,0:T(8,128)(2,1)S(1)}, bf16[64,2304]{1,0:T(8,128)(2,1)S(1)}, u32[]{:S(2)}, u32[]{:S(2)}) collective-permute-start(bf16[64,2304]{1,0:T(8,128)(2,1)S(1)} %collective-permute-done.2.refs_5_), channel_id=1, source_target_pairs={{0,4},{2,6},{4,8},{6,10},{8,12},{10,14},{12,0},{14,2},{1,5},{3,7},... | collective-permute-start | bytes 884744 | tf_op jit(solution)/shard_map/ppermute | solution.py:204
  44.3 10.5 %collective-permute-start.10 = (bf16[64,2304]{1,0:T(8,128)(2,1)S(1)}, bf16[64,2304]{1,0:T(8,128)(2,1)S(1)}, u32[]{:S(2)}, u32[]{:S(2)}) collective-permute-start(bf16[64,2304]{1,0:T(8,128)(2,1)S(1)} %collective-permute-done.9.refs_8_), channel_id=1, source_target_pairs={{0,2},{2,0},{4,6},{6,4},{8,10},{10,8},{12,14},{14,12},{1,3},{3,1},... | collective-permute-start | bytes 884744 | tf_op jit(solution)/shard_map/ppermute | solution.py:207
  45.8 9.9 %collective-permute-start.5 = (bf16[64,2304]{1,0:T(8,128)(2,1)S(1)}, bf16[64,2304]{1,0:T(8,128)(2,1)S(1)}, u32[]{:S(2)}, u32[]{:S(2)}) collective-permute-start(bf16[64,2304]{1,0:T(8,128)(2,1)S(1)} %collective-permute-done.4.refs_9_), channel_id=1, source_target_pairs={{0,16},{16,0},{1,17},{17,1},{2,18},{18,2},{3,19},{19,3},{4,20},{20... | collective-permute-start | bytes 884744 | tf_op jit(solution)/shard_map/ppermute | solution.py:210
  46.3 13.3 %collective-permute-start.8 = (bf16[64,2304]{1,0:T(8,128)(2,1)S(1)}, bf16[64,2304]{1,0:T(8,128)(2,1)S(1)}, u32[]{:S(2)}, u32[]{:S(2)}) collective-permute-start(bf16[64,2304]{1,0:T(8,128)(2,1)S(1)} %collective-permute-done.7.refs_10_), channel_id=1, source_target_pairs={{0,16},{16,0},{1,17},{17,1},{2,18},{18,2},{3,19},{19,3},{4,20},{20... | collective-permute-start | bytes 884744 | tf_op jit(solution)/shard_map/ppermute | solution.py:210
  47.8 11.8 %collective-permute-start.11 = (bf16[64,2304]{1,0:T(8,128)(2,1)S(1)}, bf16[64,2304]{1,0:T(8,128)(2,1)S(1)}, u32[]{:S(2)}, u32[]{:S(2)}) collective-permute-start(bf16[64,2304]{1,0:T(8,128)(2,1)S(1)} %collective-permute-done.3.refs_0_.refs_11_), channel_id=1, source_target_pairs={{0,2},{2,0},{4,6},{6,4},{8,10},{10,8},{12,14},{14,12},{1,3},{3,1},... | collective-permute-start | bytes 884744 | tf_op jit(solution)/shard_map/ppermute | solution.py:207
  65.7 8.5 %copy-start.1 = (bf16[1,64,512]{2,1,0:T(8,128)(2,1)S(1)}, bf16[1,64,512]{2,1,0:T(8,128)(2,1)}, u32[]{:S(2)}) copy-start(bf16[1,64,512]{2,1,0:T(8,128)(2,1)} %param.10) | copy-start | bytes 196612
  65.7 8.5 %copy-start.4 = (s32[48]{0:T(128)S(1)}, s32[48]{0:T(128)}, u32[]{:S(2)}) copy-start(s32[48]{0:T(128)} %live.1) | copy-start | bytes 580
  65.7 7.3 %collective-permute-start.14 = (f32[64,768]{1,0:T(8,128)S(1)}, f32[64,768]{1,0:T(8,128)S(1)}, u32[]{:S(2)}, u32[]{:S(2)}) collective-permute-start(f32[64,768]{1,0:T(8,128)S(1)} %shard_map.76.sum_ref), channel_id=1, source_target_pairs={{0,1},{1,0},{2,3},{3,2},{4,5},{5,4},{6,7},{7,6},{8,9},{9,8},{10,11... | collective-permute-start | bytes 589832 | tf_op jit(solution)/shard_map/ppermute | solution.py:213
  73.1 1.2 %copy-start.5 = (f32[768,512]{1,0:T(8,128)}, f32[768,512]{1,0:T(8,128)S(1)}, u32[]{:S(2)}) copy-start(f32[768,512]{1,0:T(8,128)S(1)} %collective-permute-done.far_ref) | copy-start | bytes 4718596

commit v2 on v0

v2 whole, which is shorter than its diff:
```python
import functools

import jax
import jax.numpy as jnp
from jax import lax
from jax.experimental import pallas as pl
from jax.experimental.pallas import tpu as pltpu
from jax.sharding import PartitionSpec as P

ADAPTER_RANK = 64
BLK = 128
FAR_PARTS = 3
SWAP = [(0, 1), (1, 0)]
NT = (((1,), (1,)), ((), ()))
TN = (((0,), (0,)), ((), ()))


def kernel_params(mebibytes):
    return pltpu.CompilerParams(vmem_limit_bytes=mebibytes * 1024 * 1024)


def cost(flops, bytes_accessed):
    return pl.CostEstimate(flops=1, bytes_accessed=1, transcendentals=0)


def after(array, *others):
    return lax.optimization_barrier((array, *others))[0]


SMEM = pl.BlockSpec(memory_space=pltpu.SMEM)
VMEM = pl.BlockSpec(memory_space=pltpu.VMEM)
ANY = pl.BlockSpec(memory_space=pl.ANY)


def base_kernel(cuts, place, tokens, weight, *refs):
    *fars, mine, tokens_v, weight_v, t_sem, w_sem = refs
    rows, half = mine.shape
    part = rows // len(fars)
    copies = []
    for step, (start, depth) in enumerate(cuts):
        span = pl.ds(start, depth)
        token_copy = pltpu.make_async_copy(tokens.at[:, span], tokens_v.at[:, span], t_sem.at[step])
        weight_copy = pltpu.make_async_copy(weight.at[span, :], weight_v.at[span, :], w_sem.at[step])
        token_copy.start()
        weight_copy.start()
        copies.append((token_copy, weight_copy))
    for step, (start, depth) in enumerate(cuts):
        for copy in copies[step]:
            copy.wait()
        outs = [(mine, 0, rows, place[2])]
        outs += [(far, at * part, part, 1 - place[2]) for at, far in enumerate(fars)]
        for out, first, count, core in outs:
            columns = pl.ds(pl.multiple_of(core * half, half), half)
            product = jnp.dot(
                tokens_v[pl.ds(first, count), pl.ds(start, depth)],
                weight_v[pl.ds(start, depth), columns],
                preferred_element_type=jnp.float32,
            )
            out[...] = product if step == 0 else out[...] + product


def base_sums(place, tokens, weight):
    rows, width = tokens.shape
    features = weight.shape[1]
    first = width // 8
    cuts = [(0, first), (first, first)] + [(at * width // 4, width // 4) for at in range(1, 4)]
    far = jax.ShapeDtypeStruct((rows // FAR_PARTS, features // 2), jnp.float32)
    mine = jax.ShapeDtypeStruct((rows, features // 2), jnp.float32)
    return pl.pallas_call(
        functools.partial(base_kernel, cuts),
        in_specs=[SMEM, ANY, ANY],
        out_specs=[VMEM] * (FAR_PARTS + 1),
        out_shape=[far] * FAR_PARTS + [mine],
        scratch_shapes=[
            pltpu.VMEM((rows, width), tokens.dtype),
            pltpu.VMEM((width, features), weight.dtype),
            pltpu.SemaphoreType.DMA((len(cuts),)),
            pltpu.SemaphoreType.DMA((len(cuts),)),
        ],
        compiler_params=kernel_params(52),
        cost_estimate=cost(
            2 * rows * width * features, 2 * width * (rows + features) + 4 * rows * features
        ),
    )(place, tokens, weight)


def pool_of(place, step, other):
    depth = place[1] // 2
    column = place[1] - 2 * depth
    level = lax.rem(depth + 4 - step, 4)
    return 2 * level + (1 - column if other else column)


def half_of(place, kind):
    return {"a": 0, "b": 1, "own": place[0], "far": 1 - place[0]}[kind]


def shrink_kernel(pieces, has_prior, place, pool_index, adapter_index, tokens, *refs):
    refs = list(refs)
    arrays = [refs.pop(0) for _ in range(len({at for _, at, *_ in pieces}))]
    prior = refs.pop(0) if has_prior else None
    sums, tokens_v, sems = refs
    blocks, half = sums.shape[0], tokens_v.shape[3]

    def slot_of(block):
        return pool_index[adapter_index[place[1] * blocks + block]]

    def copy_of(block, side):
        return pltpu.make_async_copy(
            tokens.at[pl.ds(block * BLK, BLK), pl.ds(side * half, half)],
            tokens_v.at[block, side],
            sems.at[block, side],
        )

    def wanted(block, side):
        slot = slot_of(block)
        found = jnp.bool_(False)
        for (step, other, kind), *_ in pieces:
            found |= (slot == pool_of(place, step, other)) & (half_of(place, kind) == side)
        return found

    for block in range(blocks):
        for side in range(2):
            pl.when(wanted(block, side))(copy_of(block, side).start)
    sums[...] = prior[...] if has_prior else jnp.zeros_like(sums)

    def per_block(block, carry):
        slot = slot_of(block)
        for (step, other, kind), at, column, *_ in pieces:

            @pl.when(slot == pool_of(place, step, other))
            def _(kind=kind, at=at, column=column):
                side = half_of(place, kind)
                pltpu.make_async_copy(
                    tokens_v.at[block, side], tokens_v.at[block, side], sems.at[block, side]
                ).wait()
                sums[block] += lax.dot_general(
                    arrays[at][:, column : column + half],
                    tokens_v[block, side],
                    NT,
                    preferred_element_type=jnp.float32,
                )

        return carry

    lax.fori_loop(0, blocks, per_block, 0)


def shrink_sums(scalars, tokens, arrays, pieces, prior=None):
    rows, width = tokens.shape
    blocks = rows // BLK
    has_prior = prior is not None
    return pl.pallas_call(
        functools.partial(shrink_kernel, pieces, has_prior),
        in_specs=[SMEM, SMEM, SMEM, ANY] + [VMEM] * (len(arrays) + has_prior),
        out_specs=VMEM,
        out_shape=jax.ShapeDtypeStruct((blocks, ADAPTER_RANK, BLK), jnp.float32),
        scratch_shapes=[
            pltpu.VMEM((blocks, 2, BLK, width // 2), tokens.dtype),
            pltpu.SemaphoreType.DMA((blocks, 2)),
        ],
        compiler_params=kernel_params(52),
        cost_estimate=cost(rows * width * ADAPTER_RANK * len(pieces), rows * width),
    )(*scalars, tokens, *arrays, *([prior] if has_prior else []))


def select_kernel(pieces, place, pool_index, adapter_index, *refs):
    refs = list(refs)
    arrays = [refs.pop(0) for _ in range(len({at for _, at, _ in pieces}))]
    mine, *fars, base, ups = refs
    part = base.shape[0] // len(fars)
    blocks, _, half = ups.shape
    half = half // 2
    for at, far in enumerate(fars):
        span = slice(at * part, (at + 1) * part)
        base[span, :] = mine[span, :] + far[...]

    def per_block(block, carry):
        slot = pool_index[adapter_index[place[1] * blocks + block]]
        for (step, other, kind), at, column in pieces:

            @pl.when(slot == pool_of(place, step, other))
            def _(kind=kind, at=at, column=column):
                start = pl.multiple_of(half_of(place, kind) * half, half)
                ups[block, :, pl.ds(start, half)] = arrays[at][:, column : column + half]

        return carry

    lax.fori_loop(0, blocks, per_block, 0)


def select_ups(scalars, arrays, pieces, mine, fars):
    rows, half = mine.shape
    blocks = rows // BLK
    return pl.pallas_call(
        functools.partial(select_kernel, pieces),
        in_specs=[SMEM, SMEM, SMEM] + [VMEM] * (len(arrays) + 1 + len(fars)),
        out_specs=[VMEM, VMEM],
        out_shape=[
            jax.ShapeDtypeStruct((rows, half), jnp.float32),
            jax.ShapeDtypeStruct((blocks, ADAPTER_RANK, half), jnp.bfloat16),
        ],
        compiler_params=kernel_params(16),
        cost_estimate=cost(rows * half, 12 * rows * half),
    )(*scalars, *arrays, mine, *fars)


def final_kernel(
    last, place, pool_index, adapter_index, live, base, sums, far_sums, ups, piece, keys, up_v
):
    (step, other, kind), column = last
    blocks, rank, half = ups.shape
    for block in range(blocks):
        index = place[1] * blocks + block
        up_v[...] = ups[block]

        @pl.when(pool_index[adapter_index[index]] == pool_of(place, step, other))
        def _():
            start = pl.multiple_of(half_of(place, kind) * (half // 2), half // 2)
            up_v[:, pl.ds(start, half // 2)] = piece[:, column : column + half // 2]

        total = sums[block] + far_sums[block]
        high = total.astype(jnp.bfloat16)
        rest = total - high.astype(jnp.float32)
        middle = rest.astype(jnp.bfloat16)
        low = (rest - middle.astype(jnp.float32)).astype(jnp.bfloat16)
        up = up_v[...]
        delta = lax.dot_general(
            jnp.concatenate([high, middle, low], axis=0),
            jnp.concatenate([up, up, up], axis=0),
            TN,
            preferred_element_type=jnp.float32,
        )
        row = lax.broadcasted_iota(jnp.int32, (BLK, half), 0)
        span = slice(block * BLK, (block + 1) * BLK)
        keys[span, :] = jnp.where(row < live[index], base[span, :] + delta, 0.0).astype(keys.dtype)


def final_keys(scalars, base, sums, far_sums, ups, piece, last):
    rows, half = base.shape
    return pl.pallas_call(
        functools.partial(final_kernel, last),
        in_specs=[SMEM] * len(scalars) + [VMEM] * 5,
        out_specs=VMEM,
        out_shape=jax.ShapeDtypeStruct((rows, half), jnp.bfloat16),
        scratch_shapes=[pltpu.VMEM((ADAPTER_RANK, half), jnp.bfloat16)],
        compiler_params=kernel_params(12),
        cost_estimate=cost(6 * rows * half * ADAPTER_RANK, 6 * rows * half),
    )(*scalars, base, sums, far_sums, ups, piece)


def per_device_planes(
    tokens,
    key_projection_weight,
    adapter_down_weight,
    adapter_up_weight,
    adapter_pool_index,
    block_adapter_index,
    block_live_tokens,
):
    place = jnp.stack(
        [lax.axis_index("groups"), lax.axis_index("dp"), lax.axis_index("tensor")]
    ).astype(jnp.int32)
    down, up = adapter_down_weight[0], adapter_up_weight[0]
    width, half = down.shape[1] // 2, up.shape[1] // 2
    piece = width + half
    own = jnp.concatenate([down[:, :width], up[:, :half], down[:, width:], up[:, half:]], axis=1)
    first = lax.axis_index("groups") == 0
    own_half = jnp.where(first, own[:, :piece], own[:, piece:])

    def ring(array, step):
        pairs = [(2 * z + y, 2 * ((z + step) % 4) + y) for z in range(4) for y in range(2)]
        return lax.ppermute(array, "dp", pairs)

    def over_y(array):
        return lax.ppermute(array, "dp", [(i, i ^ 1) for i in range(8)])

    def over_x(array):
        return lax.ppermute(array, "groups", SWAP)

    def over_cores(array):
        return lax.ppermute(array, "tensor", SWAP)

    scalars = (place, adapter_pool_index, block_adapter_index[:, 0])
    z1 = ring(own_half, 1)
    y0 = over_y(own)
    z3 = ring(own_half, -1)
    *fars, mine = base_sums(place, tokens, key_projection_weight)
    z1_ = after(z1, mine)
    x1 = over_x(z1_)
    y1 = over_y(z1_)
    z2a = ring(z1_, 1)
    z3_ = after(z3, z1_)
    x3 = over_x(z3_)
    y3 = over_y(after(z3_, y0))
    z2b = ring(x1, 1)
    y2a = over_y(z2a)
    x1y = over_x(y1)
    x3y = over_x(y3)

    sides = [((0, False, "a"), 0, 0), ((0, False, "b"), 0, width),
             ((0, True, "a"), 1, 0), ((0, True, "b"), 1, piece)]
    names = [(1, False, "own"), (1, False, "far"), (3, False, "own"), (3, False, "far"),
             (2, False, "own"), (1, True, "own"), (3, True, "own")]
    sums = shrink_sums(
        scalars,
        after(tokens, z2a),
        [down, y0, z1, x1, z3, x3, z2a, y1, y3],
        sides + [(name, at + 2, 0) for at, name in enumerate(names)],
    )
    y2b = over_y(z2b)
    base_fars = [over_cores(far) for far in fars]
    late_names = [(2, False, "far"), (1, True, "far"), (3, True, "far"), (2, True, "own")]
    late_arrays = [z2b, x1y, x3y, y2a]
    sums = shrink_sums(
        scalars,
        tokens,
        late_arrays,
        [(name, at, 0) for at, name in enumerate(late_names)],
        sums,
    )
    base, ups = select_ups(
        scalars,
        [up, y0, z1, x1, z3, x3, z2a, y1, y3] + late_arrays,
        [((0, False, "a"), 0, 0), ((0, False, "b"), 0, half),
         ((0, True, "a"), 1, width), ((0, True, "b"), 1, piece + width)]
        + [(name, at + 2, width) for at, name in enumerate(names + late_names)],
        mine,
        base_fars,
    )
    last = (2, True, "far")
    sums = shrink_sums(scalars, after(tokens, base), [y2b], [(last, 0, 0)], sums)
    far_sums = over_cores(sums)
    return final_keys(
        (*scalars, block_live_tokens), base, sums, far_sums, ups, y2b, (last, width)
    )


def per_device_gathered(
    tokens,
    key_projection_weight,
    adapter_down_weight,
    adapter_up_weight,
    adapter_pool_index,
    block_adapter_index,
    block_live_tokens,
):
    rows = tokens.shape[0]
    blocks = rows // BLK
    first_block = lax.axis_index("dp") * blocks
    slots = lax.dynamic_slice_in_dim(
        adapter_pool_index[block_adapter_index[:, 0]], first_block, blocks
    )
    fill = lax.dynamic_slice_in_dim(block_live_tokens, first_block, blocks)
    base_part = jnp.dot(tokens, key_projection_weight, preferred_element_type=jnp.float32)
    down = lax.all_gather(adapter_down_weight, "dp", axis=0, tiled=True)
    up = lax.all_gather(adapter_up_weight, "dp", axis=0, tiled=True)
    token_blocks = tokens.reshape(blocks, BLK, tokens.shape[1])
    shrink = jnp.einsum(
        "nrd,nbd->rnb",
        jnp.take(down, slots, axis=0),
        token_blocks,
        preferred_element_type=jnp.float32,
    )
    shrink = lax.psum(shrink.reshape(ADAPTER_RANK, rows), "tensor")
    delta = jnp.einsum(
        "rnb,nrc->nbc",
        shrink.reshape(ADAPTER_RANK, blocks, BLK),
        jnp.take(up, slots, axis=0).astype(jnp.float32),
        precision=lax.Precision.HIGHEST,
        preferred_element_type=jnp.float32,
    )
    base = lax.psum_scatter(base_part, "tensor", scatter_dimension=1, tiled=True)
    mask = jnp.arange(BLK, dtype=jnp.int32)[None, :] < fill[:, None]
    keys = base + delta.reshape(rows, base.shape[1])
    return jnp.where(mask.reshape(rows, 1), keys, 0.0).astype(jnp.bfloat16)


def solution(mesh):
    in_specs = (
        P(("groups", "dp"), "tensor"),
        P("tensor", None),
        P("dp", None, "tensor"),
        P("dp", None, "tensor"),
        P(),
        P("groups", None),
        P("groups"),
    )
    out_specs = P(("groups", "dp"), "tensor")
    planes = dict(mesh.shape) == {"groups": 2, "dp": 8, "tensor": 2}
    return jax.shard_map(
        per_device_planes if planes else per_device_gathered,
        mesh=mesh,
        in_specs=in_specs,
        out_specs=out_specs,
        check_vma=False,
    )
```

time: 151 us -> 60.5 us (0.40)
  waiting for transfers between devices: 71.7 us -> 15.4 us
  blocking collectives: 31.3 us -> 0 us
  Pallas kernels: 0 us -> 27.3 us
  matrix products: 19.7 us -> 0 us
  starting transfers between devices: 0.08 us -> 15.8 us
  between operations: 13.2 us -> 0.18 us
  other arithmetic: 8.4 us -> 0.19 us
  local copies, waits for them, and re-layouts: 6.03 us -> 1.88 us
    all_gather x1 -> x0, waiting for transfers between devices: 70.9 us -> none  [per_device(): lax.all_gather(adapter_down_weight, 'dp', axis=0, tiled=True)]
    all_gather x1 -> x0, blocking collectives: 31.3 us -> none  [per_device(): lax.all_gather(adapter_up_weight, 'dp', axis=0, tiled=True)]
    pallas_call x0 -> x6, Pallas kernels: none -> 27.3 us  [the longest x3 11 us: shrink_sums(): pl.pallas_call(functools.partial(shrink_kernel, pieces, has_prior), in_sp...]
    dot_general x3 -> x0, matrix products: 19.7 us -> none  [the longest x1 12.1 us: per_device(): jnp.dot(tokens, key_projection_weight, preferred_element_type=jnp.float32)]
    ppermute x0 -> x17, starting transfers between devices: none -> 15.8 us  [the longest x5 7.31 us: over_y(): return lax.ppermute(array, 'dp', [(i, i ^ 1) for i in range(8)])]
    ppermute x0 -> x17, waiting for transfers between devices: none -> 15.4 us  [the longest x4 10.3 us: over_x(): return lax.ppermute(array, 'groups', SWAP)]
    gather x2 -> x0, other arithmetic: 5.71 us -> none  [the longest x1 5.7 us: per_device(): block_pool_index = adapter_pool_index[block_adapter_index[:, 0]]]
    gather x3 -> x0, local copies, waits for them, and re-layouts: 5.13 us -> none  [the longest x1 2.93 us: per_device(): jnp.take(down_matrix_block, pick_index, axis=0)]
  transfers between devices with their start and end apart: 3 -> 17, of which waited for: 1 -> 8; matrix products, arithmetic and copies ran while one was open for 15% -> 0% of each run, Pallas kernels for 0% -> 36%
where the time goes in v2:
time: 60.5 us; the launch traced here: 60.8 us
  Pallas kernels  27.3 us (45%)
  starting transfers between devices  15.8 us (26%)
  waiting for transfers between devices  15.4 us (25%)
  local copies, waits for them, and re-layouts  1.88 us (3%)
    pallas_call x3, Pallas kernels, shrink_sums(): pl.pallas_call(functools.partial(shrink_kernel, pieces, has_prior), in_sp...  11 us
    pallas_call x1, Pallas kernels, base_sums(): pl.pallas_call(functools.partial(base_kernel, cuts), in_specs=[SMEM, ANY,...  10.6 us
    ppermute x4, waiting for transfers between devices, over_x(): return lax.ppermute(array, 'groups', SWAP)  10.3 us
    ppermute x5, starting transfers between devices, over_y(): return lax.ppermute(array, 'dp', [(i, i ^ 1) for i in range(8)])  7.31 us
    ppermute x4, starting transfers between devices, over_x(): return lax.ppermute(array, 'groups', SWAP)  4.58 us
    ppermute x4, starting transfers between devices, ring(): return lax.ppermute(array, 'dp', pairs)  3.88 us
    ppermute x5, waiting for transfers between devices, over_y(): return lax.ppermute(array, 'dp', [(i, i ^ 1) for i in range(8)])  3.07 us
    pallas_call x1, Pallas kernels, select_ups(): pl.pallas_call(functools.partial(select_kernel, pieces), in_specs=[SMEM,...  2.9 us
  transfers between devices with their start and end apart: 17, of which 8 were waited for; matrix products, arithmetic and copies ran while one was open for 0% of the time, Pallas kernels for 36%

profile of v2, /device:TPU:0, one launch (start us, length us, event | category | flops | bytes accessed | tf_op | source)
XLA Modules:
  0.0 60.8 jit_solution(2199273800218211790)
XLA Ops:
  0.0 0.8 %fusion.1 = (bf16[64,256]{1,0:T(8,128)(2,1)S(1)}, bf16[64,256]{1,0:T(8,128)(2,1)S(1)}) fusion(bf16[64,512]{1,0:T(8,128)(2,1)} %bitcast.6), kind=kLoop, calls=%fused_computation.4 | loop fusion | bytes 131072 | tf_op jit(solution)/shard_map/slice | solution.py:267
  0.8 1.1 %fusion = (bf16[64,2048]{1,0:T(8,128)(2,1)S(1)}, bf16[64,2048]{1,0:T(8,128)(2,1)S(1)}) fusion(bf16[64,4096]{1,0:T(8,128)(2,1)} %bitcast.13), kind=kLoop, calls=%fused_computation.3 | loop fusion | bytes 1048576 | tf_op jit(solution)/shard_map/slice | solution.py:267
  1.9 3.0 %collective-permute-start = (bf16[64,4608]{1,0:T(8,128)(2,1)S(1)}, bf16[64,4608]{1,0:T(8,128)(2,1)S(1)}, u32[]{:S(2)}, u32[]{:S(2)}) collective-permute-start(bf16[64,4608]{1,0:T(8,128)(2,1)S(1)} %pad_maximum_fusion), channel_id=1, source_target_pairs={{0,2},{2,0},{4,6},{6,4},{8,10},{10,8},{12,14},{14,12},{1,3},{3,1},... | collective-permute-start | bytes 1769480 | tf_op jit(solution)/shard_map/ppermute | solution.py:276
  4.9 0.1 maximum_select_fusion
  5.0 1.6 %collective-permute-start.1 = (bf16[64,2304]{1,0:T(8,128)(2,1)S(1)}, bf16[64,2304]{1,0:T(8,128)(2,1)S(1)}, u32[]{:S(2)}, u32[]{:S(2)}) collective-permute-start(bf16[64,2304]{1,0:T(8,128)(2,1)S(1)} %maximum_select_fusion), channel_id=1, source_target_pairs={{0,4},{2,6},{4,8},{6,10},{8,12},{10,14},{12,0},{14,2},{1,5},{3,7},... | collective-permute-start | bytes 884744 | tf_op jit(solution)/shard_map/ppermute | solution.py:273
  6.6 2.2 %collective-permute-start.3 = (bf16[64,2304]{1,0:T(8,128)(2,1)S(1)}, bf16[64,2304]{1,0:T(8,128)(2,1)S(1)}, u32[]{:S(2)}, u32[]{:S(2)}) collective-permute-start(bf16[64,2304]{1,0:T(8,128)(2,1)S(1)} %maximum_select_fusion), channel_id=1, source_target_pairs={{0,12},{2,14},{4,0},{6,2},{8,4},{10,6},{12,8},{14,10},{1,13},{3,15... | collective-permute-start | bytes 884744 | tf_op jit(solution)/shard_map/ppermute | solution.py:273
  8.9 0.1 pad_add_fusion.place
  9.0 10.6 %shard_map.73 = (f32[256,512]{1,0:T(8,128)S(1)}, f32[256,512]{1,0:T(8,128)S(1)}, f32[256,512]{1,0:T(8,128)S(1)}, f32[768,512]{1,0:T(8,128)}) custom-call(s32[3]{0:T(128)S(1)} %pad_add_fusion.place, bf16[768,4096]{1,0:T(8,128)(2,1)} %tokens.5, bf16[4096,1024]{1,0:T(8,128)(2,1)} %weight.1), custom_call_target="tpu_custom_call" | custom-call | flops 1 | bytes 1 | tf_op jit(solution)/shard_map/pallas_call | solution.py:69
  19.5 0.0 collective-permute-done.1.refs_2_
  19.6 1.5 %collective-permute-start.2 = (bf16[64,2304]{1,0:T(8,128)(2,1)S(1)}, bf16[64,2304]{1,0:T(8,128)(2,1)S(1)}, u32[]{:S(2)}, u32[]{:S(2)}) collective-permute-start(bf16[64,2304]{1,0:T(8,128)(2,1)S(1)} %collective-permute-done.1.refs_2_), channel_id=1, source_target_pairs={{0,16},{16,0},{1,17},{17,1},{2,18},{18,2},{3,19},{19,3},{4,20},{20... | collective-permute-start | bytes 884744 | tf_op jit(solution)/shard_map/ppermute | solution.py:279
  21.1 0.5 collective-permute-start.6
  21.6 0.0 collective-permute-start.5
  21.6 0.0 collective-permute-done.3.refs_4_
  21.6 1.0 %collective-permute-start.4 = (bf16[64,2304]{1,0:T(8,128)(2,1)S(1)}, bf16[64,2304]{1,0:T(8,128)(2,1)S(1)}, u32[]{:S(2)}, u32[]{:S(2)}) collective-permute-start(bf16[64,2304]{1,0:T(8,128)(2,1)S(1)} %collective-permute-done.3.refs_4_), channel_id=1, source_target_pairs={{0,16},{16,0},{1,17},{17,1},{2,18},{18,2},{3,19},{19,3},{4,20},{20... | collective-permute-start | bytes 884744 | tf_op jit(solution)/shard_map/ppermute | solution.py:279
  22.6 0.0 collective-permute-done.refs_1_
  22.6 1.0 %collective-permute-start.7 = (bf16[64,2304]{1,0:T(8,128)(2,1)S(1)}, bf16[64,2304]{1,0:T(8,128)(2,1)}, u32[]{:S(2)}, u32[]{:S(2)}) collective-permute-start(bf16[64,2304]{1,0:T(8,128)(2,1)S(1)} %collective-permute-done.3.refs_4_), channel_id=1, source_target_pairs={{0,2},{2,0},{4,6},{6,4},{8,10},{10,8},{12,14},{14,12},{1,3},{3,1},... | collective-permute-start | bytes 884744 | tf_op jit(solution)/shard_map/ppermute | solution.py:276
  23.7 5.9 %collective-permute-done.2.refs_3_ = bf16[64,2304]{1,0:T(8,128)(2,1)S(1)} collective-permute-done((bf16[64,2304]{1,0:T(8,128)(2,1)S(1)}, bf16[64,2304]{1,0:T(8,128)(2,1)S(1)}, u32[]{:S(2)}, u32[]{:S(2)}) %collective-permute-start.2) | collective-permute-done | bytes 294944 | tf_op jit(solution)/shard_map/ppermute | solution.py:279
  29.6 0.0 collective-permute-start.8
  29.6 1.5 %collective-permute-done.6.refs_7_ = bf16[64,2304]{1,0:T(8,128)(2,1)S(1)} collective-permute-done((bf16[64,2304]{1,0:T(8,128)(2,1)S(1)}, bf16[64,2304]{1,0:T(8,128)(2,1)S(1)}, u32[]{:S(2)}, u32[]{:S(2)}) %collective-permute-start.6) | collective-permute-done | bytes 294944 | tf_op jit(solution)/shard_map/ppermute | solution.py:276
  31.0 0.5 collective-permute-start.9
  31.6 0.0 collective-permute-done.5.refs_6_
  31.6 2.2 %collective-permute-start.11 = (bf16[64,2304]{1,0:T(8,128)(2,1)S(1)}, bf16[64,2304]{1,0:T(8,128)(2,1)S(1)}, u32[]{:S(2)}, u32[]{:S(2)}) collective-permute-start(bf16[64,2304]{1,0:T(8,128)(2,1)S(1)} %collective-permute-done.5.refs_6_), channel_id=1, source_target_pairs={{0,2},{2,0},{4,6},{6,4},{8,10},{10,8},{12,14},{14,12},{1,3},{3,1},... | collective-permute-start | bytes 884744 | tf_op jit(solution)/shard_map/ppermute | solution.py:276
  33.8 2.1 %collective-permute-done.4.refs_5_ = bf16[64,2304]{1,0:T(8,128)(2,1)S(1)} collective-permute-done((bf16[64,2304]{1,0:T(8,128)(2,1)S(1)}, bf16[64,2304]{1,0:T(8,128)(2,1)S(1)}, u32[]{:S(2)}, u32[]{:S(2)}) %collective-permute-start.4) | collective-permute-done | bytes 294944 | tf_op jit(solution)/shard_map/ppermute | solution.py:279
  35.9 0.0 collective-permute-start.12
  35.9 1.6 %collective-permute-done.7.refs_8_ = bf16[64,2304]{1,0:T(8,128)(2,1)} collective-permute-done((bf16[64,2304]{1,0:T(8,128)(2,1)S(1)}, bf16[64,2304]{1,0:T(8,128)(2,1)}, u32[]{:S(2)}, u32[]{:S(2)}) %collective-permute-start.7) | collective-permute-done | bytes 294944 | tf_op jit(solution)/shard_map/ppermute | solution.py:276
  37.5 0.0 collective-permute-start.13
  37.5 0.6 %collective-permute-done.8.refs_9_.refs_0_ = bf16[64,2304]{1,0:T(8,128)(2,1)S(1)} collective-permute-done((bf16[64,2304]{1,0:T(8,128)(2,1)S(1)}, bf16[64,2304]{1,0:T(8,128)(2,1)S(1)}, u32[]{:S(2)}, u32[]{:S(2)}) %collective-permute-start.8) | collective-permute-done | bytes 294944 | tf_op jit(solution)/shard_map/ppermute | solution.py:273
  38.1 0.0 collective-permute-start.14
  38.1 2.1 %collective-permute-done.9.refs_10_.refs_1_ = bf16[64,2304]{1,0:T(8,128)(2,1)S(1)} collective-permute-done((bf16[64,2304]{1,0:T(8,128)(2,1)S(1)}, bf16[64,2304]{1,0:T(8,128)(2,1)S(1)}, u32[]{:S(2)}, u32[]{:S(2)}) %collective-permute-start.9) | collective-permute-done | bytes 294944 | tf_op jit(solution)/shard_map/ppermute | solution.py:279
  40.2 1.5 %collective-permute-start.10 = (bf16[64,2304]{1,0:T(8,128)(2,1)}, bf16[64,2304]{1,0:T(8,128)(2,1)S(1)}, u32[]{:S(2)}, u32[]{:S(2)}) collective-permute-start(bf16[64,2304]{1,0:T(8,128)(2,1)} %collective-permute-done.7.refs_8_), channel_id=1, source_target_pairs={{0,16},{16,0},{1,17},{17,1},{2,18},{18,2},{3,19},{19,3},{4,20},{20... | collective-permute-start | bytes 884744 | tf_op jit(solution)/shard_map/ppermute | solution.py:279
  41.7 0.0 collective-permute-done.11.refs_12_.refs_3_
  41.7 0.5 collective-permute-start.15
  42.2 5.3 %shard_map.75.refs_4_ = f32[6,64,128]{2,1,0:T(8,128)S(1)} custom-call(s32[3]{0:T(128)S(1)} %pad_add_fusion.place, s32[8]{0:T(128)S(1)} %copy-done.4, s32[48]{0:T(128)S(1)} %bitcast.8, bf16[768,4096]{1,0:T(8,128)(2,1)} %tokens.5, bf16[64,4096]{1,0:T(8,128)(2,1)} %bitcast.14, bf16[64,4608]{1,0:T(8,128)(2,1)} %copy-done, ...), custom_call_target="tpu_custom_call" | custom-call | flops 1 | bytes 1 | tf_op jit(solution)/shard_map/pallas_call | solution.py:153
  47.5 0.0 copy-start.1
  47.5 0.0 copy-start.2
  47.5 0.0 copy-start.3
  47.5 0.2 collective-permute-done.10.refs_11_.refs_2_
  47.7 3.3 %shard_map.76.refs_1_ = f32[6,64,128]{2,1,0:T(8,128)S(1)} custom-call(s32[3]{0:T(128)S(1)} %pad_add_fusion.place, s32[8]{0:T(128)S(1)} %copy-done.4, s32[48]{0:T(128)S(1)} %bitcast.9, bf16[768,4096]{1,0:T(8,128)(2,1)} %tokens.5, bf16[64,2304]{1,0:T(8,128)(2,1)S(1)} %collective-permute-done.8.refs_9_.refs_0_, ...), custom_call_target="tpu_custom_call" | custom-call | flops 1 | bytes 1 | tf_op jit(solution)/shard_map/pallas_call | solution.py:153
  51.1 0.0 collective-permute-done.12.refs_14_
  51.1 0.0 collective-permute-done.13.refs_15_
  51.1 0.0 collective-permute-done.14.refs_16_
  51.1 2.9 %shard_map.74 = (f32[768,512]{1,0:T(8,128)S(1)}, bf16[6,64,512]{2,1,0:T(8,128)(2,1)S(1)}) custom-call(s32[3]{0:T(128)S(1)} %pad_add_fusion.place, s32[8]{0:T(128)S(1)} %copy-done.4, s32[48]{0:T(128)S(1)} %bitcast.10, bf16[64,512]{1,0:T(8,128)(2,1)S(1)} %bitcast.7, bf16[64,4608]{1,0:T(8,128)(2,1)S(1)} %copy-done.1, ...), custom_call_target="tpu_custom_call" | custom-call | flops 1 | bytes 1 | tf_op jit(solution)/shard_map/pallas_call | solution.py:195
  54.0 0.0 copy-start.6
  54.0 0.0 collective-permute-done.15.refs_0_.piece
  54.0 2.4 %shard_map.77.sums = f32[6,64,128]{2,1,0:T(8,128)S(1)} custom-call(s32[3]{0:T(128)S(1)} %pad_add_fusion.place, s32[8]{0:T(128)S(1)} %copy-done.4, s32[48]{0:T(128)S(1)} %bitcast.11, bf16[768,4096]{1,0:T(8,128)(2,1)} %tokens.5, bf16[64,2304]{1,0:T(8,128)(2,1)S(1)} %collective-permute-done.15.refs_0_.piece, f32[6,64,128]{2,1,0:T(8,128)S(1)} %shard_map.76.refs_1_), custom_call_target="tpu_custom_call" | custom-call | flops 1 | bytes 1 | tf_op jit(solution)/shard_map/pallas_call | solution.py:153
  56.5 0.1 collective-permute-start.16
  56.6 1.4 %collective-permute-done.16.far_sums = f32[6,64,128]{2,1,0:T(8,128)S(1)} collective-permute-done((f32[6,64,128]{2,1,0:T(8,128)S(1)}, f32[6,64,128]{2,1,0:T(8,128)S(1)}, u32[]{:S(2)}, u32[]{:S(2)}) %collective-permute-start.16) | collective-permute-done | bytes 196640 | tf_op jit(solution)/shard_map/ppermute | solution.py:282
  58.0 2.8 %shard_map.78 = bf16[768,512]{1,0:T(8,128)(2,1)} custom-call(s32[3]{0:T(128)S(1)} %pad_add_fusion.place, s32[8]{0:T(128)S(1)} %copy-done.4, s32[48]{0:T(128)S(1)} %bitcast.12, s32[48]{0:T(128)S(1)} %copy-done.6, f32[768,512]{1,0:T(8,128)S(1)} %get-tuple-element.23.base, f32[6,64,128]{2,1,0:T(8,128)S(1)} %shard_map.77.sums, ...), custom_call_target="tpu_custom_call" | custom-call | flops 1 | bytes 1 | tf_op jit(solution)/shard_map/pallas_call | solution.py:241
  (11 shorter events, 0.1 us)
Async XLA Ops:
  1.9 20.7 %collective-permute-start = (bf16[64,4608]{1,0:T(8,128)(2,1)S(1)}, bf16[64,4608]{1,0:T(8,128)(2,1)S(1)}, u32[]{:S(2)}, u32[]{:S(2)}) collective-permute-start(bf16[64,4608]{1,0:T(8,128)(2,1)S(1)} %pad_maximum_fusion), channel_id=1, source_target_pairs={{0,2},{2,0},{4,6},{6,4},{8,10},{10,8},{12,14},{14,12},{1,3},{3,1},... | collective-permute-start | bytes 1769480 | tf_op jit(solution)/shard_map/ppermute | solution.py:276
  5.0 14.5 %collective-permute-start.1 = (bf16[64,2304]{1,0:T(8,128)(2,1)S(1)}, bf16[64,2304]{1,0:T(8,128)(2,1)S(1)}, u32[]{:S(2)}, u32[]{:S(2)}) collective-permute-start(bf16[64,2304]{1,0:T(8,128)(2,1)S(1)} %maximum_select_fusion), channel_id=1, source_target_pairs={{0,4},{2,6},{4,8},{6,10},{8,12},{10,14},{12,0},{14,2},{1,5},{3,7},... | collective-permute-start | bytes 884744 | tf_op jit(solution)/shard_map/ppermute | solution.py:273
  6.6 15.0 %collective-permute-start.3 = (bf16[64,2304]{1,0:T(8,128)(2,1)S(1)}, bf16[64,2304]{1,0:T(8,128)(2,1)S(1)}, u32[]{:S(2)}, u32[]{:S(2)}) collective-permute-start(bf16[64,2304]{1,0:T(8,128)(2,1)S(1)} %maximum_select_fusion), channel_id=1, source_target_pairs={{0,12},{2,14},{4,0},{6,2},{8,4},{10,6},{12,8},{14,10},{1,13},{3,15... | collective-permute-start | bytes 884744 | tf_op jit(solution)/shard_map/ppermute | solution.py:273
  9.0 33.2 %copy-start.4 = (s32[8]{0:T(128)S(1)}, s32[8]{0:T(128)}, u32[]{:S(2)}) copy-start(s32[8]{0:T(128)} %pool_index.9) | copy-start | bytes 100
  9.0 33.2 %copy-start.5 = (s32[48,1]{0,1:T(1,128)S(1)}, s32[48,1]{0,1:T(1,128)}, u32[]{:S(2)}) copy-start(s32[48,1]{0,1:T(1,128)} %param.12) | copy-start | bytes 580
  19.6 10.0 %collective-permute-start.2 = (bf16[64,2304]{1,0:T(8,128)(2,1)S(1)}, bf16[64,2304]{1,0:T(8,128)(2,1)S(1)}, u32[]{:S(2)}, u32[]{:S(2)}) collective-permute-start(bf16[64,2304]{1,0:T(8,128)(2,1)S(1)} %collective-permute-done.1.refs_2_), channel_id=1, source_target_pairs={{0,16},{16,0},{1,17},{17,1},{2,18},{18,2},{3,19},{19,3},{4,20},{20... | collective-permute-start | bytes 884744 | tf_op jit(solution)/shard_map/ppermute | solution.py:279
  21.1 9.9 %collective-permute-start.6 = (bf16[64,2304]{1,0:T(8,128)(2,1)S(1)}, bf16[64,2304]{1,0:T(8,128)(2,1)S(1)}, u32[]{:S(2)}, u32[]{:S(2)}) collective-permute-start(bf16[64,2304]{1,0:T(8,128)(2,1)S(1)} %collective-permute-done.1.refs_2_), channel_id=1, source_target_pairs={{0,2},{2,0},{4,6},{6,4},{8,10},{10,8},{12,14},{14,12},{1,3},{3,1},... | collective-permute-start | bytes 884744 | tf_op jit(solution)/shard_map/ppermute | solution.py:276
  21.6 10.0 %collective-permute-start.5 = (bf16[64,2304]{1,0:T(8,128)(2,1)S(1)}, bf16[64,2304]{1,0:T(8,128)(2,1)S(1)}, u32[]{:S(2)}, u32[]{:S(2)}) collective-permute-start(bf16[64,2304]{1,0:T(8,128)(2,1)S(1)} %collective-permute-done.1.refs_2_), channel_id=1, source_target_pairs={{0,4},{2,6},{4,8},{6,10},{8,12},{10,14},{12,0},{14,2},{1,5},{3,7},... | collective-permute-start | bytes 884744 | tf_op jit(solution)/shard_map/ppermute | solution.py:273
  21.6 14.3 %collective-permute-start.4 = (bf16[64,2304]{1,0:T(8,128)(2,1)S(1)}, bf16[64,2304]{1,0:T(8,128)(2,1)S(1)}, u32[]{:S(2)}, u32[]{:S(2)}) collective-permute-start(bf16[64,2304]{1,0:T(8,128)(2,1)S(1)} %collective-permute-done.3.refs_4_), channel_id=1, source_target_pairs={{0,16},{16,0},{1,17},{17,1},{2,18},{18,2},{3,19},{19,3},{4,20},{20... | collective-permute-start | bytes 884744 | tf_op jit(solution)/shard_map/ppermute | solution.py:279
  22.6 19.6 %copy-start = (bf16[64,4608]{1,0:T(8,128)(2,1)}, bf16[64,4608]{1,0:T(8,128)(2,1)S(1)}, u32[]{:S(2)}) copy-start(bf16[64,4608]{1,0:T(8,128)(2,1)S(1)} %collective-permute-done.refs_1_) | copy-start | bytes 1769476
  22.6 14.8 %collective-permute-start.7 = (bf16[64,2304]{1,0:T(8,128)(2,1)S(1)}, bf16[64,2304]{1,0:T(8,128)(2,1)}, u32[]{:S(2)}, u32[]{:S(2)}) collective-permute-start(bf16[64,2304]{1,0:T(8,128)(2,1)S(1)} %collective-permute-done.3.refs_4_), channel_id=1, source_target_pairs={{0,2},{2,0},{4,6},{6,4},{8,10},{10,8},{12,14},{14,12},{1,3},{3,1},... | collective-permute-start | bytes 884744 | tf_op jit(solution)/shard_map/ppermute | solution.py:276
  29.6 8.5 %collective-permute-start.8 = (bf16[64,2304]{1,0:T(8,128)(2,1)S(1)}, bf16[64,2304]{1,0:T(8,128)(2,1)S(1)}, u32[]{:S(2)}, u32[]{:S(2)}) collective-permute-start(bf16[64,2304]{1,0:T(8,128)(2,1)S(1)} %collective-permute-done.2.refs_3_), channel_id=1, source_target_pairs={{0,4},{2,6},{4,8},{6,10},{8,12},{10,14},{12,0},{14,2},{1,5},{3,7},... | collective-permute-start | bytes 884744 | tf_op jit(solution)/shard_map/ppermute | solution.py:273
  31.0 9.1 %collective-permute-start.9 = (bf16[64,2304]{1,0:T(8,128)(2,1)S(1)}, bf16[64,2304]{1,0:T(8,128)(2,1)S(1)}, u32[]{:S(2)}, u32[]{:S(2)}) collective-permute-start(bf16[64,2304]{1,0:T(8,128)(2,1)S(1)} %collective-permute-done.6.refs_7_), channel_id=1, source_target_pairs={{0,16},{16,0},{1,17},{17,1},{2,18},{18,2},{3,19},{19,3},{4,20},{20... | collective-permute-start | bytes 884744 | tf_op jit(solution)/shard_map/ppermute | solution.py:279
  31.6 10.1 %collective-permute-start.11 = (bf16[64,2304]{1,0:T(8,128)(2,1)S(1)}, bf16[64,2304]{1,0:T(8,128)(2,1)S(1)}, u32[]{:S(2)}, u32[]{:S(2)}) collective-permute-start(bf16[64,2304]{1,0:T(8,128)(2,1)S(1)} %collective-permute-done.5.refs_6_), channel_id=1, source_target_pairs={{0,2},{2,0},{4,6},{6,4},{8,10},{10,8},{12,14},{14,12},{1,3},{3,1},... | collective-permute-start | bytes 884744 | tf_op jit(solution)/shard_map/ppermute | solution.py:276
  35.9 15.2 %collective-permute-start.12 = (f32[256,512]{1,0:T(8,128)S(1)}, f32[256,512]{1,0:T(8,128)S(1)}, u32[]{:S(2)}, u32[]{:S(2)}) collective-permute-start(f32[256,512]{1,0:T(8,128)S(1)} %get-tuple-element.20), channel_id=1, source_target_pairs={{0,1},{1,0},{2,3},{3,2},{4,5},{5,4},{6,7},{7,6},{8,9},{9,8},{10,11... | collective-permute-start | bytes 1572872 | tf_op jit(solution)/shard_map/ppermute | solution.py:282
  37.5 13.6 %collective-permute-start.13 = (f32[256,512]{1,0:T(8,128)S(1)}, f32[256,512]{1,0:T(8,128)S(1)}, u32[]{:S(2)}, u32[]{:S(2)}) collective-permute-start(f32[256,512]{1,0:T(8,128)S(1)} %get-tuple-element.21), channel_id=1, source_target_pairs={{0,1},{1,0},{2,3},{3,2},{4,5},{5,4},{6,7},{7,6},{8,9},{9,8},{10,11... | collective-permute-start | bytes 1572872 | tf_op jit(solution)/shard_map/ppermute | solution.py:282
  38.1 13.0 %collective-permute-start.14 = (f32[256,512]{1,0:T(8,128)S(1)}, f32[256,512]{1,0:T(8,128)S(1)}, u32[]{:S(2)}, u32[]{:S(2)}) collective-permute-start(f32[256,512]{1,0:T(8,128)S(1)} %get-tuple-element.22), channel_id=1, source_target_pairs={{0,1},{1,0},{2,3},{3,2},{4,5},{5,4},{6,7},{7,6},{8,9},{9,8},{10,11... | collective-permute-start | bytes 1572872 | tf_op jit(solution)/shard_map/ppermute | solution.py:282
  40.2 7.5 %collective-permute-start.10 = (bf16[64,2304]{1,0:T(8,128)(2,1)}, bf16[64,2304]{1,0:T(8,128)(2,1)S(1)}, u32[]{:S(2)}, u32[]{:S(2)}) collective-permute-start(bf16[64,2304]{1,0:T(8,128)(2,1)} %collective-permute-done.7.refs_8_), channel_id=1, source_target_pairs={{0,16},{16,0},{1,17},{17,1},{2,18},{18,2},{3,19},{19,3},{4,20},{20... | collective-permute-start | bytes 884744 | tf_op jit(solution)/shard_map/ppermute | solution.py:279
  41.7 12.4 %collective-permute-start.15 = (bf16[64,2304]{1,0:T(8,128)(2,1)S(1)}, bf16[64,2304]{1,0:T(8,128)(2,1)S(1)}, u32[]{:S(2)}, u32[]{:S(2)}) collective-permute-start(bf16[64,2304]{1,0:T(8,128)(2,1)S(1)} %collective-permute-done.8.refs_9_.refs_0_), channel_id=1, source_target_pairs={{0,2},{2,0},{4,6},{6,4},{8,10},{10,8},{12,14},{14,12},{1,3},{3,1},... | collective-permute-start | bytes 884744 | tf_op jit(solution)/shard_map/ppermute | solution.py:276
  47.5 3.6 %copy-start.1 = (bf16[64,4608]{1,0:T(8,128)(2,1)S(1)}, bf16[64,4608]{1,0:T(8,128)(2,1)}, u32[]{:S(2)}) copy-start(bf16[64,4608]{1,0:T(8,128)(2,1)} %copy-done) | copy-start | bytes 1769476
  47.5 3.6 %copy-start.2 = (f32[768,512]{1,0:T(8,128)S(1)}, f32[768,512]{1,0:T(8,128)}, u32[]{:S(2)}) copy-start(f32[768,512]{1,0:T(8,128)} %get-tuple-element.16.refs_13_) | copy-start | bytes 4718596
  47.5 3.6 %copy-start.3 = (bf16[1,64,512]{2,1,0:T(8,128)(2,1)S(1)}, bf16[1,64,512]{2,1,0:T(8,128)(2,1)}, u32[]{:S(2)}) copy-start(bf16[1,64,512]{2,1,0:T(8,128)(2,1)} %param.10) | copy-start | bytes 196612
  54.0 4.0 %copy-start.6 = (s32[48]{0:T(128)S(1)}, s32[48]{0:T(128)}, u32[]{:S(2)}) copy-start(s32[48]{0:T(128)} %live.1) | copy-start | bytes 580
  56.5 1.5 %collective-permute-start.16 = (f32[6,64,128]{2,1,0:T(8,128)S(1)}, f32[6,64,128]{2,1,0:T(8,128)S(1)}, u32[]{:S(2)}, u32[]{:S(2)}) collective-permute-start(f32[6,64,128]{2,1,0:T(8,128)S(1)} %shard_map.77.sums), channel_id=1, source_target_pairs={{0,1},{1,0},{2,3},{3,2},{4,5},{5,4},{6,7},{7,6},{8,9},{9,8},{10,11... | collective-permute-start | bytes 589832 | tf_op jit(solution)/shard_map/ppermute | solution.py:282

commit v3 on v2

v3 whole, which is shorter than its diff:
```python
import functools

import jax
import jax.numpy as jnp
from jax import lax
from jax.experimental import pallas as pl
from jax.experimental.pallas import tpu as pltpu
from jax.sharding import PartitionSpec as P

ADAPTER_RANK = 64
BLK = 128
FAR_PARTS = 3
SWAP = [(0, 1), (1, 0)]
NT = (((1,), (1,)), ((), ()))
TN = (((0,), (0,)), ((), ()))


def kernel_params(mebibytes):
    return pltpu.CompilerParams(vmem_limit_bytes=mebibytes * 1024 * 1024)


LIGHT = pl.CostEstimate(flops=1, bytes_accessed=1, transcendentals=0)


def after(array, *others):
    return lax.optimization_barrier((array, *others))[0]


SMEM = pl.BlockSpec(memory_space=pltpu.SMEM)
VMEM = pl.BlockSpec(memory_space=pltpu.VMEM)
ANY = pl.BlockSpec(memory_space=pl.ANY)


def base_kernel(cuts, other, place, tokens, weight, *refs):
    *outs, tokens_v, weight_v, t_sem, w_sem = refs
    part, half = outs[0].shape
    core = 1 - place[2] if other else place[2]
    columns = pl.ds(pl.multiple_of(core * half, half), half)
    copies = []
    for step, (start, depth) in enumerate(cuts):
        span = pl.ds(start, depth)
        pair = (
            pltpu.make_async_copy(tokens.at[:, span], tokens_v.at[:, span], t_sem.at[step]),
            pltpu.make_async_copy(weight.at[span, columns], weight_v.at[span, :], w_sem.at[step]),
        )
        for copy in pair:
            copy.start()
        copies.append(pair)
    for step, (start, depth) in enumerate(cuts):
        for copy in copies[step]:
            copy.wait()
        for at, out in enumerate(outs):
            product = jnp.dot(
                tokens_v[pl.ds(at * part, part), pl.ds(start, depth)],
                weight_v[pl.ds(start, depth), :],
                preferred_element_type=jnp.float32,
            )
            out[...] = product if step == 0 else out[...] + product


def base_sums(place, tokens, weight, other, parts):
    rows, width = tokens.shape
    half = weight.shape[1] // 2
    first = width // 8
    cuts = [(0, first), (first, first)] + [(at * width // 4, width // 4) for at in range(1, 4)]
    return pl.pallas_call(
        functools.partial(base_kernel, cuts, other),
        in_specs=[SMEM, ANY, ANY],
        out_specs=[VMEM] * parts,
        out_shape=[jax.ShapeDtypeStruct((rows // parts, half), jnp.float32)] * parts,
        scratch_shapes=[
            pltpu.VMEM((rows, width), tokens.dtype),
            pltpu.VMEM((width, half), weight.dtype),
            pltpu.SemaphoreType.DMA((len(cuts),)),
            pltpu.SemaphoreType.DMA((len(cuts),)),
        ],
        compiler_params=kernel_params(46),
        cost_estimate=LIGHT,
    )(place, tokens, weight)


def pool_of(place, step, other):
    depth = place[1] // 2
    column = place[1] - 2 * depth
    level = lax.rem(depth + 4 - step, 4)
    return 2 * level + (1 - column if other else column)


def half_of(place, kind):
    return {"a": 0, "b": 1, "own": place[0], "far": 1 - place[0]}[kind]


def shrink_kernel(pieces, has_prior, place, pool_index, adapter_index, tokens, *refs):
    refs = list(refs)
    arrays = [refs.pop(0) for _ in range(len({at for _, at, _ in pieces}))]
    prior = refs.pop(0) if has_prior else None
    sums, tokens_v, maps_v, t_sem, m_sem = refs
    blocks, half = sums.shape[0], tokens_v.shape[3]

    def slot_of(block):
        return pool_index[adapter_index[place[1] * blocks + block]]

    def token_copy(block, side):
        return pltpu.make_async_copy(
            tokens.at[pl.ds(block * BLK, BLK), pl.ds(side * half, half)],
            tokens_v.at[block, side],
            t_sem.at[block, side],
        )

    def start(block, carry):
        slot = slot_of(block)
        for (step, other, kind), at, column in pieces:

            @pl.when(slot == pool_of(place, step, other))
            def _(kind=kind, at=at, column=column):
                side = half_of(place, kind)
                token_copy(block, side).start()
                pltpu.make_async_copy(
                    arrays[at].at[:, column : column + half],
                    maps_v.at[block, side],
                    m_sem.at[block, side],
                ).start()

        return carry

    lax.fori_loop(0, blocks, start, 0)
    sums[...] = prior[...] if has_prior else jnp.zeros_like(sums)

    def add(block, carry):
        slot = slot_of(block)
        for side in range(2):
            wanted = jnp.bool_(False)
            for (step, other, kind), *_ in pieces:
                same = half_of(place, kind) == side
                wanted |= (slot == pool_of(place, step, other)) & same

            @pl.when(wanted)
            def _(side=side):
                token_copy(block, side).wait()
                pltpu.make_async_copy(
                    maps_v.at[block, side], maps_v.at[block, side], m_sem.at[block, side]
                ).wait()
                sums[block] += lax.dot_general(
                    maps_v[block, side],
                    tokens_v[block, side],
                    NT,
                    preferred_element_type=jnp.float32,
                )

        return carry

    lax.fori_loop(0, blocks, add, 0)


def shrink_sums(scalars, tokens, arrays, pieces, prior=None):
    rows, width = tokens.shape
    blocks, half = rows // BLK, width // 2
    has_prior = prior is not None
    return pl.pallas_call(
        functools.partial(shrink_kernel, pieces, has_prior),
        in_specs=[SMEM, SMEM, SMEM, ANY] + [ANY] * len(arrays) + [VMEM] * has_prior,
        out_specs=VMEM,
        out_shape=jax.ShapeDtypeStruct((blocks, ADAPTER_RANK, BLK), jnp.float32),
        scratch_shapes=[
            pltpu.VMEM((blocks, 2, BLK, half), tokens.dtype),
            pltpu.VMEM((blocks, 2, ADAPTER_RANK, half), tokens.dtype),
            pltpu.SemaphoreType.DMA((blocks, 2)),
            pltpu.SemaphoreType.DMA((blocks, 2)),
        ],
        compiler_params=kernel_params(46),
        cost_estimate=LIGHT,
    )(*scalars, tokens, *arrays, *([prior] if has_prior else []))


def select_kernel(pieces, place, pool_index, adapter_index, *refs):
    *arrays, ups, sem = refs
    blocks, _, half = ups.shape
    half = half // 2

    def copies(block, act):
        slot = pool_index[adapter_index[place[1] * blocks + block]]
        for (step, other, kind), at, column in pieces:

            @pl.when(slot == pool_of(place, step, other))
            def _(kind=kind, at=at, column=column):
                side = half_of(place, kind)
                start = pl.multiple_of(side * half, half)
                act(
                    pltpu.make_async_copy(
                        arrays[at].at[:, column : column + half],
                        ups.at[block, :, pl.ds(start, half)],
                        sem.at[block, side],
                    )
                )

    def start(block, carry):
        copies(block, lambda copy: copy.start())
        return carry

    def wait(block, carry):
        copies(block, lambda copy: copy.wait())
        return carry

    lax.fori_loop(0, blocks, start, 0)
    lax.fori_loop(0, blocks, wait, 0)


def select_ups(scalars, arrays, pieces, blocks, half):
    return pl.pallas_call(
        functools.partial(select_kernel, pieces),
        in_specs=[SMEM, SMEM, SMEM] + [ANY] * len(arrays),
        out_specs=VMEM,
        out_shape=jax.ShapeDtypeStruct((blocks, ADAPTER_RANK, half), jnp.bfloat16),
        scratch_shapes=[pltpu.SemaphoreType.DMA((blocks, 2))],
        compiler_params=kernel_params(16),
        cost_estimate=LIGHT,
    )(*scalars, *arrays)


def final_kernel(
    last, place, pool_index, adapter_index, live, base, sums, far_sums, ups, piece, keys, up_v
):
    (step, other, kind), column = last
    blocks, rank, half = ups.shape
    for block in range(blocks):
        index = place[1] * blocks + block
        up_v[...] = ups[block]

        @pl.when(pool_index[adapter_index[index]] == pool_of(place, step, other))
        def _():
            start = pl.multiple_of(half_of(place, kind) * (half // 2), half // 2)
            up_v[:, pl.ds(start, half // 2)] = piece[:, column : column + half // 2]

        total = sums[block] + far_sums[block]
        high = total.astype(jnp.bfloat16)
        rest = total - high.astype(jnp.float32)
        middle = rest.astype(jnp.bfloat16)
        low = (rest - middle.astype(jnp.float32)).astype(jnp.bfloat16)
        up = up_v[...]
        delta = lax.dot_general(
            jnp.concatenate([high, middle, low], axis=0),
            jnp.concatenate([up, up, up], axis=0),
            TN,
            preferred_element_type=jnp.float32,
        )
        row = lax.broadcasted_iota(jnp.int32, (BLK, half), 0)
        span = slice(block * BLK, (block + 1) * BLK)
        keys[span, :] = jnp.where(row < live[index], base[span, :] + delta, 0.0).astype(keys.dtype)


def final_keys(scalars, base, sums, far_sums, ups, piece, last):
    rows, half = base.shape
    return pl.pallas_call(
        functools.partial(final_kernel, last),
        in_specs=[SMEM] * len(scalars) + [VMEM] * 5,
        out_specs=VMEM,
        out_shape=jax.ShapeDtypeStruct((rows, half), jnp.bfloat16),
        scratch_shapes=[pltpu.VMEM((ADAPTER_RANK, half), jnp.bfloat16)],
        compiler_params=kernel_params(12),
        cost_estimate=LIGHT,
    )(*scalars, base, sums, far_sums, ups, piece)


def per_device_planes(
    tokens,
    key_projection_weight,
    adapter_down_weight,
    adapter_up_weight,
    adapter_pool_index,
    block_adapter_index,
    block_live_tokens,
):
    place = jnp.stack(
        [lax.axis_index("groups"), lax.axis_index("dp"), lax.axis_index("tensor")]
    ).astype(jnp.int32)
    down, up = adapter_down_weight[0], adapter_up_weight[0]
    width, half = down.shape[1] // 2, up.shape[1] // 2
    piece = width + half
    own = jnp.concatenate([down[:, :width], up[:, :half], down[:, width:], up[:, half:]], axis=1)
    first = lax.axis_index("groups") == 0
    own_half = jnp.where(first, own[:, :piece], own[:, piece:])

    def ring(array, step):
        pairs = [(2 * z + y, 2 * ((z + step) % 4) + y) for z in range(4) for y in range(2)]
        return lax.ppermute(array, "dp", pairs)

    def over_y(array):
        return lax.ppermute(array, "dp", [(i, i ^ 1) for i in range(8)])

    def over_x(array):
        return lax.ppermute(array, "groups", SWAP)

    def over_cores(array):
        return lax.ppermute(array, "tensor", SWAP)

    scalars = (place, adapter_pool_index, block_adapter_index[:, 0])
    z1 = ring(own_half, 1)
    y0 = over_y(own)
    z3 = ring(own_half, -1)
    fars = base_sums(place, tokens, key_projection_weight, True, FAR_PARTS)
    z1_ = after(z1, fars[0])
    x1 = over_x(z1_)
    y1 = over_y(z1_)
    z2a = ring(z1_, 1)
    z3_ = after(z3, z1_)
    x3 = over_x(z3_)
    y3 = over_y(after(z3_, y0))
    (mine,) = base_sums(place, after(tokens, z3_, y0), key_projection_weight, False, 1)
    z2b = ring(after(x1, mine), 1)
    y2a = over_y(after(z2a, mine))
    x1y = over_x(y1)
    x3y = over_x(y3)
    base_fars = [over_cores(far) for far in fars]

    group_1 = [
        ((0, False, "a"), 0, 0),
        ((0, False, "b"), 0, width),
        ((0, True, "a"), 1, 0),
        ((0, True, "b"), 1, piece),
        ((1, False, "own"), 2, 0),
        ((3, False, "own"), 3, 0),
    ]
    group_2 = [
        ((1, False, "far"), 0, 0),
        ((1, True, "own"), 1, 0),
        ((2, False, "own"), 2, 0),
        ((3, False, "far"), 3, 0),
        ((3, True, "own"), 4, 0),
    ]
    group_3 = [
        ((2, False, "far"), 0, 0),
        ((1, True, "far"), 1, 0),
        ((3, True, "far"), 2, 0),
        ((2, True, "own"), 3, 0),
    ]
    last = (2, True, "far")
    arrays_1, arrays_2, arrays_3 = [down, y0, z1, z3], [x1, y1, z2a, x3, y3], [z2b, x1y, x3y, y2a]
    sums = shrink_sums(scalars, after(tokens, y1, z2a, mine), arrays_1, group_1)
    y2b = over_y(after(z2b, x1y, x3y, y2a))
    sums = shrink_sums(scalars, after(tokens, z2b), arrays_2, group_2, sums)
    sums = shrink_sums(scalars, tokens, arrays_3, group_3, sums)
    up_group = [((0, False, "a"), 0, 0), ((0, False, "b"), 0, half)]
    up_group += [((0, True, "a"), 1, width), ((0, True, "b"), 1, piece + width)]
    up_group += [(name, at, width) for name, at, _ in group_1[4:]]
    up_group += [(name, at + 4, width) for name, at, _ in group_2]
    up_group += [(name, at + 9, width) for name, at, _ in group_3]
    ups = select_ups(
        scalars,
        [up] + arrays_1[1:] + arrays_2 + arrays_3,
        up_group,
        tokens.shape[0] // BLK,
        up.shape[1],
    )
    base = mine + jnp.concatenate(base_fars, axis=0)
    sums = shrink_sums(scalars, after(tokens, base, ups), [y2b], [(last, 0, 0)], sums)
    far_sums = over_cores(sums)
    return final_keys(
        (*scalars, block_live_tokens), base, sums, far_sums, ups, y2b, (last, width)
    )


def per_device_gathered(
    tokens,
    key_projection_weight,
    adapter_down_weight,
    adapter_up_weight,
    adapter_pool_index,
    block_adapter_index,
    block_live_tokens,
):
    rows = tokens.shape[0]
    blocks = rows // BLK
    first_block = lax.axis_index("dp") * blocks
    slots = lax.dynamic_slice_in_dim(
        adapter_pool_index[block_adapter_index[:, 0]], first_block, blocks
    )
    fill = lax.dynamic_slice_in_dim(block_live_tokens, first_block, blocks)
    base_part = jnp.dot(tokens, key_projection_weight, preferred_element_type=jnp.float32)
    down = lax.all_gather(adapter_down_weight, "dp", axis=0, tiled=True)
    up = lax.all_gather(adapter_up_weight, "dp", axis=0, tiled=True)
    token_blocks = tokens.reshape(blocks, BLK, tokens.shape[1])
    shrink = jnp.einsum(
        "nrd,nbd->rnb",
        jnp.take(down, slots, axis=0),
        token_blocks,
        preferred_element_type=jnp.float32,
    )
    shrink = lax.psum(shrink.reshape(ADAPTER_RANK, rows), "tensor")
    delta = jnp.einsum(
        "rnb,nrc->nbc",
        shrink.reshape(ADAPTER_RANK, blocks, BLK),
        jnp.take(up, slots, axis=0).astype(jnp.float32),
        precision=lax.Precision.HIGHEST,
        preferred_element_type=jnp.float32,
    )
    base = lax.psum_scatter(base_part, "tensor", scatter_dimension=1, tiled=True)
    mask = jnp.arange(BLK, dtype=jnp.int32)[None, :] < fill[:, None]
    keys = base + delta.reshape(rows, base.shape[1])
    return jnp.where(mask.reshape(rows, 1), keys, 0.0).astype(jnp.bfloat16)


def solution(mesh):
    in_specs = (
        P(("groups", "dp"), "tensor"),
        P("tensor", None),
        P("dp", None, "tensor"),
        P("dp", None, "tensor"),
        P(),
        P("groups", None),
        P("groups"),
    )
    out_specs = P(("groups", "dp"), "tensor")
    planes = dict(mesh.shape) == {"groups": 2, "dp": 8, "tensor": 2}
    return jax.shard_map(
        per_device_planes if planes else per_device_gathered,
        mesh=mesh,
        in_specs=in_specs,
        out_specs=out_specs,
        check_vma=False,
    )
```

time: 60.5 us -> 61.6 us (1.018)
  the two profiles are of different devices: /device:TPU:0 before, /device:TPU:9 now
where the time goes in v3:
time: 61.6 us; the launch traced here: 60.6 us
  Pallas kernels  28 us (45%)
  starting transfers between devices  22.6 us (37%)
  local copies, waits for them, and re-layouts  4.66 us (8%)
  waiting for transfers between devices  4.65 us (8%)
    ppermute x4, starting transfers between devices, over_cores(): return lax.ppermute(array, 'tensor', SWAP)  12.2 us
    pallas_call x2, Pallas kernels, base_sums(): pl.pallas_call(functools.partial(base_kernel, cuts, other), in_specs=[SME...  10.8 us
    pallas_call x4, Pallas kernels, shrink_sums(): pl.pallas_call(functools.partial(shrink_kernel, pieces, has_prior), in_sp...  10.6 us
    ppermute x5, starting transfers between devices, over_y(): return lax.ppermute(array, 'dp', [(i, i ^ 1) for i in range(8)])  3.99 us
    pallas_call x1, Pallas kernels, select_ups(): pl.pallas_call(functools.partial(select_kernel, pieces), in_specs=[SMEM,...  3.81 us
    ppermute x4, waiting for transfers between devices, ring(): return lax.ppermute(array, 'dp', pairs)  3.53 us
    ppermute x4, starting transfers between devices, over_x(): return lax.ppermute(array, 'groups', SWAP)  3.49 us
    ppermute x4, starting transfers between devices, ring(): return lax.ppermute(array, 'dp', pairs)  2.87 us
  transfers between devices with their start and end apart: 17, of which 2 were waited for; matrix products, arithmetic and copies ran while one was open for 1% of the time, Pallas kernels for 40%

profile of v3, /device:TPU:9, one launch (start us, length us, event | category | flops | bytes accessed | tf_op | source)
XLA Modules:
  0.0 60.6 jit_solution(6271625832628648126)
XLA Ops:
  0.0 0.8 %fusion.1 = (bf16[64,256]{1,0:T(8,128)(2,1)S(1)}, bf16[64,256]{1,0:T(8,128)(2,1)S(1)}) fusion(bf16[64,512]{1,0:T(8,128)(2,1)} %bitcast.8), kind=kLoop, calls=%fused_computation.5 | loop fusion | bytes 131072 | tf_op jit(solution)/shard_map/slice | solution.py:279
  0.8 1.1 %fusion = (bf16[64,2048]{1,0:T(8,128)(2,1)S(1)}, bf16[64,2048]{1,0:T(8,128)(2,1)S(1)}) fusion(bf16[64,4096]{1,0:T(8,128)(2,1)} %bitcast.6), kind=kLoop, calls=%fused_computation.4 | loop fusion | bytes 1048576 | tf_op jit(solution)/shard_map/slice | solution.py:279
  1.9 1.3 %collective-permute-start.2 = (bf16[64,4608]{1,0:T(8,128)(2,1)S(1)}, bf16[64,4608]{1,0:T(8,128)(2,1)S(1)}, u32[]{:S(2)}, u32[]{:S(2)}) collective-permute-start(bf16[64,4608]{1,0:T(8,128)(2,1)S(1)} %pad_maximum_fusion), channel_id=1, source_target_pairs={{0,2},{2,0},{4,6},{6,4},{8,10},{10,8},{12,14},{14,12},{1,3},{3,1},... | collective-permute-start | bytes 1769480 | tf_op jit(solution)/shard_map/ppermute | solution.py:288
  3.2 0.1 maximum_select_fusion
  3.3 1.3 %collective-permute-start.1 = (bf16[64,2304]{1,0:T(8,128)(2,1)S(1)}, bf16[64,2304]{1,0:T(8,128)(2,1)S(1)}, u32[]{:S(2)}, u32[]{:S(2)}) collective-permute-start(bf16[64,2304]{1,0:T(8,128)(2,1)S(1)} %maximum_select_fusion), channel_id=1, source_target_pairs={{0,4},{2,6},{4,8},{6,10},{8,12},{10,14},{12,0},{14,2},{1,5},{3,7},... | collective-permute-start | bytes 884744 | tf_op jit(solution)/shard_map/ppermute | solution.py:285
  4.6 0.2 collective-permute-start
  4.8 0.1 pad_add_fusion.place
  4.9 2.8 %copy-done = bf16[768,4096]{1,0:T(8,128)(2,1)S(1)} copy-done((bf16[768,4096]{1,0:T(8,128)(2,1)S(1)}, bf16[768,4096]{1,0:T(8,128)(2,1)}, u32[]{:S(2)}) %copy-start) | copy-done | bytes 6291480
  7.7 5.4 %shard_map.73 = (f32[256,512]{1,0:T(8,128)S(1)}, f32[256,512]{1,0:T(8,128)S(1)}, f32[256,512]{1,0:T(8,128)S(1)}) custom-call(s32[3]{0:T(128)S(1)} %pad_add_fusion.place, bf16[768,4096]{1,0:T(8,128)(2,1)S(1)} %copy-done, bf16[4096,1024]{1,0:T(8,128)(2,1)} %weight.3), custom_call_target="tpu_custom_call" | custom-call | flops 1 | bytes 1 | tf_op jit(solution)/shard_map/pallas_call | solution.py:66
  13.1 0.0 collective-permute-done.1.refs_2_
  13.1 0.0 copy-start.1
  13.1 0.0 copy-start.3
  13.1 0.0 copy-start.4
  13.1 1.3 %collective-permute-start.6 = (bf16[64,2304]{1,0:T(8,128)(2,1)S(1)}, bf16[64,2304]{1,0:T(8,128)(2,1)S(1)}, u32[]{:S(2)}, u32[]{:S(2)}) collective-permute-start(bf16[64,2304]{1,0:T(8,128)(2,1)S(1)} %collective-permute-done.1.refs_2_), channel_id=1, source_target_pairs={{0,16},{16,0},{1,17},{17,1},{2,18},{18,2},{3,19},{19,3},{4,20},{20... | collective-permute-start | bytes 884744 | tf_op jit(solution)/shard_map/ppermute | solution.py:291
  14.4 0.2 collective-permute-start.7
  14.6 1.3 %collective-permute-start.8 = (bf16[64,2304]{1,0:T(8,128)(2,1)S(1)}, bf16[64,2304]{1,0:T(8,128)(2,1)S(1)}, u32[]{:S(2)}, u32[]{:S(2)}) collective-permute-start(bf16[64,2304]{1,0:T(8,128)(2,1)S(1)} %collective-permute-done.1.refs_2_), channel_id=1, source_target_pairs={{0,4},{2,6},{4,8},{6,10},{8,12},{10,14},{12,0},{14,2},{1,5},{3,7},... | collective-permute-start | bytes 884744 | tf_op jit(solution)/shard_map/ppermute | solution.py:285
  15.9 3.5 %collective-permute-done.refs_3_ = bf16[64,2304]{1,0:T(8,128)(2,1)S(1)} collective-permute-done((bf16[64,2304]{1,0:T(8,128)(2,1)S(1)}, bf16[64,2304]{1,0:T(8,128)(2,1)S(1)}, u32[]{:S(2)}, u32[]{:S(2)}) %collective-permute-start) | collective-permute-done | bytes 294944 | tf_op jit(solution)/shard_map/ppermute | solution.py:285
  19.4 1.5 %collective-permute-start.9 = (bf16[64,2304]{1,0:T(8,128)(2,1)S(1)}, bf16[64,2304]{1,0:T(8,128)(2,1)S(1)}, u32[]{:S(2)}, u32[]{:S(2)}) collective-permute-start(bf16[64,2304]{1,0:T(8,128)(2,1)S(1)} %collective-permute-done.refs_3_), channel_id=1, source_target_pairs={{0,16},{16,0},{1,17},{17,1},{2,18},{18,2},{3,19},{19,3},{4,20},{20... | collective-permute-start | bytes 884744 | tf_op jit(solution)/shard_map/ppermute | solution.py:291
  20.9 0.0 collective-permute-done.2.refs_1_
  20.9 0.0 collective-permute-start.10
  20.9 5.4 %shard_map.74 = f32[768,512]{1,0:T(8,128)S(1)} custom-call(s32[3]{0:T(128)S(1)} %pad_add_fusion.place, bf16[768,4096]{1,0:T(8,128)(2,1)S(1)} %copy-done, bf16[4096,1024]{1,0:T(8,128)(2,1)} %weight.3), custom_call_target="tpu_custom_call" | custom-call | flops 1 | bytes 1 | tf_op jit(solution)/shard_map/pallas_call | solution.py:66
  26.3 0.0 collective-permute-done.6.refs_4_.refs_0_
  26.3 0.1 collective-permute-start.11
  26.4 0.0 collective-permute-done.7.refs_5_.refs_1_
  26.4 0.3 collective-permute-start.12
  26.7 0.0 collective-permute-done.8.refs_6_.refs_2_
  26.7 5.3 %collective-permute-start.5 = (f32[256,512]{1,0:T(8,128)S(1)}, f32[256,512]{1,0:T(8,128)S(1)}, u32[]{:S(2)}, u32[]{:S(2)}) collective-permute-start(f32[256,512]{1,0:T(8,128)S(1)} %get-tuple-element.23), channel_id=1, source_target_pairs={{0,1},{1,0},{2,3},{3,2},{4,5},{5,4},{6,7},{7,6},{8,9},{9,8},{10,11... | collective-permute-start | bytes 1572872 | tf_op jit(solution)/shard_map/ppermute | solution.py:294
  32.0 0.0 collective-permute-done.9.refs_7_.refs_3_
  32.0 0.1 collective-permute-start.4
  32.0 0.0 collective-permute-done.10.refs_8_.refs_4_
  32.1 0.4 collective-permute-start.3
  32.5 0.0 collective-permute-done.11.refs_9_.refs_0_
  32.5 1.3 %collective-permute-start.14 = (bf16[64,2304]{1,0:T(8,128)(2,1)S(1)}, bf16[64,2304]{1,0:T(8,128)(2,1)S(1)}, u32[]{:S(2)}, u32[]{:S(2)}) collective-permute-start(bf16[64,2304]{1,0:T(8,128)(2,1)S(1)} %collective-permute-done.8.refs_6_.refs_2_), channel_id=1, source_target_pairs={{0,2},{2,0},{4,6},{6,4},{8,10},{10,8},{12,14},{14,12},{1,3},{3,1},... | collective-permute-start | bytes 884744 | tf_op jit(solution)/shard_map/ppermute | solution.py:288
  33.8 0.5 collective-permute-start.13
  34.3 3.2 %shard_map.76.refs_5_ = f32[6,64,128]{2,1,0:T(8,128)S(1)} custom-call(s32[3]{0:T(128)S(1)} %pad_add_fusion.place, s32[8]{0:T(128)S(1)} %copy-done.3, s32[48]{0:T(128)S(1)} %bitcast.10, bf16[768,4096]{1,0:T(8,128)(2,1)S(1)} %copy-done, bf16[64,4096]{1,0:T(8,128)(2,1)S(1)} %bitcast.7, bf16[64,4608]{1,0:T(8,128)(2,1)S(1)} %collective-permute-done.2.refs_1_, ...), custom_call_target="tpu_custom_call" | custom-call | flops 1 | bytes 1 | tf_op jit(solution)/shard_map/pallas_call | solution.py:159
  37.5 3.2 %shard_map.77.refs_4_ = f32[6,64,128]{2,1,0:T(8,128)S(1)} custom-call(s32[3]{0:T(128)S(1)} %pad_add_fusion.place, s32[8]{0:T(128)S(1)} %copy-done.3, s32[48]{0:T(128)S(1)} %bitcast.11, bf16[768,4096]{1,0:T(8,128)(2,1)S(1)} %copy-done, bf16[64,2304]{1,0:T(8,128)(2,1)S(1)} %collective-permute-done.6.refs_4_.refs_0_, ...), custom_call_target="tpu_custom_call" | custom-call | flops 1 | bytes 1 | tf_op jit(solution)/shard_map/pallas_call | solution.py:159
  40.7 0.0 copy-start.2
  40.7 0.0 collective-permute-done.13.refs_11_.refs_2_
  40.7 1.1 %collective-permute-start.15 = (bf16[64,2304]{1,0:T(8,128)(2,1)S(1)}, bf16[64,2304]{1,0:T(8,128)(2,1)S(1)}, u32[]{:S(2)}, u32[]{:S(2)}) collective-permute-start(bf16[64,2304]{1,0:T(8,128)(2,1)S(1)} %collective-permute-done.11.refs_9_.refs_0_), channel_id=1, source_target_pairs={{0,2},{2,0},{4,6},{6,4},{8,10},{10,8},{12,14},{14,12},{1,3},{3,1},... | collective-permute-start | bytes 884744 | tf_op jit(solution)/shard_map/ppermute | solution.py:288
  41.9 0.0 collective-permute-done.3
  41.9 0.3 maximum_add_fusion.base
  42.2 3.8 %shard_map.75.ups = bf16[6,64,512]{2,1,0:T(8,128)(2,1)S(1)} custom-call(s32[3]{0:T(128)S(1)} %pad_add_fusion.place, s32[8]{0:T(128)S(1)} %copy-done.3, s32[48]{0:T(128)S(1)} %bitcast.12, bf16[64,512]{1,0:T(8,128)(2,1)S(1)} %bitcast.9, bf16[64,4608]{1,0:T(8,128)(2,1)S(1)} %collective-permute-done.2.refs_1_, ...), custom_call_target="tpu_custom_call" | custom-call | flops 1 | bytes 1 | tf_op jit(solution)/shard_map/pallas_call | solution.py:209
  46.1 3.0 %shard_map.78.refs_1_ = f32[6,64,128]{2,1,0:T(8,128)S(1)} custom-call(s32[3]{0:T(128)S(1)} %pad_add_fusion.place, s32[8]{0:T(128)S(1)} %copy-done.3, s32[48]{0:T(128)S(1)} %bitcast.13, bf16[768,4096]{1,0:T(8,128)(2,1)S(1)} %copy-done, bf16[64,2304]{1,0:T(8,128)(2,1)S(1)} %collective-permute-done.11.refs_9_.refs_0_, ...), custom_call_target="tpu_custom_call" | custom-call | flops 1 | bytes 1 | tf_op jit(solution)/shard_map/pallas_call | solution.py:159
  49.1 0.0 copy-start.5
  49.1 1.2 %shard_map.79.sums = f32[6,64,128]{2,1,0:T(8,128)S(1)} custom-call(s32[3]{0:T(128)S(1)} %pad_add_fusion.place, s32[8]{0:T(128)S(1)} %copy-done.3, s32[48]{0:T(128)S(1)} %bitcast.14, bf16[768,4096]{1,0:T(8,128)(2,1)S(1)} %copy-done, bf16[64,2304]{1,0:T(8,128)(2,1)S(1)} %collective-permute-done.15.refs_0_.piece, f32[6,64,128]{2,1,0:T(8,128)S(1)} %shard_map.78.refs_1_), custom_call_target="tpu_custom_call" | custom-call | flops 1 | bytes 1 | tf_op jit(solution)/shard_map/pallas_call | solution.py:159
  50.3 6.4 %collective-permute-start.16 = (f32[6,64,128]{2,1,0:T(8,128)S(1)}, f32[6,64,128]{2,1,0:T(8,128)S(1)}, u32[]{:S(2)}, u32[]{:S(2)}) collective-permute-start(f32[6,64,128]{2,1,0:T(8,128)S(1)} %shard_map.79.sums), channel_id=1, source_target_pairs={{0,1},{1,0},{2,3},{3,2},{4,5},{5,4},{6,7},{7,6},{8,9},{9,8},{10,11... | collective-permute-start | bytes 589832 | tf_op jit(solution)/shard_map/ppermute | solution.py:294
  56.7 1.1 %collective-permute-done.16.far_sums = f32[6,64,128]{2,1,0:T(8,128)S(1)} collective-permute-done((f32[6,64,128]{2,1,0:T(8,128)S(1)}, f32[6,64,128]{2,1,0:T(8,128)S(1)}, u32[]{:S(2)}, u32[]{:S(2)}) %collective-permute-start.16) | collective-permute-done | bytes 196640 | tf_op jit(solution)/shard_map/ppermute | solution.py:294
  57.8 2.8 %shard_map.80 = bf16[768,512]{1,0:T(8,128)(2,1)} custom-call(s32[3]{0:T(128)S(1)} %pad_add_fusion.place, s32[8]{0:T(128)S(1)} %copy-done.3, s32[48]{0:T(128)S(1)} %bitcast.15, s32[48]{0:T(128)S(1)} %copy-done.5, f32[768,512]{1,0:T(8,128)S(1)} %maximum_add_fusion.base, f32[6,64,128]{2,1,0:T(8,128)S(1)} %shard_map.79.sums, ...), custom_call_target="tpu_custom_call" | custom-call | flops 1 | bytes 1 | tf_op jit(solution)/shard_map/pallas_call | solution.py:253
  (12 shorter events, 0.1 us)
Async XLA Ops:
  1.9 19.0 %collective-permute-start.2 = (bf16[64,4608]{1,0:T(8,128)(2,1)S(1)}, bf16[64,4608]{1,0:T(8,128)(2,1)S(1)}, u32[]{:S(2)}, u32[]{:S(2)}) collective-permute-start(bf16[64,4608]{1,0:T(8,128)(2,1)S(1)} %pad_maximum_fusion), channel_id=1, source_target_pairs={{0,2},{2,0},{4,6},{6,4},{8,10},{10,8},{12,14},{14,12},{1,3},{3,1},... | collective-permute-start | bytes 1769480 | tf_op jit(solution)/shard_map/ppermute | solution.py:288
  3.3 9.8 %collective-permute-start.1 = (bf16[64,2304]{1,0:T(8,128)(2,1)S(1)}, bf16[64,2304]{1,0:T(8,128)(2,1)S(1)}, u32[]{:S(2)}, u32[]{:S(2)}) collective-permute-start(bf16[64,2304]{1,0:T(8,128)(2,1)S(1)} %maximum_select_fusion), channel_id=1, source_target_pairs={{0,4},{2,6},{4,8},{6,10},{8,12},{10,14},{12,0},{14,2},{1,5},{3,7},... | collective-permute-start | bytes 884744 | tf_op jit(solution)/shard_map/ppermute | solution.py:285
  4.6 14.8 %collective-permute-start = (bf16[64,2304]{1,0:T(8,128)(2,1)S(1)}, bf16[64,2304]{1,0:T(8,128)(2,1)S(1)}, u32[]{:S(2)}, u32[]{:S(2)}) collective-permute-start(bf16[64,2304]{1,0:T(8,128)(2,1)S(1)} %maximum_select_fusion), channel_id=1, source_target_pairs={{0,12},{2,14},{4,0},{6,2},{8,4},{10,6},{12,8},{14,10},{1,13},{3,15... | collective-permute-start | bytes 884744 | tf_op jit(solution)/shard_map/ppermute | solution.py:285
  4.9 2.8 %copy-start = (bf16[768,4096]{1,0:T(8,128)(2,1)S(1)}, bf16[768,4096]{1,0:T(8,128)(2,1)}, u32[]{:S(2)}) copy-start(bf16[768,4096]{1,0:T(8,128)(2,1)} %tokens.7) | copy-start | bytes 18874372
  13.1 21.2 %copy-start.1 = (bf16[1,64,4096]{2,1,0:T(8,128)(2,1)S(1)}, bf16[1,64,4096]{2,1,0:T(8,128)(2,1)}, u32[]{:S(2)}) copy-start(bf16[1,64,4096]{2,1,0:T(8,128)(2,1)} %param.9) | copy-start | bytes 1572868
  13.1 21.2 %copy-start.3 = (s32[8]{0:T(128)S(1)}, s32[8]{0:T(128)}, u32[]{:S(2)}) copy-start(s32[8]{0:T(128)} %pool_index.11) | copy-start | bytes 100
  13.1 21.2 %copy-start.4 = (s32[48,1]{0,1:T(1,128)S(1)}, s32[48,1]{0,1:T(1,128)}, u32[]{:S(2)}) copy-start(s32[48,1]{0,1:T(1,128)} %param.12) | copy-start | bytes 580
  13.1 13.2 %collective-permute-start.6 = (bf16[64,2304]{1,0:T(8,128)(2,1)S(1)}, bf16[64,2304]{1,0:T(8,128)(2,1)S(1)}, u32[]{:S(2)}, u32[]{:S(2)}) collective-permute-start(bf16[64,2304]{1,0:T(8,128)(2,1)S(1)} %collective-permute-done.1.refs_2_), channel_id=1, source_target_pairs={{0,16},{16,0},{1,17},{17,1},{2,18},{18,2},{3,19},{19,3},{4,20},{20... | collective-permute-start | bytes 884744 | tf_op jit(solution)/shard_map/ppermute | solution.py:291
  14.4 12.0 %collective-permute-start.7 = (bf16[64,2304]{1,0:T(8,128)(2,1)S(1)}, bf16[64,2304]{1,0:T(8,128)(2,1)S(1)}, u32[]{:S(2)}, u32[]{:S(2)}) collective-permute-start(bf16[64,2304]{1,0:T(8,128)(2,1)S(1)} %collective-permute-done.1.refs_2_), channel_id=1, source_target_pairs={{0,2},{2,0},{4,6},{6,4},{8,10},{10,8},{12,14},{14,12},{1,3},{3,1},... | collective-permute-start | bytes 884744 | tf_op jit(solution)/shard_map/ppermute | solution.py:288
  14.6 12.1 %collective-permute-start.8 = (bf16[64,2304]{1,0:T(8,128)(2,1)S(1)}, bf16[64,2304]{1,0:T(8,128)(2,1)S(1)}, u32[]{:S(2)}, u32[]{:S(2)}) collective-permute-start(bf16[64,2304]{1,0:T(8,128)(2,1)S(1)} %collective-permute-done.1.refs_2_), channel_id=1, source_target_pairs={{0,4},{2,6},{4,8},{6,10},{8,12},{10,14},{12,0},{14,2},{1,5},{3,7},... | collective-permute-start | bytes 884744 | tf_op jit(solution)/shard_map/ppermute | solution.py:285
  19.4 12.6 %collective-permute-start.9 = (bf16[64,2304]{1,0:T(8,128)(2,1)S(1)}, bf16[64,2304]{1,0:T(8,128)(2,1)S(1)}, u32[]{:S(2)}, u32[]{:S(2)}) collective-permute-start(bf16[64,2304]{1,0:T(8,128)(2,1)S(1)} %collective-permute-done.refs_3_), channel_id=1, source_target_pairs={{0,16},{16,0},{1,17},{17,1},{2,18},{18,2},{3,19},{19,3},{4,20},{20... | collective-permute-start | bytes 884744 | tf_op jit(solution)/shard_map/ppermute | solution.py:291
  20.9 11.1 %collective-permute-start.10 = (bf16[64,2304]{1,0:T(8,128)(2,1)S(1)}, bf16[64,2304]{1,0:T(8,128)(2,1)S(1)}, u32[]{:S(2)}, u32[]{:S(2)}) collective-permute-start(bf16[64,2304]{1,0:T(8,128)(2,1)S(1)} %collective-permute-done.refs_3_), channel_id=1, source_target_pairs={{0,2},{2,0},{4,6},{6,4},{8,10},{10,8},{12,14},{14,12},{1,3},{3,1},... | collective-permute-start | bytes 884744 | tf_op jit(solution)/shard_map/ppermute | solution.py:288
  26.3 6.2 %collective-permute-start.11 = (bf16[64,2304]{1,0:T(8,128)(2,1)S(1)}, bf16[64,2304]{1,0:T(8,128)(2,1)S(1)}, u32[]{:S(2)}, u32[]{:S(2)}) collective-permute-start(bf16[64,2304]{1,0:T(8,128)(2,1)S(1)} %collective-permute-done.6.refs_4_.refs_0_), channel_id=1, source_target_pairs={{0,4},{2,6},{4,8},{6,10},{8,12},{10,14},{12,0},{14,2},{1,5},{3,7},... | collective-permute-start | bytes 884744 | tf_op jit(solution)/shard_map/ppermute | solution.py:285
  26.4 7.4 %collective-permute-start.12 = (bf16[64,2304]{1,0:T(8,128)(2,1)S(1)}, bf16[64,2304]{1,0:T(8,128)(2,1)S(1)}, u32[]{:S(2)}, u32[]{:S(2)}) collective-permute-start(bf16[64,2304]{1,0:T(8,128)(2,1)S(1)} %collective-permute-done.7.refs_5_.refs_1_), channel_id=1, source_target_pairs={{0,16},{16,0},{1,17},{17,1},{2,18},{18,2},{3,19},{19,3},{4,20},{20... | collective-permute-start | bytes 884744 | tf_op jit(solution)/shard_map/ppermute | solution.py:291
  26.7 15.2 %collective-permute-start.5 = (f32[256,512]{1,0:T(8,128)S(1)}, f32[256,512]{1,0:T(8,128)S(1)}, u32[]{:S(2)}, u32[]{:S(2)}) collective-permute-start(f32[256,512]{1,0:T(8,128)S(1)} %get-tuple-element.23), channel_id=1, source_target_pairs={{0,1},{1,0},{2,3},{3,2},{4,5},{5,4},{6,7},{7,6},{8,9},{9,8},{10,11... | collective-permute-start | bytes 1572872 | tf_op jit(solution)/shard_map/ppermute | solution.py:294
  32.0 9.9 %collective-permute-start.4 = (f32[256,512]{1,0:T(8,128)S(1)}, f32[256,512]{1,0:T(8,128)S(1)}, u32[]{:S(2)}, u32[]{:S(2)}) collective-permute-start(f32[256,512]{1,0:T(8,128)S(1)} %get-tuple-element.22), channel_id=1, source_target_pairs={{0,1},{1,0},{2,3},{3,2},{4,5},{5,4},{6,7},{7,6},{8,9},{9,8},{10,11... | collective-permute-start | bytes 1572872 | tf_op jit(solution)/shard_map/ppermute | solution.py:294
  32.1 9.8 %collective-permute-start.3 = (f32[256,512]{1,0:T(8,128)S(1)}, f32[256,512]{1,0:T(8,128)S(1)}, u32[]{:S(2)}, u32[]{:S(2)}) collective-permute-start(f32[256,512]{1,0:T(8,128)S(1)} %get-tuple-element.18), channel_id=1, source_target_pairs={{0,1},{1,0},{2,3},{3,2},{4,5},{5,4},{6,7},{7,6},{8,9},{9,8},{10,11... | collective-permute-start | bytes 1572872 | tf_op jit(solution)/shard_map/ppermute | solution.py:294
  32.5 8.2 %collective-permute-start.14 = (bf16[64,2304]{1,0:T(8,128)(2,1)S(1)}, bf16[64,2304]{1,0:T(8,128)(2,1)S(1)}, u32[]{:S(2)}, u32[]{:S(2)}) collective-permute-start(bf16[64,2304]{1,0:T(8,128)(2,1)S(1)} %collective-permute-done.8.refs_6_.refs_2_), channel_id=1, source_target_pairs={{0,2},{2,0},{4,6},{6,4},{8,10},{10,8},{12,14},{14,12},{1,3},{3,1},... | collective-permute-start | bytes 884744 | tf_op jit(solution)/shard_map/ppermute | solution.py:288
  33.8 6.9 %collective-permute-start.13 = (bf16[64,2304]{1,0:T(8,128)(2,1)S(1)}, bf16[64,2304]{1,0:T(8,128)(2,1)S(1)}, u32[]{:S(2)}, u32[]{:S(2)}) collective-permute-start(bf16[64,2304]{1,0:T(8,128)(2,1)S(1)} %collective-permute-done.10.refs_8_.refs_4_), channel_id=1, source_target_pairs={{0,16},{16,0},{1,17},{17,1},{2,18},{18,2},{3,19},{19,3},{4,20},{20... | collective-permute-start | bytes 884744 | tf_op jit(solution)/shard_map/ppermute | solution.py:291
  40.7 1.5 %copy-start.2 = (bf16[1,64,512]{2,1,0:T(8,128)(2,1)S(1)}, bf16[1,64,512]{2,1,0:T(8,128)(2,1)}, u32[]{:S(2)}) copy-start(bf16[1,64,512]{2,1,0:T(8,128)(2,1)} %param.10) | copy-start | bytes 196612
  40.7 8.4 %collective-permute-start.15 = (bf16[64,2304]{1,0:T(8,128)(2,1)S(1)}, bf16[64,2304]{1,0:T(8,128)(2,1)S(1)}, u32[]{:S(2)}, u32[]{:S(2)}) collective-permute-start(bf16[64,2304]{1,0:T(8,128)(2,1)S(1)} %collective-permute-done.11.refs_9_.refs_0_), channel_id=1, source_target_pairs={{0,2},{2,0},{4,6},{6,4},{8,10},{10,8},{12,14},{14,12},{1,3},{3,1},... | collective-permute-start | bytes 884744 | tf_op jit(solution)/shard_map/ppermute | solution.py:288
  49.1 8.7 %copy-start.5 = (s32[48]{0:T(128)S(1)}, s32[48]{0:T(128)}, u32[]{:S(2)}) copy-start(s32[48]{0:T(128)} %live.1) | copy-start | bytes 580
  50.3 7.5 %collective-permute-start.16 = (f32[6,64,128]{2,1,0:T(8,128)S(1)}, f32[6,64,128]{2,1,0:T(8,128)S(1)}, u32[]{:S(2)}, u32[]{:S(2)}) collective-permute-start(f32[6,64,128]{2,1,0:T(8,128)S(1)} %shard_map.79.sums), channel_id=1, source_target_pairs={{0,1},{1,0},{2,3},{3,2},{4,5},{5,4},{6,7},{7,6},{8,9},{9,8},{10,11... | collective-permute-start | bytes 589832 | tf_op jit(solution)/shard_map/ppermute | solution.py:294

commit v4 on v3

v4 whole, which is shorter than its diff:
```python
import functools

import jax
import jax.numpy as jnp
from jax import lax
from jax.experimental import pallas as pl
from jax.experimental.pallas import tpu as pltpu
from jax.sharding import PartitionSpec as P

ADAPTER_RANK = 64
BLK = 128
FAR_PARTS = 3
SWAP = [(0, 1), (1, 0)]
NT = (((1,), (1,)), ((), ()))
TN = (((0,), (0,)), ((), ()))


def kernel_params(mebibytes):
    return pltpu.CompilerParams(vmem_limit_bytes=mebibytes * 1024 * 1024)


LIGHT = pl.CostEstimate(flops=1, bytes_accessed=1, transcendentals=0)


HEAVY = pl.CostEstimate(flops=30000000000, bytes_accessed=1, transcendentals=0)


def after(array, *others):
    return lax.optimization_barrier((array, *others))[0]


SMEM = pl.BlockSpec(memory_space=pltpu.SMEM)
VMEM = pl.BlockSpec(memory_space=pltpu.VMEM)
ANY = pl.BlockSpec(memory_space=pl.ANY)


def base_kernel(cuts, other, place, tokens, weight, *refs):
    *outs, tokens_v, weight_v, t_sem, w_sem = refs
    base_steps(cuts, 1 - place[2] if other else place[2], tokens, weight, outs, refs[-4:])


def base_steps(cuts, core, tokens, weight, outs, scratch):
    tokens_v, weight_v, t_sem, w_sem = scratch
    part, half = outs[0].shape
    columns = pl.ds(pl.multiple_of(core * half, half), half)
    copies = []
    for step, (start, depth) in enumerate(cuts):
        span = pl.ds(start, depth)
        pair = (
            pltpu.make_async_copy(tokens.at[:, span], tokens_v.at[:, span], t_sem.at[step]),
            pltpu.make_async_copy(weight.at[span, columns], weight_v.at[span, :], w_sem.at[step]),
        )
        for copy in pair:
            copy.start()
        copies.append(pair)
    for step, (start, depth) in enumerate(cuts):
        for copy in copies[step]:
            copy.wait()
        for at, out in enumerate(outs):
            product = jnp.dot(
                tokens_v[pl.ds(at * part, part), pl.ds(start, depth)],
                weight_v[pl.ds(start, depth), :],
                preferred_element_type=jnp.float32,
            )
            out[...] = product if step == 0 else out[...] + product


def base_cuts(width):
    first = width // 8
    return [(0, first), (first, first)] + [(at * width // 4, width // 4) for at in range(1, 4)]


def base_scratch(tokens, weight):
    rows, width = tokens.shape
    steps = len(base_cuts(width))
    return [
        pltpu.VMEM((rows, width), tokens.dtype),
        pltpu.VMEM((width, weight.shape[1] // 2), weight.dtype),
        pltpu.SemaphoreType.DMA((steps,)),
        pltpu.SemaphoreType.DMA((steps,)),
    ]


def base_far(place, tokens, weight, parts):
    rows, width = tokens.shape
    half = weight.shape[1] // 2
    return pl.pallas_call(
        functools.partial(base_kernel, base_cuts(width), True),
        in_specs=[SMEM, ANY, ANY],
        out_specs=[VMEM] * parts,
        out_shape=[jax.ShapeDtypeStruct((rows // parts, half), jnp.float32)] * parts,
        scratch_shapes=base_scratch(tokens, weight),
        compiler_params=kernel_params(50),
        cost_estimate=HEAVY,
    )(place, tokens, weight)


def entry_of(place, slot):
    back = ((place[1] >> 1) - (slot >> 1)) & 3
    return 2 * back + ((slot ^ place[1]) & 1)


def side_of(place, kind):
    return {"a": 0, "b": 1, "own": place[0], "far": 1 - place[0]}[kind]


def start_maps(pieces, entry_at, place, downs, ups, maps_v, up_map, sems, start_tokens=None):
    m_sem, u_sem = sems
    blocks, _, _, wide = maps_v.shape
    half = up_map.shape[2] // 2

    def start(block, carry):
        entry = entry_at(block)
        for at_entry, kind, at, column, up_column in pieces:

            @pl.when(entry == at_entry)
            def _(kind=kind, at=at, column=column, up_column=up_column):
                side = side_of(place, kind)
                if start_tokens is not None:
                    start_tokens(block, side)
                pltpu.make_async_copy(
                    downs[at].at[:, column : column + wide],
                    maps_v.at[block, side],
                    m_sem.at[block, side],
                ).start()
                pltpu.make_async_copy(
                    ups[at].at[:, up_column : up_column + half],
                    up_map.at[block, :, pl.ds(pl.multiple_of(side * half, half), half)],
                    u_sem.at[block, side],
                ).start()

        return carry

    lax.fori_loop(0, blocks, start, 0)


def add_maps(pieces, entry_at, place, maps_v, tokens_v, up_map, sums, sems, wait_tokens=None):
    m_sem, u_sem = sems
    blocks, _, _, wide = maps_v.shape
    half = up_map.shape[2] // 2
    masks = []
    for side in range(2):
        bits = {"a": 0, "b": 0, "own": 0, "far": 0}
        for entry, kind, *_ in pieces:
            bits[kind] |= 1 << entry
        masks.append(
            bits["a" if side == 0 else "b"]
            | jnp.where(place[0] == side, bits["own"], bits["far"])
        )

    def add(block, carry):
        entry = entry_at(block)
        for side in range(2):

            @pl.when(((masks[side] >> entry) & 1) == 1)
            def _(side=side):
                if wait_tokens is not None:
                    wait_tokens(block, side)
                pltpu.make_async_copy(
                    maps_v.at[block, side], maps_v.at[block, side], m_sem.at[block, side]
                ).wait()
                sums[block] += lax.dot_general(
                    maps_v[block, side],
                    tokens_v[pl.ds(pl.multiple_of(block * BLK, BLK), BLK), pl.ds(side * wide, wide)],
                    NT,
                    preferred_element_type=jnp.float32,
                )
                half_map = up_map.at[block, :, pl.ds(side * half, half)]
                pltpu.make_async_copy(half_map, half_map, u_sem.at[block, side]).wait()

        return carry

    lax.fori_loop(0, blocks, add, 0)


def mine_kernel(cuts, pieces, count, place, pool_index, adapter_index, tokens, weight, *refs):
    downs, ups = refs[:count], refs[count : 2 * count]
    mine, sums, up_map, tokens_v, weight_v, t_sem, w_sem, maps_v, m_sem, u_sem = refs[2 * count :]
    blocks = sums.shape[0]

    def entry_at(block):
        return entry_of(place, pool_index[adapter_index[place[1] * blocks + block]])

    start_maps(pieces, entry_at, place, downs, ups, maps_v, up_map, (m_sem, u_sem))
    base_steps(cuts, place[2], tokens, weight, [mine], (tokens_v, weight_v, t_sem, w_sem))
    sums[...] = jnp.zeros_like(sums)
    add_maps(pieces, entry_at, place, maps_v, tokens_v, up_map, sums, (m_sem, u_sem))


def map_scratch(blocks, wide, dtype):
    return [
        pltpu.VMEM((blocks, 2, ADAPTER_RANK, wide), dtype),
        pltpu.SemaphoreType.DMA((blocks, 2)),
        pltpu.SemaphoreType.DMA((blocks, 2)),
    ]


def base_mine(scalars, tokens, weight, downs, ups, pieces):
    rows, width = tokens.shape
    blocks, half = rows // BLK, weight.shape[1] // 2
    return pl.pallas_call(
        functools.partial(mine_kernel, base_cuts(width), pieces, len(downs)),
        in_specs=[SMEM, SMEM, SMEM] + [ANY] * (2 + 2 * len(downs)),
        out_specs=[VMEM, VMEM, ANY],
        out_shape=[
            jax.ShapeDtypeStruct((rows, half), jnp.float32),
            jax.ShapeDtypeStruct((blocks, ADAPTER_RANK, BLK), jnp.float32),
            jax.ShapeDtypeStruct((blocks, ADAPTER_RANK, half), jnp.bfloat16),
        ],
        scratch_shapes=base_scratch(tokens, weight) + map_scratch(blocks, width // 2, tokens.dtype),
        compiler_params=kernel_params(50),
        cost_estimate=HEAVY,
    )(*scalars, tokens, weight, *downs, *ups)


def shrink_kernel(pieces, count, place, pool_index, adapter_index, tokens, *refs):
    arrays = refs[:count]
    prior, _, sums, up_map, tokens_v, t_sem, maps_v, m_sem, u_sem = refs[count:]
    blocks, wide = sums.shape[0], maps_v.shape[3]

    def entry_at(block):
        return entry_of(place, pool_index[adapter_index[place[1] * blocks + block]])

    def token_copy(block, side):
        place_of = (
            pl.ds(pl.multiple_of(block * BLK, BLK), BLK),
            pl.ds(pl.multiple_of(side * wide, wide), wide),
        )
        return pltpu.make_async_copy(
            tokens.at[place_of], tokens_v.at[place_of], t_sem.at[block, side]
        )

    start_maps(
        pieces, entry_at, place, arrays, arrays, maps_v, up_map, (m_sem, u_sem),
        lambda block, side: token_copy(block, side).start(),
    )
    sums[...] = prior[...]
    add_maps(
        pieces, entry_at, place, maps_v, tokens_v, up_map, sums, (m_sem, u_sem),
        lambda block, side: token_copy(block, side).wait(),
    )


def shrink_sums(scalars, tokens, arrays, pieces, sums, up_map):
    rows, width = tokens.shape
    blocks = rows // BLK
    count = len(arrays)
    return pl.pallas_call(
        functools.partial(shrink_kernel, pieces, count),
        in_specs=[SMEM, SMEM, SMEM] + [ANY] * (1 + count) + [VMEM, ANY],
        out_specs=[VMEM, ANY],
        out_shape=[
            jax.ShapeDtypeStruct(sums.shape, sums.dtype),
            jax.ShapeDtypeStruct(up_map.shape, up_map.dtype),
        ],
        input_output_aliases={5 + count: 1},
        scratch_shapes=[
            pltpu.VMEM((rows, width), tokens.dtype),
            pltpu.SemaphoreType.DMA((blocks, 2)),
        ]
        + map_scratch(blocks, width // 2, tokens.dtype),
        compiler_params=kernel_params(50),
        cost_estimate=HEAVY,
    )(*scalars, tokens, *arrays, sums, up_map)


def final_kernel(place, live, base, sums, far_sums, ups, keys):
    blocks, _, half = ups.shape
    for block in range(blocks):
        total = sums[block] + far_sums[block]
        high = total.astype(jnp.bfloat16)
        rest = total - high.astype(jnp.float32)
        middle = rest.astype(jnp.bfloat16)
        low = (rest - middle.astype(jnp.float32)).astype(jnp.bfloat16)
        up = ups[block]
        delta = lax.dot_general(
            jnp.concatenate([high, middle, low], axis=0),
            jnp.concatenate([up, up, up], axis=0),
            TN,
            preferred_element_type=jnp.float32,
        )
        row = lax.broadcasted_iota(jnp.int32, (BLK, half), 0)
        fill = live[place[1] * blocks + block]
        span = slice(block * BLK, (block + 1) * BLK)
        keys[span, :] = jnp.where(row < fill, base[span, :] + delta, 0.0).astype(keys.dtype)


def final_keys(place, live, base, sums, far_sums, ups):
    rows, half = base.shape
    return pl.pallas_call(
        final_kernel,
        in_specs=[SMEM, SMEM] + [VMEM] * 4,
        out_specs=VMEM,
        out_shape=jax.ShapeDtypeStruct((rows, half), jnp.bfloat16),
        compiler_params=kernel_params(12),
        cost_estimate=LIGHT,
    )(place, live, base, sums, far_sums, ups)


def per_device_planes(
    tokens,
    key_projection_weight,
    adapter_down_weight,
    adapter_up_weight,
    adapter_pool_index,
    block_adapter_index,
    block_live_tokens,
):
    place = jnp.stack(
        [lax.axis_index("groups"), lax.axis_index("dp"), lax.axis_index("tensor")]
    ).astype(jnp.int32)
    down, up = adapter_down_weight[0], adapter_up_weight[0]
    width, half = down.shape[1] // 2, up.shape[1] // 2
    piece = width + half
    own = jnp.concatenate([down[:, :width], up[:, :half], down[:, width:], up[:, half:]], axis=1)
    first = lax.axis_index("groups") == 0
    own_half = jnp.where(first, own[:, :piece], own[:, piece:])

    def ring(array, step):
        pairs = [(2 * z + y, 2 * ((z + step) % 4) + y) for z in range(4) for y in range(2)]
        return lax.ppermute(array, "dp", pairs)

    def over_y(array):
        return lax.ppermute(array, "dp", [(i, i ^ 1) for i in range(8)])

    def over_x(array):
        return lax.ppermute(array, "groups", SWAP)

    def over_cores(array):
        return lax.ppermute(array, "tensor", SWAP)

    scalars = (place, adapter_pool_index, block_adapter_index[:, 0])
    weight = key_projection_weight
    z1 = ring(own_half, 1)
    y0 = over_y(own)
    z3 = ring(own_half, -1)
    fars = base_far(place, tokens, weight, FAR_PARTS)
    z1_ = after(z1, fars[0])
    x1 = over_x(z1_)
    y1 = over_y(z1_)
    z2a = ring(z1_, 1)
    z3_ = after(z3, z1_)
    x3 = over_x(z3_)
    y3 = over_y(after(z3_, y0))
    mine, sums, ups = base_mine(
        scalars,
        after(tokens, z3_, y0),
        weight,
        [down, y0, z1, z3],
        [up, y0, z1, z3],
        [
            (0, "a", 0, 0, 0),
            (0, "b", 0, width, half),
            (1, "a", 1, 0, width),
            (1, "b", 1, piece, piece + width),
            (2, "own", 2, 0, width),
            (6, "own", 3, 0, width),
        ],
    )

    def add_terms(tokens, named, sums, ups):
        pieces = [(entry, kind, at, 0, width) for at, (entry, kind, _) in enumerate(named)]
        return shrink_sums(scalars, tokens, [array for *_, array in named], pieces, sums, ups)

    z2b = ring(after(x1, mine), 1)
    y2a = over_y(z2a)
    x1y = over_x(y1)
    x3y = over_x(y3)
    sums, ups = add_terms(
        after(tokens, mine),
        [(2, "far", x1), (3, "own", y1), (4, "own", z2a), (6, "far", x3), (7, "own", y3)],
        sums,
        ups,
    )
    base_fars = [over_cores(after(far, sums)) for far in fars]
    y2b = over_y(after(z2b, sums))
    base = mine + jnp.concatenate(base_fars, axis=0)
    sums, ups = add_terms(
        tokens, [(4, "far", z2b), (3, "far", x1y), (7, "far", x3y), (5, "own", y2a)], sums, ups
    )
    sums, ups = add_terms(after(tokens, base), [(5, "far", y2b)], sums, ups)
    far_sums = over_cores(sums)
    return final_keys(place, block_live_tokens, base, sums, far_sums, ups)


def per_device_gathered(
    tokens,
    key_projection_weight,
    adapter_down_weight,
    adapter_up_weight,
    adapter_pool_index,
    block_adapter_index,
    block_live_tokens,
):
    rows = tokens.shape[0]
    blocks = rows // BLK
    first_block = lax.axis_index("dp") * blocks
    slots = lax.dynamic_slice_in_dim(
        adapter_pool_index[block_adapter_index[:, 0]], first_block, blocks
    )
    fill = lax.dynamic_slice_in_dim(block_live_tokens, first_block, blocks)
    base_part = jnp.dot(tokens, key_projection_weight, preferred_element_type=jnp.float32)
    down = lax.all_gather(adapter_down_weight, "dp", axis=0, tiled=True)
    up = lax.all_gather(adapter_up_weight, "dp", axis=0, tiled=True)
    token_blocks = tokens.reshape(blocks, BLK, tokens.shape[1])
    shrink = jnp.einsum(
        "nrd,nbd->rnb",
        jnp.take(down, slots, axis=0),
        token_blocks,
        preferred_element_type=jnp.float32,
    )
    shrink = lax.psum(shrink.reshape(ADAPTER_RANK, rows), "tensor")
    delta = jnp.einsum(
        "rnb,nrc->nbc",
        shrink.reshape(ADAPTER_RANK, blocks, BLK),
        jnp.take(up, slots, axis=0).astype(jnp.float32),
        precision=lax.Precision.HIGHEST,
        preferred_element_type=jnp.float32,
    )
    base = lax.psum_scatter(base_part, "tensor", scatter_dimension=1, tiled=True)
    mask = jnp.arange(BLK, dtype=jnp.int32)[None, :] < fill[:, None]
    keys = base + delta.reshape(rows, base.shape[1])
    return jnp.where(mask.reshape(rows, 1), keys, 0.0).astype(jnp.bfloat16)


def solution(mesh):
    in_specs = (
        P(("groups", "dp"), "tensor"),
        P("tensor", None),
        P("dp", None, "tensor"),
        P("dp", None, "tensor"),
        P(),
        P("groups", None),
        P("groups"),
    )
    out_specs = P(("groups", "dp"), "tensor")
    planes = dict(mesh.shape) == {"groups": 2, "dp": 8, "tensor": 2}
    return jax.shard_map(
        per_device_planes if planes else per_device_gathered,
        mesh=mesh,
        in_specs=in_specs,
        out_specs=out_specs,
        check_vma=False,
    )
```

time: 61.6 us -> 56.2 us (0.912)
  the two profiles are of different devices: /device:TPU:9 before, /device:TPU:0 now
where the time goes in v4:
time: 56.2 us; the launch traced here: 55.8 us
  Pallas kernels  24.2 us (43%)
  starting transfers between devices  17.7 us (31%)
  waiting for transfers between devices  11.3 us (20%)
  local copies, waits for them, and re-layouts  1.87 us (3%)
    pallas_call x3, Pallas kernels, shrink_sums(): pl.pallas_call(functools.partial(shrink_kernel, pieces, count), in_specs=...  8.43 us
    pallas_call x1, Pallas kernels, base_mine(): pl.pallas_call(functools.partial(mine_kernel, base_cuts(width), pieces, l...  8.11 us
    ppermute x5, starting transfers between devices, over_y(): return lax.ppermute(array, 'dp', [(i, i ^ 1) for i in range(8)])  6.43 us
    pallas_call x1, Pallas kernels, base_far(): pl.pallas_call(functools.partial(base_kernel, base_cuts(width), True), in...  5.85 us
    ppermute x4, starting transfers between devices, over_x(): return lax.ppermute(array, 'groups', SWAP)  5.46 us
    ppermute x4, starting transfers between devices, ring(): return lax.ppermute(array, 'dp', pairs)  5.23 us
    ppermute x4, waiting for transfers between devices, over_x(): return lax.ppermute(array, 'groups', SWAP)  4.13 us
    ppermute x4, waiting for transfers between devices, ring(): return lax.ppermute(array, 'dp', pairs)  3.98 us
  transfers between devices with their start and end apart: 17, of which 7 were waited for; matrix products, arithmetic and copies ran while one was open for 1% of the time, Pallas kernels for 36%

profile of v4, /device:TPU:0, one launch (start us, length us, event | category | flops | bytes accessed | tf_op | source)
XLA Modules:
  0.0 55.8 jit_solution(9161444276340044258)
XLA Ops:
  0.0 1.1 %fusion = (bf16[64,2048]{1,0:T(8,128)(2,1)S(1)}, bf16[64,2048]{1,0:T(8,128)(2,1)S(1)}) fusion(bf16[64,4096]{1,0:T(8,128)(2,1)} %bitcast.6), kind=kLoop, calls=%fused_computation.4 | loop fusion | bytes 1048576 | tf_op jit(solution)/shard_map/slice | solution.py:315
  1.1 0.8 %fusion.1 = (bf16[64,256]{1,0:T(8,128)(2,1)S(1)}, bf16[64,256]{1,0:T(8,128)(2,1)S(1)}) fusion(bf16[64,512]{1,0:T(8,128)(2,1)} %bitcast.8), kind=kLoop, calls=%fused_computation.5 | loop fusion | bytes 131072 | tf_op jit(solution)/shard_map/slice | solution.py:315
  1.9 0.1 maximum_select_fusion
  1.9 3.1 %collective-permute-start.1 = (bf16[64,2304]{1,0:T(8,128)(2,1)S(1)}, bf16[64,2304]{1,0:T(8,128)(2,1)S(1)}, u32[]{:S(2)}, u32[]{:S(2)}) collective-permute-start(bf16[64,2304]{1,0:T(8,128)(2,1)S(1)} %maximum_select_fusion), channel_id=1, source_target_pairs={{0,4},{2,6},{4,8},{6,10},{8,12},{10,14},{12,0},{14,2},{1,5},{3,7},... | collective-permute-start | bytes 884744 | tf_op jit(solution)/shard_map/ppermute | solution.py:321
  5.0 2.1 %collective-permute-start = (bf16[64,2304]{1,0:T(8,128)(2,1)S(1)}, bf16[64,2304]{1,0:T(8,128)(2,1)S(1)}, u32[]{:S(2)}, u32[]{:S(2)}) collective-permute-start(bf16[64,2304]{1,0:T(8,128)(2,1)S(1)} %maximum_select_fusion), channel_id=1, source_target_pairs={{0,12},{2,14},{4,0},{6,2},{8,4},{10,6},{12,8},{14,10},{1,13},{3,15... | collective-permute-start | bytes 884744 | tf_op jit(solution)/shard_map/ppermute | solution.py:321
  7.1 1.7 %collective-permute-start.2 = (bf16[64,4608]{1,0:T(8,128)(2,1)S(1)}, bf16[64,4608]{1,0:T(8,128)(2,1)S(1)}, u32[]{:S(2)}, u32[]{:S(2)}) collective-permute-start(bf16[64,4608]{1,0:T(8,128)(2,1)S(1)} %pad_maximum_fusion), channel_id=1, source_target_pairs={{0,2},{2,0},{4,6},{6,4},{8,10},{10,8},{12,14},{14,12},{1,3},{3,1},... | collective-permute-start | bytes 1769480 | tf_op jit(solution)/shard_map/ppermute | solution.py:324
  8.9 0.1 pad_add_fusion.place
  9.0 5.8 %shard_map.73 = (f32[256,512]{1,0:T(8,128)S(1)}, f32[256,512]{1,0:T(8,128)S(1)}, f32[256,512]{1,0:T(8,128)S(1)}) custom-call(s32[3]{0:T(128)S(1)} %pad_add_fusion.place, bf16[768,4096]{1,0:T(8,128)(2,1)} %tokens.6, bf16[4096,1024]{1,0:T(8,128)(2,1)} %weight.3), custom_call_target="tpu_custom_call" | custom-call | flops 30000001024 | bytes 1 | tf_op jit(solution)/shard_map/pallas_call | solution.py:87
  14.8 0.1 collective-permute-done.1.refs_2_.refs_6_
  14.9 1.7 %collective-permute-start.3 = (bf16[64,2304]{1,0:T(8,128)(2,1)S(1)}, bf16[64,2304]{1,0:T(8,128)(2,1)S(1)}, u32[]{:S(2)}, u32[]{:S(2)}) collective-permute-start(bf16[64,2304]{1,0:T(8,128)(2,1)S(1)} %collective-permute-done.1.refs_2_.refs_6_), channel_id=1, source_target_pairs={{0,16},{16,0},{1,17},{17,1},{2,18},{18,2},{3,19},{19,3},{4,20},{20... | collective-permute-start | bytes 884744 | tf_op jit(solution)/shard_map/ppermute | solution.py:327
  16.6 1.5 %collective-permute-start.4 = (bf16[64,2304]{1,0:T(8,128)(2,1)S(1)}, bf16[64,2304]{1,0:T(8,128)(2,1)S(1)}, u32[]{:S(2)}, u32[]{:S(2)}) collective-permute-start(bf16[64,2304]{1,0:T(8,128)(2,1)S(1)} %collective-permute-done.1.refs_2_.refs_6_), channel_id=1, source_target_pairs={{0,2},{2,0},{4,6},{6,4},{8,10},{10,8},{12,14},{14,12},{1,3},{3,1},... | collective-permute-start | bytes 884744 | tf_op jit(solution)/shard_map/ppermute | solution.py:324
  18.2 0.0 collective-permute-start.5
  18.2 1.6 %collective-permute-done.refs_3_.refs_7_ = bf16[64,2304]{1,0:T(8,128)(2,1)S(1)} collective-permute-done((bf16[64,2304]{1,0:T(8,128)(2,1)S(1)}, bf16[64,2304]{1,0:T(8,128)(2,1)S(1)}, u32[]{:S(2)}, u32[]{:S(2)}) %collective-permute-start) | collective-permute-done | bytes 294944 | tf_op jit(solution)/shard_map/ppermute | solution.py:321
  19.8 2.0 %collective-permute-start.6 = (bf16[64,2304]{1,0:T(8,128)(2,1)S(1)}, bf16[64,2304]{1,0:T(8,128)(2,1)S(1)}, u32[]{:S(2)}, u32[]{:S(2)}) collective-permute-start(bf16[64,2304]{1,0:T(8,128)(2,1)S(1)} %collective-permute-done.refs_3_.refs_7_), channel_id=1, source_target_pairs={{0,16},{16,0},{1,17},{17,1},{2,18},{18,2},{3,19},{19,3},{4,20},{20... | collective-permute-start | bytes 884744 | tf_op jit(solution)/shard_map/ppermute | solution.py:327
  21.7 1.7 %collective-permute-done.2.refs_1_.refs_5_ = bf16[64,4608]{1,0:T(8,128)(2,1)S(1)} collective-permute-done((bf16[64,4608]{1,0:T(8,128)(2,1)S(1)}, bf16[64,4608]{1,0:T(8,128)(2,1)S(1)}, u32[]{:S(2)}, u32[]{:S(2)}) %collective-permute-start.2) | collective-permute-done | bytes 589856 | tf_op jit(solution)/shard_map/ppermute | solution.py:324
  23.5 1.7 %collective-permute-start.7 = (bf16[64,2304]{1,0:T(8,128)(2,1)S(1)}, bf16[64,2304]{1,0:T(8,128)(2,1)S(1)}, u32[]{:S(2)}, u32[]{:S(2)}) collective-permute-start(bf16[64,2304]{1,0:T(8,128)(2,1)S(1)} %collective-permute-done.refs_3_.refs_7_), channel_id=1, source_target_pairs={{0,2},{2,0},{4,6},{6,4},{8,10},{10,8},{12,14},{14,12},{1,3},{3,1},... | collective-permute-start | bytes 884744 | tf_op jit(solution)/shard_map/ppermute | solution.py:324
  25.1 0.0 copy-done
  25.1 0.0 copy-done.1
  25.2 8.1 %shard_map.74 = (f32[768,512]{1,0:T(8,128)S(1)}, f32[6,64,128]{2,1,0:T(8,128)S(1)}, bf16[6,64,512]{2,1,0:T(8,128)(2,1)S(1)}) custom-call(s32[3]{0:T(128)S(1)} %pad_add_fusion.place, s32[8]{0:T(128)S(1)} %copy-done.3, s32[48]{0:T(128)S(1)} %bitcast.10, bf16[768,4096]{1,0:T(8,128)(2,1)} %tokens.6, bf16[4096,1024]{1,0:T(8,128)(2,1)} %weight.3, ...), custom_call_target="tpu_custom_call" | custom-call | flops 30000001024 | bytes 1 | tf_op jit(solution)/shard_map/pallas_call | solution.py:201
  33.3 0.0 collective-permute-done.3.refs_0_
  33.3 0.1 collective-permute-start.11
  33.4 0.0 collective-permute-done.4.refs_1_
  33.4 0.9 %collective-permute-start.13 = (bf16[64,2304]{1,0:T(8,128)(2,1)S(1)}, bf16[64,2304]{1,0:T(8,128)(2,1)S(1)}, u32[]{:S(2)}, u32[]{:S(2)}) collective-permute-start(bf16[64,2304]{1,0:T(8,128)(2,1)S(1)} %collective-permute-done.4.refs_1_), channel_id=1, source_target_pairs={{0,16},{16,0},{1,17},{17,1},{2,18},{18,2},{3,19},{19,3},{4,20},{20... | collective-permute-start | bytes 884744 | tf_op jit(solution)/shard_map/ppermute | solution.py:327
  34.3 0.0 collective-permute-done.5.refs_2_
  34.3 1.1 %collective-permute-start.15 = (bf16[64,2304]{1,0:T(8,128)(2,1)S(1)}, bf16[64,2304]{1,0:T(8,128)(2,1)S(1)}, u32[]{:S(2)}, u32[]{:S(2)}) collective-permute-start(bf16[64,2304]{1,0:T(8,128)(2,1)S(1)} %collective-permute-done.5.refs_2_), channel_id=1, source_target_pairs={{0,2},{2,0},{4,6},{6,4},{8,10},{10,8},{12,14},{14,12},{1,3},{3,1},... | collective-permute-start | bytes 884744 | tf_op jit(solution)/shard_map/ppermute | solution.py:324
  35.4 0.0 collective-permute-done.7.refs_4_
  35.4 0.9 %collective-permute-start.14 = (bf16[64,2304]{1,0:T(8,128)(2,1)S(1)}, bf16[64,2304]{1,0:T(8,128)(2,1)S(1)}, u32[]{:S(2)}, u32[]{:S(2)}) collective-permute-start(bf16[64,2304]{1,0:T(8,128)(2,1)S(1)} %collective-permute-done.7.refs_4_), channel_id=1, source_target_pairs={{0,16},{16,0},{1,17},{17,1},{2,18},{18,2},{3,19},{19,3},{4,20},{20... | collective-permute-start | bytes 884744 | tf_op jit(solution)/shard_map/ppermute | solution.py:327
  36.3 0.0 collective-permute-done.6.refs_3_
  36.3 3.3 %shard_map.75 = (f32[6,64,128]{2,1,0:T(8,128)S(1)}, bf16[6,64,512]{2,1,0:T(8,128)(2,1)S(1)}) custom-call(s32[3]{0:T(128)S(1)} %pad_add_fusion.place, s32[8]{0:T(128)S(1)} %copy-done.3, s32[48]{0:T(128)S(1)} %bitcast.11, bf16[768,4096]{1,0:T(8,128)(2,1)} %tokens.6, ...), custom_call_target="tpu_custom_call", output_to_operand_aliasing={{1}: (10, {})} | custom-call | flops 30000001024 | bytes 1 | tf_op jit(solution)/shard_map/pallas_call | solution.py:248
  39.6 2.3 %collective-permute-done.11.refs_0_ = bf16[64,2304]{1,0:T(8,128)(2,1)S(1)} collective-permute-done((bf16[64,2304]{1,0:T(8,128)(2,1)S(1)}, bf16[64,2304]{1,0:T(8,128)(2,1)S(1)}, u32[]{:S(2)}, u32[]{:S(2)}) %collective-permute-start.11) | collective-permute-done | bytes 294944 | tf_op jit(solution)/shard_map/ppermute | solution.py:321
  41.9 0.3 collective-permute-start.12
  42.2 0.0 collective-permute-start.8
  42.2 1.2 %collective-permute-done.13.refs_1_ = bf16[64,2304]{1,0:T(8,128)(2,1)S(1)} collective-permute-done((bf16[64,2304]{1,0:T(8,128)(2,1)S(1)}, bf16[64,2304]{1,0:T(8,128)(2,1)S(1)}, u32[]{:S(2)}, u32[]{:S(2)}) %collective-permute-start.13) | collective-permute-done | bytes 294944 | tf_op jit(solution)/shard_map/ppermute | solution.py:327
  43.4 0.0 collective-permute-start.9
  43.4 0.0 collective-permute-done.15.refs_3_
  43.4 0.5 collective-permute-start.10
  43.9 3.0 %collective-permute-done.14.refs_2_ = bf16[64,2304]{1,0:T(8,128)(2,1)S(1)} collective-permute-done((bf16[64,2304]{1,0:T(8,128)(2,1)S(1)}, bf16[64,2304]{1,0:T(8,128)(2,1)S(1)}, u32[]{:S(2)}, u32[]{:S(2)}) %collective-permute-start.14) | collective-permute-done | bytes 294944 | tf_op jit(solution)/shard_map/ppermute | solution.py:327
  46.8 2.8 %shard_map.76 = (f32[6,64,128]{2,1,0:T(8,128)S(1)}, bf16[6,64,512]{2,1,0:T(8,128)(2,1)S(1)}) custom-call(s32[3]{0:T(128)S(1)} %pad_add_fusion.place, s32[8]{0:T(128)S(1)} %copy-done.3, s32[48]{0:T(128)S(1)} %bitcast.12, bf16[768,4096]{1,0:T(8,128)(2,1)} %tokens.6, ...), custom_call_target="tpu_custom_call", output_to_operand_aliasing={{1}: (9, {})} | custom-call | flops 30000001024 | bytes 1 | tf_op jit(solution)/shard_map/pallas_call | solution.py:248
  49.6 0.0 collective-permute-done.8
  49.6 0.0 collective-permute-done.9
  49.6 0.0 collective-permute-done.10
  49.6 0.3 maximum_add_fusion.base
  50.0 0.0 collective-permute-done.12.refs_0_
  50.0 0.0 copy-start.2
  50.0 2.4 %shard_map.77 = (f32[6,64,128]{2,1,0:T(8,128)S(1)}, bf16[6,64,512]{2,1,0:T(8,128)(2,1)S(1)}) custom-call(s32[3]{0:T(128)S(1)} %pad_add_fusion.place, s32[8]{0:T(128)S(1)} %copy-done.3, s32[48]{0:T(128)S(1)} %bitcast.13, bf16[768,4096]{1,0:T(8,128)(2,1)} %tokens.6, ...), custom_call_target="tpu_custom_call", output_to_operand_aliasing={{1}: (6, {})} | custom-call | flops 30000001024 | bytes 1 | tf_op jit(solution)/shard_map/pallas_call | solution.py:248
  52.4 0.1 collective-permute-start.16
  52.5 1.4 %collective-permute-done.16.far_sums = f32[6,64,128]{2,1,0:T(8,128)S(1)} collective-permute-done((f32[6,64,128]{2,1,0:T(8,128)S(1)}, f32[6,64,128]{2,1,0:T(8,128)S(1)}, u32[]{:S(2)}, u32[]{:S(2)}) %collective-permute-start.16) | collective-permute-done | bytes 196640 | tf_op jit(solution)/shard_map/ppermute | solution.py:330
  53.9 1.9 %shard_map.78 = bf16[768,512]{1,0:T(8,128)(2,1)} custom-call(s32[3]{0:T(128)S(1)} %pad_add_fusion.place, s32[48]{0:T(128)S(1)} %copy-done.2, f32[768,512]{1,0:T(8,128)S(1)} %maximum_add_fusion.base, f32[6,64,128]{2,1,0:T(8,128)S(1)} %get-tuple-element.49.sums, f32[6,64,128]{2,1,0:T(8,128)S(1)} %collective-permute-done.16.far_sums, ...), custom_call_target="tpu_custom_call" | custom-call | flops 1 | bytes 1 | tf_op jit(solution)/shard_map/pallas_call | solution.py:290
  (8 shorter events, 0.1 us)
Async XLA Ops:
  1.9 13.0 %collective-permute-start.1 = (bf16[64,2304]{1,0:T(8,128)(2,1)S(1)}, bf16[64,2304]{1,0:T(8,128)(2,1)S(1)}, u32[]{:S(2)}, u32[]{:S(2)}) collective-permute-start(bf16[64,2304]{1,0:T(8,128)(2,1)S(1)} %maximum_select_fusion), channel_id=1, source_target_pairs={{0,4},{2,6},{4,8},{6,10},{8,12},{10,14},{12,0},{14,2},{1,5},{3,7},... | collective-permute-start | bytes 884744 | tf_op jit(solution)/shard_map/ppermute | solution.py:321
  5.0 14.8 %collective-permute-start = (bf16[64,2304]{1,0:T(8,128)(2,1)S(1)}, bf16[64,2304]{1,0:T(8,128)(2,1)S(1)}, u32[]{:S(2)}, u32[]{:S(2)}) collective-permute-start(bf16[64,2304]{1,0:T(8,128)(2,1)S(1)} %maximum_select_fusion), channel_id=1, source_target_pairs={{0,12},{2,14},{4,0},{6,2},{8,4},{10,6},{12,8},{14,10},{1,13},{3,15... | collective-permute-start | bytes 884744 | tf_op jit(solution)/shard_map/ppermute | solution.py:321
  7.1 16.3 %collective-permute-start.2 = (bf16[64,4608]{1,0:T(8,128)(2,1)S(1)}, bf16[64,4608]{1,0:T(8,128)(2,1)S(1)}, u32[]{:S(2)}, u32[]{:S(2)}) collective-permute-start(bf16[64,4608]{1,0:T(8,128)(2,1)S(1)} %pad_maximum_fusion), channel_id=1, source_target_pairs={{0,2},{2,0},{4,6},{6,4},{8,10},{10,8},{12,14},{14,12},{1,3},{3,1},... | collective-permute-start | bytes 1769480 | tf_op jit(solution)/shard_map/ppermute | solution.py:324
  9.0 16.2 %copy-start = (bf16[1,64,4096]{2,1,0:T(8,128)(2,1)S(1)}, bf16[1,64,4096]{2,1,0:T(8,128)(2,1)}, u32[]{:S(2)}) copy-start(bf16[1,64,4096]{2,1,0:T(8,128)(2,1)} %param.9) | copy-start | bytes 1572868
  9.0 16.2 %copy-start.1 = (bf16[1,64,512]{2,1,0:T(8,128)(2,1)S(1)}, bf16[1,64,512]{2,1,0:T(8,128)(2,1)}, u32[]{:S(2)}) copy-start(bf16[1,64,512]{2,1,0:T(8,128)(2,1)} %param.10) | copy-start | bytes 196612
  9.0 16.2 %copy-start.3 = (s32[8]{0:T(128)S(1)}, s32[8]{0:T(128)}, u32[]{:S(2)}) copy-start(s32[8]{0:T(128)} %pool_index.7) | copy-start | bytes 100
  9.0 16.2 %copy-start.4 = (s32[48,1]{0,1:T(1,128)S(1)}, s32[48,1]{0,1:T(1,128)}, u32[]{:S(2)}) copy-start(s32[48,1]{0,1:T(1,128)} %param.12) | copy-start | bytes 580
  14.9 18.4 %collective-permute-start.3 = (bf16[64,2304]{1,0:T(8,128)(2,1)S(1)}, bf16[64,2304]{1,0:T(8,128)(2,1)S(1)}, u32[]{:S(2)}, u32[]{:S(2)}) collective-permute-start(bf16[64,2304]{1,0:T(8,128)(2,1)S(1)} %collective-permute-done.1.refs_2_.refs_6_), channel_id=1, source_target_pairs={{0,16},{16,0},{1,17},{17,1},{2,18},{18,2},{3,19},{19,3},{4,20},{20... | collective-permute-start | bytes 884744 | tf_op jit(solution)/shard_map/ppermute | solution.py:327
  16.6 16.7 %collective-permute-start.4 = (bf16[64,2304]{1,0:T(8,128)(2,1)S(1)}, bf16[64,2304]{1,0:T(8,128)(2,1)S(1)}, u32[]{:S(2)}, u32[]{:S(2)}) collective-permute-start(bf16[64,2304]{1,0:T(8,128)(2,1)S(1)} %collective-permute-done.1.refs_2_.refs_6_), channel_id=1, source_target_pairs={{0,2},{2,0},{4,6},{6,4},{8,10},{10,8},{12,14},{14,12},{1,3},{3,1},... | collective-permute-start | bytes 884744 | tf_op jit(solution)/shard_map/ppermute | solution.py:324
  18.2 16.1 %collective-permute-start.5 = (bf16[64,2304]{1,0:T(8,128)(2,1)S(1)}, bf16[64,2304]{1,0:T(8,128)(2,1)S(1)}, u32[]{:S(2)}, u32[]{:S(2)}) collective-permute-start(bf16[64,2304]{1,0:T(8,128)(2,1)S(1)} %collective-permute-done.1.refs_2_.refs_6_), channel_id=1, source_target_pairs={{0,4},{2,6},{4,8},{6,10},{8,12},{10,14},{12,0},{14,2},{1,5},{3,7},... | collective-permute-start | bytes 884744 | tf_op jit(solution)/shard_map/ppermute | solution.py:321
  19.8 16.5 %collective-permute-start.6 = (bf16[64,2304]{1,0:T(8,128)(2,1)S(1)}, bf16[64,2304]{1,0:T(8,128)(2,1)S(1)}, u32[]{:S(2)}, u32[]{:S(2)}) collective-permute-start(bf16[64,2304]{1,0:T(8,128)(2,1)S(1)} %collective-permute-done.refs_3_.refs_7_), channel_id=1, source_target_pairs={{0,16},{16,0},{1,17},{17,1},{2,18},{18,2},{3,19},{19,3},{4,20},{20... | collective-permute-start | bytes 884744 | tf_op jit(solution)/shard_map/ppermute | solution.py:327
  23.5 12.0 %collective-permute-start.7 = (bf16[64,2304]{1,0:T(8,128)(2,1)S(1)}, bf16[64,2304]{1,0:T(8,128)(2,1)S(1)}, u32[]{:S(2)}, u32[]{:S(2)}) collective-permute-start(bf16[64,2304]{1,0:T(8,128)(2,1)S(1)} %collective-permute-done.refs_3_.refs_7_), channel_id=1, source_target_pairs={{0,2},{2,0},{4,6},{6,4},{8,10},{10,8},{12,14},{14,12},{1,3},{3,1},... | collective-permute-start | bytes 884744 | tf_op jit(solution)/shard_map/ppermute | solution.py:324
  33.3 8.6 %collective-permute-start.11 = (bf16[64,2304]{1,0:T(8,128)(2,1)S(1)}, bf16[64,2304]{1,0:T(8,128)(2,1)S(1)}, u32[]{:S(2)}, u32[]{:S(2)}) collective-permute-start(bf16[64,2304]{1,0:T(8,128)(2,1)S(1)} %collective-permute-done.3.refs_0_), channel_id=1, source_target_pairs={{0,4},{2,6},{4,8},{6,10},{8,12},{10,14},{12,0},{14,2},{1,5},{3,7},... | collective-permute-start | bytes 884744 | tf_op jit(solution)/shard_map/ppermute | solution.py:321
  33.4 10.0 %collective-permute-start.13 = (bf16[64,2304]{1,0:T(8,128)(2,1)S(1)}, bf16[64,2304]{1,0:T(8,128)(2,1)S(1)}, u32[]{:S(2)}, u32[]{:S(2)}) collective-permute-start(bf16[64,2304]{1,0:T(8,128)(2,1)S(1)} %collective-permute-done.4.refs_1_), channel_id=1, source_target_pairs={{0,16},{16,0},{1,17},{17,1},{2,18},{18,2},{3,19},{19,3},{4,20},{20... | collective-permute-start | bytes 884744 | tf_op jit(solution)/shard_map/ppermute | solution.py:327
  34.3 9.1 %collective-permute-start.15 = (bf16[64,2304]{1,0:T(8,128)(2,1)S(1)}, bf16[64,2304]{1,0:T(8,128)(2,1)S(1)}, u32[]{:S(2)}, u32[]{:S(2)}) collective-permute-start(bf16[64,2304]{1,0:T(8,128)(2,1)S(1)} %collective-permute-done.5.refs_2_), channel_id=1, source_target_pairs={{0,2},{2,0},{4,6},{6,4},{8,10},{10,8},{12,14},{14,12},{1,3},{3,1},... | collective-permute-start | bytes 884744 | tf_op jit(solution)/shard_map/ppermute | solution.py:324
  35.4 11.4 %collective-permute-start.14 = (bf16[64,2304]{1,0:T(8,128)(2,1)S(1)}, bf16[64,2304]{1,0:T(8,128)(2,1)S(1)}, u32[]{:S(2)}, u32[]{:S(2)}) collective-permute-start(bf16[64,2304]{1,0:T(8,128)(2,1)S(1)} %collective-permute-done.7.refs_4_), channel_id=1, source_target_pairs={{0,16},{16,0},{1,17},{17,1},{2,18},{18,2},{3,19},{19,3},{4,20},{20... | collective-permute-start | bytes 884744 | tf_op jit(solution)/shard_map/ppermute | solution.py:327
  41.9 8.1 %collective-permute-start.12 = (bf16[64,2304]{1,0:T(8,128)(2,1)S(1)}, bf16[64,2304]{1,0:T(8,128)(2,1)S(1)}, u32[]{:S(2)}, u32[]{:S(2)}) collective-permute-start(bf16[64,2304]{1,0:T(8,128)(2,1)S(1)} %collective-permute-done.11.refs_0_), channel_id=1, source_target_pairs={{0,2},{2,0},{4,6},{6,4},{8,10},{10,8},{12,14},{14,12},{1,3},{3,1},... | collective-permute-start | bytes 884744 | tf_op jit(solution)/shard_map/ppermute | solution.py:324
  42.2 7.4 %collective-permute-start.8 = (f32[256,512]{1,0:T(8,128)S(1)}, f32[256,512]{1,0:T(8,128)S(1)}, u32[]{:S(2)}, u32[]{:S(2)}) collective-permute-start(f32[256,512]{1,0:T(8,128)S(1)} %get-tuple-element.38), channel_id=1, source_target_pairs={{0,1},{1,0},{2,3},{3,2},{4,5},{5,4},{6,7},{7,6},{8,9},{9,8},{10,11... | collective-permute-start | bytes 1572872 | tf_op jit(solution)/shard_map/ppermute | solution.py:330
  43.4 6.2 %collective-permute-start.9 = (f32[256,512]{1,0:T(8,128)S(1)}, f32[256,512]{1,0:T(8,128)S(1)}, u32[]{:S(2)}, u32[]{:S(2)}) collective-permute-start(f32[256,512]{1,0:T(8,128)S(1)} %get-tuple-element.40), channel_id=1, source_target_pairs={{0,1},{1,0},{2,3},{3,2},{4,5},{5,4},{6,7},{7,6},{8,9},{9,8},{10,11... | collective-permute-start | bytes 1572872 | tf_op jit(solution)/shard_map/ppermute | solution.py:330
  43.4 6.2 %collective-permute-start.10 = (f32[256,512]{1,0:T(8,128)S(1)}, f32[256,512]{1,0:T(8,128)S(1)}, u32[]{:S(2)}, u32[]{:S(2)}) collective-permute-start(f32[256,512]{1,0:T(8,128)S(1)} %get-tuple-element.42), channel_id=1, source_target_pairs={{0,1},{1,0},{2,3},{3,2},{4,5},{5,4},{6,7},{7,6},{8,9},{9,8},{10,11... | collective-permute-start | bytes 1572872 | tf_op jit(solution)/shard_map/ppermute | solution.py:330
  50.0 3.9 %copy-start.2 = (s32[48]{0:T(128)S(1)}, s32[48]{0:T(128)}, u32[]{:S(2)}) copy-start(s32[48]{0:T(128)} %live.1) | copy-start | bytes 580
  52.4 1.5 %collective-permute-start.16 = (f32[6,64,128]{2,1,0:T(8,128)S(1)}, f32[6,64,128]{2,1,0:T(8,128)S(1)}, u32[]{:S(2)}, u32[]{:S(2)}) collective-permute-start(f32[6,64,128]{2,1,0:T(8,128)S(1)} %get-tuple-element.49.sums), channel_id=1, source_target_pairs={{0,1},{1,0},{2,3},{3,2},{4,5},{5,4},{6,7},{7,6},{8,9},{9,8},{10,11... | collective-permute-start | bytes 589832 | tf_op jit(solution)/shard_map/ppermute | solution.py:330

commit v5 on v4

--- a/solution.py
+++ b/solution.py
@@ -20,8 +20,6 @@
 
 
 LIGHT = pl.CostEstimate(flops=1, bytes_accessed=1, transcendentals=0)
-
-
 HEAVY = pl.CostEstimate(flops=30000000000, bytes_accessed=1, transcendentals=0)
 
 
@@ -35,8 +33,8 @@
 
 
 def base_kernel(cuts, other, place, tokens, weight, *refs):
-    *outs, tokens_v, weight_v, t_sem, w_sem = refs
-    base_steps(cuts, 1 - place[2] if other else place[2], tokens, weight, outs, refs[-4:])
+    core = 1 - place[2] if other else place[2]
+    base_steps(cuts, core, tokens, weight, refs[:-4], refs[-4:])
 
 
 def base_steps(cuts, core, tokens, weight, outs, scratch):
@@ -66,8 +64,8 @@
 
 
 def base_cuts(width):
-    first = width // 8
-    return [(0, first), (first, first)] + [(at * width // 4, width // 4) for at in range(1, 4)]
+    eighth = width // 8
+    return [(0, eighth)] + [(at * eighth, 2 * eighth) for at in (1, 3, 5)] + [(7 * eighth, eighth)]
 
 
 def base_scratch(tokens, weight):
@@ -81,17 +79,17 @@
     ]
 
 
-def base_far(place, tokens, weight, parts):
+def base_sums(place, tokens, weight, other, parts, hint):
     rows, width = tokens.shape
     half = weight.shape[1] // 2
     return pl.pallas_call(
-        functools.partial(base_kernel, base_cuts(width), True),
+        functools.partial(base_kernel, base_cuts(width), other),
         in_specs=[SMEM, ANY, ANY],
         out_specs=[VMEM] * parts,
         out_shape=[jax.ShapeDtypeStruct((rows // parts, half), jnp.float32)] * parts,
         scratch_shapes=base_scratch(tokens, weight),
         compiler_params=kernel_params(50),
-        cost_estimate=HEAVY,
+        cost_estimate=hint,
     )(place, tokens, weight)
 
 
@@ -104,27 +102,25 @@
     return {"a": 0, "b": 1, "own": place[0], "far": 1 - place[0]}[kind]
 
 
-def start_maps(pieces, entry_at, place, downs, ups, maps_v, up_map, sems, start_tokens=None):
+def start_maps(pieces, entry_at, place, arrays, maps_v, up_map, sems, start_tokens):
     m_sem, u_sem = sems
     blocks, _, _, wide = maps_v.shape
-    half = up_map.shape[2] // 2
 
     def start(block, carry):
         entry = entry_at(block)
-        for at_entry, kind, at, column, up_column in pieces:
+        for at_entry, kind, (at, column), (up_at, up_column), half in pieces:
 
             @pl.when(entry == at_entry)
-            def _(kind=kind, at=at, column=column, up_column=up_column):
+            def _(kind=kind, at=at, column=column, up_at=up_at, up_column=up_column):
                 side = side_of(place, kind)
-                if start_tokens is not None:
-                    start_tokens(block, side)
+                start_tokens(block, side)
                 pltpu.make_async_copy(
-                    downs[at].at[:, column : column + wide],
+                    arrays[at].at[:, column : column + wide],
                     maps_v.at[block, side],
                     m_sem.at[block, side],
                 ).start()
                 pltpu.make_async_copy(
-                    ups[at].at[:, up_column : up_column + half],
+                    arrays[up_at].at[:, up_column : up_column + half],
                     up_map.at[block, :, pl.ds(pl.multiple_of(side * half, half), half)],
                     u_sem.at[block, side],
                 ).start()
@@ -134,7 +130,7 @@
     lax.fori_loop(0, blocks, start, 0)
 
 
-def add_maps(pieces, entry_at, place, maps_v, tokens_v, up_map, sums, sems, wait_tokens=None):
+def add_maps(pieces, entry_at, place, maps_v, tokens_v, up_map, sums, sems, wait_tokens):
     m_sem, u_sem = sems
     blocks, _, _, wide = maps_v.shape
     half = up_map.shape[2] // 2
@@ -154,8 +150,7 @@
 
             @pl.when(((masks[side] >> entry) & 1) == 1)
             def _(side=side):
-                if wait_tokens is not None:
-                    wait_tokens(block, side)
+                wait_tokens(block, side)
                 pltpu.make_async_copy(
                     maps_v.at[block, side], maps_v.at[block, side], m_sem.at[block, side]
                 ).wait()
@@ -173,20 +168,6 @@
     lax.fori_loop(0, blocks, add, 0)
 
 
-def mine_kernel(cuts, pieces, count, place, pool_index, adapter_index, tokens, weight, *refs):
-    downs, ups = refs[:count], refs[count : 2 * count]
-    mine, sums, up_map, tokens_v, weight_v, t_sem, w_sem, maps_v, m_sem, u_sem = refs[2 * count :]
-    blocks = sums.shape[0]
-
-    def entry_at(block):
-        return entry_of(place, pool_index[adapter_index[place[1] * blocks + block]])
-
-    start_maps(pieces, entry_at, place, downs, ups, maps_v, up_map, (m_sem, u_sem))
-    base_steps(cuts, place[2], tokens, weight, [mine], (tokens_v, weight_v, t_sem, w_sem))
-    sums[...] = jnp.zeros_like(sums)
-    add_maps(pieces, entry_at, place, maps_v, tokens_v, up_map, sums, (m_sem, u_sem))
-
-
 def map_scratch(blocks, wide, dtype):
     return [
         pltpu.VMEM((blocks, 2, ADAPTER_RANK, wide), dtype),
@@ -195,27 +176,9 @@
     ]
 
 
-def base_mine(scalars, tokens, weight, downs, ups, pieces):
-    rows, width = tokens.shape
-    blocks, half = rows // BLK, weight.shape[1] // 2
-    return pl.pallas_call(
-        functools.partial(mine_kernel, base_cuts(width), pieces, len(downs)),
-        in_specs=[SMEM, SMEM, SMEM] + [ANY] * (2 + 2 * len(downs)),
-        out_specs=[VMEM, VMEM, ANY],
-        out_shape=[
-            jax.ShapeDtypeStruct((rows, half), jnp.float32),
-            jax.ShapeDtypeStruct((blocks, ADAPTER_RANK, BLK), jnp.float32),
-            jax.ShapeDtypeStruct((blocks, ADAPTER_RANK, half), jnp.bfloat16),
-        ],
-        scratch_shapes=base_scratch(tokens, weight) + map_scratch(blocks, width // 2, tokens.dtype),
-        compiler_params=kernel_params(50),
-        cost_estimate=HEAVY,
-    )(*scalars, tokens, weight, *downs, *ups)
-
-
-def shrink_kernel(pieces, count, place, pool_index, adapter_index, tokens, *refs):
-    arrays = refs[:count]
-    prior, _, sums, up_map, tokens_v, t_sem, maps_v, m_sem, u_sem = refs[count:]
+def shrink_kernel(pieces, count, prior_count, place, pool_index, adapter_index, tokens, *refs):
+    arrays, priors = refs[:count], refs[count : count + prior_count]
+    sums, up_map, tokens_v, t_sem, maps_v, m_sem, u_sem = refs[count + prior_count :]
     blocks, wide = sums.shape[0], maps_v.shape[3]
 
     def entry_at(block):
@@ -231,37 +194,37 @@
         )
 
     start_maps(
-        pieces, entry_at, place, arrays, arrays, maps_v, up_map, (m_sem, u_sem),
+        pieces, entry_at, place, arrays, maps_v, up_map, (m_sem, u_sem),
         lambda block, side: token_copy(block, side).start(),
     )
-    sums[...] = prior[...]
+    sums[...] = priors[0][...] if priors else jnp.zeros_like(sums)
     add_maps(
         pieces, entry_at, place, maps_v, tokens_v, up_map, sums, (m_sem, u_sem),
         lambda block, side: token_copy(block, side).wait(),
     )
 
 
-def shrink_sums(scalars, tokens, arrays, pieces, sums, up_map):
+def shrink_sums(scalars, tokens, arrays, pieces, prior, hint):
     rows, width = tokens.shape
-    blocks = rows // BLK
-    count = len(arrays)
+    blocks, count = rows // BLK, len(arrays)
+    half = pieces[0][-1]
     return pl.pallas_call(
-        functools.partial(shrink_kernel, pieces, count),
-        in_specs=[SMEM, SMEM, SMEM] + [ANY] * (1 + count) + [VMEM, ANY],
+        functools.partial(shrink_kernel, pieces, count, len(prior)),
+        in_specs=[SMEM, SMEM, SMEM] + [ANY] * (1 + count) + [VMEM, ANY][: len(prior)],
         out_specs=[VMEM, ANY],
         out_shape=[
-            jax.ShapeDtypeStruct(sums.shape, sums.dtype),
-            jax.ShapeDtypeStruct(up_map.shape, up_map.dtype),
+            jax.ShapeDtypeStruct((blocks, ADAPTER_RANK, BLK), jnp.float32),
+            jax.ShapeDtypeStruct((blocks, ADAPTER_RANK, 2 * half), jnp.bfloat16),
         ],
-        input_output_aliases={5 + count: 1},
+        input_output_aliases={5 + count: 1} if prior else {},
         scratch_shapes=[
             pltpu.VMEM((rows, width), tokens.dtype),
             pltpu.SemaphoreType.DMA((blocks, 2)),
         ]
         + map_scratch(blocks, width // 2, tokens.dtype),
         compiler_params=kernel_params(50),
-        cost_estimate=HEAVY,
-    )(*scalars, tokens, *arrays, sums, up_map)
+        cost_estimate=hint,
+    )(*scalars, tokens, *arrays, *prior)
 
 
 def final_kernel(place, live, base, sums, far_sums, ups, keys):
@@ -334,7 +297,7 @@
     z1 = ring(own_half, 1)
     y0 = over_y(own)
     z3 = ring(own_half, -1)
-    fars = base_far(place, tokens, weight, FAR_PARTS)
+    fars = base_sums(place, tokens, weight, True, FAR_PARTS, LIGHT)
     z1_ = after(z1, fars[0])
     x1 = over_x(z1_)
     y1 = over_y(z1_)
@@ -342,43 +305,49 @@
     z3_ = after(z3, z1_)
     x3 = over_x(z3_)
     y3 = over_y(after(z3_, y0))
-    mine, sums, ups = base_mine(
-        scalars,
-        after(tokens, z3_, y0),
-        weight,
-        [down, y0, z1, z3],
-        [up, y0, z1, z3],
-        [
-            (0, "a", 0, 0, 0),
-            (0, "b", 0, width, half),
-            (1, "a", 1, 0, width),
-            (1, "b", 1, piece, piece + width),
-            (2, "own", 2, 0, width),
-            (6, "own", 3, 0, width),
-        ],
-    )
-
-    def add_terms(tokens, named, sums, ups):
-        pieces = [(entry, kind, at, 0, width) for at, (entry, kind, _) in enumerate(named)]
-        return shrink_sums(scalars, tokens, [array for *_, array in named], pieces, sums, ups)
-
-    z2b = ring(after(x1, mine), 1)
+    z2b = ring(x1, 1)
     y2a = over_y(z2a)
     x1y = over_x(y1)
+    (mine,) = base_sums(place, after(tokens, x1, z2a, y1), weight, False, 1, HEAVY)
     x3y = over_x(y3)
-    sums, ups = add_terms(
-        after(tokens, mine),
-        [(2, "far", x1), (3, "own", y1), (4, "own", z2a), (6, "far", x3), (7, "own", y3)],
-        sums,
-        ups,
-    )
-    base_fars = [over_cores(after(far, sums)) for far in fars]
-    y2b = over_y(after(z2b, sums))
+    y2b = over_y(after(z2b, mine))
+
+    def named(first, entries):
+        return [
+            (entry, kind, (first + at, 0), (first + at, width), half)
+            for at, (entry, kind) in enumerate(entries)
+        ]
+
+    prior = shrink_sums(
+        scalars,
+        after(tokens, z2b, x1y, y2a, mine),
+        [down, up, y0, z1, z3, x1, y1, z2a, x3, y3],
+        [
+            (0, "a", (0, 0), (1, 0), half),
+            (0, "b", (0, width), (1, half), half),
+            (1, "a", (2, 0), (2, width), half),
+            (1, "b", (2, piece), (2, piece + width), half),
+        ]
+        + named(
+            3,
+            [(2, "own"), (6, "own"), (2, "far"), (3, "own"), (4, "own"), (6, "far"), (7, "own")],
+        ),
+        [],
+        HEAVY,
+    )
+    base_fars = [over_cores(after(far, prior[0])) for far in fars]
+    prior = shrink_sums(
+        scalars,
+        tokens,
+        [z2b, x1y, x3y, y2a],
+        named(0, [(4, "far"), (3, "far"), (7, "far"), (5, "own")]),
+        prior,
+        HEAVY,
+    )
     base = mine + jnp.concatenate(base_fars, axis=0)
-    sums, ups = add_terms(
-        tokens, [(4, "far", z2b), (3, "far", x1y), (7, "far", x3y), (5, "own", y2a)], sums, ups
-    )
-    sums, ups = add_terms(after(tokens, base), [(5, "far", y2b)], sums, ups)
+    sums, ups = shrink_sums(
+        scalars, tokens, [y2b], named(0, [(5, "far")]), prior, LIGHT
+    )
     far_sums = over_cores(sums)
     return final_keys(place, block_live_tokens, base, sums, far_sums, ups)
 

time: 56.2 us -> 59 us (1.050)
  the two profiles are of different devices: /device:TPU:0 before, /device:TPU:17 now
where the time goes in v5:
time: 59 us; the launch traced here: 58 us
  Pallas kernels  23.5 us (40%)
  starting transfers between devices  21.4 us (36%)
  waiting for transfers between devices  10.6 us (18%)
  local copies, waits for them, and re-layouts  1.88 us (3%)
    pallas_call x2, Pallas kernels, base_sums(): pl.pallas_call(functools.partial(base_kernel, base_cuts(width), other), i...  11.8 us
    pallas_call x3, Pallas kernels, shrink_sums(): pl.pallas_call(functools.partial(shrink_kernel, pieces, count, len(prior)...  9.87 us
    ppermute x4, starting transfers between devices, over_cores(): return lax.ppermute(array, 'tensor', SWAP)  9.36 us
    ppermute x4, waiting for transfers between devices, ring(): return lax.ppermute(array, 'dp', pairs)  5.27 us
    ppermute x4, starting transfers between devices, over_x(): return lax.ppermute(array, 'groups', SWAP)  4.69 us
    ppermute x5, starting transfers between devices, over_y(): return lax.ppermute(array, 'dp', [(i, i ^ 1) for i in range(8)])  4.5 us
    ppermute x5, waiting for transfers between devices, over_y(): return lax.ppermute(array, 'dp', [(i, i ^ 1) for i in range(8)])  3.36 us
    ppermute x4, starting transfers between devices, ring(): return lax.ppermute(array, 'dp', pairs)  2.83 us
  transfers between devices with their start and end apart: 17, of which 6 were waited for; matrix products, arithmetic and copies ran while one was open for 1% of the time, Pallas kernels for 37%

profile of v5, /device:TPU:17, one launch (start us, length us, event | category | flops | bytes accessed | tf_op | source)
XLA Modules:
  0.0 58.0 jit_solution(2820991684072942666)
XLA Ops:
  0.0 1.1 %fusion = (bf16[64,2048]{1,0:T(8,128)(2,1)S(1)}, bf16[64,2048]{1,0:T(8,128)(2,1)S(1)}) fusion(bf16[64,4096]{1,0:T(8,128)(2,1)} %bitcast.6), kind=kLoop, calls=%fused_computation.4 | loop fusion | bytes 1048576 | tf_op jit(solution)/shard_map/slice | solution.py:278
  1.1 0.8 %fusion.1 = (bf16[64,256]{1,0:T(8,128)(2,1)S(1)}, bf16[64,256]{1,0:T(8,128)(2,1)S(1)}) fusion(bf16[64,512]{1,0:T(8,128)(2,1)} %bitcast.8), kind=kLoop, calls=%fused_computation.5 | loop fusion | bytes 131072 | tf_op jit(solution)/shard_map/slice | solution.py:278
  1.9 0.1 maximum_select_fusion
  1.9 1.3 %collective-permute-start = (bf16[64,2304]{1,0:T(8,128)(2,1)S(1)}, bf16[64,2304]{1,0:T(8,128)(2,1)S(1)}, u32[]{:S(2)}, u32[]{:S(2)}) collective-permute-start(bf16[64,2304]{1,0:T(8,128)(2,1)S(1)} %maximum_select_fusion), channel_id=1, source_target_pairs={{0,4},{2,6},{4,8},{6,10},{8,12},{10,14},{12,0},{14,2},{1,5},{3,7},... | collective-permute-start | bytes 884744 | tf_op jit(solution)/shard_map/ppermute | solution.py:284
  3.3 1.3 %collective-permute-start.7 = (bf16[64,4608]{1,0:T(8,128)(2,1)S(1)}, bf16[64,4608]{1,0:T(8,128)(2,1)S(1)}, u32[]{:S(2)}, u32[]{:S(2)}) collective-permute-start(bf16[64,4608]{1,0:T(8,128)(2,1)S(1)} %pad_maximum_fusion), channel_id=1, source_target_pairs={{0,2},{2,0},{4,6},{6,4},{8,10},{10,8},{12,14},{14,12},{1,3},{3,1},... | collective-permute-start | bytes 1769480 | tf_op jit(solution)/shard_map/ppermute | solution.py:287
  4.6 0.2 collective-permute-start.8
  4.8 0.1 pad_add_fusion.place
  4.9 5.9 %shard_map.73 = (f32[256,512]{1,0:T(8,128)S(1)}, f32[256,512]{1,0:T(8,128)S(1)}, f32[256,512]{1,0:T(8,128)S(1)}) custom-call(s32[3]{0:T(128)S(1)} %pad_add_fusion.place, bf16[768,4096]{1,0:T(8,128)(2,1)} %tokens.7, bf16[4096,1024]{1,0:T(8,128)(2,1)} %weight.3), custom_call_target="tpu_custom_call" | custom-call | flops 1 | bytes 1 | tf_op jit(solution)/shard_map/pallas_call | solution.py:85
  10.8 0.0 collective-permute-done.refs_3_
  10.8 0.0 copy-start
  10.8 0.0 copy-start.1
  10.8 0.0 copy-start.2
  10.8 0.0 copy-start.3
  10.8 1.3 %collective-permute-start.1 = (bf16[64,2304]{1,0:T(8,128)(2,1)S(1)}, bf16[64,2304]{1,0:T(8,128)(2,1)S(1)}, u32[]{:S(2)}, u32[]{:S(2)}) collective-permute-start(bf16[64,2304]{1,0:T(8,128)(2,1)S(1)} %collective-permute-done.refs_3_), channel_id=1, source_target_pairs={{0,16},{16,0},{1,17},{17,1},{2,18},{18,2},{3,19},{19,3},{4,20},{20... | collective-permute-start | bytes 884744 | tf_op jit(solution)/shard_map/ppermute | solution.py:290
  12.1 1.3 %collective-permute-start.2 = (bf16[64,2304]{1,0:T(8,128)(2,1)S(1)}, bf16[64,2304]{1,0:T(8,128)(2,1)S(1)}, u32[]{:S(2)}, u32[]{:S(2)}) collective-permute-start(bf16[64,2304]{1,0:T(8,128)(2,1)S(1)} %collective-permute-done.refs_3_), channel_id=1, source_target_pairs={{0,4},{2,6},{4,8},{6,10},{8,12},{10,14},{12,0},{14,2},{1,5},{3,7},... | collective-permute-start | bytes 884744 | tf_op jit(solution)/shard_map/ppermute | solution.py:284
  13.4 0.5 collective-permute-start.3
  13.9 2.5 %collective-permute-done.8.refs_4_ = bf16[64,2304]{1,0:T(8,128)(2,1)S(1)} collective-permute-done((bf16[64,2304]{1,0:T(8,128)(2,1)S(1)}, bf16[64,2304]{1,0:T(8,128)(2,1)S(1)}, u32[]{:S(2)}, u32[]{:S(2)}) %collective-permute-start.8) | collective-permute-done | bytes 294944 | tf_op jit(solution)/shard_map/ppermute | solution.py:284
  16.4 1.3 %collective-permute-start.9 = (bf16[64,2304]{1,0:T(8,128)(2,1)S(1)}, bf16[64,2304]{1,0:T(8,128)(2,1)S(1)}, u32[]{:S(2)}, u32[]{:S(2)}) collective-permute-start(bf16[64,2304]{1,0:T(8,128)(2,1)S(1)} %collective-permute-done.8.refs_4_), channel_id=1, source_target_pairs={{0,16},{16,0},{1,17},{17,1},{2,18},{18,2},{3,19},{19,3},{4,20},{20... | collective-permute-start | bytes 884744 | tf_op jit(solution)/shard_map/ppermute | solution.py:290
  17.7 0.0 collective-permute-done.1.refs_5_
  17.7 2.8 %collective-permute-done.2.refs_7_ = bf16[64,2304]{1,0:T(8,128)(2,1)S(1)} collective-permute-done((bf16[64,2304]{1,0:T(8,128)(2,1)S(1)}, bf16[64,2304]{1,0:T(8,128)(2,1)S(1)}, u32[]{:S(2)}, u32[]{:S(2)}) %collective-permute-start.2) | collective-permute-done | bytes 294944 | tf_op jit(solution)/shard_map/ppermute | solution.py:284
  20.5 1.4 %collective-permute-done.3.refs_6_ = bf16[64,2304]{1,0:T(8,128)(2,1)S(1)} collective-permute-done((bf16[64,2304]{1,0:T(8,128)(2,1)S(1)}, bf16[64,2304]{1,0:T(8,128)(2,1)S(1)}, u32[]{:S(2)}, u32[]{:S(2)}) %collective-permute-start.3) | collective-permute-done | bytes 294944 | tf_op jit(solution)/shard_map/ppermute | solution.py:287
  21.9 1.2 %collective-permute-start.10 = (bf16[64,2304]{1,0:T(8,128)(2,1)S(1)}, bf16[64,2304]{1,0:T(8,128)(2,1)S(1)}, u32[]{:S(2)}, u32[]{:S(2)}) collective-permute-start(bf16[64,2304]{1,0:T(8,128)(2,1)S(1)} %collective-permute-done.8.refs_4_), channel_id=1, source_target_pairs={{0,2},{2,0},{4,6},{6,4},{8,10},{10,8},{12,14},{14,12},{1,3},{3,1},... | collective-permute-start | bytes 884744 | tf_op jit(solution)/shard_map/ppermute | solution.py:287
  23.1 0.0 collective-permute-start.4
  23.2 1.2 %collective-permute-start.5 = (bf16[64,2304]{1,0:T(8,128)(2,1)S(1)}, bf16[64,2304]{1,0:T(8,128)(2,1)S(1)}, u32[]{:S(2)}, u32[]{:S(2)}) collective-permute-start(bf16[64,2304]{1,0:T(8,128)(2,1)S(1)} %collective-permute-done.3.refs_6_), channel_id=1, source_target_pairs={{0,16},{16,0},{1,17},{17,1},{2,18},{18,2},{3,19},{19,3},{4,20},{20... | collective-permute-start | bytes 884744 | tf_op jit(solution)/shard_map/ppermute | solution.py:290
  24.4 0.2 collective-permute-start.6
  24.6 5.9 %shard_map.74 = f32[768,512]{1,0:T(8,128)S(1)} custom-call(s32[3]{0:T(128)S(1)} %pad_add_fusion.place, bf16[768,4096]{1,0:T(8,128)(2,1)} %tokens.7, bf16[4096,1024]{1,0:T(8,128)(2,1)} %weight.3), custom_call_target="tpu_custom_call" | custom-call | flops 30000001024 | bytes 1 | tf_op jit(solution)/shard_map/pallas_call | solution.py:85
  30.5 0.0 collective-permute-done.4.refs_0_
  30.5 1.2 %collective-permute-done.5.refs_1_ = bf16[64,2304]{1,0:T(8,128)(2,1)S(1)} collective-permute-done((bf16[64,2304]{1,0:T(8,128)(2,1)S(1)}, bf16[64,2304]{1,0:T(8,128)(2,1)S(1)}, u32[]{:S(2)}, u32[]{:S(2)}) %collective-permute-start.5) | collective-permute-done | bytes 294944 | tf_op jit(solution)/shard_map/ppermute | solution.py:290
  31.7 2.0 %collective-permute-done.6.refs_3_ = bf16[64,2304]{1,0:T(8,128)(2,1)S(1)} collective-permute-done((bf16[64,2304]{1,0:T(8,128)(2,1)S(1)}, bf16[64,2304]{1,0:T(8,128)(2,1)S(1)}, u32[]{:S(2)}, u32[]{:S(2)}) %collective-permute-start.6) | collective-permute-done | bytes 294944 | tf_op jit(solution)/shard_map/ppermute | solution.py:287
  33.7 1.2 %collective-permute-start.14 = (bf16[64,2304]{1,0:T(8,128)(2,1)S(1)}, bf16[64,2304]{1,0:T(8,128)(2,1)S(1)}, u32[]{:S(2)}, u32[]{:S(2)}) collective-permute-start(bf16[64,2304]{1,0:T(8,128)(2,1)S(1)} %collective-permute-done.4.refs_0_), channel_id=1, source_target_pairs={{0,2},{2,0},{4,6},{6,4},{8,10},{10,8},{12,14},{14,12},{1,3},{3,1},... | collective-permute-start | bytes 884744 | tf_op jit(solution)/shard_map/ppermute | solution.py:287
  34.9 0.0 collective-permute-done.10.refs_9_
  34.9 0.9 %collective-permute-start.15 = (bf16[64,2304]{1,0:T(8,128)(2,1)S(1)}, bf16[64,2304]{1,0:T(8,128)(2,1)S(1)}, u32[]{:S(2)}, u32[]{:S(2)}) collective-permute-start(bf16[64,2304]{1,0:T(8,128)(2,1)S(1)} %collective-permute-done.10.refs_9_), channel_id=1, source_target_pairs={{0,16},{16,0},{1,17},{17,1},{2,18},{18,2},{3,19},{19,3},{4,20},{20... | collective-permute-start | bytes 884744 | tf_op jit(solution)/shard_map/ppermute | solution.py:290
  35.8 0.0 collective-permute-done.9.refs_8_
  35.8 4.8 %shard_map.75 = (f32[6,64,128]{2,1,0:T(8,128)S(1)}, bf16[6,64,512]{2,1,0:T(8,128)(2,1)S(1)}) custom-call(s32[3]{0:T(128)S(1)} %pad_add_fusion.place, s32[8]{0:T(128)S(1)} %copy-done.2, s32[48]{0:T(128)S(1)} %bitcast.10, bf16[768,4096]{1,0:T(8,128)(2,1)} %tokens.7, bf16[64,4096]{1,0:T(8,128)(2,1)S(1)} %bitcast.7, bf16[64,512]{1,0:T(8,128)(2,1)S(1)} %bitcast.9, ...), custom_call_target="tpu_custom_call" | custom-call | flops 30000001024 | bytes 1 | tf_op jit(solution)/shard_map/pallas_call | solution.py:211
  40.6 7.5 %collective-permute-start.11 = (f32[256,512]{1,0:T(8,128)S(1)}, f32[256,512]{1,0:T(8,128)S(1)}, u32[]{:S(2)}, u32[]{:S(2)}) collective-permute-start(f32[256,512]{1,0:T(8,128)S(1)} %get-tuple-element.30), channel_id=1, source_target_pairs={{0,1},{1,0},{2,3},{3,2},{4,5},{5,4},{6,7},{7,6},{8,9},{9,8},{10,11... | collective-permute-start | bytes 1572872 | tf_op jit(solution)/shard_map/ppermute | solution.py:293
  48.1 0.1 collective-permute-start.12
  48.2 0.4 collective-permute-start.13
  48.6 0.0 collective-permute-done.15.refs_2_
  48.6 2.7 %shard_map.76 = (f32[6,64,128]{2,1,0:T(8,128)S(1)}, bf16[6,64,512]{2,1,0:T(8,128)(2,1)S(1)}) custom-call(s32[3]{0:T(128)S(1)} %pad_add_fusion.place, s32[8]{0:T(128)S(1)} %copy-done.2, s32[48]{0:T(128)S(1)} %bitcast.11, bf16[768,4096]{1,0:T(8,128)(2,1)} %tokens.7, ...), custom_call_target="tpu_custom_call", output_to_operand_aliasing={{1}: (9, {})} | custom-call | flops 30000001024 | bytes 1 | tf_op jit(solution)/shard_map/pallas_call | solution.py:211
  51.4 2.4 %shard_map.77 = (f32[6,64,128]{2,1,0:T(8,128)S(1)}, bf16[6,64,512]{2,1,0:T(8,128)(2,1)S(1)}) custom-call(s32[3]{0:T(128)S(1)} %pad_add_fusion.place, s32[8]{0:T(128)S(1)} %copy-done.2, s32[48]{0:T(128)S(1)} %bitcast.12, bf16[768,4096]{1,0:T(8,128)(2,1)} %tokens.7, ...), custom_call_target="tpu_custom_call", output_to_operand_aliasing={{1}: (6, {})} | custom-call | flops 1 | bytes 1 | tf_op jit(solution)/shard_map/pallas_call | solution.py:211
  53.7 0.0 copy-start.4
  53.7 1.4 %collective-permute-start.16 = (f32[6,64,128]{2,1,0:T(8,128)S(1)}, f32[6,64,128]{2,1,0:T(8,128)S(1)}, u32[]{:S(2)}, u32[]{:S(2)}) collective-permute-start(f32[6,64,128]{2,1,0:T(8,128)S(1)} %get-tuple-element.39.sums), channel_id=1, source_target_pairs={{0,1},{1,0},{2,3},{3,2},{4,5},{5,4},{6,7},{7,6},{8,9},{9,8},{10,11... | collective-permute-start | bytes 589832 | tf_op jit(solution)/shard_map/ppermute | solution.py:293
  55.1 0.0 collective-permute-done.11
  55.1 0.0 collective-permute-done.12
  55.1 0.0 collective-permute-done.13
  55.1 0.3 maximum_add_fusion.base
  55.5 0.7 %collective-permute-done.16.far_sums = f32[6,64,128]{2,1,0:T(8,128)S(1)} collective-permute-done((f32[6,64,128]{2,1,0:T(8,128)S(1)}, f32[6,64,128]{2,1,0:T(8,128)S(1)}, u32[]{:S(2)}, u32[]{:S(2)}) %collective-permute-start.16) | collective-permute-done | bytes 196640 | tf_op jit(solution)/shard_map/ppermute | solution.py:293
  56.2 1.8 %shard_map.78 = bf16[768,512]{1,0:T(8,128)(2,1)} custom-call(s32[3]{0:T(128)S(1)} %pad_add_fusion.place, s32[48]{0:T(128)S(1)} %copy-done.4, f32[768,512]{1,0:T(8,128)S(1)} %maximum_add_fusion.base, f32[6,64,128]{2,1,0:T(8,128)S(1)} %get-tuple-element.39.sums, f32[6,64,128]{2,1,0:T(8,128)S(1)} %collective-permute-done.16.far_sums, ...), custom_call_target="tpu_custom_call" | custom-call | flops 1 | bytes 1 | tf_op jit(solution)/shard_map/pallas_call | solution.py:253
  (8 shorter events, 0.1 us)
Async XLA Ops:
  1.9 8.9 %collective-permute-start = (bf16[64,2304]{1,0:T(8,128)(2,1)S(1)}, bf16[64,2304]{1,0:T(8,128)(2,1)S(1)}, u32[]{:S(2)}, u32[]{:S(2)}) collective-permute-start(bf16[64,2304]{1,0:T(8,128)(2,1)S(1)} %maximum_select_fusion), channel_id=1, source_target_pairs={{0,4},{2,6},{4,8},{6,10},{8,12},{10,14},{12,0},{14,2},{1,5},{3,7},... | collective-permute-start | bytes 884744 | tf_op jit(solution)/shard_map/ppermute | solution.py:284
  3.3 18.6 %collective-permute-start.7 = (bf16[64,4608]{1,0:T(8,128)(2,1)S(1)}, bf16[64,4608]{1,0:T(8,128)(2,1)S(1)}, u32[]{:S(2)}, u32[]{:S(2)}) collective-permute-start(bf16[64,4608]{1,0:T(8,128)(2,1)S(1)} %pad_maximum_fusion), channel_id=1, source_target_pairs={{0,2},{2,0},{4,6},{6,4},{8,10},{10,8},{12,14},{14,12},{1,3},{3,1},... | collective-permute-start | bytes 1769480 | tf_op jit(solution)/shard_map/ppermute | solution.py:287
  4.6 11.8 %collective-permute-start.8 = (bf16[64,2304]{1,0:T(8,128)(2,1)S(1)}, bf16[64,2304]{1,0:T(8,128)(2,1)S(1)}, u32[]{:S(2)}, u32[]{:S(2)}) collective-permute-start(bf16[64,2304]{1,0:T(8,128)(2,1)S(1)} %maximum_select_fusion), channel_id=1, source_target_pairs={{0,12},{2,14},{4,0},{6,2},{8,4},{10,6},{12,8},{14,10},{1,13},{3,15... | collective-permute-start | bytes 884744 | tf_op jit(solution)/shard_map/ppermute | solution.py:284
  10.8 25.0 %copy-start = (bf16[1,64,4096]{2,1,0:T(8,128)(2,1)S(1)}, bf16[1,64,4096]{2,1,0:T(8,128)(2,1)}, u32[]{:S(2)}) copy-start(bf16[1,64,4096]{2,1,0:T(8,128)(2,1)} %param.9) | copy-start | bytes 1572868
  10.8 25.0 %copy-start.1 = (bf16[1,64,512]{2,1,0:T(8,128)(2,1)S(1)}, bf16[1,64,512]{2,1,0:T(8,128)(2,1)}, u32[]{:S(2)}) copy-start(bf16[1,64,512]{2,1,0:T(8,128)(2,1)} %param.10) | copy-start | bytes 196612
  10.8 25.0 %copy-start.2 = (s32[8]{0:T(128)S(1)}, s32[8]{0:T(128)}, u32[]{:S(2)}) copy-start(s32[8]{0:T(128)} %pool_index.5) | copy-start | bytes 100
  10.8 25.0 %copy-start.3 = (s32[48,1]{0,1:T(1,128)S(1)}, s32[48,1]{0,1:T(1,128)}, u32[]{:S(2)}) copy-start(s32[48,1]{0,1:T(1,128)} %param.12) | copy-start | bytes 580
  10.8 6.9 %collective-permute-start.1 = (bf16[64,2304]{1,0:T(8,128)(2,1)S(1)}, bf16[64,2304]{1,0:T(8,128)(2,1)S(1)}, u32[]{:S(2)}, u32[]{:S(2)}) collective-permute-start(bf16[64,2304]{1,0:T(8,128)(2,1)S(1)} %collective-permute-done.refs_3_), channel_id=1, source_target_pairs={{0,16},{16,0},{1,17},{17,1},{2,18},{18,2},{3,19},{19,3},{4,20},{20... | collective-permute-start | bytes 884744 | tf_op jit(solution)/shard_map/ppermute | solution.py:290
  12.1 8.4 %collective-permute-start.2 = (bf16[64,2304]{1,0:T(8,128)(2,1)S(1)}, bf16[64,2304]{1,0:T(8,128)(2,1)S(1)}, u32[]{:S(2)}, u32[]{:S(2)}) collective-permute-start(bf16[64,2304]{1,0:T(8,128)(2,1)S(1)} %collective-permute-done.refs_3_), channel_id=1, source_target_pairs={{0,4},{2,6},{4,8},{6,10},{8,12},{10,14},{12,0},{14,2},{1,5},{3,7},... | collective-permute-start | bytes 884744 | tf_op jit(solution)/shard_map/ppermute | solution.py:284
  13.4 8.5 %collective-permute-start.3 = (bf16[64,2304]{1,0:T(8,128)(2,1)S(1)}, bf16[64,2304]{1,0:T(8,128)(2,1)S(1)}, u32[]{:S(2)}, u32[]{:S(2)}) collective-permute-start(bf16[64,2304]{1,0:T(8,128)(2,1)S(1)} %collective-permute-done.refs_3_), channel_id=1, source_target_pairs={{0,2},{2,0},{4,6},{6,4},{8,10},{10,8},{12,14},{14,12},{1,3},{3,1},... | collective-permute-start | bytes 884744 | tf_op jit(solution)/shard_map/ppermute | solution.py:287
  16.4 19.4 %collective-permute-start.9 = (bf16[64,2304]{1,0:T(8,128)(2,1)S(1)}, bf16[64,2304]{1,0:T(8,128)(2,1)S(1)}, u32[]{:S(2)}, u32[]{:S(2)}) collective-permute-start(bf16[64,2304]{1,0:T(8,128)(2,1)S(1)} %collective-permute-done.8.refs_4_), channel_id=1, source_target_pairs={{0,16},{16,0},{1,17},{17,1},{2,18},{18,2},{3,19},{19,3},{4,20},{20... | collective-permute-start | bytes 884744 | tf_op jit(solution)/shard_map/ppermute | solution.py:290
  21.9 13.0 %collective-permute-start.10 = (bf16[64,2304]{1,0:T(8,128)(2,1)S(1)}, bf16[64,2304]{1,0:T(8,128)(2,1)S(1)}, u32[]{:S(2)}, u32[]{:S(2)}) collective-permute-start(bf16[64,2304]{1,0:T(8,128)(2,1)S(1)} %collective-permute-done.8.refs_4_), channel_id=1, source_target_pairs={{0,2},{2,0},{4,6},{6,4},{8,10},{10,8},{12,14},{14,12},{1,3},{3,1},... | collective-permute-start | bytes 884744 | tf_op jit(solution)/shard_map/ppermute | solution.py:287
  23.1 7.4 %collective-permute-start.4 = (bf16[64,2304]{1,0:T(8,128)(2,1)S(1)}, bf16[64,2304]{1,0:T(8,128)(2,1)S(1)}, u32[]{:S(2)}, u32[]{:S(2)}) collective-permute-start(bf16[64,2304]{1,0:T(8,128)(2,1)S(1)} %collective-permute-done.1.refs_5_), channel_id=1, source_target_pairs={{0,4},{2,6},{4,8},{6,10},{8,12},{10,14},{12,0},{14,2},{1,5},{3,7},... | collective-permute-start | bytes 884744 | tf_op jit(solution)/shard_map/ppermute | solution.py:284
  23.2 8.6 %collective-permute-start.5 = (bf16[64,2304]{1,0:T(8,128)(2,1)S(1)}, bf16[64,2304]{1,0:T(8,128)(2,1)S(1)}, u32[]{:S(2)}, u32[]{:S(2)}) collective-permute-start(bf16[64,2304]{1,0:T(8,128)(2,1)S(1)} %collective-permute-done.3.refs_6_), channel_id=1, source_target_pairs={{0,16},{16,0},{1,17},{17,1},{2,18},{18,2},{3,19},{19,3},{4,20},{20... | collective-permute-start | bytes 884744 | tf_op jit(solution)/shard_map/ppermute | solution.py:290
  24.4 9.3 %collective-permute-start.6 = (bf16[64,2304]{1,0:T(8,128)(2,1)S(1)}, bf16[64,2304]{1,0:T(8,128)(2,1)S(1)}, u32[]{:S(2)}, u32[]{:S(2)}) collective-permute-start(bf16[64,2304]{1,0:T(8,128)(2,1)S(1)} %collective-permute-done.2.refs_7_), channel_id=1, source_target_pairs={{0,2},{2,0},{4,6},{6,4},{8,10},{10,8},{12,14},{14,12},{1,3},{3,1},... | collective-permute-start | bytes 884744 | tf_op jit(solution)/shard_map/ppermute | solution.py:287
  33.7 17.7 %collective-permute-start.14 = (bf16[64,2304]{1,0:T(8,128)(2,1)S(1)}, bf16[64,2304]{1,0:T(8,128)(2,1)S(1)}, u32[]{:S(2)}, u32[]{:S(2)}) collective-permute-start(bf16[64,2304]{1,0:T(8,128)(2,1)S(1)} %collective-permute-done.4.refs_0_), channel_id=1, source_target_pairs={{0,2},{2,0},{4,6},{6,4},{8,10},{10,8},{12,14},{14,12},{1,3},{3,1},... | collective-permute-start | bytes 884744 | tf_op jit(solution)/shard_map/ppermute | solution.py:287
  34.9 13.7 %collective-permute-start.15 = (bf16[64,2304]{1,0:T(8,128)(2,1)S(1)}, bf16[64,2304]{1,0:T(8,128)(2,1)S(1)}, u32[]{:S(2)}, u32[]{:S(2)}) collective-permute-start(bf16[64,2304]{1,0:T(8,128)(2,1)S(1)} %collective-permute-done.10.refs_9_), channel_id=1, source_target_pairs={{0,16},{16,0},{1,17},{17,1},{2,18},{18,2},{3,19},{19,3},{4,20},{20... | collective-permute-start | bytes 884744 | tf_op jit(solution)/shard_map/ppermute | solution.py:290
  40.6 14.5 %collective-permute-start.11 = (f32[256,512]{1,0:T(8,128)S(1)}, f32[256,512]{1,0:T(8,128)S(1)}, u32[]{:S(2)}, u32[]{:S(2)}) collective-permute-start(f32[256,512]{1,0:T(8,128)S(1)} %get-tuple-element.30), channel_id=1, source_target_pairs={{0,1},{1,0},{2,3},{3,2},{4,5},{5,4},{6,7},{7,6},{8,9},{9,8},{10,11... | collective-permute-start | bytes 1572872 | tf_op jit(solution)/shard_map/ppermute | solution.py:293
  48.1 7.0 %collective-permute-start.12 = (f32[256,512]{1,0:T(8,128)S(1)}, f32[256,512]{1,0:T(8,128)S(1)}, u32[]{:S(2)}, u32[]{:S(2)}) collective-permute-start(f32[256,512]{1,0:T(8,128)S(1)} %get-tuple-element.32), channel_id=1, source_target_pairs={{0,1},{1,0},{2,3},{3,2},{4,5},{5,4},{6,7},{7,6},{8,9},{9,8},{10,11... | collective-permute-start | bytes 1572872 | tf_op jit(solution)/shard_map/ppermute | solution.py:293
  48.2 6.9 %collective-permute-start.13 = (f32[256,512]{1,0:T(8,128)S(1)}, f32[256,512]{1,0:T(8,128)S(1)}, u32[]{:S(2)}, u32[]{:S(2)}) collective-permute-start(f32[256,512]{1,0:T(8,128)S(1)} %get-tuple-element.34), channel_id=1, source_target_pairs={{0,1},{1,0},{2,3},{3,2},{4,5},{5,4},{6,7},{7,6},{8,9},{9,8},{10,11... | collective-permute-start | bytes 1572872 | tf_op jit(solution)/shard_map/ppermute | solution.py:293
  53.7 2.4 %copy-start.4 = (s32[48]{0:T(128)S(1)}, s32[48]{0:T(128)}, u32[]{:S(2)}) copy-start(s32[48]{0:T(128)} %live.1) | copy-start | bytes 580
  53.7 2.4 %collective-permute-start.16 = (f32[6,64,128]{2,1,0:T(8,128)S(1)}, f32[6,64,128]{2,1,0:T(8,128)S(1)}, u32[]{:S(2)}, u32[]{:S(2)}) collective-permute-start(f32[6,64,128]{2,1,0:T(8,128)S(1)} %get-tuple-element.39.sums), channel_id=1, source_target_pairs={{0,1},{1,0},{2,3},{3,2},{4,5},{5,4},{6,7},{7,6},{8,9},{9,8},{10,11... | collective-permute-start | bytes 589832 | tf_op jit(solution)/shard_map/ppermute | solution.py:293

commit v6 on v5

--- a/solution.py
+++ b/solution.py
@@ -301,17 +301,15 @@
     z1_ = after(z1, fars[0])
     x1 = over_x(z1_)
     y1 = over_y(z1_)
-    z2a = ring(z1_, 1)
     z3_ = after(z3, z1_)
+    z2a = ring(after(z1_, z3), 1)
     x3 = over_x(z3_)
     y3 = over_y(after(z3_, y0))
     z2b = ring(x1, 1)
     y2a = over_y(z2a)
     x1y = over_x(y1)
-    (mine,) = base_sums(place, after(tokens, x1, z2a, y1), weight, False, 1, HEAVY)
-    x3y = over_x(y3)
-    y2b = over_y(after(z2b, mine))
-
+
+    (mine,) = base_sums(place, after(tokens, z3_, y0), weight, False, 1, HEAVY)
     def named(first, entries):
         return [
             (entry, kind, (first + at, 0), (first + at, width), half)
@@ -320,20 +318,27 @@
 
     prior = shrink_sums(
         scalars,
-        after(tokens, z2b, x1y, y2a, mine),
-        [down, up, y0, z1, z3, x1, y1, z2a, x3, y3],
+        after(tokens, mine, x1, y1, z2a),
+        [down, up, y0, z1, z3],
         [
             (0, "a", (0, 0), (1, 0), half),
             (0, "b", (0, width), (1, half), half),
             (1, "a", (2, 0), (2, width), half),
             (1, "b", (2, piece), (2, piece + width), half),
         ]
-        + named(
-            3,
-            [(2, "own"), (6, "own"), (2, "far"), (3, "own"), (4, "own"), (6, "far"), (7, "own")],
-        ),
+        + named(3, [(2, "own"), (6, "own")]),
         [],
         HEAVY,
+    )
+    x3y = over_x(y3)
+    y2b = over_y(after(z2b, prior[0]))
+    prior = shrink_sums(
+        scalars,
+        after(tokens, z2b),
+        [x1, y1, z2a, x3, y3],
+        named(0, [(2, "far"), (3, "own"), (4, "own"), (6, "far"), (7, "own")]),
+        prior,
+        LIGHT,
     )
     base_fars = [over_cores(after(far, prior[0])) for far in fars]
     prior = shrink_sums(

time: 59 us -> 54.3 us (0.920)
  the two profiles are of different devices: /device:TPU:17 before, /device:TPU:0 now
where the time goes in v6:
time: 54.3 us; the launch traced here: 54.5 us
  Pallas kernels  24.7 us (45%)
  starting transfers between devices  19.2 us (35%)
  waiting for transfers between devices  8.03 us (15%)
  local copies, waits for them, and re-layouts  1.87 us (3%)
    pallas_call x2, Pallas kernels, base_sums(): pl.pallas_call(functools.partial(base_kernel, base_cuts(width), other), i...  11.8 us
    pallas_call x4, Pallas kernels, shrink_sums(): pl.pallas_call(functools.partial(shrink_kernel, pieces, count, len(prior)...  11.1 us
    ppermute x4, waiting for transfers between devices, ring(): return lax.ppermute(array, 'dp', pairs)  7.29 us
    ppermute x4, starting transfers between devices, ring(): return lax.ppermute(array, 'dp', pairs)  6.9 us
    ppermute x5, starting transfers between devices, over_y(): return lax.ppermute(array, 'dp', [(i, i ^ 1) for i in range(8)])  6.07 us
    ppermute x4, starting transfers between devices, over_x(): return lax.ppermute(array, 'groups', SWAP)  5.07 us
    pallas_call x1, Pallas kernels, final_keys(): pl.pallas_call(final_kernel, in_specs=[SMEM, SMEM] + [VMEM] * 4, out_spec...  1.85 us
    ppermute x4, starting transfers between devices, over_cores(): return lax.ppermute(array, 'tensor', SWAP)  1.13 us
  transfers between devices with their start and end apart: 17, of which 5 were waited for; matrix products, arithmetic and copies ran while one was open for 1% of the time, Pallas kernels for 42%

profile of v6, /device:TPU:0, one launch (start us, length us, event | category | flops | bytes accessed | tf_op | source)
XLA Modules:
  0.0 54.5 jit_solution(9971338363072271869)
XLA Ops:
  0.0 1.1 %fusion = (bf16[64,2048]{1,0:T(8,128)(2,1)S(1)}, bf16[64,2048]{1,0:T(8,128)(2,1)S(1)}) fusion(bf16[64,4096]{1,0:T(8,128)(2,1)} %bitcast.6), kind=kLoop, calls=%fused_computation.4 | loop fusion | bytes 1048576 | tf_op jit(solution)/shard_map/slice | solution.py:278
  1.1 0.8 %fusion.1 = (bf16[64,256]{1,0:T(8,128)(2,1)S(1)}, bf16[64,256]{1,0:T(8,128)(2,1)S(1)}) fusion(bf16[64,512]{1,0:T(8,128)(2,1)} %bitcast.8), kind=kLoop, calls=%fused_computation.5 | loop fusion | bytes 131072 | tf_op jit(solution)/shard_map/slice | solution.py:278
  1.9 3.0 %collective-permute-start.2 = (bf16[64,4608]{1,0:T(8,128)(2,1)S(1)}, bf16[64,4608]{1,0:T(8,128)(2,1)S(1)}, u32[]{:S(2)}, u32[]{:S(2)}) collective-permute-start(bf16[64,4608]{1,0:T(8,128)(2,1)S(1)} %pad_maximum_fusion), channel_id=1, source_target_pairs={{0,2},{2,0},{4,6},{6,4},{8,10},{10,8},{12,14},{14,12},{1,3},{3,1},... | collective-permute-start | bytes 1769480 | tf_op jit(solution)/shard_map/ppermute | solution.py:287
  4.9 0.1 maximum_select_fusion
  5.0 1.6 %collective-permute-start.1 = (bf16[64,2304]{1,0:T(8,128)(2,1)S(1)}, bf16[64,2304]{1,0:T(8,128)(2,1)S(1)}, u32[]{:S(2)}, u32[]{:S(2)}) collective-permute-start(bf16[64,2304]{1,0:T(8,128)(2,1)S(1)} %maximum_select_fusion), channel_id=1, source_target_pairs={{0,4},{2,6},{4,8},{6,10},{8,12},{10,14},{12,0},{14,2},{1,5},{3,7},... | collective-permute-start | bytes 884744 | tf_op jit(solution)/shard_map/ppermute | solution.py:284
  6.6 2.2 %collective-permute-start = (bf16[64,2304]{1,0:T(8,128)(2,1)S(1)}, bf16[64,2304]{1,0:T(8,128)(2,1)S(1)}, u32[]{:S(2)}, u32[]{:S(2)}) collective-permute-start(bf16[64,2304]{1,0:T(8,128)(2,1)S(1)} %maximum_select_fusion), channel_id=1, source_target_pairs={{0,12},{2,14},{4,0},{6,2},{8,4},{10,6},{12,8},{14,10},{1,13},{3,15... | collective-permute-start | bytes 884744 | tf_op jit(solution)/shard_map/ppermute | solution.py:284
  8.9 0.1 pad_add_fusion.place
  9.0 5.9 %shard_map.73 = (f32[256,512]{1,0:T(8,128)S(1)}, f32[256,512]{1,0:T(8,128)S(1)}, f32[256,512]{1,0:T(8,128)S(1)}) custom-call(s32[3]{0:T(128)S(1)} %pad_add_fusion.place, bf16[768,4096]{1,0:T(8,128)(2,1)} %tokens.8, bf16[4096,1024]{1,0:T(8,128)(2,1)} %weight.3), custom_call_target="tpu_custom_call" | custom-call | flops 1 | bytes 1 | tf_op jit(solution)/shard_map/pallas_call | solution.py:85
  14.9 2.0 %collective-permute-done.1.refs_3_ = bf16[64,2304]{1,0:T(8,128)(2,1)S(1)} collective-permute-done((bf16[64,2304]{1,0:T(8,128)(2,1)S(1)}, bf16[64,2304]{1,0:T(8,128)(2,1)S(1)}, u32[]{:S(2)}, u32[]{:S(2)}) %collective-permute-start.1) | collective-permute-done | bytes 294944 | tf_op jit(solution)/shard_map/ppermute | solution.py:284
  16.8 1.6 %collective-permute-start.3 = (bf16[64,2304]{1,0:T(8,128)(2,1)S(1)}, bf16[64,2304]{1,0:T(8,128)(2,1)S(1)}, u32[]{:S(2)}, u32[]{:S(2)}) collective-permute-start(bf16[64,2304]{1,0:T(8,128)(2,1)S(1)} %collective-permute-done.1.refs_3_), channel_id=1, source_target_pairs={{0,16},{16,0},{1,17},{17,1},{2,18},{18,2},{3,19},{19,3},{4,20},{20... | collective-permute-start | bytes 884744 | tf_op jit(solution)/shard_map/ppermute | solution.py:290
  18.4 0.5 collective-permute-start.5
  18.9 2.2 %collective-permute-done.refs_4_ = bf16[64,2304]{1,0:T(8,128)(2,1)S(1)} collective-permute-done((bf16[64,2304]{1,0:T(8,128)(2,1)S(1)}, bf16[64,2304]{1,0:T(8,128)(2,1)S(1)}, u32[]{:S(2)}, u32[]{:S(2)}) %collective-permute-start) | collective-permute-done | bytes 294944 | tf_op jit(solution)/shard_map/ppermute | solution.py:284
  21.1 1.1 %collective-permute-start.6 = (bf16[64,2304]{1,0:T(8,128)(2,1)S(1)}, bf16[64,2304]{1,0:T(8,128)(2,1)S(1)}, u32[]{:S(2)}, u32[]{:S(2)}) collective-permute-start(bf16[64,2304]{1,0:T(8,128)(2,1)S(1)} %collective-permute-done.1.refs_3_), channel_id=1, source_target_pairs={{0,4},{2,6},{4,8},{6,10},{8,12},{10,14},{12,0},{14,2},{1,5},{3,7},... | collective-permute-start | bytes 884744 | tf_op jit(solution)/shard_map/ppermute | solution.py:284
  22.3 1.5 %collective-permute-start.7 = (bf16[64,2304]{1,0:T(8,128)(2,1)S(1)}, bf16[64,2304]{1,0:T(8,128)(2,1)S(1)}, u32[]{:S(2)}, u32[]{:S(2)}) collective-permute-start(bf16[64,2304]{1,0:T(8,128)(2,1)S(1)} %collective-permute-done.refs_4_), channel_id=1, source_target_pairs={{0,16},{16,0},{1,17},{17,1},{2,18},{18,2},{3,19},{19,3},{4,20},{20... | collective-permute-start | bytes 884744 | tf_op jit(solution)/shard_map/ppermute | solution.py:290
  23.8 0.0 collective-permute-done.2.refs_2_
  23.8 0.5 collective-permute-start.8
  24.3 5.9 %shard_map.74 = f32[768,512]{1,0:T(8,128)S(1)} custom-call(s32[3]{0:T(128)S(1)} %pad_add_fusion.place, bf16[768,4096]{1,0:T(8,128)(2,1)} %tokens.8, bf16[4096,1024]{1,0:T(8,128)(2,1)} %weight.3), custom_call_target="tpu_custom_call" | custom-call | flops 30000001024 | bytes 1 | tf_op jit(solution)/shard_map/pallas_call | solution.py:85
  30.2 1.0 %collective-permute-done.6.refs_2_ = bf16[64,2304]{1,0:T(8,128)(2,1)S(1)} collective-permute-done((bf16[64,2304]{1,0:T(8,128)(2,1)S(1)}, bf16[64,2304]{1,0:T(8,128)(2,1)S(1)}, u32[]{:S(2)}, u32[]{:S(2)}) %collective-permute-start.6) | collective-permute-done | bytes 294944 | tf_op jit(solution)/shard_map/ppermute | solution.py:284
  31.2 0.0 collective-permute-done.3.refs_0_
  31.2 0.0 collective-permute-done.5.refs_1_
  31.2 1.9 %collective-permute-start.4 = (bf16[64,2304]{1,0:T(8,128)(2,1)S(1)}, bf16[64,2304]{1,0:T(8,128)(2,1)S(1)}, u32[]{:S(2)}, u32[]{:S(2)}) collective-permute-start(bf16[64,2304]{1,0:T(8,128)(2,1)S(1)} %collective-permute-done.3.refs_0_), channel_id=1, source_target_pairs={{0,4},{2,6},{4,8},{6,10},{8,12},{10,14},{12,0},{14,2},{1,5},{3,7},... | collective-permute-start | bytes 884744 | tf_op jit(solution)/shard_map/ppermute | solution.py:284
  33.1 0.5 collective-permute-start.15
  33.6 1.5 %collective-permute-start.13 = (bf16[64,2304]{1,0:T(8,128)(2,1)S(1)}, bf16[64,2304]{1,0:T(8,128)(2,1)S(1)}, u32[]{:S(2)}, u32[]{:S(2)}) collective-permute-start(bf16[64,2304]{1,0:T(8,128)(2,1)S(1)} %collective-permute-done.5.refs_1_), channel_id=1, source_target_pairs={{0,16},{16,0},{1,17},{17,1},{2,18},{18,2},{3,19},{19,3},{4,20},{20... | collective-permute-start | bytes 884744 | tf_op jit(solution)/shard_map/ppermute | solution.py:290
  35.1 0.0 collective-permute-done.8.refs_4_
  35.1 0.5 collective-permute-start.14
  35.7 0.0 copy-done
  35.7 2.4 %shard_map.75 = (f32[6,64,128]{2,1,0:T(8,128)S(1)}, bf16[6,64,512]{2,1,0:T(8,128)(2,1)S(1)}) custom-call(s32[3]{0:T(128)S(1)} %pad_add_fusion.place, s32[8]{0:T(128)S(1)} %copy-done.2, s32[48]{0:T(128)S(1)} %bitcast.10, bf16[768,4096]{1,0:T(8,128)(2,1)} %tokens.8, bf16[64,4096]{1,0:T(8,128)(2,1)S(1)} %bitcast.7, bf16[64,512]{1,0:T(8,128)(2,1)S(1)} %bitcast.9, ...), custom_call_target="tpu_custom_call" | custom-call | flops 30000001024 | bytes 1 | tf_op jit(solution)/shard_map/pallas_call | solution.py:211
  38.1 2.0 %collective-permute-done.4.refs_0_ = bf16[64,2304]{1,0:T(8,128)(2,1)S(1)} collective-permute-done((bf16[64,2304]{1,0:T(8,128)(2,1)S(1)}, bf16[64,2304]{1,0:T(8,128)(2,1)S(1)}, u32[]{:S(2)}, u32[]{:S(2)}) %collective-permute-start.4) | collective-permute-done | bytes 294944 | tf_op jit(solution)/shard_map/ppermute | solution.py:284
  40.1 1.5 %collective-permute-start.12 = (bf16[64,2304]{1,0:T(8,128)(2,1)S(1)}, bf16[64,2304]{1,0:T(8,128)(2,1)S(1)}, u32[]{:S(2)}, u32[]{:S(2)}) collective-permute-start(bf16[64,2304]{1,0:T(8,128)(2,1)S(1)} %collective-permute-done.4.refs_0_), channel_id=1, source_target_pairs={{0,2},{2,0},{4,6},{6,4},{8,10},{10,8},{12,14},{14,12},{1,3},{3,1},... | collective-permute-start | bytes 884744 | tf_op jit(solution)/shard_map/ppermute | solution.py:287
  41.7 0.0 collective-permute-done.7.refs_3_
  41.7 3.9 %shard_map.76 = (f32[6,64,128]{2,1,0:T(8,128)S(1)}, bf16[6,64,512]{2,1,0:T(8,128)(2,1)S(1)}) custom-call(s32[3]{0:T(128)S(1)} %pad_add_fusion.place, s32[8]{0:T(128)S(1)} %copy-done.2, s32[48]{0:T(128)S(1)} %bitcast.11, bf16[768,4096]{1,0:T(8,128)(2,1)} %tokens.8, ...), custom_call_target="tpu_custom_call", output_to_operand_aliasing={{1}: (10, {})} | custom-call | flops 1 | bytes 1 | tf_op jit(solution)/shard_map/pallas_call | solution.py:211
  45.5 0.1 collective-permute-start.9
  45.6 0.0 collective-permute-done.15.refs_3_
  45.6 0.5 collective-permute-start.10
  46.1 0.0 collective-permute-done.13.refs_1_
  46.1 0.1 collective-permute-start.11
  46.2 0.0 collective-permute-done.14.refs_2_
  46.2 3.6 %shard_map.77 = (f32[6,64,128]{2,1,0:T(8,128)S(1)}, bf16[6,64,512]{2,1,0:T(8,128)(2,1)S(1)}) custom-call(s32[3]{0:T(128)S(1)} %pad_add_fusion.place, s32[8]{0:T(128)S(1)} %copy-done.2, s32[48]{0:T(128)S(1)} %bitcast.12, bf16[768,4096]{1,0:T(8,128)(2,1)} %tokens.8, ...), custom_call_target="tpu_custom_call", output_to_operand_aliasing={{1}: (9, {})} | custom-call | flops 30000001024 | bytes 1 | tf_op jit(solution)/shard_map/pallas_call | solution.py:211
  49.8 0.0 collective-permute-done.12.refs_0_
  49.8 1.2 %shard_map.78 = (f32[6,64,128]{2,1,0:T(8,128)S(1)}, bf16[6,64,512]{2,1,0:T(8,128)(2,1)S(1)}) custom-call(s32[3]{0:T(128)S(1)} %pad_add_fusion.place, s32[8]{0:T(128)S(1)} %copy-done.2, s32[48]{0:T(128)S(1)} %bitcast.13, bf16[768,4096]{1,0:T(8,128)(2,1)} %tokens.8, ...), custom_call_target="tpu_custom_call", output_to_operand_aliasing={{1}: (6, {})} | custom-call | flops 1 | bytes 1 | tf_op jit(solution)/shard_map/pallas_call | solution.py:211
  51.0 0.0 copy-start.4
  51.1 0.5 collective-permute-start.16
  51.5 0.0 collective-permute-done.9
  51.5 0.0 collective-permute-done.10
  51.5 0.0 collective-permute-done.11
  51.6 0.3 maximum_add_fusion.base
  51.9 0.7 %collective-permute-done.16.far_sums = f32[6,64,128]{2,1,0:T(8,128)S(1)} collective-permute-done((f32[6,64,128]{2,1,0:T(8,128)S(1)}, f32[6,64,128]{2,1,0:T(8,128)S(1)}, u32[]{:S(2)}, u32[]{:S(2)}) %collective-permute-start.16) | collective-permute-done | bytes 196640 | tf_op jit(solution)/shard_map/ppermute | solution.py:293
  52.6 1.8 %shard_map.79 = bf16[768,512]{1,0:T(8,128)(2,1)} custom-call(s32[3]{0:T(128)S(1)} %pad_add_fusion.place, s32[48]{0:T(128)S(1)} %copy-done.4, f32[768,512]{1,0:T(8,128)S(1)} %maximum_add_fusion.base, f32[6,64,128]{2,1,0:T(8,128)S(1)} %get-tuple-element.47.sums, f32[6,64,128]{2,1,0:T(8,128)S(1)} %collective-permute-done.16.far_sums, ...), custom_call_target="tpu_custom_call" | custom-call | flops 1 | bytes 1 | tf_op jit(solution)/shard_map/pallas_call | solution.py:253
  (9 shorter events, 0.1 us)
Async XLA Ops:
  1.9 21.9 %collective-permute-start.2 = (bf16[64,4608]{1,0:T(8,128)(2,1)S(1)}, bf16[64,4608]{1,0:T(8,128)(2,1)S(1)}, u32[]{:S(2)}, u32[]{:S(2)}) collective-permute-start(bf16[64,4608]{1,0:T(8,128)(2,1)S(1)} %pad_maximum_fusion), channel_id=1, source_target_pairs={{0,2},{2,0},{4,6},{6,4},{8,10},{10,8},{12,14},{14,12},{1,3},{3,1},... | collective-permute-start | bytes 1769480 | tf_op jit(solution)/shard_map/ppermute | solution.py:287
  5.0 11.8 %collective-permute-start.1 = (bf16[64,2304]{1,0:T(8,128)(2,1)S(1)}, bf16[64,2304]{1,0:T(8,128)(2,1)S(1)}, u32[]{:S(2)}, u32[]{:S(2)}) collective-permute-start(bf16[64,2304]{1,0:T(8,128)(2,1)S(1)} %maximum_select_fusion), channel_id=1, source_target_pairs={{0,4},{2,6},{4,8},{6,10},{8,12},{10,14},{12,0},{14,2},{1,5},{3,7},... | collective-permute-start | bytes 884744 | tf_op jit(solution)/shard_map/ppermute | solution.py:284
  6.6 14.5 %collective-permute-start = (bf16[64,2304]{1,0:T(8,128)(2,1)S(1)}, bf16[64,2304]{1,0:T(8,128)(2,1)S(1)}, u32[]{:S(2)}, u32[]{:S(2)}) collective-permute-start(bf16[64,2304]{1,0:T(8,128)(2,1)S(1)} %maximum_select_fusion), channel_id=1, source_target_pairs={{0,12},{2,14},{4,0},{6,2},{8,4},{10,6},{12,8},{14,10},{1,13},{3,15... | collective-permute-start | bytes 884744 | tf_op jit(solution)/shard_map/ppermute | solution.py:284
  16.8 18.8 %copy-start = (bf16[1,64,4096]{2,1,0:T(8,128)(2,1)S(1)}, bf16[1,64,4096]{2,1,0:T(8,128)(2,1)}, u32[]{:S(2)}) copy-start(bf16[1,64,4096]{2,1,0:T(8,128)(2,1)} %param.9) | copy-start | bytes 1572868
  16.8 18.8 %copy-start.1 = (bf16[1,64,512]{2,1,0:T(8,128)(2,1)S(1)}, bf16[1,64,512]{2,1,0:T(8,128)(2,1)}, u32[]{:S(2)}) copy-start(bf16[1,64,512]{2,1,0:T(8,128)(2,1)} %param.10) | copy-start | bytes 196612
  16.8 18.8 %copy-start.2 = (s32[8]{0:T(128)S(1)}, s32[8]{0:T(128)}, u32[]{:S(2)}) copy-start(s32[8]{0:T(128)} %pool_index.7) | copy-start | bytes 100
  16.8 18.8 %copy-start.3 = (s32[48,1]{0,1:T(1,128)S(1)}, s32[48,1]{0,1:T(1,128)}, u32[]{:S(2)}) copy-start(s32[48,1]{0,1:T(1,128)} %param.12) | copy-start | bytes 580
  16.8 14.4 %collective-permute-start.3 = (bf16[64,2304]{1,0:T(8,128)(2,1)S(1)}, bf16[64,2304]{1,0:T(8,128)(2,1)S(1)}, u32[]{:S(2)}, u32[]{:S(2)}) collective-permute-start(bf16[64,2304]{1,0:T(8,128)(2,1)S(1)} %collective-permute-done.1.refs_3_), channel_id=1, source_target_pairs={{0,16},{16,0},{1,17},{17,1},{2,18},{18,2},{3,19},{19,3},{4,20},{20... | collective-permute-start | bytes 884744 | tf_op jit(solution)/shard_map/ppermute | solution.py:290
  18.4 12.8 %collective-permute-start.5 = (bf16[64,2304]{1,0:T(8,128)(2,1)S(1)}, bf16[64,2304]{1,0:T(8,128)(2,1)S(1)}, u32[]{:S(2)}, u32[]{:S(2)}) collective-permute-start(bf16[64,2304]{1,0:T(8,128)(2,1)S(1)} %collective-permute-done.1.refs_3_), channel_id=1, source_target_pairs={{0,2},{2,0},{4,6},{6,4},{8,10},{10,8},{12,14},{14,12},{1,3},{3,1},... | collective-permute-start | bytes 884744 | tf_op jit(solution)/shard_map/ppermute | solution.py:287
  21.1 10.1 %collective-permute-start.6 = (bf16[64,2304]{1,0:T(8,128)(2,1)S(1)}, bf16[64,2304]{1,0:T(8,128)(2,1)S(1)}, u32[]{:S(2)}, u32[]{:S(2)}) collective-permute-start(bf16[64,2304]{1,0:T(8,128)(2,1)S(1)} %collective-permute-done.1.refs_3_), channel_id=1, source_target_pairs={{0,4},{2,6},{4,8},{6,10},{8,12},{10,14},{12,0},{14,2},{1,5},{3,7},... | collective-permute-start | bytes 884744 | tf_op jit(solution)/shard_map/ppermute | solution.py:284
  22.3 19.4 %collective-permute-start.7 = (bf16[64,2304]{1,0:T(8,128)(2,1)S(1)}, bf16[64,2304]{1,0:T(8,128)(2,1)S(1)}, u32[]{:S(2)}, u32[]{:S(2)}) collective-permute-start(bf16[64,2304]{1,0:T(8,128)(2,1)S(1)} %collective-permute-done.refs_4_), channel_id=1, source_target_pairs={{0,16},{16,0},{1,17},{17,1},{2,18},{18,2},{3,19},{19,3},{4,20},{20... | collective-permute-start | bytes 884744 | tf_op jit(solution)/shard_map/ppermute | solution.py:290
  23.8 11.4 %collective-permute-start.8 = (bf16[64,2304]{1,0:T(8,128)(2,1)S(1)}, bf16[64,2304]{1,0:T(8,128)(2,1)S(1)}, u32[]{:S(2)}, u32[]{:S(2)}) collective-permute-start(bf16[64,2304]{1,0:T(8,128)(2,1)S(1)} %collective-permute-done.refs_4_), channel_id=1, source_target_pairs={{0,2},{2,0},{4,6},{6,4},{8,10},{10,8},{12,14},{14,12},{1,3},{3,1},... | collective-permute-start | bytes 884744 | tf_op jit(solution)/shard_map/ppermute | solution.py:287
  31.2 8.9 %collective-permute-start.4 = (bf16[64,2304]{1,0:T(8,128)(2,1)S(1)}, bf16[64,2304]{1,0:T(8,128)(2,1)S(1)}, u32[]{:S(2)}, u32[]{:S(2)}) collective-permute-start(bf16[64,2304]{1,0:T(8,128)(2,1)S(1)} %collective-permute-done.3.refs_0_), channel_id=1, source_target_pairs={{0,4},{2,6},{4,8},{6,10},{8,12},{10,14},{12,0},{14,2},{1,5},{3,7},... | collective-permute-start | bytes 884744 | tf_op jit(solution)/shard_map/ppermute | solution.py:284
  33.1 12.5 %collective-permute-start.15 = (bf16[64,2304]{1,0:T(8,128)(2,1)S(1)}, bf16[64,2304]{1,0:T(8,128)(2,1)S(1)}, u32[]{:S(2)}, u32[]{:S(2)}) collective-permute-start(bf16[64,2304]{1,0:T(8,128)(2,1)S(1)} %collective-permute-done.6.refs_2_), channel_id=1, source_target_pairs={{0,2},{2,0},{4,6},{6,4},{8,10},{10,8},{12,14},{14,12},{1,3},{3,1},... | collective-permute-start | bytes 884744 | tf_op jit(solution)/shard_map/ppermute | solution.py:287
  33.6 12.5 %collective-permute-start.13 = (bf16[64,2304]{1,0:T(8,128)(2,1)S(1)}, bf16[64,2304]{1,0:T(8,128)(2,1)S(1)}, u32[]{:S(2)}, u32[]{:S(2)}) collective-permute-start(bf16[64,2304]{1,0:T(8,128)(2,1)S(1)} %collective-permute-done.5.refs_1_), channel_id=1, source_target_pairs={{0,16},{16,0},{1,17},{17,1},{2,18},{18,2},{3,19},{19,3},{4,20},{20... | collective-permute-start | bytes 884744 | tf_op jit(solution)/shard_map/ppermute | solution.py:290
  35.1 11.1 %collective-permute-start.14 = (bf16[64,2304]{1,0:T(8,128)(2,1)S(1)}, bf16[64,2304]{1,0:T(8,128)(2,1)S(1)}, u32[]{:S(2)}, u32[]{:S(2)}) collective-permute-start(bf16[64,2304]{1,0:T(8,128)(2,1)S(1)} %collective-permute-done.8.refs_4_), channel_id=1, source_target_pairs={{0,16},{16,0},{1,17},{17,1},{2,18},{18,2},{3,19},{19,3},{4,20},{20... | collective-permute-start | bytes 884744 | tf_op jit(solution)/shard_map/ppermute | solution.py:290
  40.1 9.7 %collective-permute-start.12 = (bf16[64,2304]{1,0:T(8,128)(2,1)S(1)}, bf16[64,2304]{1,0:T(8,128)(2,1)S(1)}, u32[]{:S(2)}, u32[]{:S(2)}) collective-permute-start(bf16[64,2304]{1,0:T(8,128)(2,1)S(1)} %collective-permute-done.4.refs_0_), channel_id=1, source_target_pairs={{0,2},{2,0},{4,6},{6,4},{8,10},{10,8},{12,14},{14,12},{1,3},{3,1},... | collective-permute-start | bytes 884744 | tf_op jit(solution)/shard_map/ppermute | solution.py:287
  45.5 6.0 %collective-permute-start.9 = (f32[256,512]{1,0:T(8,128)S(1)}, f32[256,512]{1,0:T(8,128)S(1)}, u32[]{:S(2)}, u32[]{:S(2)}) collective-permute-start(f32[256,512]{1,0:T(8,128)S(1)} %get-tuple-element.38), channel_id=1, source_target_pairs={{0,1},{1,0},{2,3},{3,2},{4,5},{5,4},{6,7},{7,6},{8,9},{9,8},{10,11... | collective-permute-start | bytes 1572872 | tf_op jit(solution)/shard_map/ppermute | solution.py:293
  45.6 5.9 %collective-permute-start.10 = (f32[256,512]{1,0:T(8,128)S(1)}, f32[256,512]{1,0:T(8,128)S(1)}, u32[]{:S(2)}, u32[]{:S(2)}) collective-permute-start(f32[256,512]{1,0:T(8,128)S(1)} %get-tuple-element.40), channel_id=1, source_target_pairs={{0,1},{1,0},{2,3},{3,2},{4,5},{5,4},{6,7},{7,6},{8,9},{9,8},{10,11... | collective-permute-start | bytes 1572872 | tf_op jit(solution)/shard_map/ppermute | solution.py:293
  46.1 5.4 %collective-permute-start.11 = (f32[256,512]{1,0:T(8,128)S(1)}, f32[256,512]{1,0:T(8,128)S(1)}, u32[]{:S(2)}, u32[]{:S(2)}) collective-permute-start(f32[256,512]{1,0:T(8,128)S(1)} %get-tuple-element.42), channel_id=1, source_target_pairs={{0,1},{1,0},{2,3},{3,2},{4,5},{5,4},{6,7},{7,6},{8,9},{9,8},{10,11... | collective-permute-start | bytes 1572872 | tf_op jit(solution)/shard_map/ppermute | solution.py:293
  51.0 1.6 %copy-start.4 = (s32[48]{0:T(128)S(1)}, s32[48]{0:T(128)}, u32[]{:S(2)}) copy-start(s32[48]{0:T(128)} %live.1) | copy-start | bytes 580
  51.1 1.6 %collective-permute-start.16 = (f32[6,64,128]{2,1,0:T(8,128)S(1)}, f32[6,64,128]{2,1,0:T(8,128)S(1)}, u32[]{:S(2)}, u32[]{:S(2)}) collective-permute-start(f32[6,64,128]{2,1,0:T(8,128)S(1)} %get-tuple-element.47.sums), channel_id=1, source_target_pairs={{0,1},{1,0},{2,3},{3,2},{4,5},{5,4},{6,7},{7,6},{8,9},{9,8},{10,11... | collective-permute-start | bytes 589832 | tf_op jit(solution)/shard_map/ppermute | solution.py:293

commit v7 on v6

--- a/solution.py
+++ b/solution.py
@@ -30,6 +30,45 @@
 SMEM = pl.BlockSpec(memory_space=pltpu.SMEM)
 VMEM = pl.BlockSpec(memory_space=pltpu.VMEM)
 ANY = pl.BlockSpec(memory_space=pl.ANY)
+
+
+def pack_kernel(place, down, up, own, own_half, sems):
+    width, half = down.shape[1] // 2, up.shape[1] // 2
+    piece = width + half
+
+    def copies(side, out, column, at):
+        down_span = pl.ds(pl.multiple_of(side * width, width), width)
+        up_span = pl.ds(pl.multiple_of(side * half, half), half)
+        return [
+            pltpu.make_async_copy(
+                down.at[:, down_span], out.at[:, pl.ds(column, width)], sems.at[at]
+            ),
+            pltpu.make_async_copy(
+                up.at[:, up_span], out.at[:, pl.ds(column + width, half)], sems.at[at + 1]
+            ),
+        ]
+
+    every = copies(0, own, 0, 0) + copies(1, own, piece, 2) + copies(place[0], own_half, 0, 4)
+    for copy in every:
+        copy.start()
+    for copy in every:
+        copy.wait()
+
+
+def pack_own(place, down, up):
+    rank, total = down.shape[0], down.shape[1] + up.shape[1]
+    return pl.pallas_call(
+        pack_kernel,
+        in_specs=[SMEM, ANY, ANY],
+        out_specs=[ANY, ANY],
+        out_shape=[
+            jax.ShapeDtypeStruct((rank, total), down.dtype),
+            jax.ShapeDtypeStruct((rank, total // 2), down.dtype),
+        ],
+        scratch_shapes=[pltpu.SemaphoreType.DMA((6,))],
+        compiler_params=kernel_params(58),
+        cost_estimate=LIGHT,
+    )(place, down, up)
 
 
 def base_kernel(cuts, other, place, tokens, weight, *refs):
@@ -227,8 +266,22 @@
     )(*scalars, tokens, *arrays, *prior)
 
 
-def final_kernel(place, live, base, sums, far_sums, ups, keys):
+def final_kernel(place, live, base, sums, far_sums, ups, keys, base_v, keys_v, in_sem, out_sem):
     blocks, _, half = ups.shape
+
+    def rows_of(block):
+        return pl.ds(block * BLK, BLK)
+
+    def load(block):
+        rows = rows_of(block)
+        return pltpu.make_async_copy(base.at[rows, :], base_v.at[rows, :], in_sem.at[block])
+
+    def store(block):
+        rows = rows_of(block)
+        return pltpu.make_async_copy(keys_v.at[rows, :], keys.at[rows, :], out_sem.at[block])
+
+    for block in range(blocks):
+        load(block).start()
     for block in range(blocks):
         total = sums[block] + far_sums[block]
         high = total.astype(jnp.bfloat16)
@@ -242,19 +295,30 @@
             TN,
             preferred_element_type=jnp.float32,
         )
+        load(block).wait()
         row = lax.broadcasted_iota(jnp.int32, (BLK, half), 0)
         fill = live[place[1] * blocks + block]
-        span = slice(block * BLK, (block + 1) * BLK)
-        keys[span, :] = jnp.where(row < fill, base[span, :] + delta, 0.0).astype(keys.dtype)
+        rows = rows_of(block)
+        keys_v[rows, :] = jnp.where(row < fill, base_v[rows, :] + delta, 0.0).astype(keys.dtype)
+        store(block).start()
+    for block in range(blocks):
+        store(block).wait()
 
 
 def final_keys(place, live, base, sums, far_sums, ups):
     rows, half = base.shape
+    blocks = rows // BLK
     return pl.pallas_call(
         final_kernel,
-        in_specs=[SMEM, SMEM] + [VMEM] * 4,
-        out_specs=VMEM,
+        in_specs=[SMEM, SMEM, ANY, VMEM, VMEM, VMEM],
+        out_specs=ANY,
         out_shape=jax.ShapeDtypeStruct((rows, half), jnp.bfloat16),
+        scratch_shapes=[
+            pltpu.VMEM((rows, half), base.dtype),
+            pltpu.VMEM((rows, half), jnp.bfloat16),
+            pltpu.SemaphoreType.DMA((blocks,)),
+            pltpu.SemaphoreType.DMA((blocks,)),
+        ],
         compiler_params=kernel_params(12),
         cost_estimate=LIGHT,
     )(place, live, base, sums, far_sums, ups)
@@ -275,9 +339,7 @@
     down, up = adapter_down_weight[0], adapter_up_weight[0]
     width, half = down.shape[1] // 2, up.shape[1] // 2
     piece = width + half
-    own = jnp.concatenate([down[:, :width], up[:, :half], down[:, width:], up[:, half:]], axis=1)
-    first = lax.axis_index("groups") == 0
-    own_half = jnp.where(first, own[:, :piece], own[:, piece:])
+    own, own_half = pack_own(place, down, up)
 
     def ring(array, step):
         pairs = [(2 * z + y, 2 * ((z + step) % 4) + y) for z in range(4) for y in range(2)]

time: 54.3 us -> 82.7 us (1.52)
  Pallas kernels: 24.7 us -> 54.3 us
  local copies, waits for them, and re-layouts: 1.87 us -> 0.59 us
  waiting for transfers between devices: 8.03 us -> 7.19 us
    pallas_call x1 -> x2, Pallas kernels: 1.85 us -> 31.4 us  [the longest x1 28.6 us: pack_own(): pl.pallas_call(pack_kernel, in_specs=[SMEM, ANY, ANY], out_specs=[ANY, AN...]
    slice x2 -> x0, local copies, waits for them, and re-layouts: 1.85 us -> none  [the longest x1 1.06 us: per_device_planes(): down[:, width:]]
    ppermute x4, waiting for transfers between devices: 7.29 us -> 6.41 us  [ring(): return lax.ppermute(array, 'dp', pairs)]
  transfers between devices with their start and end apart: 17 -> 17, of which waited for: 5 -> 5; matrix products, arithmetic and copies ran while one was open for 1% -> 0% of each run, Pallas kernels for 42% -> 28%
where the time goes in v7:
time: 82.7 us; the launch traced here: 82.2 us
  Pallas kernels  54.3 us (66%)
  starting transfers between devices  19.1 us (23%)
  waiting for transfers between devices  7.19 us (9%)
  other arithmetic  0.9 us (1%)
    pallas_call x1, Pallas kernels, pack_own(): pl.pallas_call(pack_kernel, in_specs=[SMEM, ANY, ANY], out_specs=[ANY, AN...  28.6 us
    pallas_call x2, Pallas kernels, base_sums(): pl.pallas_call(functools.partial(base_kernel, base_cuts(width), other), i...  11.8 us
    pallas_call x4, Pallas kernels, shrink_sums(): pl.pallas_call(functools.partial(shrink_kernel, pieces, count, len(prior)...  11.1 us
    ppermute x4, starting transfers between devices, ring(): return lax.ppermute(array, 'dp', pairs)  6.84 us
    ppermute x4, waiting for transfers between devices, ring(): return lax.ppermute(array, 'dp', pairs)  6.41 us
    ppermute x5, starting transfers between devices, over_y(): return lax.ppermute(array, 'dp', [(i, i ^ 1) for i in range(8)])  6.07 us
    ppermute x4, starting transfers between devices, over_x(): return lax.ppermute(array, 'groups', SWAP)  5.07 us
    pallas_call x1, Pallas kernels, final_keys(): pl.pallas_call(final_kernel, in_specs=[SMEM, SMEM, ANY, VMEM, VMEM, VMEM]...  2.76 us
  transfers between devices with their start and end apart: 17, of which 5 were waited for; matrix products, arithmetic and copies ran while one was open for 0% of the time, Pallas kernels for 28%

profile of v7, /device:TPU:0, one launch (start us, length us, event | category | flops | bytes accessed | tf_op | source)
XLA Modules:
  0.0 82.2 jit_solution(1129225825843049824)
XLA Ops:
  0.0 0.6 pad_add_fusion.place
  0.6 28.6 %shard_map.73 = (bf16[64,4608]{1,0:T(8,128)(2,1)}, bf16[64,2304]{1,0:T(8,128)(2,1)}) custom-call(s32[3]{0:T(128)} %pad_add_fusion.place, bf16[64,4096]{1,0:T(8,128)(2,1)} %bitcast.6, bf16[64,512]{1,0:T(8,128)(2,1)} %bitcast.8), custom_call_target="tpu_custom_call" | custom-call | flops 1 | bytes 1 | tf_op jit(solution)/shard_map/pallas_call | solution.py:60
  29.2 3.0 %collective-permute-start.2 = (bf16[64,4608]{1,0:T(8,128)(2,1)}, bf16[64,4608]{1,0:T(8,128)(2,1)S(1)}, u32[]{:S(2)}, u32[]{:S(2)}) collective-permute-start(bf16[64,4608]{1,0:T(8,128)(2,1)} %get-tuple-element.33), channel_id=1, source_target_pairs={{0,2},{2,0},{4,6},{6,4},{8,10},{10,8},{12,14},{14,12},{1,3},{3,1},... | collective-permute-start | bytes 1769480 | tf_op jit(solution)/shard_map/ppermute | solution.py:349
  32.2 1.6 %collective-permute-start.1 = (bf16[64,2304]{1,0:T(8,128)(2,1)}, bf16[64,2304]{1,0:T(8,128)(2,1)S(1)}, u32[]{:S(2)}, u32[]{:S(2)}) collective-permute-start(bf16[64,2304]{1,0:T(8,128)(2,1)} %get-tuple-element.29), channel_id=1, source_target_pairs={{0,4},{2,6},{4,8},{6,10},{8,12},{10,14},{12,0},{14,2},{1,5},{3,7},... | collective-permute-start | bytes 884744 | tf_op jit(solution)/shard_map/ppermute | solution.py:346
  33.8 2.2 %collective-permute-start = (bf16[64,2304]{1,0:T(8,128)(2,1)}, bf16[64,2304]{1,0:T(8,128)(2,1)S(1)}, u32[]{:S(2)}, u32[]{:S(2)}) collective-permute-start(bf16[64,2304]{1,0:T(8,128)(2,1)} %get-tuple-element.29), channel_id=1, source_target_pairs={{0,12},{2,14},{4,0},{6,2},{8,4},{10,6},{12,8},{14,10},{1,13},{3,15... | collective-permute-start | bytes 884744 | tf_op jit(solution)/shard_map/ppermute | solution.py:346
  36.0 0.6 copy-done.2
  36.6 5.9 %shard_map.74 = (f32[256,512]{1,0:T(8,128)S(1)}, f32[256,512]{1,0:T(8,128)S(1)}, f32[256,512]{1,0:T(8,128)S(1)}) custom-call(s32[3]{0:T(128)S(1)} %copy-done.2, bf16[768,4096]{1,0:T(8,128)(2,1)} %tokens.8, bf16[4096,1024]{1,0:T(8,128)(2,1)} %weight.3), custom_call_target="tpu_custom_call" | custom-call | flops 1 | bytes 1 | tf_op jit(solution)/shard_map/pallas_call | solution.py:124
  42.5 1.7 %collective-permute-done.1.refs_3_ = bf16[64,2304]{1,0:T(8,128)(2,1)S(1)} collective-permute-done((bf16[64,2304]{1,0:T(8,128)(2,1)}, bf16[64,2304]{1,0:T(8,128)(2,1)S(1)}, u32[]{:S(2)}, u32[]{:S(2)}) %collective-permute-start.1) | collective-permute-done | bytes 294944 | tf_op jit(solution)/shard_map/ppermute | solution.py:346
  44.2 1.6 %collective-permute-start.3 = (bf16[64,2304]{1,0:T(8,128)(2,1)S(1)}, bf16[64,2304]{1,0:T(8,128)(2,1)S(1)}, u32[]{:S(2)}, u32[]{:S(2)}) collective-permute-start(bf16[64,2304]{1,0:T(8,128)(2,1)S(1)} %collective-permute-done.1.refs_3_), channel_id=1, source_target_pairs={{0,16},{16,0},{1,17},{17,1},{2,18},{18,2},{3,19},{19,3},{4,20},{20... | collective-permute-start | bytes 884744 | tf_op jit(solution)/shard_map/ppermute | solution.py:352
  45.8 0.5 collective-permute-start.5
  46.3 2.2 %collective-permute-done.refs_4_ = bf16[64,2304]{1,0:T(8,128)(2,1)S(1)} collective-permute-done((bf16[64,2304]{1,0:T(8,128)(2,1)}, bf16[64,2304]{1,0:T(8,128)(2,1)S(1)}, u32[]{:S(2)}, u32[]{:S(2)}) %collective-permute-start) | collective-permute-done | bytes 294944 | tf_op jit(solution)/shard_map/ppermute | solution.py:346
  48.5 1.1 %collective-permute-start.6 = (bf16[64,2304]{1,0:T(8,128)(2,1)S(1)}, bf16[64,2304]{1,0:T(8,128)(2,1)S(1)}, u32[]{:S(2)}, u32[]{:S(2)}) collective-permute-start(bf16[64,2304]{1,0:T(8,128)(2,1)S(1)} %collective-permute-done.1.refs_3_), channel_id=1, source_target_pairs={{0,4},{2,6},{4,8},{6,10},{8,12},{10,14},{12,0},{14,2},{1,5},{3,7},... | collective-permute-start | bytes 884744 | tf_op jit(solution)/shard_map/ppermute | solution.py:346
  49.6 1.5 %collective-permute-start.7 = (bf16[64,2304]{1,0:T(8,128)(2,1)S(1)}, bf16[64,2304]{1,0:T(8,128)(2,1)S(1)}, u32[]{:S(2)}, u32[]{:S(2)}) collective-permute-start(bf16[64,2304]{1,0:T(8,128)(2,1)S(1)} %collective-permute-done.refs_4_), channel_id=1, source_target_pairs={{0,16},{16,0},{1,17},{17,1},{2,18},{18,2},{3,19},{19,3},{4,20},{20... | collective-permute-start | bytes 884744 | tf_op jit(solution)/shard_map/ppermute | solution.py:352
  51.1 0.0 collective-permute-done.2.refs_2_
  51.1 0.5 collective-permute-start.8
  51.6 5.9 %shard_map.75 = f32[768,512]{1,0:T(8,128)S(1)} custom-call(s32[3]{0:T(128)S(1)} %copy-done.2, bf16[768,4096]{1,0:T(8,128)(2,1)} %tokens.8, bf16[4096,1024]{1,0:T(8,128)(2,1)} %weight.3), custom_call_target="tpu_custom_call" | custom-call | flops 30000001024 | bytes 1 | tf_op jit(solution)/shard_map/pallas_call | solution.py:124
  57.5 1.1 %collective-permute-done.6.refs_2_ = bf16[64,2304]{1,0:T(8,128)(2,1)S(1)} collective-permute-done((bf16[64,2304]{1,0:T(8,128)(2,1)S(1)}, bf16[64,2304]{1,0:T(8,128)(2,1)S(1)}, u32[]{:S(2)}, u32[]{:S(2)}) %collective-permute-start.6) | collective-permute-done | bytes 294944 | tf_op jit(solution)/shard_map/ppermute | solution.py:346
  58.6 0.0 collective-permute-done.3.refs_0_
  58.6 0.0 collective-permute-done.5.refs_1_
  58.6 1.9 %collective-permute-start.4 = (bf16[64,2304]{1,0:T(8,128)(2,1)S(1)}, bf16[64,2304]{1,0:T(8,128)(2,1)S(1)}, u32[]{:S(2)}, u32[]{:S(2)}) collective-permute-start(bf16[64,2304]{1,0:T(8,128)(2,1)S(1)} %collective-permute-done.3.refs_0_), channel_id=1, source_target_pairs={{0,4},{2,6},{4,8},{6,10},{8,12},{10,14},{12,0},{14,2},{1,5},{3,7},... | collective-permute-start | bytes 884744 | tf_op jit(solution)/shard_map/ppermute | solution.py:346
  60.5 0.5 collective-permute-start.15
  61.0 1.5 %collective-permute-start.13 = (bf16[64,2304]{1,0:T(8,128)(2,1)S(1)}, bf16[64,2304]{1,0:T(8,128)(2,1)S(1)}, u32[]{:S(2)}, u32[]{:S(2)}) collective-permute-start(bf16[64,2304]{1,0:T(8,128)(2,1)S(1)} %collective-permute-done.5.refs_1_), channel_id=1, source_target_pairs={{0,16},{16,0},{1,17},{17,1},{2,18},{18,2},{3,19},{19,3},{4,20},{20... | collective-permute-start | bytes 884744 | tf_op jit(solution)/shard_map/ppermute | solution.py:352
  62.5 0.0 collective-permute-done.8.refs_4_
  62.5 0.5 collective-permute-start.14
  63.0 0.0 copy-done
  63.0 0.0 copy-done.1
  63.0 3.0 %shard_map.76 = (f32[6,64,128]{2,1,0:T(8,128)S(1)}, bf16[6,64,512]{2,1,0:T(8,128)(2,1)S(1)}) custom-call(s32[3]{0:T(128)S(1)} %copy-done.2, s32[8]{0:T(128)S(1)} %copy-done.3, s32[48]{0:T(128)S(1)} %bitcast.10, bf16[768,4096]{1,0:T(8,128)(2,1)} %tokens.8, bf16[64,4096]{1,0:T(8,128)(2,1)S(1)} %bitcast.7, bf16[64,512]{1,0:T(8,128)(2,1)S(1)} %bitcast.9, ...), custom_call_target="tpu_custom_call" | custom-call | flops 30000001024 | bytes 1 | tf_op jit(solution)/shard_map/pallas_call | solution.py:250
  66.1 1.4 %collective-permute-done.4.refs_0_ = bf16[64,2304]{1,0:T(8,128)(2,1)S(1)} collective-permute-done((bf16[64,2304]{1,0:T(8,128)(2,1)S(1)}, bf16[64,2304]{1,0:T(8,128)(2,1)S(1)}, u32[]{:S(2)}, u32[]{:S(2)}) %collective-permute-start.4) | collective-permute-done | bytes 294944 | tf_op jit(solution)/shard_map/ppermute | solution.py:346
  67.5 1.5 %collective-permute-start.12 = (bf16[64,2304]{1,0:T(8,128)(2,1)S(1)}, bf16[64,2304]{1,0:T(8,128)(2,1)S(1)}, u32[]{:S(2)}, u32[]{:S(2)}) collective-permute-start(bf16[64,2304]{1,0:T(8,128)(2,1)S(1)} %collective-permute-done.4.refs_0_), channel_id=1, source_target_pairs={{0,2},{2,0},{4,6},{6,4},{8,10},{10,8},{12,14},{14,12},{1,3},{3,1},... | collective-permute-start | bytes 884744 | tf_op jit(solution)/shard_map/ppermute | solution.py:349
  69.0 0.0 collective-permute-done.7.refs_3_
  69.0 3.6 %shard_map.77 = (f32[6,64,128]{2,1,0:T(8,128)S(1)}, bf16[6,64,512]{2,1,0:T(8,128)(2,1)S(1)}) custom-call(s32[3]{0:T(128)S(1)} %copy-done.2, s32[8]{0:T(128)S(1)} %copy-done.3, s32[48]{0:T(128)S(1)} %bitcast.11, bf16[768,4096]{1,0:T(8,128)(2,1)} %tokens.8, bf16[64,2304]{1,0:T(8,128)(2,1)S(1)} %collective-permute-done.3.refs_0_, ...), custom_call_target="tpu_custom_call", output_to_operand_aliasing={{1}: (10, {})} | custom-call | flops 1 | bytes 1 | tf_op jit(solution)/shard_map/pallas_call | solution.py:250
  72.6 0.1 collective-permute-start.9
  72.7 0.0 collective-permute-done.15.refs_3_
  72.7 0.5 collective-permute-start.10
  73.2 0.0 collective-permute-done.13.refs_1_
  73.2 0.1 collective-permute-start.11
  73.3 0.0 collective-permute-done.14.refs_2_
  73.4 3.3 %shard_map.78 = (f32[6,64,128]{2,1,0:T(8,128)S(1)}, bf16[6,64,512]{2,1,0:T(8,128)(2,1)S(1)}) custom-call(s32[3]{0:T(128)S(1)} %copy-done.2, s32[8]{0:T(128)S(1)} %copy-done.3, s32[48]{0:T(128)S(1)} %bitcast.12, bf16[768,4096]{1,0:T(8,128)(2,1)} %tokens.8, bf16[64,2304]{1,0:T(8,128)(2,1)S(1)} %collective-permute-done.4.refs_0_, ...), custom_call_target="tpu_custom_call", output_to_operand_aliasing={{1}: (9, {})} | custom-call | flops 30000001024 | bytes 1 | tf_op jit(solution)/shard_map/pallas_call | solution.py:250
  76.7 0.0 collective-permute-done.12.refs_0_
  76.7 1.2 %shard_map.79 = (f32[6,64,128]{2,1,0:T(8,128)S(1)}, bf16[6,64,512]{2,1,0:T(8,128)(2,1)S(1)}) custom-call(s32[3]{0:T(128)S(1)} %copy-done.2, s32[8]{0:T(128)S(1)} %copy-done.3, s32[48]{0:T(128)S(1)} %bitcast.13, bf16[768,4096]{1,0:T(8,128)(2,1)} %tokens.8, bf16[64,2304]{1,0:T(8,128)(2,1)S(1)} %collective-permute-done.12.refs_0_, ...), custom_call_target="tpu_custom_call", output_to_operand_aliasing={{1}: (6, {})} | custom-call | flops 1 | bytes 1 | tf_op jit(solution)/shard_map/pallas_call | solution.py:250
  77.9 0.0 copy-start.5
  77.9 0.5 collective-permute-start.16
  78.4 0.0 collective-permute-done.9
  78.4 0.0 collective-permute-done.10
  78.4 0.0 collective-permute-done.11
  78.4 0.3 maximum_add_fusion.base
  78.7 0.7 collective-permute-done.16.far_sums
  79.4 2.8 %shard_map.80 = bf16[768,512]{1,0:T(8,128)(2,1)} custom-call(s32[3]{0:T(128)S(1)} %copy-done.2, s32[48]{0:T(128)S(1)} %copy-done.5, f32[768,512]{1,0:T(8,128)S(1)} %maximum_add_fusion.base, f32[6,64,128]{2,1,0:T(8,128)S(1)} %get-tuple-element.51.sums, f32[6,64,128]{2,1,0:T(8,128)S(1)} %collective-permute-done.16.far_sums, ...), custom_call_target="tpu_custom_call" | custom-call | flops 1 | bytes 1 | tf_op jit(solution)/shard_map/pallas_call | solution.py:311
  (8 shorter events, 0.0 us)
Async XLA Ops:
  29.2 21.9 %collective-permute-start.2 = (bf16[64,4608]{1,0:T(8,128)(2,1)}, bf16[64,4608]{1,0:T(8,128)(2,1)S(1)}, u32[]{:S(2)}, u32[]{:S(2)}) collective-permute-start(bf16[64,4608]{1,0:T(8,128)(2,1)} %get-tuple-element.33), channel_id=1, source_target_pairs={{0,2},{2,0},{4,6},{6,4},{8,10},{10,8},{12,14},{14,12},{1,3},{3,1},... | collective-permute-start | bytes 1769480 | tf_op jit(solution)/shard_map/ppermute | solution.py:349
  32.2 12.0 %collective-permute-start.1 = (bf16[64,2304]{1,0:T(8,128)(2,1)}, bf16[64,2304]{1,0:T(8,128)(2,1)S(1)}, u32[]{:S(2)}, u32[]{:S(2)}) collective-permute-start(bf16[64,2304]{1,0:T(8,128)(2,1)} %get-tuple-element.29), channel_id=1, source_target_pairs={{0,4},{2,6},{4,8},{6,10},{8,12},{10,14},{12,0},{14,2},{1,5},{3,7},... | collective-permute-start | bytes 884744 | tf_op jit(solution)/shard_map/ppermute | solution.py:346
  33.8 14.7 %collective-permute-start = (bf16[64,2304]{1,0:T(8,128)(2,1)}, bf16[64,2304]{1,0:T(8,128)(2,1)S(1)}, u32[]{:S(2)}, u32[]{:S(2)}) collective-permute-start(bf16[64,2304]{1,0:T(8,128)(2,1)} %get-tuple-element.29), channel_id=1, source_target_pairs={{0,12},{2,14},{4,0},{6,2},{8,4},{10,6},{12,8},{14,10},{1,13},{3,15... | collective-permute-start | bytes 884744 | tf_op jit(solution)/shard_map/ppermute | solution.py:346
  36.0 0.6 copy-start.2
  44.2 18.8 %copy-start = (bf16[1,64,4096]{2,1,0:T(8,128)(2,1)S(1)}, bf16[1,64,4096]{2,1,0:T(8,128)(2,1)}, u32[]{:S(2)}) copy-start(bf16[1,64,4096]{2,1,0:T(8,128)(2,1)} %param.9) | copy-start | bytes 1572868
  44.2 18.8 %copy-start.1 = (bf16[1,64,512]{2,1,0:T(8,128)(2,1)S(1)}, bf16[1,64,512]{2,1,0:T(8,128)(2,1)}, u32[]{:S(2)}) copy-start(bf16[1,64,512]{2,1,0:T(8,128)(2,1)} %param.10) | copy-start | bytes 196612
  44.2 18.8 %copy-start.3 = (s32[8]{0:T(128)S(1)}, s32[8]{0:T(128)}, u32[]{:S(2)}) copy-start(s32[8]{0:T(128)} %pool_index.7) | copy-start | bytes 100
  44.2 18.8 %copy-start.4 = (s32[48,1]{0,1:T(1,128)S(1)}, s32[48,1]{0,1:T(1,128)}, u32[]{:S(2)}) copy-start(s32[48,1]{0,1:T(1,128)} %param.12) | copy-start | bytes 580
  44.2 14.4 %collective-permute-start.3 = (bf16[64,2304]{1,0:T(8,128)(2,1)S(1)}, bf16[64,2304]{1,0:T(8,128)(2,1)S(1)}, u32[]{:S(2)}, u32[]{:S(2)}) collective-permute-start(bf16[64,2304]{1,0:T(8,128)(2,1)S(1)} %collective-permute-done.1.refs_3_), channel_id=1, source_target_pairs={{0,16},{16,0},{1,17},{17,1},{2,18},{18,2},{3,19},{19,3},{4,20},{20... | collective-permute-start | bytes 884744 | tf_op jit(solution)/shard_map/ppermute | solution.py:352
  45.8 12.8 %collective-permute-start.5 = (bf16[64,2304]{1,0:T(8,128)(2,1)S(1)}, bf16[64,2304]{1,0:T(8,128)(2,1)S(1)}, u32[]{:S(2)}, u32[]{:S(2)}) collective-permute-start(bf16[64,2304]{1,0:T(8,128)(2,1)S(1)} %collective-permute-done.1.refs_3_), channel_id=1, source_target_pairs={{0,2},{2,0},{4,6},{6,4},{8,10},{10,8},{12,14},{14,12},{1,3},{3,1},... | collective-permute-start | bytes 884744 | tf_op jit(solution)/shard_map/ppermute | solution.py:349
  48.5 10.1 %collective-permute-start.6 = (bf16[64,2304]{1,0:T(8,128)(2,1)S(1)}, bf16[64,2304]{1,0:T(8,128)(2,1)S(1)}, u32[]{:S(2)}, u32[]{:S(2)}) collective-permute-start(bf16[64,2304]{1,0:T(8,128)(2,1)S(1)} %collective-permute-done.1.refs_3_), channel_id=1, source_target_pairs={{0,4},{2,6},{4,8},{6,10},{8,12},{10,14},{12,0},{14,2},{1,5},{3,7},... | collective-permute-start | bytes 884744 | tf_op jit(solution)/shard_map/ppermute | solution.py:346
  49.6 19.4 %collective-permute-start.7 = (bf16[64,2304]{1,0:T(8,128)(2,1)S(1)}, bf16[64,2304]{1,0:T(8,128)(2,1)S(1)}, u32[]{:S(2)}, u32[]{:S(2)}) collective-permute-start(bf16[64,2304]{1,0:T(8,128)(2,1)S(1)} %collective-permute-done.refs_4_), channel_id=1, source_target_pairs={{0,16},{16,0},{1,17},{17,1},{2,18},{18,2},{3,19},{19,3},{4,20},{20... | collective-permute-start | bytes 884744 | tf_op jit(solution)/shard_map/ppermute | solution.py:352
  51.1 11.4 %collective-permute-start.8 = (bf16[64,2304]{1,0:T(8,128)(2,1)S(1)}, bf16[64,2304]{1,0:T(8,128)(2,1)S(1)}, u32[]{:S(2)}, u32[]{:S(2)}) collective-permute-start(bf16[64,2304]{1,0:T(8,128)(2,1)S(1)} %collective-permute-done.refs_4_), channel_id=1, source_target_pairs={{0,2},{2,0},{4,6},{6,4},{8,10},{10,8},{12,14},{14,12},{1,3},{3,1},... | collective-permute-start | bytes 884744 | tf_op jit(solution)/shard_map/ppermute | solution.py:349
  58.6 8.9 %collective-permute-start.4 = (bf16[64,2304]{1,0:T(8,128)(2,1)S(1)}, bf16[64,2304]{1,0:T(8,128)(2,1)S(1)}, u32[]{:S(2)}, u32[]{:S(2)}) collective-permute-start(bf16[64,2304]{1,0:T(8,128)(2,1)S(1)} %collective-permute-done.3.refs_0_), channel_id=1, source_target_pairs={{0,4},{2,6},{4,8},{6,10},{8,12},{10,14},{12,0},{14,2},{1,5},{3,7},... | collective-permute-start | bytes 884744 | tf_op jit(solution)/shard_map/ppermute | solution.py:346
  60.5 12.2 %collective-permute-start.15 = (bf16[64,2304]{1,0:T(8,128)(2,1)S(1)}, bf16[64,2304]{1,0:T(8,128)(2,1)S(1)}, u32[]{:S(2)}, u32[]{:S(2)}) collective-permute-start(bf16[64,2304]{1,0:T(8,128)(2,1)S(1)} %collective-permute-done.6.refs_2_), channel_id=1, source_target_pairs={{0,2},{2,0},{4,6},{6,4},{8,10},{10,8},{12,14},{14,12},{1,3},{3,1},... | collective-permute-start | bytes 884744 | tf_op jit(solution)/shard_map/ppermute | solution.py:349
  61.0 12.2 %collective-permute-start.13 = (bf16[64,2304]{1,0:T(8,128)(2,1)S(1)}, bf16[64,2304]{1,0:T(8,128)(2,1)S(1)}, u32[]{:S(2)}, u32[]{:S(2)}) collective-permute-start(bf16[64,2304]{1,0:T(8,128)(2,1)S(1)} %collective-permute-done.5.refs_1_), channel_id=1, source_target_pairs={{0,16},{16,0},{1,17},{17,1},{2,18},{18,2},{3,19},{19,3},{4,20},{20... | collective-permute-start | bytes 884744 | tf_op jit(solution)/shard_map/ppermute | solution.py:352
  62.5 10.9 %collective-permute-start.14 = (bf16[64,2304]{1,0:T(8,128)(2,1)S(1)}, bf16[64,2304]{1,0:T(8,128)(2,1)S(1)}, u32[]{:S(2)}, u32[]{:S(2)}) collective-permute-start(bf16[64,2304]{1,0:T(8,128)(2,1)S(1)} %collective-permute-done.8.refs_4_), channel_id=1, source_target_pairs={{0,16},{16,0},{1,17},{17,1},{2,18},{18,2},{3,19},{19,3},{4,20},{20... | collective-permute-start | bytes 884744 | tf_op jit(solution)/shard_map/ppermute | solution.py:352
  67.5 9.1 %collective-permute-start.12 = (bf16[64,2304]{1,0:T(8,128)(2,1)S(1)}, bf16[64,2304]{1,0:T(8,128)(2,1)S(1)}, u32[]{:S(2)}, u32[]{:S(2)}) collective-permute-start(bf16[64,2304]{1,0:T(8,128)(2,1)S(1)} %collective-permute-done.4.refs_0_), channel_id=1, source_target_pairs={{0,2},{2,0},{4,6},{6,4},{8,10},{10,8},{12,14},{14,12},{1,3},{3,1},... | collective-permute-start | bytes 884744 | tf_op jit(solution)/shard_map/ppermute | solution.py:349
  72.6 5.7 %collective-permute-start.9 = (f32[256,512]{1,0:T(8,128)S(1)}, f32[256,512]{1,0:T(8,128)S(1)}, u32[]{:S(2)}, u32[]{:S(2)}) collective-permute-start(f32[256,512]{1,0:T(8,128)S(1)} %get-tuple-element.42), channel_id=1, source_target_pairs={{0,1},{1,0},{2,3},{3,2},{4,5},{5,4},{6,7},{7,6},{8,9},{9,8},{10,11... | collective-permute-start | bytes 1572872 | tf_op jit(solution)/shard_map/ppermute | solution.py:355
  72.7 5.6 %collective-permute-start.10 = (f32[256,512]{1,0:T(8,128)S(1)}, f32[256,512]{1,0:T(8,128)S(1)}, u32[]{:S(2)}, u32[]{:S(2)}) collective-permute-start(f32[256,512]{1,0:T(8,128)S(1)} %get-tuple-element.44), channel_id=1, source_target_pairs={{0,1},{1,0},{2,3},{3,2},{4,5},{5,4},{6,7},{7,6},{8,9},{9,8},{10,11... | collective-permute-start | bytes 1572872 | tf_op jit(solution)/shard_map/ppermute | solution.py:355
  73.2 5.1 %collective-permute-start.11 = (f32[256,512]{1,0:T(8,128)S(1)}, f32[256,512]{1,0:T(8,128)S(1)}, u32[]{:S(2)}, u32[]{:S(2)}) collective-permute-start(f32[256,512]{1,0:T(8,128)S(1)} %get-tuple-element.46), channel_id=1, source_target_pairs={{0,1},{1,0},{2,3},{3,2},{4,5},{5,4},{6,7},{7,6},{8,9},{9,8},{10,11... | collective-permute-start | bytes 1572872 | tf_op jit(solution)/shard_map/ppermute | solution.py:355
  77.9 1.5 %copy-start.5 = (s32[48]{0:T(128)S(1)}, s32[48]{0:T(128)}, u32[]{:S(2)}) copy-start(s32[48]{0:T(128)} %live.1) | copy-start | bytes 580
  77.9 1.5 %collective-permute-start.16 = (f32[6,64,128]{2,1,0:T(8,128)S(1)}, f32[6,64,128]{2,1,0:T(8,128)S(1)}, u32[]{:S(2)}, u32[]{:S(2)}) collective-permute-start(f32[6,64,128]{2,1,0:T(8,128)S(1)} %get-tuple-element.51.sums), channel_id=1, source_target_pairs={{0,1},{1,0},{2,3},{3,2},{4,5},{5,4},{6,7},{7,6},{8,9},{9,8},{10,11... | collective-permute-start | bytes 589832 | tf_op jit(solution)/shard_map/ppermute | solution.py:355

commit v8 on v6

--- a/solution.py
+++ b/solution.py
@@ -32,35 +32,44 @@
 ANY = pl.BlockSpec(memory_space=pl.ANY)
 
 
-def base_kernel(cuts, other, place, tokens, weight, *refs):
-    core = 1 - place[2] if other else place[2]
-    base_steps(cuts, core, tokens, weight, refs[:-4], refs[-4:])
-
-
-def base_steps(cuts, core, tokens, weight, outs, scratch):
-    tokens_v, weight_v, t_sem, w_sem = scratch
-    part, half = outs[0].shape
-    columns = pl.ds(pl.multiple_of(core * half, half), half)
-    copies = []
+def base_kernel(cuts, runs, half, place, tokens, weight, *refs):
+    outs, (tokens_v, weight_v, t_sem, w_sem) = list(refs[:-4]), refs[-4:]
+    copies, first = [], 0
     for step, (start, depth) in enumerate(cuts):
         span = pl.ds(start, depth)
-        pair = (
-            pltpu.make_async_copy(tokens.at[:, span], tokens_v.at[:, span], t_sem.at[step]),
-            pltpu.make_async_copy(weight.at[span, columns], weight_v.at[span, :], w_sem.at[step]),
+        copies.append(
+            [pltpu.make_async_copy(tokens.at[:, span], tokens_v.at[:, span], t_sem.at[step])]
         )
-        for copy in pair:
+        first = 0
+        for at, (other, column, count, _) in enumerate(runs):
+            core = 1 - place[2] if other else place[2]
+            columns = pl.ds(pl.multiple_of(core * half + column, count), count)
+            copies[-1].append(
+                pltpu.make_async_copy(
+                    weight.at[span, columns],
+                    weight_v.at[span, pl.ds(first, count)],
+                    w_sem.at[step, at],
+                )
+            )
+            first += count
+        for copy in copies[-1]:
             copy.start()
-        copies.append(pair)
     for step, (start, depth) in enumerate(cuts):
         for copy in copies[step]:
             copy.wait()
-        for at, out in enumerate(outs):
-            product = jnp.dot(
-                tokens_v[pl.ds(at * part, part), pl.ds(start, depth)],
-                weight_v[pl.ds(start, depth), :],
-                preferred_element_type=jnp.float32,
-            )
-            out[...] = product if step == 0 else out[...] + product
+        first, place_of = 0, 0
+        for _, _, count, parts in runs:
+            for at in range(parts):
+                out = outs[place_of + at]
+                part = out.shape[0]
+                product = jnp.dot(
+                    tokens_v[pl.ds(at * part, part), pl.ds(start, depth)],
+                    weight_v[pl.ds(start, depth), pl.ds(first, count)],
+                    preferred_element_type=jnp.float32,
+                )
+                out[...] = product if step == 0 else out[...] + product
+            first += count
+            place_of += parts
 
 
 def base_cuts(width):
@@ -68,26 +77,25 @@
     return [(0, eighth)] + [(at * eighth, 2 * eighth) for at in (1, 3, 5)] + [(7 * eighth, eighth)]
 
 
-def base_scratch(tokens, weight):
+def base_sums(place, tokens, weight, runs, hint):
     rows, width = tokens.shape
     steps = len(base_cuts(width))
-    return [
-        pltpu.VMEM((rows, width), tokens.dtype),
-        pltpu.VMEM((width, weight.shape[1] // 2), weight.dtype),
-        pltpu.SemaphoreType.DMA((steps,)),
-        pltpu.SemaphoreType.DMA((steps,)),
+    shapes = [
+        jax.ShapeDtypeStruct((rows // parts, count), jnp.float32)
+        for _, _, count, parts in runs
+        for _ in range(parts)
     ]
-
-
-def base_sums(place, tokens, weight, other, parts, hint):
-    rows, width = tokens.shape
-    half = weight.shape[1] // 2
     return pl.pallas_call(
-        functools.partial(base_kernel, base_cuts(width), other),
+        functools.partial(base_kernel, base_cuts(width), runs, weight.shape[1] // 2),
         in_specs=[SMEM, ANY, ANY],
-        out_specs=[VMEM] * parts,
-        out_shape=[jax.ShapeDtypeStruct((rows // parts, half), jnp.float32)] * parts,
-        scratch_shapes=base_scratch(tokens, weight),
+        out_specs=[VMEM] * len(shapes),
+        out_shape=shapes,
+        scratch_shapes=[
+            pltpu.VMEM((rows, width), tokens.dtype),
+            pltpu.VMEM((width, sum(count for _, _, count, _ in runs)), weight.dtype),
+            pltpu.SemaphoreType.DMA((steps,)),
+            pltpu.SemaphoreType.DMA((steps, len(runs))),
+        ],
         compiler_params=kernel_params(50),
         cost_estimate=hint,
     )(place, tokens, weight)
@@ -275,9 +283,16 @@
     down, up = adapter_down_weight[0], adapter_up_weight[0]
     width, half = down.shape[1] // 2, up.shape[1] // 2
     piece = width + half
-    own = jnp.concatenate([down[:, :width], up[:, :half], down[:, width:], up[:, half:]], axis=1)
+    own = jnp.concatenate([down, up], axis=1)
     first = lax.axis_index("groups") == 0
-    own_half = jnp.where(first, own[:, :piece], own[:, piece:])
+    own_ = lax.optimization_barrier(own)
+    own_half = jnp.concatenate(
+        [
+            jnp.where(first, own_[:, :width], own_[:, width : 2 * width]),
+            jnp.where(first, own_[:, 2 * width : 2 * width + half], own_[:, 2 * width + half :]),
+        ],
+        axis=1,
+    )
 
     def ring(array, step):
         pairs = [(2 * z + y, 2 * ((z + step) % 4) + y) for z in range(4) for y in range(2)]
@@ -297,7 +312,14 @@
     z1 = ring(own_half, 1)
     y0 = over_y(own)
     z3 = ring(own_half, -1)
-    fars = base_sums(place, tokens, weight, True, FAR_PARTS, LIGHT)
+    features = up.shape[1]
+    *fars, mine_a = base_sums(
+        place,
+        tokens,
+        weight,
+        [(True, 0, features, FAR_PARTS), (False, 0, features // 2, 1)],
+        LIGHT,
+    )
     z1_ = after(z1, fars[0])
     x1 = over_x(z1_)
     y1 = over_y(z1_)
@@ -309,7 +331,13 @@
     y2a = over_y(z2a)
     x1y = over_x(y1)
 
-    (mine,) = base_sums(place, after(tokens, z3_, y0), weight, False, 1, HEAVY)
+    (mine_b,) = base_sums(
+        place,
+        after(tokens, z3_, y0),
+        weight,
+        [(False, features // 2, features // 2, 1)],
+        HEAVY,
+    )
     def named(first, entries):
         return [
             (entry, kind, (first + at, 0), (first + at, width), half)
@@ -318,13 +346,13 @@
 
     prior = shrink_sums(
         scalars,
-        after(tokens, mine, x1, y1, z2a),
+        after(tokens, mine_b, x1, y1, z2a),
         [down, up, y0, z1, z3],
         [
             (0, "a", (0, 0), (1, 0), half),
             (0, "b", (0, width), (1, half), half),
-            (1, "a", (2, 0), (2, width), half),
-            (1, "b", (2, piece), (2, piece + width), half),
+            (1, "a", (2, 0), (2, 2 * width), half),
+            (1, "b", (2, width), (2, 2 * width + half), half),
         ]
         + named(3, [(2, "own"), (6, "own")]),
         [],
@@ -349,6 +377,7 @@
         prior,
         HEAVY,
     )
+    mine = jnp.concatenate([mine_a, mine_b], axis=1)
     base = mine + jnp.concatenate(base_fars, axis=0)
     sums, ups = shrink_sums(
         scalars, tokens, [y2b], named(0, [(5, "far")]), prior, LIGHT

time: 54.3 us -> 54.1 us (level)
  Pallas kernels: 24.7 us -> 28.9 us
  starting transfers between devices: 19.2 us -> 17.3 us
  local copies, waits for them, and re-layouts: 1.87 us -> 0.03 us
  waiting for transfers between devices: 8.03 us -> 6.43 us
  other arithmetic: 0.53 us -> 1.51 us
    ppermute x4, waiting for transfers between devices: 7.29 us -> 2.63 us  [ring(): return lax.ppermute(array, 'dp', pairs)]
    pallas_call x2, Pallas kernels: 11.8 us -> 15.1 us  [base_sums(): pl.pallas_call(functools.partial(base_kernel, base_cuts(width), runs, wei...]
    slice x2 -> x0, local copies, waits for them, and re-layouts: 1.85 us -> none  [the longest x1 1.06 us: per_device_planes(): down[:, width:]]
    ppermute x5, waiting for transfers between devices: 0.01 us -> 1.6 us  [over_y(): return lax.ppermute(array, 'dp', [(i, i ^ 1) for i in range(8)])]
    concatenate x1 -> x2, other arithmetic: 0.04 us -> 1.14 us  [the longest x1 1.12 us: per_device_planes(): own = jnp.concatenate([down, up], axis=1)]
    ppermute x4, waiting for transfers between devices: 0.01 us -> 1.08 us  [over_x(): return lax.ppermute(array, 'groups', SWAP)]
    pallas_call x4, Pallas kernels: 11.1 us -> 12 us  [shrink_sums(): pl.pallas_call(functools.partial(shrink_kernel, pieces, count, len(prior)...]
    ppermute x4, starting transfers between devices: 6.9 us -> 6.28 us  [ring(): return lax.ppermute(array, 'dp', pairs)]
  transfers between devices with their start and end apart: 17 -> 17, of which waited for: 5 -> 6; matrix products, arithmetic and copies ran while one was open for 1% -> 1% of each run, Pallas kernels for 42% -> 50%
where the time goes in v8:
time: 54.1 us; the launch traced here: 54.5 us
  Pallas kernels  28.9 us (53%)
  starting transfers between devices  17.3 us (32%)
  waiting for transfers between devices  6.43 us (12%)
  other arithmetic  1.51 us (3%)
    pallas_call x2, Pallas kernels, base_sums(): pl.pallas_call(functools.partial(base_kernel, base_cuts(width), runs, wei...  15.1 us
    pallas_call x4, Pallas kernels, shrink_sums(): pl.pallas_call(functools.partial(shrink_kernel, pieces, count, len(prior)...  12 us
    ppermute x4, starting transfers between devices, ring(): return lax.ppermute(array, 'dp', pairs)  6.28 us
    ppermute x5, starting transfers between devices, over_y(): return lax.ppermute(array, 'dp', [(i, i ^ 1) for i in range(8)])  5.78 us
    ppermute x4, starting transfers between devices, over_x(): return lax.ppermute(array, 'groups', SWAP)  4.54 us
    ppermute x4, waiting for transfers between devices, ring(): return lax.ppermute(array, 'dp', pairs)  2.63 us
    pallas_call x1, Pallas kernels, final_keys(): pl.pallas_call(final_kernel, in_specs=[SMEM, SMEM] + [VMEM] * 4, out_spec...  1.85 us
    ppermute x5, waiting for transfers between devices, over_y(): return lax.ppermute(array, 'dp', [(i, i ^ 1) for i in range(8)])  1.6 us
  transfers between devices with their start and end apart: 17, of which 6 were waited for; matrix products, arithmetic and copies ran while one was open for 1% of the time, Pallas kernels for 50%

profile of v8, /device:TPU:0, one launch (start us, length us, event | category | flops | bytes accessed | tf_op | source)
XLA Modules:
  0.0 54.5 jit_solution(6794573646565485662)
XLA Ops:
  0.0 1.1 %pad_maximum_fusion = bf16[64,4608]{1,0:T(8,128)(2,1)S(1)} fusion(bf16[64,512]{1,0:T(8,128)(2,1)} %bitcast.8, bf16[64,4096]{1,0:T(8,128)(2,1)} %bitcast.6), kind=kLoop, calls=%fused_computation.1 | loop fusion | flops 1179648 | bytes 1179648 | tf_op jit(solution)/shard_map/concatenate | solution.py:286
  1.1 3.0 %collective-permute-start.2 = (bf16[64,4608]{1,0:T(8,128)(2,1)S(1)}, bf16[64,4608]{1,0:T(8,128)(2,1)S(1)}, u32[]{:S(2)}, u32[]{:S(2)}) collective-permute-start(bf16[64,4608]{1,0:T(8,128)(2,1)S(1)} %pad_maximum_fusion), channel_id=1, source_target_pairs={{0,2},{2,0},{4,6},{6,4},{8,10},{10,8},{12,14},{14,12},{1,3},{3,1},... | collective-permute-start | bytes 1769480 | tf_op jit(solution)/shard_map/ppermute | solution.py:302
  4.2 1.6 %collective-permute-start.1 = (bf16[64,2304]{1,0:T(8,128)(2,1)S(1)}, bf16[64,2304]{1,0:T(8,128)(2,1)S(1)}, u32[]{:S(2)}, u32[]{:S(2)}) collective-permute-start(bf16[64,2304]{1,0:T(8,128)(2,1)S(1)} %pad_maximum_fusion.1), channel_id=1, source_target_pairs={{0,4},{2,6},{4,8},{6,10},{8,12},{10,14},{12,0},{14,2},{1,5},{3,7},... | collective-permute-start | bytes 884744 | tf_op jit(solution)/shard_map/ppermute | solution.py:299
  5.9 2.2 %collective-permute-start = (bf16[64,2304]{1,0:T(8,128)(2,1)S(1)}, bf16[64,2304]{1,0:T(8,128)(2,1)S(1)}, u32[]{:S(2)}, u32[]{:S(2)}) collective-permute-start(bf16[64,2304]{1,0:T(8,128)(2,1)S(1)} %pad_maximum_fusion.1), channel_id=1, source_target_pairs={{0,12},{2,14},{4,0},{6,2},{8,4},{10,6},{12,8},{14,10},{1,13},{3,15... | collective-permute-start | bytes 884744 | tf_op jit(solution)/shard_map/ppermute | solution.py:299
  8.1 0.1 pad_add_fusion.place
  8.2 9.8 %shard_map.73 = (f32[256,512]{1,0:T(8,128)S(1)}, f32[256,512]{1,0:T(8,128)S(1)}, f32[256,512]{1,0:T(8,128)S(1)}, f32[768,256]{1,0:T(8,128)S(1)}) custom-call(s32[3]{0:T(128)S(1)} %pad_add_fusion.place, bf16[768,4096]{1,0:T(8,128)(2,1)} %tokens.8, bf16[4096,1024]{1,0:T(8,128)(2,1)} %weight.3), custom_call_target="tpu_custom_call" | custom-call | flops 1 | bytes 1 | tf_op jit(solution)/shard_map/pallas_call | solution.py:88
  18.0 0.0 collective-permute-done.1.refs_3_
  18.0 0.0 copy-start
  18.0 0.0 copy-start.1
  18.0 0.0 copy-start.2
  18.0 0.0 copy-start.3
  18.0 1.6 %collective-permute-start.3 = (bf16[64,2304]{1,0:T(8,128)(2,1)S(1)}, bf16[64,2304]{1,0:T(8,128)(2,1)S(1)}, u32[]{:S(2)}, u32[]{:S(2)}) collective-permute-start(bf16[64,2304]{1,0:T(8,128)(2,1)S(1)} %collective-permute-done.1.refs_3_), channel_id=1, source_target_pairs={{0,16},{16,0},{1,17},{17,1},{2,18},{18,2},{3,19},{19,3},{4,20},{20... | collective-permute-start | bytes 884744 | tf_op jit(solution)/shard_map/ppermute | solution.py:305
  19.6 0.5 collective-permute-start.5
  20.1 0.3 collective-permute-done.refs_4_
  20.4 1.1 %collective-permute-start.6 = (bf16[64,2304]{1,0:T(8,128)(2,1)S(1)}, bf16[64,2304]{1,0:T(8,128)(2,1)S(1)}, u32[]{:S(2)}, u32[]{:S(2)}) collective-permute-start(bf16[64,2304]{1,0:T(8,128)(2,1)S(1)} %collective-permute-done.1.refs_3_), channel_id=1, source_target_pairs={{0,4},{2,6},{4,8},{6,10},{8,12},{10,14},{12,0},{14,2},{1,5},{3,7},... | collective-permute-start | bytes 884744 | tf_op jit(solution)/shard_map/ppermute | solution.py:299
  21.5 1.5 %collective-permute-start.7 = (bf16[64,2304]{1,0:T(8,128)(2,1)S(1)}, bf16[64,2304]{1,0:T(8,128)(2,1)S(1)}, u32[]{:S(2)}, u32[]{:S(2)}) collective-permute-start(bf16[64,2304]{1,0:T(8,128)(2,1)S(1)} %collective-permute-done.refs_4_), channel_id=1, source_target_pairs={{0,16},{16,0},{1,17},{17,1},{2,18},{18,2},{3,19},{19,3},{4,20},{20... | collective-permute-start | bytes 884744 | tf_op jit(solution)/shard_map/ppermute | solution.py:305
  23.0 0.0 collective-permute-done.2.refs_2_
  23.0 0.5 collective-permute-start.8
  23.5 5.3 %shard_map.74 = f32[768,256]{1,0:T(8,128)S(1)} custom-call(s32[3]{0:T(128)S(1)} %pad_add_fusion.place, bf16[768,4096]{1,0:T(8,128)(2,1)} %tokens.8, bf16[4096,1024]{1,0:T(8,128)(2,1)} %weight.3), custom_call_target="tpu_custom_call" | custom-call | flops 30000001024 | bytes 1 | tf_op jit(solution)/shard_map/pallas_call | solution.py:88
  28.8 1.7 %collective-permute-done.6.refs_2_ = bf16[64,2304]{1,0:T(8,128)(2,1)S(1)} collective-permute-done((bf16[64,2304]{1,0:T(8,128)(2,1)S(1)}, bf16[64,2304]{1,0:T(8,128)(2,1)S(1)}, u32[]{:S(2)}, u32[]{:S(2)}) %collective-permute-start.6) | collective-permute-done | bytes 294944 | tf_op jit(solution)/shard_map/ppermute | solution.py:299
  30.5 0.0 collective-permute-done.3.refs_0_
  30.5 0.0 collective-permute-done.5.refs_1_
  30.5 1.3 %collective-permute-start.4 = (bf16[64,2304]{1,0:T(8,128)(2,1)S(1)}, bf16[64,2304]{1,0:T(8,128)(2,1)S(1)}, u32[]{:S(2)}, u32[]{:S(2)}) collective-permute-start(bf16[64,2304]{1,0:T(8,128)(2,1)S(1)} %collective-permute-done.3.refs_0_), channel_id=1, source_target_pairs={{0,4},{2,6},{4,8},{6,10},{8,12},{10,14},{12,0},{14,2},{1,5},{3,7},... | collective-permute-start | bytes 884744 | tf_op jit(solution)/shard_map/ppermute | solution.py:299
  31.7 0.5 collective-permute-start.15
  32.2 1.5 %collective-permute-start.13 = (bf16[64,2304]{1,0:T(8,128)(2,1)S(1)}, bf16[64,2304]{1,0:T(8,128)(2,1)S(1)}, u32[]{:S(2)}, u32[]{:S(2)}) collective-permute-start(bf16[64,2304]{1,0:T(8,128)(2,1)S(1)} %collective-permute-done.5.refs_1_), channel_id=1, source_target_pairs={{0,16},{16,0},{1,17},{17,1},{2,18},{18,2},{3,19},{19,3},{4,20},{20... | collective-permute-start | bytes 884744 | tf_op jit(solution)/shard_map/ppermute | solution.py:305
  33.7 1.6 %collective-permute-done.8.refs_4_ = bf16[64,2304]{1,0:T(8,128)(2,1)S(1)} collective-permute-done((bf16[64,2304]{1,0:T(8,128)(2,1)S(1)}, bf16[64,2304]{1,0:T(8,128)(2,1)S(1)}, u32[]{:S(2)}, u32[]{:S(2)}) %collective-permute-start.8) | collective-permute-done | bytes 294944 | tf_op jit(solution)/shard_map/ppermute | solution.py:302
  35.3 0.0 collective-permute-start.14
  35.4 3.0 %shard_map.75 = (f32[6,64,128]{2,1,0:T(8,128)S(1)}, bf16[6,64,512]{2,1,0:T(8,128)(2,1)S(1)}) custom-call(s32[3]{0:T(128)S(1)} %pad_add_fusion.place, s32[8]{0:T(128)S(1)} %copy-done.2, s32[48]{0:T(128)S(1)} %bitcast.10, bf16[768,4096]{1,0:T(8,128)(2,1)} %tokens.8, bf16[64,4096]{1,0:T(8,128)(2,1)S(1)} %bitcast.7, bf16[64,512]{1,0:T(8,128)(2,1)S(1)} %bitcast.9, ...), custom_call_target="tpu_custom_call" | custom-call | flops 30000001024 | bytes 1 | tf_op jit(solution)/shard_map/pallas_call | solution.py:219
  38.4 0.7 %collective-permute-done.4.refs_0_ = bf16[64,2304]{1,0:T(8,128)(2,1)S(1)} collective-permute-done((bf16[64,2304]{1,0:T(8,128)(2,1)S(1)}, bf16[64,2304]{1,0:T(8,128)(2,1)S(1)}, u32[]{:S(2)}, u32[]{:S(2)}) %collective-permute-start.4) | collective-permute-done | bytes 294944 | tf_op jit(solution)/shard_map/ppermute | solution.py:299
  39.1 1.2 %collective-permute-start.12 = (bf16[64,2304]{1,0:T(8,128)(2,1)S(1)}, bf16[64,2304]{1,0:T(8,128)(2,1)S(1)}, u32[]{:S(2)}, u32[]{:S(2)}) collective-permute-start(bf16[64,2304]{1,0:T(8,128)(2,1)S(1)} %collective-permute-done.4.refs_0_), channel_id=1, source_target_pairs={{0,2},{2,0},{4,6},{6,4},{8,10},{10,8},{12,14},{14,12},{1,3},{3,1},... | collective-permute-start | bytes 884744 | tf_op jit(solution)/shard_map/ppermute | solution.py:302
  40.3 0.0 collective-permute-done.7.refs_3_
  40.3 3.0 %shard_map.76 = (f32[6,64,128]{2,1,0:T(8,128)S(1)}, bf16[6,64,512]{2,1,0:T(8,128)(2,1)S(1)}) custom-call(s32[3]{0:T(128)S(1)} %pad_add_fusion.place, s32[8]{0:T(128)S(1)} %copy-done.2, s32[48]{0:T(128)S(1)} %bitcast.11, bf16[768,4096]{1,0:T(8,128)(2,1)} %tokens.8, ...), custom_call_target="tpu_custom_call", output_to_operand_aliasing={{1}: (10, {})} | custom-call | flops 1 | bytes 1 | tf_op jit(solution)/shard_map/pallas_call | solution.py:219
  43.4 0.1 collective-permute-start.9
  43.4 0.0 collective-permute-done.15.refs_3_
  43.4 0.5 collective-permute-start.10
  43.9 0.0 collective-permute-done.13.refs_1_
  43.9 0.1 collective-permute-start.11
  44.0 1.1 %collective-permute-done.14.refs_2_ = bf16[64,2304]{1,0:T(8,128)(2,1)S(1)} collective-permute-done((bf16[64,2304]{1,0:T(8,128)(2,1)S(1)}, bf16[64,2304]{1,0:T(8,128)(2,1)S(1)}, u32[]{:S(2)}, u32[]{:S(2)}) %collective-permute-start.14) | collective-permute-done | bytes 294944 | tf_op jit(solution)/shard_map/ppermute | solution.py:305
  45.1 3.3 %shard_map.77 = (f32[6,64,128]{2,1,0:T(8,128)S(1)}, bf16[6,64,512]{2,1,0:T(8,128)(2,1)S(1)}) custom-call(s32[3]{0:T(128)S(1)} %pad_add_fusion.place, s32[8]{0:T(128)S(1)} %copy-done.2, s32[48]{0:T(128)S(1)} %bitcast.12, bf16[768,4096]{1,0:T(8,128)(2,1)} %tokens.8, ...), custom_call_target="tpu_custom_call", output_to_operand_aliasing={{1}: (9, {})} | custom-call | flops 30000001024 | bytes 1 | tf_op jit(solution)/shard_map/pallas_call | solution.py:219
  48.4 0.0 collective-permute-done.12.refs_0_
  48.4 2.7 %shard_map.78 = (f32[6,64,128]{2,1,0:T(8,128)S(1)}, bf16[6,64,512]{2,1,0:T(8,128)(2,1)S(1)}) custom-call(s32[3]{0:T(128)S(1)} %pad_add_fusion.place, s32[8]{0:T(128)S(1)} %copy-done.2, s32[48]{0:T(128)S(1)} %bitcast.13, bf16[768,4096]{1,0:T(8,128)(2,1)} %tokens.8, ...), custom_call_target="tpu_custom_call", output_to_operand_aliasing={{1}: (6, {})} | custom-call | flops 1 | bytes 1 | tf_op jit(solution)/shard_map/pallas_call | solution.py:219
  51.1 0.1 collective-permute-start.16
  51.2 0.0 collective-permute-done.9
  51.2 0.0 collective-permute-done.11
  51.2 0.0 copy-start.4
  51.2 0.3 maximum_add_fusion.base
  51.5 1.1 %collective-permute-done.16.far_sums = f32[6,64,128]{2,1,0:T(8,128)S(1)} collective-permute-done((f32[6,64,128]{2,1,0:T(8,128)S(1)}, f32[6,64,128]{2,1,0:T(8,128)S(1)}, u32[]{:S(2)}, u32[]{:S(2)}) %collective-permute-start.16) | collective-permute-done | bytes 196640 | tf_op jit(solution)/shard_map/ppermute | solution.py:308
  52.6 1.8 %shard_map.79 = bf16[768,512]{1,0:T(8,128)(2,1)} custom-call(s32[3]{0:T(128)S(1)} %pad_add_fusion.place, s32[48]{0:T(128)S(1)} %copy-done.4, f32[768,512]{1,0:T(8,128)S(1)} %maximum_add_fusion.base, f32[6,64,128]{2,1,0:T(8,128)S(1)} %get-tuple-element.49.sums, f32[6,64,128]{2,1,0:T(8,128)S(1)} %collective-permute-done.16.far_sums, ...), custom_call_target="tpu_custom_call" | custom-call | flops 1 | bytes 1 | tf_op jit(solution)/shard_map/pallas_call | solution.py:261
  (9 shorter events, 0.1 us)
Async XLA Ops:
  1.1 21.9 %collective-permute-start.2 = (bf16[64,4608]{1,0:T(8,128)(2,1)S(1)}, bf16[64,4608]{1,0:T(8,128)(2,1)S(1)}, u32[]{:S(2)}, u32[]{:S(2)}) collective-permute-start(bf16[64,4608]{1,0:T(8,128)(2,1)S(1)} %pad_maximum_fusion), channel_id=1, source_target_pairs={{0,2},{2,0},{4,6},{6,4},{8,10},{10,8},{12,14},{14,12},{1,3},{3,1},... | collective-permute-start | bytes 1769480 | tf_op jit(solution)/shard_map/ppermute | solution.py:302
  4.2 13.7 %collective-permute-start.1 = (bf16[64,2304]{1,0:T(8,128)(2,1)S(1)}, bf16[64,2304]{1,0:T(8,128)(2,1)S(1)}, u32[]{:S(2)}, u32[]{:S(2)}) collective-permute-start(bf16[64,2304]{1,0:T(8,128)(2,1)S(1)} %pad_maximum_fusion.1), channel_id=1, source_target_pairs={{0,4},{2,6},{4,8},{6,10},{8,12},{10,14},{12,0},{14,2},{1,5},{3,7},... | collective-permute-start | bytes 884744 | tf_op jit(solution)/shard_map/ppermute | solution.py:299
  5.9 14.5 %collective-permute-start = (bf16[64,2304]{1,0:T(8,128)(2,1)S(1)}, bf16[64,2304]{1,0:T(8,128)(2,1)S(1)}, u32[]{:S(2)}, u32[]{:S(2)}) collective-permute-start(bf16[64,2304]{1,0:T(8,128)(2,1)S(1)} %pad_maximum_fusion.1), channel_id=1, source_target_pairs={{0,12},{2,14},{4,0},{6,2},{8,4},{10,6},{12,8},{14,10},{1,13},{3,15... | collective-permute-start | bytes 884744 | tf_op jit(solution)/shard_map/ppermute | solution.py:299
  18.0 17.4 %copy-start = (bf16[1,64,4096]{2,1,0:T(8,128)(2,1)S(1)}, bf16[1,64,4096]{2,1,0:T(8,128)(2,1)}, u32[]{:S(2)}) copy-start(bf16[1,64,4096]{2,1,0:T(8,128)(2,1)} %param.9) | copy-start | bytes 1572868
  18.0 17.3 %copy-start.1 = (bf16[1,64,512]{2,1,0:T(8,128)(2,1)S(1)}, bf16[1,64,512]{2,1,0:T(8,128)(2,1)}, u32[]{:S(2)}) copy-start(bf16[1,64,512]{2,1,0:T(8,128)(2,1)} %param.10) | copy-start | bytes 196612
  18.0 17.3 %copy-start.2 = (s32[8]{0:T(128)S(1)}, s32[8]{0:T(128)}, u32[]{:S(2)}) copy-start(s32[8]{0:T(128)} %pool_index.7) | copy-start | bytes 100
  18.0 17.3 %copy-start.3 = (s32[48,1]{0,1:T(1,128)S(1)}, s32[48,1]{0,1:T(1,128)}, u32[]{:S(2)}) copy-start(s32[48,1]{0,1:T(1,128)} %param.12) | copy-start | bytes 580
  18.0 12.4 %collective-permute-start.3 = (bf16[64,2304]{1,0:T(8,128)(2,1)S(1)}, bf16[64,2304]{1,0:T(8,128)(2,1)S(1)}, u32[]{:S(2)}, u32[]{:S(2)}) collective-permute-start(bf16[64,2304]{1,0:T(8,128)(2,1)S(1)} %collective-permute-done.1.refs_3_), channel_id=1, source_target_pairs={{0,16},{16,0},{1,17},{17,1},{2,18},{18,2},{3,19},{19,3},{4,20},{20... | collective-permute-start | bytes 884744 | tf_op jit(solution)/shard_map/ppermute | solution.py:305
  19.6 10.9 %collective-permute-start.5 = (bf16[64,2304]{1,0:T(8,128)(2,1)S(1)}, bf16[64,2304]{1,0:T(8,128)(2,1)S(1)}, u32[]{:S(2)}, u32[]{:S(2)}) collective-permute-start(bf16[64,2304]{1,0:T(8,128)(2,1)S(1)} %collective-permute-done.1.refs_3_), channel_id=1, source_target_pairs={{0,2},{2,0},{4,6},{6,4},{8,10},{10,8},{12,14},{14,12},{1,3},{3,1},... | collective-permute-start | bytes 884744 | tf_op jit(solution)/shard_map/ppermute | solution.py:302
  20.4 10.1 %collective-permute-start.6 = (bf16[64,2304]{1,0:T(8,128)(2,1)S(1)}, bf16[64,2304]{1,0:T(8,128)(2,1)S(1)}, u32[]{:S(2)}, u32[]{:S(2)}) collective-permute-start(bf16[64,2304]{1,0:T(8,128)(2,1)S(1)} %collective-permute-done.1.refs_3_), channel_id=1, source_target_pairs={{0,4},{2,6},{4,8},{6,10},{8,12},{10,14},{12,0},{14,2},{1,5},{3,7},... | collective-permute-start | bytes 884744 | tf_op jit(solution)/shard_map/ppermute | solution.py:299
  21.5 18.8 %collective-permute-start.7 = (bf16[64,2304]{1,0:T(8,128)(2,1)S(1)}, bf16[64,2304]{1,0:T(8,128)(2,1)S(1)}, u32[]{:S(2)}, u32[]{:S(2)}) collective-permute-start(bf16[64,2304]{1,0:T(8,128)(2,1)S(1)} %collective-permute-done.refs_4_), channel_id=1, source_target_pairs={{0,16},{16,0},{1,17},{17,1},{2,18},{18,2},{3,19},{19,3},{4,20},{20... | collective-permute-start | bytes 884744 | tf_op jit(solution)/shard_map/ppermute | solution.py:305
  23.0 12.3 %collective-permute-start.8 = (bf16[64,2304]{1,0:T(8,128)(2,1)S(1)}, bf16[64,2304]{1,0:T(8,128)(2,1)S(1)}, u32[]{:S(2)}, u32[]{:S(2)}) collective-permute-start(bf16[64,2304]{1,0:T(8,128)(2,1)S(1)} %collective-permute-done.refs_4_), channel_id=1, source_target_pairs={{0,2},{2,0},{4,6},{6,4},{8,10},{10,8},{12,14},{14,12},{1,3},{3,1},... | collective-permute-start | bytes 884744 | tf_op jit(solution)/shard_map/ppermute | solution.py:302
  30.5 8.6 %collective-permute-start.4 = (bf16[64,2304]{1,0:T(8,128)(2,1)S(1)}, bf16[64,2304]{1,0:T(8,128)(2,1)S(1)}, u32[]{:S(2)}, u32[]{:S(2)}) collective-permute-start(bf16[64,2304]{1,0:T(8,128)(2,1)S(1)} %collective-permute-done.3.refs_0_), channel_id=1, source_target_pairs={{0,4},{2,6},{4,8},{6,10},{8,12},{10,14},{12,0},{14,2},{1,5},{3,7},... | collective-permute-start | bytes 884744 | tf_op jit(solution)/shard_map/ppermute | solution.py:299
  31.7 11.7 %collective-permute-start.15 = (bf16[64,2304]{1,0:T(8,128)(2,1)S(1)}, bf16[64,2304]{1,0:T(8,128)(2,1)S(1)}, u32[]{:S(2)}, u32[]{:S(2)}) collective-permute-start(bf16[64,2304]{1,0:T(8,128)(2,1)S(1)} %collective-permute-done.6.refs_2_), channel_id=1, source_target_pairs={{0,2},{2,0},{4,6},{6,4},{8,10},{10,8},{12,14},{14,12},{1,3},{3,1},... | collective-permute-start | bytes 884744 | tf_op jit(solution)/shard_map/ppermute | solution.py:302
  32.2 11.7 %collective-permute-start.13 = (bf16[64,2304]{1,0:T(8,128)(2,1)S(1)}, bf16[64,2304]{1,0:T(8,128)(2,1)S(1)}, u32[]{:S(2)}, u32[]{:S(2)}) collective-permute-start(bf16[64,2304]{1,0:T(8,128)(2,1)S(1)} %collective-permute-done.5.refs_1_), channel_id=1, source_target_pairs={{0,16},{16,0},{1,17},{17,1},{2,18},{18,2},{3,19},{19,3},{4,20},{20... | collective-permute-start | bytes 884744 | tf_op jit(solution)/shard_map/ppermute | solution.py:305
  35.3 9.8 %collective-permute-start.14 = (bf16[64,2304]{1,0:T(8,128)(2,1)S(1)}, bf16[64,2304]{1,0:T(8,128)(2,1)S(1)}, u32[]{:S(2)}, u32[]{:S(2)}) collective-permute-start(bf16[64,2304]{1,0:T(8,128)(2,1)S(1)} %collective-permute-done.8.refs_4_), channel_id=1, source_target_pairs={{0,16},{16,0},{1,17},{17,1},{2,18},{18,2},{3,19},{19,3},{4,20},{20... | collective-permute-start | bytes 884744 | tf_op jit(solution)/shard_map/ppermute | solution.py:305
  39.1 9.3 %collective-permute-start.12 = (bf16[64,2304]{1,0:T(8,128)(2,1)S(1)}, bf16[64,2304]{1,0:T(8,128)(2,1)S(1)}, u32[]{:S(2)}, u32[]{:S(2)}) collective-permute-start(bf16[64,2304]{1,0:T(8,128)(2,1)S(1)} %collective-permute-done.4.refs_0_), channel_id=1, source_target_pairs={{0,2},{2,0},{4,6},{6,4},{8,10},{10,8},{12,14},{14,12},{1,3},{3,1},... | collective-permute-start | bytes 884744 | tf_op jit(solution)/shard_map/ppermute | solution.py:302
  43.4 7.8 %collective-permute-start.9 = (f32[256,512]{1,0:T(8,128)S(1)}, f32[256,512]{1,0:T(8,128)S(1)}, u32[]{:S(2)}, u32[]{:S(2)}) collective-permute-start(f32[256,512]{1,0:T(8,128)S(1)} %get-tuple-element.40), channel_id=1, source_target_pairs={{0,1},{1,0},{2,3},{3,2},{4,5},{5,4},{6,7},{7,6},{8,9},{9,8},{10,11... | collective-permute-start | bytes 1572872 | tf_op jit(solution)/shard_map/ppermute | solution.py:308
  43.4 7.8 %collective-permute-start.10 = (f32[256,512]{1,0:T(8,128)S(1)}, f32[256,512]{1,0:T(8,128)S(1)}, u32[]{:S(2)}, u32[]{:S(2)}) collective-permute-start(f32[256,512]{1,0:T(8,128)S(1)} %get-tuple-element.42), channel_id=1, source_target_pairs={{0,1},{1,0},{2,3},{3,2},{4,5},{5,4},{6,7},{7,6},{8,9},{9,8},{10,11... | collective-permute-start | bytes 1572872 | tf_op jit(solution)/shard_map/ppermute | solution.py:308
  43.9 7.3 %collective-permute-start.11 = (f32[256,512]{1,0:T(8,128)S(1)}, f32[256,512]{1,0:T(8,128)S(1)}, u32[]{:S(2)}, u32[]{:S(2)}) collective-permute-start(f32[256,512]{1,0:T(8,128)S(1)} %get-tuple-element.44), channel_id=1, source_target_pairs={{0,1},{1,0},{2,3},{3,2},{4,5},{5,4},{6,7},{7,6},{8,9},{9,8},{10,11... | collective-permute-start | bytes 1572872 | tf_op jit(solution)/shard_map/ppermute | solution.py:308
  51.1 1.5 %collective-permute-start.16 = (f32[6,64,128]{2,1,0:T(8,128)S(1)}, f32[6,64,128]{2,1,0:T(8,128)S(1)}, u32[]{:S(2)}, u32[]{:S(2)}) collective-permute-start(f32[6,64,128]{2,1,0:T(8,128)S(1)} %get-tuple-element.49.sums), channel_id=1, source_target_pairs={{0,1},{1,0},{2,3},{3,2},{4,5},{5,4},{6,7},{7,6},{8,9},{9,8},{10,11... | collective-permute-start | bytes 589832 | tf_op jit(solution)/shard_map/ppermute | solution.py:308
  51.2 1.4 %copy-start.4 = (s32[48]{0:T(128)S(1)}, s32[48]{0:T(128)}, u32[]{:S(2)}) copy-start(s32[48]{0:T(128)} %live.1) | copy-start | bytes 580

commit v9 on v6

--- a/solution.py
+++ b/solution.py
@@ -275,9 +275,16 @@
     down, up = adapter_down_weight[0], adapter_up_weight[0]
     width, half = down.shape[1] // 2, up.shape[1] // 2
     piece = width + half
-    own = jnp.concatenate([down[:, :width], up[:, :half], down[:, width:], up[:, half:]], axis=1)
+    own = jnp.concatenate([down, up], axis=1)
     first = lax.axis_index("groups") == 0
-    own_half = jnp.where(first, own[:, :piece], own[:, piece:])
+    own_ = lax.optimization_barrier(own)
+    own_half = jnp.concatenate(
+        [
+            jnp.where(first, own_[:, :width], own_[:, width : 2 * width]),
+            jnp.where(first, own_[:, 2 * width : 2 * width + half], own_[:, 2 * width + half :]),
+        ],
+        axis=1,
+    )
 
     def ring(array, step):
         pairs = [(2 * z + y, 2 * ((z + step) % 4) + y) for z in range(4) for y in range(2)]
@@ -306,7 +313,7 @@
     x3 = over_x(z3_)
     y3 = over_y(after(z3_, y0))
     z2b = ring(x1, 1)
-    y2a = over_y(z2a)
+    y2a = over_y(after(z2a, y3))
     x1y = over_x(y1)
 
     (mine,) = base_sums(place, after(tokens, z3_, y0), weight, False, 1, HEAVY)
@@ -318,13 +325,13 @@
 
     prior = shrink_sums(
         scalars,
-        after(tokens, mine, x1, y1, z2a),
+        after(tokens, mine, x1, y1, z2a, y3),
         [down, up, y0, z1, z3],
         [
             (0, "a", (0, 0), (1, 0), half),
             (0, "b", (0, width), (1, half), half),
-            (1, "a", (2, 0), (2, width), half),
-            (1, "b", (2, piece), (2, piece + width), half),
+            (1, "a", (2, 0), (2, 2 * width), half),
+            (1, "b", (2, width), (2, 2 * width + half), half),
         ]
         + named(3, [(2, "own"), (6, "own")]),
         [],

time: 54.3 us -> 53.8 us (level)
  local copies, waits for them, and re-layouts: 1.87 us -> 0.02 us
  waiting for transfers between devices: 8.03 us -> 6.39 us
  starting transfers between devices: 19.2 us -> 20.6 us
  other arithmetic: 0.53 us -> 1.6 us
    slice x2 -> x0, local copies, waits for them, and re-layouts: 1.85 us -> none  [the longest x1 1.06 us: per_device_planes(): down[:, width:]]
    ppermute x4, waiting for transfers between devices: 7.29 us -> 5.66 us  [ring(): return lax.ppermute(array, 'dp', pairs)]
    concatenate x1 -> x2, other arithmetic: 0.04 us -> 1.14 us  [the longest x1 1.12 us: per_device_planes(): own = jnp.concatenate([down, up], axis=1)]
    ppermute x4, starting transfers between devices: 6.9 us -> 7.92 us  [ring(): return lax.ppermute(array, 'dp', pairs)]
  transfers between devices with their start and end apart: 17 -> 17, of which waited for: 5 -> 4; matrix products, arithmetic and copies ran while one was open for 1% -> 1% of each run, Pallas kernels for 42% -> 43%
where the time goes in v9:
time: 53.8 us; the launch traced here: 53.5 us
  Pallas kernels  24.7 us (46%)
  starting transfers between devices  20.6 us (38%)
  waiting for transfers between devices  6.39 us (12%)
  other arithmetic  1.6 us (3%)
    pallas_call x2, Pallas kernels, base_sums(): pl.pallas_call(functools.partial(base_kernel, base_cuts(width), other), i...  11.8 us
    pallas_call x4, Pallas kernels, shrink_sums(): pl.pallas_call(functools.partial(shrink_kernel, pieces, count, len(prior)...  11.1 us
    ppermute x4, starting transfers between devices, ring(): return lax.ppermute(array, 'dp', pairs)  7.92 us
    ppermute x5, starting transfers between devices, over_y(): return lax.ppermute(array, 'dp', [(i, i ^ 1) for i in range(8)])  6.49 us
    ppermute x4, waiting for transfers between devices, ring(): return lax.ppermute(array, 'dp', pairs)  5.66 us
    ppermute x4, starting transfers between devices, over_x(): return lax.ppermute(array, 'groups', SWAP)  5.07 us
    pallas_call x1, Pallas kernels, final_keys(): pl.pallas_call(final_kernel, in_specs=[SMEM, SMEM] + [VMEM] * 4, out_spec...  1.84 us
    ppermute x4, starting transfers between devices, over_cores(): return lax.ppermute(array, 'tensor', SWAP)  1.13 us
  transfers between devices with their start and end apart: 17, of which 4 were waited for; matrix products, arithmetic and copies ran while one was open for 1% of the time, Pallas kernels for 43%

profile of v9, /device:TPU:0, one launch (start us, length us, event | category | flops | bytes accessed | tf_op | source)
XLA Modules:
  0.0 53.5 jit_solution(12280357750298371739)
XLA Ops:
  0.0 1.1 %pad_maximum_fusion = bf16[64,4608]{1,0:T(8,128)(2,1)S(1)} fusion(bf16[64,512]{1,0:T(8,128)(2,1)} %bitcast.8, bf16[64,4096]{1,0:T(8,128)(2,1)} %bitcast.6), kind=kLoop, calls=%fused_computation.1 | loop fusion | flops 1179648 | bytes 1179648 | tf_op jit(solution)/shard_map/concatenate | solution.py:278
  1.1 3.0 %collective-permute-start.2 = (bf16[64,4608]{1,0:T(8,128)(2,1)S(1)}, bf16[64,4608]{1,0:T(8,128)(2,1)S(1)}, u32[]{:S(2)}, u32[]{:S(2)}) collective-permute-start(bf16[64,4608]{1,0:T(8,128)(2,1)S(1)} %pad_maximum_fusion), channel_id=1, source_target_pairs={{0,2},{2,0},{4,6},{6,4},{8,10},{10,8},{12,14},{14,12},{1,3},{3,1},... | collective-permute-start | bytes 1769480 | tf_op jit(solution)/shard_map/ppermute | solution.py:294
  4.2 1.6 %collective-permute-start.1 = (bf16[64,2304]{1,0:T(8,128)(2,1)S(1)}, bf16[64,2304]{1,0:T(8,128)(2,1)S(1)}, u32[]{:S(2)}, u32[]{:S(2)}) collective-permute-start(bf16[64,2304]{1,0:T(8,128)(2,1)S(1)} %pad_maximum_fusion.1), channel_id=1, source_target_pairs={{0,4},{2,6},{4,8},{6,10},{8,12},{10,14},{12,0},{14,2},{1,5},{3,7},... | collective-permute-start | bytes 884744 | tf_op jit(solution)/shard_map/ppermute | solution.py:291
  5.9 2.2 %collective-permute-start = (bf16[64,2304]{1,0:T(8,128)(2,1)S(1)}, bf16[64,2304]{1,0:T(8,128)(2,1)S(1)}, u32[]{:S(2)}, u32[]{:S(2)}) collective-permute-start(bf16[64,2304]{1,0:T(8,128)(2,1)S(1)} %pad_maximum_fusion.1), channel_id=1, source_target_pairs={{0,12},{2,14},{4,0},{6,2},{8,4},{10,6},{12,8},{14,10},{1,13},{3,15... | collective-permute-start | bytes 884744 | tf_op jit(solution)/shard_map/ppermute | solution.py:291
  8.1 0.1 pad_add_fusion.place
  8.2 5.9 %shard_map.73 = (f32[256,512]{1,0:T(8,128)S(1)}, f32[256,512]{1,0:T(8,128)S(1)}, f32[256,512]{1,0:T(8,128)S(1)}) custom-call(s32[3]{0:T(128)S(1)} %pad_add_fusion.place, bf16[768,4096]{1,0:T(8,128)(2,1)} %tokens.8, bf16[4096,1024]{1,0:T(8,128)(2,1)} %weight.3), custom_call_target="tpu_custom_call" | custom-call | flops 1 | bytes 1 | tf_op jit(solution)/shard_map/pallas_call | solution.py:85
  14.1 2.0 %collective-permute-done.1.refs_3_ = bf16[64,2304]{1,0:T(8,128)(2,1)S(1)} collective-permute-done((bf16[64,2304]{1,0:T(8,128)(2,1)S(1)}, bf16[64,2304]{1,0:T(8,128)(2,1)S(1)}, u32[]{:S(2)}, u32[]{:S(2)}) %collective-permute-start.1) | collective-permute-done | bytes 294944 | tf_op jit(solution)/shard_map/ppermute | solution.py:291
  16.1 1.6 %collective-permute-start.3 = (bf16[64,2304]{1,0:T(8,128)(2,1)S(1)}, bf16[64,2304]{1,0:T(8,128)(2,1)S(1)}, u32[]{:S(2)}, u32[]{:S(2)}) collective-permute-start(bf16[64,2304]{1,0:T(8,128)(2,1)S(1)} %collective-permute-done.1.refs_3_), channel_id=1, source_target_pairs={{0,16},{16,0},{1,17},{17,1},{2,18},{18,2},{3,19},{19,3},{4,20},{20... | collective-permute-start | bytes 884744 | tf_op jit(solution)/shard_map/ppermute | solution.py:297
  17.6 0.5 collective-permute-start.5
  18.1 2.2 %collective-permute-done.refs_4_ = bf16[64,2304]{1,0:T(8,128)(2,1)S(1)} collective-permute-done((bf16[64,2304]{1,0:T(8,128)(2,1)S(1)}, bf16[64,2304]{1,0:T(8,128)(2,1)S(1)}, u32[]{:S(2)}, u32[]{:S(2)}) %collective-permute-start) | collective-permute-done | bytes 294944 | tf_op jit(solution)/shard_map/ppermute | solution.py:291
  20.4 1.1 %collective-permute-start.6 = (bf16[64,2304]{1,0:T(8,128)(2,1)S(1)}, bf16[64,2304]{1,0:T(8,128)(2,1)S(1)}, u32[]{:S(2)}, u32[]{:S(2)}) collective-permute-start(bf16[64,2304]{1,0:T(8,128)(2,1)S(1)} %collective-permute-done.1.refs_3_), channel_id=1, source_target_pairs={{0,4},{2,6},{4,8},{6,10},{8,12},{10,14},{12,0},{14,2},{1,5},{3,7},... | collective-permute-start | bytes 884744 | tf_op jit(solution)/shard_map/ppermute | solution.py:291
  21.5 1.5 %collective-permute-start.7 = (bf16[64,2304]{1,0:T(8,128)(2,1)S(1)}, bf16[64,2304]{1,0:T(8,128)(2,1)S(1)}, u32[]{:S(2)}, u32[]{:S(2)}) collective-permute-start(bf16[64,2304]{1,0:T(8,128)(2,1)S(1)} %collective-permute-done.refs_4_), channel_id=1, source_target_pairs={{0,16},{16,0},{1,17},{17,1},{2,18},{18,2},{3,19},{19,3},{4,20},{20... | collective-permute-start | bytes 884744 | tf_op jit(solution)/shard_map/ppermute | solution.py:297
  23.0 0.0 collective-permute-done.2.refs_2_
  23.0 0.5 collective-permute-start.8
  23.5 5.9 %shard_map.74 = f32[768,512]{1,0:T(8,128)S(1)} custom-call(s32[3]{0:T(128)S(1)} %pad_add_fusion.place, bf16[768,4096]{1,0:T(8,128)(2,1)} %tokens.8, bf16[4096,1024]{1,0:T(8,128)(2,1)} %weight.3), custom_call_target="tpu_custom_call" | custom-call | flops 30000001024 | bytes 1 | tf_op jit(solution)/shard_map/pallas_call | solution.py:85
  29.4 0.0 collective-permute-done.3.refs_0_
  29.4 2.9 %collective-permute-start.4 = (bf16[64,2304]{1,0:T(8,128)(2,1)S(1)}, bf16[64,2304]{1,0:T(8,128)(2,1)S(1)}, u32[]{:S(2)}, u32[]{:S(2)}) collective-permute-start(bf16[64,2304]{1,0:T(8,128)(2,1)S(1)} %collective-permute-done.3.refs_0_), channel_id=1, source_target_pairs={{0,4},{2,6},{4,8},{6,10},{8,12},{10,14},{12,0},{14,2},{1,5},{3,7},... | collective-permute-start | bytes 884744 | tf_op jit(solution)/shard_map/ppermute | solution.py:291
  32.3 0.0 collective-permute-done.5.refs_1_
  32.3 1.5 %collective-permute-start.13 = (bf16[64,2304]{1,0:T(8,128)(2,1)S(1)}, bf16[64,2304]{1,0:T(8,128)(2,1)S(1)}, u32[]{:S(2)}, u32[]{:S(2)}) collective-permute-start(bf16[64,2304]{1,0:T(8,128)(2,1)S(1)} %collective-permute-done.5.refs_1_), channel_id=1, source_target_pairs={{0,16},{16,0},{1,17},{17,1},{2,18},{18,2},{3,19},{19,3},{4,20},{20... | collective-permute-start | bytes 884744 | tf_op jit(solution)/shard_map/ppermute | solution.py:297
  33.8 0.0 collective-permute-done.6.refs_2_
  33.8 0.0 collective-permute-done.8.refs_4_
  33.8 0.5 collective-permute-start.15
  34.3 0.5 %collective-permute-start.14 = (bf16[64,2304]{1,0:T(8,128)(2,1)S(1)}, bf16[64,2304]{1,0:T(8,128)(2,1)S(1)}, u32[]{:S(2)}, u32[]{:S(2)}) collective-permute-start(bf16[64,2304]{1,0:T(8,128)(2,1)S(1)} %collective-permute-done.8.refs_4_), channel_id=1, source_target_pairs={{0,16},{16,0},{1,17},{17,1},{2,18},{18,2},{3,19},{19,3},{4,20},{20... | collective-permute-start | bytes 884744 | tf_op jit(solution)/shard_map/ppermute | solution.py:297
  34.9 0.0 copy-done
  34.9 0.0 copy-done.1
  34.9 0.0 copy-done.2
  34.9 3.0 %shard_map.75 = (f32[6,64,128]{2,1,0:T(8,128)S(1)}, bf16[6,64,512]{2,1,0:T(8,128)(2,1)S(1)}) custom-call(s32[3]{0:T(128)S(1)} %pad_add_fusion.place, s32[8]{0:T(128)S(1)} %copy-done.2, s32[48]{0:T(128)S(1)} %bitcast.10, bf16[768,4096]{1,0:T(8,128)(2,1)} %tokens.8, bf16[64,4096]{1,0:T(8,128)(2,1)S(1)} %bitcast.7, bf16[64,512]{1,0:T(8,128)(2,1)S(1)} %bitcast.9, ...), custom_call_target="tpu_custom_call" | custom-call | flops 30000001024 | bytes 1 | tf_op jit(solution)/shard_map/pallas_call | solution.py:211
  37.9 1.5 %collective-permute-done.4.refs_0_ = bf16[64,2304]{1,0:T(8,128)(2,1)S(1)} collective-permute-done((bf16[64,2304]{1,0:T(8,128)(2,1)S(1)}, bf16[64,2304]{1,0:T(8,128)(2,1)S(1)}, u32[]{:S(2)}, u32[]{:S(2)}) %collective-permute-start.4) | collective-permute-done | bytes 294944 | tf_op jit(solution)/shard_map/ppermute | solution.py:291
  39.4 1.9 %collective-permute-start.12 = (bf16[64,2304]{1,0:T(8,128)(2,1)S(1)}, bf16[64,2304]{1,0:T(8,128)(2,1)S(1)}, u32[]{:S(2)}, u32[]{:S(2)}) collective-permute-start(bf16[64,2304]{1,0:T(8,128)(2,1)S(1)} %collective-permute-done.4.refs_0_), channel_id=1, source_target_pairs={{0,2},{2,0},{4,6},{6,4},{8,10},{10,8},{12,14},{14,12},{1,3},{3,1},... | collective-permute-start | bytes 884744 | tf_op jit(solution)/shard_map/ppermute | solution.py:294
  41.3 0.0 collective-permute-done.7.refs_3_
  41.3 3.6 %shard_map.76 = (f32[6,64,128]{2,1,0:T(8,128)S(1)}, bf16[6,64,512]{2,1,0:T(8,128)(2,1)S(1)}) custom-call(s32[3]{0:T(128)S(1)} %pad_add_fusion.place, s32[8]{0:T(128)S(1)} %copy-done.2, s32[48]{0:T(128)S(1)} %bitcast.11, bf16[768,4096]{1,0:T(8,128)(2,1)} %tokens.8, ...), custom_call_target="tpu_custom_call", output_to_operand_aliasing={{1}: (10, {})} | custom-call | flops 1 | bytes 1 | tf_op jit(solution)/shard_map/pallas_call | solution.py:211
  44.9 0.1 collective-permute-start.9
  45.0 0.0 collective-permute-done.13.refs_1_
  45.0 0.5 collective-permute-start.10
  45.5 0.0 collective-permute-done.15.refs_3_
  45.5 0.1 collective-permute-start.11
  45.6 0.0 collective-permute-done.14.refs_2_
  45.6 3.3 %shard_map.77 = (f32[6,64,128]{2,1,0:T(8,128)S(1)}, bf16[6,64,512]{2,1,0:T(8,128)(2,1)S(1)}) custom-call(s32[3]{0:T(128)S(1)} %pad_add_fusion.place, s32[8]{0:T(128)S(1)} %copy-done.2, s32[48]{0:T(128)S(1)} %bitcast.12, bf16[768,4096]{1,0:T(8,128)(2,1)} %tokens.8, ...), custom_call_target="tpu_custom_call", output_to_operand_aliasing={{1}: (9, {})} | custom-call | flops 30000001024 | bytes 1 | tf_op jit(solution)/shard_map/pallas_call | solution.py:211
  48.9 0.0 collective-permute-done.12.refs_0_
  48.9 1.2 %shard_map.78 = (f32[6,64,128]{2,1,0:T(8,128)S(1)}, bf16[6,64,512]{2,1,0:T(8,128)(2,1)S(1)}) custom-call(s32[3]{0:T(128)S(1)} %pad_add_fusion.place, s32[8]{0:T(128)S(1)} %copy-done.2, s32[48]{0:T(128)S(1)} %bitcast.13, bf16[768,4096]{1,0:T(8,128)(2,1)} %tokens.8, ...), custom_call_target="tpu_custom_call", output_to_operand_aliasing={{1}: (6, {})} | custom-call | flops 1 | bytes 1 | tf_op jit(solution)/shard_map/pallas_call | solution.py:211
  50.1 0.0 copy-start.4
  50.1 0.5 collective-permute-start.16
  50.6 0.0 collective-permute-done.9
  50.6 0.0 collective-permute-done.10
  50.6 0.0 collective-permute-done.11
  50.6 0.3 maximum_add_fusion.base
  51.0 0.7 %collective-permute-done.16.far_sums = f32[6,64,128]{2,1,0:T(8,128)S(1)} collective-permute-done((f32[6,64,128]{2,1,0:T(8,128)S(1)}, f32[6,64,128]{2,1,0:T(8,128)S(1)}, u32[]{:S(2)}, u32[]{:S(2)}) %collective-permute-start.16) | collective-permute-done | bytes 196640 | tf_op jit(solution)/shard_map/ppermute | solution.py:300
  51.7 1.8 %shard_map.79 = bf16[768,512]{1,0:T(8,128)(2,1)} custom-call(s32[3]{0:T(128)S(1)} %pad_add_fusion.place, s32[48]{0:T(128)S(1)} %copy-done.4, f32[768,512]{1,0:T(8,128)S(1)} %maximum_add_fusion.base, f32[6,64,128]{2,1,0:T(8,128)S(1)} %get-tuple-element.49.sums, f32[6,64,128]{2,1,0:T(8,128)S(1)} %collective-permute-done.16.far_sums, ...), custom_call_target="tpu_custom_call" | custom-call | flops 1 | bytes 1 | tf_op jit(solution)/shard_map/pallas_call | solution.py:253
  (9 shorter events, 0.1 us)
Async XLA Ops:
  1.1 21.9 %collective-permute-start.2 = (bf16[64,4608]{1,0:T(8,128)(2,1)S(1)}, bf16[64,4608]{1,0:T(8,128)(2,1)S(1)}, u32[]{:S(2)}, u32[]{:S(2)}) collective-permute-start(bf16[64,4608]{1,0:T(8,128)(2,1)S(1)} %pad_maximum_fusion), channel_id=1, source_target_pairs={{0,2},{2,0},{4,6},{6,4},{8,10},{10,8},{12,14},{14,12},{1,3},{3,1},... | collective-permute-start | bytes 1769480 | tf_op jit(solution)/shard_map/ppermute | solution.py:294
  4.2 11.8 %collective-permute-start.1 = (bf16[64,2304]{1,0:T(8,128)(2,1)S(1)}, bf16[64,2304]{1,0:T(8,128)(2,1)S(1)}, u32[]{:S(2)}, u32[]{:S(2)}) collective-permute-start(bf16[64,2304]{1,0:T(8,128)(2,1)S(1)} %pad_maximum_fusion.1), channel_id=1, source_target_pairs={{0,4},{2,6},{4,8},{6,10},{8,12},{10,14},{12,0},{14,2},{1,5},{3,7},... | collective-permute-start | bytes 884744 | tf_op jit(solution)/shard_map/ppermute | solution.py:291
  5.9 14.5 %collective-permute-start = (bf16[64,2304]{1,0:T(8,128)(2,1)S(1)}, bf16[64,2304]{1,0:T(8,128)(2,1)S(1)}, u32[]{:S(2)}, u32[]{:S(2)}) collective-permute-start(bf16[64,2304]{1,0:T(8,128)(2,1)S(1)} %pad_maximum_fusion.1), channel_id=1, source_target_pairs={{0,12},{2,14},{4,0},{6,2},{8,4},{10,6},{12,8},{14,10},{1,13},{3,15... | collective-permute-start | bytes 884744 | tf_op jit(solution)/shard_map/ppermute | solution.py:291
  16.1 18.8 %copy-start = (bf16[1,64,4096]{2,1,0:T(8,128)(2,1)S(1)}, bf16[1,64,4096]{2,1,0:T(8,128)(2,1)}, u32[]{:S(2)}) copy-start(bf16[1,64,4096]{2,1,0:T(8,128)(2,1)} %param.9) | copy-start | bytes 1572868
  16.1 18.8 %copy-start.1 = (bf16[1,64,512]{2,1,0:T(8,128)(2,1)S(1)}, bf16[1,64,512]{2,1,0:T(8,128)(2,1)}, u32[]{:S(2)}) copy-start(bf16[1,64,512]{2,1,0:T(8,128)(2,1)} %param.10) | copy-start | bytes 196612
  16.1 18.8 %copy-start.2 = (s32[8]{0:T(128)S(1)}, s32[8]{0:T(128)}, u32[]{:S(2)}) copy-start(s32[8]{0:T(128)} %pool_index.7) | copy-start | bytes 100
  16.1 18.8 %copy-start.3 = (s32[48,1]{0,1:T(1,128)S(1)}, s32[48,1]{0,1:T(1,128)}, u32[]{:S(2)}) copy-start(s32[48,1]{0,1:T(1,128)} %param.12) | copy-start | bytes 580
  16.1 13.3 %collective-permute-start.3 = (bf16[64,2304]{1,0:T(8,128)(2,1)S(1)}, bf16[64,2304]{1,0:T(8,128)(2,1)S(1)}, u32[]{:S(2)}, u32[]{:S(2)}) collective-permute-start(bf16[64,2304]{1,0:T(8,128)(2,1)S(1)} %collective-permute-done.1.refs_3_), channel_id=1, source_target_pairs={{0,16},{16,0},{1,17},{17,1},{2,18},{18,2},{3,19},{19,3},{4,20},{20... | collective-permute-start | bytes 884744 | tf_op jit(solution)/shard_map/ppermute | solution.py:297
  17.6 14.7 %collective-permute-start.5 = (bf16[64,2304]{1,0:T(8,128)(2,1)S(1)}, bf16[64,2304]{1,0:T(8,128)(2,1)S(1)}, u32[]{:S(2)}, u32[]{:S(2)}) collective-permute-start(bf16[64,2304]{1,0:T(8,128)(2,1)S(1)} %collective-permute-done.1.refs_3_), channel_id=1, source_target_pairs={{0,2},{2,0},{4,6},{6,4},{8,10},{10,8},{12,14},{14,12},{1,3},{3,1},... | collective-permute-start | bytes 884744 | tf_op jit(solution)/shard_map/ppermute | solution.py:294
  20.4 13.5 %collective-permute-start.6 = (bf16[64,2304]{1,0:T(8,128)(2,1)S(1)}, bf16[64,2304]{1,0:T(8,128)(2,1)S(1)}, u32[]{:S(2)}, u32[]{:S(2)}) collective-permute-start(bf16[64,2304]{1,0:T(8,128)(2,1)S(1)} %collective-permute-done.1.refs_3_), channel_id=1, source_target_pairs={{0,4},{2,6},{4,8},{6,10},{8,12},{10,14},{12,0},{14,2},{1,5},{3,7},... | collective-permute-start | bytes 884744 | tf_op jit(solution)/shard_map/ppermute | solution.py:291
  21.5 19.8 %collective-permute-start.7 = (bf16[64,2304]{1,0:T(8,128)(2,1)S(1)}, bf16[64,2304]{1,0:T(8,128)(2,1)S(1)}, u32[]{:S(2)}, u32[]{:S(2)}) collective-permute-start(bf16[64,2304]{1,0:T(8,128)(2,1)S(1)} %collective-permute-done.refs_4_), channel_id=1, source_target_pairs={{0,16},{16,0},{1,17},{17,1},{2,18},{18,2},{3,19},{19,3},{4,20},{20... | collective-permute-start | bytes 884744 | tf_op jit(solution)/shard_map/ppermute | solution.py:297
  23.0 10.8 %collective-permute-start.8 = (bf16[64,2304]{1,0:T(8,128)(2,1)S(1)}, bf16[64,2304]{1,0:T(8,128)(2,1)S(1)}, u32[]{:S(2)}, u32[]{:S(2)}) collective-permute-start(bf16[64,2304]{1,0:T(8,128)(2,1)S(1)} %collective-permute-done.refs_4_), channel_id=1, source_target_pairs={{0,2},{2,0},{4,6},{6,4},{8,10},{10,8},{12,14},{14,12},{1,3},{3,1},... | collective-permute-start | bytes 884744 | tf_op jit(solution)/shard_map/ppermute | solution.py:294
  29.4 9.9 %collective-permute-start.4 = (bf16[64,2304]{1,0:T(8,128)(2,1)S(1)}, bf16[64,2304]{1,0:T(8,128)(2,1)S(1)}, u32[]{:S(2)}, u32[]{:S(2)}) collective-permute-start(bf16[64,2304]{1,0:T(8,128)(2,1)S(1)} %collective-permute-done.3.refs_0_), channel_id=1, source_target_pairs={{0,4},{2,6},{4,8},{6,10},{8,12},{10,14},{12,0},{14,2},{1,5},{3,7},... | collective-permute-start | bytes 884744 | tf_op jit(solution)/shard_map/ppermute | solution.py:291
  32.3 12.6 %collective-permute-start.13 = (bf16[64,2304]{1,0:T(8,128)(2,1)S(1)}, bf16[64,2304]{1,0:T(8,128)(2,1)S(1)}, u32[]{:S(2)}, u32[]{:S(2)}) collective-permute-start(bf16[64,2304]{1,0:T(8,128)(2,1)S(1)} %collective-permute-done.5.refs_1_), channel_id=1, source_target_pairs={{0,16},{16,0},{1,17},{17,1},{2,18},{18,2},{3,19},{19,3},{4,20},{20... | collective-permute-start | bytes 884744 | tf_op jit(solution)/shard_map/ppermute | solution.py:297
  33.8 11.6 %collective-permute-start.15 = (bf16[64,2304]{1,0:T(8,128)(2,1)S(1)}, bf16[64,2304]{1,0:T(8,128)(2,1)S(1)}, u32[]{:S(2)}, u32[]{:S(2)}) collective-permute-start(bf16[64,2304]{1,0:T(8,128)(2,1)S(1)} %collective-permute-done.6.refs_2_), channel_id=1, source_target_pairs={{0,2},{2,0},{4,6},{6,4},{8,10},{10,8},{12,14},{14,12},{1,3},{3,1},... | collective-permute-start | bytes 884744 | tf_op jit(solution)/shard_map/ppermute | solution.py:294
  34.3 11.2 %collective-permute-start.14 = (bf16[64,2304]{1,0:T(8,128)(2,1)S(1)}, bf16[64,2304]{1,0:T(8,128)(2,1)S(1)}, u32[]{:S(2)}, u32[]{:S(2)}) collective-permute-start(bf16[64,2304]{1,0:T(8,128)(2,1)S(1)} %collective-permute-done.8.refs_4_), channel_id=1, source_target_pairs={{0,16},{16,0},{1,17},{17,1},{2,18},{18,2},{3,19},{19,3},{4,20},{20... | collective-permute-start | bytes 884744 | tf_op jit(solution)/shard_map/ppermute | solution.py:297
  39.4 9.5 %collective-permute-start.12 = (bf16[64,2304]{1,0:T(8,128)(2,1)S(1)}, bf16[64,2304]{1,0:T(8,128)(2,1)S(1)}, u32[]{:S(2)}, u32[]{:S(2)}) collective-permute-start(bf16[64,2304]{1,0:T(8,128)(2,1)S(1)} %collective-permute-done.4.refs_0_), channel_id=1, source_target_pairs={{0,2},{2,0},{4,6},{6,4},{8,10},{10,8},{12,14},{14,12},{1,3},{3,1},... | collective-permute-start | bytes 884744 | tf_op jit(solution)/shard_map/ppermute | solution.py:294
  44.9 5.7 %collective-permute-start.9 = (f32[256,512]{1,0:T(8,128)S(1)}, f32[256,512]{1,0:T(8,128)S(1)}, u32[]{:S(2)}, u32[]{:S(2)}) collective-permute-start(f32[256,512]{1,0:T(8,128)S(1)} %get-tuple-element.39), channel_id=1, source_target_pairs={{0,1},{1,0},{2,3},{3,2},{4,5},{5,4},{6,7},{7,6},{8,9},{9,8},{10,11... | collective-permute-start | bytes 1572872 | tf_op jit(solution)/shard_map/ppermute | solution.py:300
  45.0 5.6 %collective-permute-start.10 = (f32[256,512]{1,0:T(8,128)S(1)}, f32[256,512]{1,0:T(8,128)S(1)}, u32[]{:S(2)}, u32[]{:S(2)}) collective-permute-start(f32[256,512]{1,0:T(8,128)S(1)} %get-tuple-element.41), channel_id=1, source_target_pairs={{0,1},{1,0},{2,3},{3,2},{4,5},{5,4},{6,7},{7,6},{8,9},{9,8},{10,11... | collective-permute-start | bytes 1572872 | tf_op jit(solution)/shard_map/ppermute | solution.py:300
  45.5 5.1 %collective-permute-start.11 = (f32[256,512]{1,0:T(8,128)S(1)}, f32[256,512]{1,0:T(8,128)S(1)}, u32[]{:S(2)}, u32[]{:S(2)}) collective-permute-start(f32[256,512]{1,0:T(8,128)S(1)} %get-tuple-element.43), channel_id=1, source_target_pairs={{0,1},{1,0},{2,3},{3,2},{4,5},{5,4},{6,7},{7,6},{8,9},{9,8},{10,11... | collective-permute-start | bytes 1572872 | tf_op jit(solution)/shard_map/ppermute | solution.py:300
  50.1 1.6 %copy-start.4 = (s32[48]{0:T(128)S(1)}, s32[48]{0:T(128)}, u32[]{:S(2)}) copy-start(s32[48]{0:T(128)} %live.1) | copy-start | bytes 580
  50.1 1.6 %collective-permute-start.16 = (f32[6,64,128]{2,1,0:T(8,128)S(1)}, f32[6,64,128]{2,1,0:T(8,128)S(1)}, u32[]{:S(2)}, u32[]{:S(2)}) collective-permute-start(f32[6,64,128]{2,1,0:T(8,128)S(1)} %get-tuple-element.49.sums), channel_id=1, source_target_pairs={{0,1},{1,0},{2,3},{3,2},{4,5},{5,4},{6,7},{7,6},{8,9},{9,8},{10,11... | collective-permute-start | bytes 589832 | tf_op jit(solution)/shard_map/ppermute | solution.py:300

commit v10 on v9

--- a/solution.py
+++ b/solution.py
@@ -308,15 +308,7 @@
     z1_ = after(z1, fars[0])
     x1 = over_x(z1_)
     y1 = over_y(z1_)
-    z3_ = after(z3, z1_)
-    z2a = ring(after(z1_, z3), 1)
-    x3 = over_x(z3_)
-    y3 = over_y(after(z3_, y0))
-    z2b = ring(x1, 1)
-    y2a = over_y(after(z2a, y3))
-    x1y = over_x(y1)
-
-    (mine,) = base_sums(place, after(tokens, z3_, y0), weight, False, 1, HEAVY)
+
     def named(first, entries):
         return [
             (entry, kind, (first + at, 0), (first + at, width), half)
@@ -325,34 +317,45 @@
 
     prior = shrink_sums(
         scalars,
-        after(tokens, mine, x1, y1, z2a, y3),
-        [down, up, y0, z1, z3],
+        after(tokens, z1_, y0),
+        [down, up, y0, z1],
         [
             (0, "a", (0, 0), (1, 0), half),
             (0, "b", (0, width), (1, half), half),
             (1, "a", (2, 0), (2, 2 * width), half),
             (1, "b", (2, width), (2, 2 * width + half), half),
         ]
-        + named(3, [(2, "own"), (6, "own")]),
+        + named(3, [(2, "own")]),
         [],
+        HEAVY,
+    )
+    z3_ = after(z3, prior[0])
+    z2a = ring(after(z1_, z3_), 1)
+    x3 = over_x(z3_)
+    y3 = over_y(after(z3_, y0))
+    z2b = ring(x1, 1)
+    y2a = over_y(after(z2a, y3))
+    x1y = over_x(y1)
+    (mine,) = base_sums(place, after(tokens, z3_, y0), weight, False, 1, HEAVY)
+    prior = shrink_sums(
+        scalars,
+        after(tokens, mine, x1, y1, z2a, y3),
+        [z3, x1, y1, z2a, y3],
+        named(0, [(6, "own"), (2, "far"), (3, "own"), (4, "own"), (7, "own")]),
+        prior,
         HEAVY,
     )
     x3y = over_x(y3)
     y2b = over_y(after(z2b, prior[0]))
     prior = shrink_sums(
-        scalars,
-        after(tokens, z2b),
-        [x1, y1, z2a, x3, y3],
-        named(0, [(2, "far"), (3, "own"), (4, "own"), (6, "far"), (7, "own")]),
-        prior,
-        LIGHT,
+        scalars, tokens, [x3, z2b], named(0, [(6, "far"), (4, "far")]), prior, LIGHT
     )
     base_fars = [over_cores(after(far, prior[0])) for far in fars]
     prior = shrink_sums(
         scalars,
         tokens,
-        [z2b, x1y, x3y, y2a],
-        named(0, [(4, "far"), (3, "far"), (7, "far"), (5, "own")]),
+        [x1y, x3y, y2a],
+        named(0, [(3, "far"), (7, "far"), (5, "own")]),
         prior,
         HEAVY,
     )

time: 53.8 us -> 55.6 us (1.033)
  the two profiles are of different devices: /device:TPU:0 before, /device:TPU:11 now
where the time goes in v10:
time: 55.6 us; the launch traced here: 54.7 us
  Pallas kernels  27.8 us (50%)
  starting transfers between devices  19.3 us (35%)
  waiting for transfers between devices  5.9 us (11%)
  other arithmetic  1.6 us (3%)
    pallas_call x5, Pallas kernels, shrink_sums(): pl.pallas_call(functools.partial(shrink_kernel, pieces, count, len(prior)...  14.1 us
    pallas_call x2, Pallas kernels, base_sums(): pl.pallas_call(functools.partial(base_kernel, base_cuts(width), other), i...  11.8 us
    ppermute x4, starting transfers between devices, over_cores(): return lax.ppermute(array, 'tensor', SWAP)  7.92 us
    ppermute x5, waiting for transfers between devices, over_y(): return lax.ppermute(array, 'dp', [(i, i ^ 1) for i in range(8)])  4.8 us
    ppermute x5, starting transfers between devices, over_y(): return lax.ppermute(array, 'dp', [(i, i ^ 1) for i in range(8)])  4.61 us
    ppermute x4, starting transfers between devices, ring(): return lax.ppermute(array, 'dp', pairs)  4.42 us
    ppermute x4, starting transfers between devices, over_x(): return lax.ppermute(array, 'groups', SWAP)  2.32 us
    pallas_call x1, Pallas kernels, final_keys(): pl.pallas_call(final_kernel, in_specs=[SMEM, SMEM] + [VMEM] * 4, out_spec...  1.84 us
  transfers between devices with their start and end apart: 17, of which 3 were waited for; matrix products, arithmetic and copies ran while one was open for 1% of the time, Pallas kernels for 47%

profile of v10, /device:TPU:11, one launch (start us, length us, event | category | flops | bytes accessed | tf_op | source)
XLA Modules:
  0.0 54.7 jit_solution(8113405881612892713)
XLA Ops:
  0.0 1.1 %pad_maximum_fusion = bf16[64,4608]{1,0:T(8,128)(2,1)S(1)} fusion(bf16[64,512]{1,0:T(8,128)(2,1)} %bitcast.8, bf16[64,4096]{1,0:T(8,128)(2,1)} %bitcast.6), kind=kLoop, calls=%fused_computation.1 | loop fusion | flops 1179648 | bytes 1179648 | tf_op jit(solution)/shard_map/concatenate | solution.py:278
  1.1 1.3 %collective-permute-start.2 = (bf16[64,4608]{1,0:T(8,128)(2,1)S(1)}, bf16[64,4608]{1,0:T(8,128)(2,1)S(1)}, u32[]{:S(2)}, u32[]{:S(2)}) collective-permute-start(bf16[64,4608]{1,0:T(8,128)(2,1)S(1)} %pad_maximum_fusion), channel_id=1, source_target_pairs={{0,2},{2,0},{4,6},{6,4},{8,10},{10,8},{12,14},{14,12},{1,3},{3,1},... | collective-permute-start | bytes 1769480 | tf_op jit(solution)/shard_map/ppermute | solution.py:294
  2.5 1.3 %collective-permute-start.1 = (bf16[64,2304]{1,0:T(8,128)(2,1)S(1)}, bf16[64,2304]{1,0:T(8,128)(2,1)S(1)}, u32[]{:S(2)}, u32[]{:S(2)}) collective-permute-start(bf16[64,2304]{1,0:T(8,128)(2,1)S(1)} %pad_maximum_fusion.1), channel_id=1, source_target_pairs={{0,4},{2,6},{4,8},{6,10},{8,12},{10,14},{12,0},{14,2},{1,5},{3,7},... | collective-permute-start | bytes 884744 | tf_op jit(solution)/shard_map/ppermute | solution.py:291
  3.9 0.2 collective-permute-start
  4.0 0.1 pad_add_fusion.place
  4.1 5.9 %shard_map.73 = (f32[256,512]{1,0:T(8,128)S(1)}, f32[256,512]{1,0:T(8,128)S(1)}, f32[256,512]{1,0:T(8,128)S(1)}) custom-call(s32[3]{0:T(128)S(1)} %pad_add_fusion.place, bf16[768,4096]{1,0:T(8,128)(2,1)} %tokens.10, bf16[4096,1024]{1,0:T(8,128)(2,1)} %weight.3), custom_call_target="tpu_custom_call" | custom-call | flops 1 | bytes 1 | tf_op jit(solution)/shard_map/pallas_call | solution.py:85
  10.0 0.1 collective-permute-done.1.refs_3_
  10.1 0.3 collective-permute-start.4
  10.4 0.2 collective-permute-start.6
  10.6 4.8 %collective-permute-done.2.refs_2_ = bf16[64,4608]{1,0:T(8,128)(2,1)S(1)} collective-permute-done((bf16[64,4608]{1,0:T(8,128)(2,1)S(1)}, bf16[64,4608]{1,0:T(8,128)(2,1)S(1)}, u32[]{:S(2)}, u32[]{:S(2)}) %collective-permute-start.2) | collective-permute-done | bytes 589856 | tf_op jit(solution)/shard_map/ppermute | solution.py:294
  15.4 0.0 copy-done.2
  15.4 0.0 copy-done.3
  15.4 3.6 %shard_map.74 = (f32[6,64,128]{2,1,0:T(8,128)S(1)}, bf16[6,64,512]{2,1,0:T(8,128)(2,1)S(1)}) custom-call(s32[3]{0:T(128)S(1)} %pad_add_fusion.place, s32[8]{0:T(128)S(1)} %copy-done.2, s32[48]{0:T(128)S(1)} %bitcast.10, bf16[768,4096]{1,0:T(8,128)(2,1)} %tokens.10, bf16[64,4096]{1,0:T(8,128)(2,1)S(1)} %bitcast.7, bf16[64,512]{1,0:T(8,128)(2,1)S(1)} %bitcast.9, ...), custom_call_target="tpu_custom_call" | custom-call | flops 30000001024 | bytes 1 | tf_op jit(solution)/shard_map/pallas_call | solution.py:211
  19.0 0.0 collective-permute-done.refs_0_
  19.0 0.1 collective-permute-start.3
  19.1 1.0 %collective-permute-start.7 = (bf16[64,2304]{1,0:T(8,128)(2,1)S(1)}, bf16[64,2304]{1,0:T(8,128)(2,1)S(1)}, u32[]{:S(2)}, u32[]{:S(2)}) collective-permute-start(bf16[64,2304]{1,0:T(8,128)(2,1)S(1)} %collective-permute-done.1.refs_3_), channel_id=1, source_target_pairs={{0,4},{2,6},{4,8},{6,10},{8,12},{10,14},{12,0},{14,2},{1,5},{3,7},... | collective-permute-start | bytes 884744 | tf_op jit(solution)/shard_map/ppermute | solution.py:291
  20.1 1.5 %collective-permute-start.8 = (bf16[64,2304]{1,0:T(8,128)(2,1)S(1)}, bf16[64,2304]{1,0:T(8,128)(2,1)S(1)}, u32[]{:S(2)}, u32[]{:S(2)}) collective-permute-start(bf16[64,2304]{1,0:T(8,128)(2,1)S(1)} %collective-permute-done.refs_0_), channel_id=1, source_target_pairs={{0,2},{2,0},{4,6},{6,4},{8,10},{10,8},{12,14},{14,12},{1,3},{3,1},... | collective-permute-start | bytes 884744 | tf_op jit(solution)/shard_map/ppermute | solution.py:294
  21.6 5.9 %shard_map.75 = f32[768,512]{1,0:T(8,128)S(1)} custom-call(s32[3]{0:T(128)S(1)} %pad_add_fusion.place, bf16[768,4096]{1,0:T(8,128)(2,1)} %tokens.10, bf16[4096,1024]{1,0:T(8,128)(2,1)} %weight.3), custom_call_target="tpu_custom_call" | custom-call | flops 30000001024 | bytes 1 | tf_op jit(solution)/shard_map/pallas_call | solution.py:85
  27.5 0.0 collective-permute-done.4.refs_1_
  27.5 1.9 %collective-permute-start.5 = (bf16[64,2304]{1,0:T(8,128)(2,1)S(1)}, bf16[64,2304]{1,0:T(8,128)(2,1)S(1)}, u32[]{:S(2)}, u32[]{:S(2)}) collective-permute-start(bf16[64,2304]{1,0:T(8,128)(2,1)S(1)} %collective-permute-done.4.refs_1_), channel_id=1, source_target_pairs={{0,4},{2,6},{4,8},{6,10},{8,12},{10,14},{12,0},{14,2},{1,5},{3,7},... | collective-permute-start | bytes 884744 | tf_op jit(solution)/shard_map/ppermute | solution.py:291
  29.4 0.0 collective-permute-done.6.refs_2_
  29.4 0.6 %collective-permute-start.13 = (bf16[64,2304]{1,0:T(8,128)(2,1)S(1)}, bf16[64,2304]{1,0:T(8,128)(2,1)S(1)}, u32[]{:S(2)}, u32[]{:S(2)}) collective-permute-start(bf16[64,2304]{1,0:T(8,128)(2,1)S(1)} %collective-permute-done.6.refs_2_), channel_id=1, source_target_pairs={{0,16},{16,0},{1,17},{17,1},{2,18},{18,2},{3,19},{19,3},{4,20},{20... | collective-permute-start | bytes 884744 | tf_op jit(solution)/shard_map/ppermute | solution.py:297
  30.1 0.0 collective-permute-done.7.refs_3_
  30.1 0.0 collective-permute-done.8.refs_4_
  30.1 0.6 %collective-permute-start.15 = (bf16[64,2304]{1,0:T(8,128)(2,1)S(1)}, bf16[64,2304]{1,0:T(8,128)(2,1)S(1)}, u32[]{:S(2)}, u32[]{:S(2)}) collective-permute-start(bf16[64,2304]{1,0:T(8,128)(2,1)S(1)} %collective-permute-done.7.refs_3_), channel_id=1, source_target_pairs={{0,2},{2,0},{4,6},{6,4},{8,10},{10,8},{12,14},{14,12},{1,3},{3,1},... | collective-permute-start | bytes 884744 | tf_op jit(solution)/shard_map/ppermute | solution.py:294
  30.7 1.4 %collective-permute-start.14 = (bf16[64,2304]{1,0:T(8,128)(2,1)S(1)}, bf16[64,2304]{1,0:T(8,128)(2,1)S(1)}, u32[]{:S(2)}, u32[]{:S(2)}) collective-permute-start(bf16[64,2304]{1,0:T(8,128)(2,1)S(1)} %collective-permute-done.8.refs_4_), channel_id=1, source_target_pairs={{0,16},{16,0},{1,17},{17,1},{2,18},{18,2},{3,19},{19,3},{4,20},{20... | collective-permute-start | bytes 884744 | tf_op jit(solution)/shard_map/ppermute | solution.py:297
  32.0 3.0 %shard_map.76 = (f32[6,64,128]{2,1,0:T(8,128)S(1)}, bf16[6,64,512]{2,1,0:T(8,128)(2,1)S(1)}) custom-call(s32[3]{0:T(128)S(1)} %pad_add_fusion.place, s32[8]{0:T(128)S(1)} %copy-done.2, s32[48]{0:T(128)S(1)} %bitcast.11, bf16[768,4096]{1,0:T(8,128)(2,1)} %tokens.10, ...), custom_call_target="tpu_custom_call", output_to_operand_aliasing={{1}: (10, {})} | custom-call | flops 30000001024 | bytes 1 | tf_op jit(solution)/shard_map/pallas_call | solution.py:211
  35.1 0.0 collective-permute-done.5.refs_1_
  35.1 1.0 %collective-permute-start.12 = (bf16[64,2304]{1,0:T(8,128)(2,1)S(1)}, bf16[64,2304]{1,0:T(8,128)(2,1)S(1)}, u32[]{:S(2)}, u32[]{:S(2)}) collective-permute-start(bf16[64,2304]{1,0:T(8,128)(2,1)S(1)} %collective-permute-done.5.refs_1_), channel_id=1, source_target_pairs={{0,2},{2,0},{4,6},{6,4},{8,10},{10,8},{12,14},{14,12},{1,3},{3,1},... | collective-permute-start | bytes 884744 | tf_op jit(solution)/shard_map/ppermute | solution.py:294
  36.0 0.0 collective-permute-done.3.refs_0_
  36.0 2.4 %shard_map.77 = (f32[6,64,128]{2,1,0:T(8,128)S(1)}, bf16[6,64,512]{2,1,0:T(8,128)(2,1)S(1)}) custom-call(s32[3]{0:T(128)S(1)} %pad_add_fusion.place, s32[8]{0:T(128)S(1)} %copy-done.2, s32[48]{0:T(128)S(1)} %bitcast.12, bf16[768,4096]{1,0:T(8,128)(2,1)} %tokens.10, ...), custom_call_target="tpu_custom_call", output_to_operand_aliasing={{1}: (7, {})} | custom-call | flops 1 | bytes 1 | tf_op jit(solution)/shard_map/pallas_call | solution.py:211
  38.5 7.3 %collective-permute-start.9 = (f32[256,512]{1,0:T(8,128)S(1)}, f32[256,512]{1,0:T(8,128)S(1)}, u32[]{:S(2)}, u32[]{:S(2)}) collective-permute-start(f32[256,512]{1,0:T(8,128)S(1)} %get-tuple-element.43), channel_id=1, source_target_pairs={{0,1},{1,0},{2,3},{3,2},{4,5},{5,4},{6,7},{7,6},{8,9},{9,8},{10,11... | collective-permute-start | bytes 1572872 | tf_op jit(solution)/shard_map/ppermute | solution.py:300
  45.7 0.0 collective-permute-done.13.refs_0_
  45.7 0.1 collective-permute-start.10
  45.8 0.0 collective-permute-done.15.refs_2_
  45.8 0.4 collective-permute-start.11
  46.2 0.0 collective-permute-done.14.refs_1_
  46.2 2.7 %shard_map.78 = (f32[6,64,128]{2,1,0:T(8,128)S(1)}, bf16[6,64,512]{2,1,0:T(8,128)(2,1)S(1)}) custom-call(s32[3]{0:T(128)S(1)} %pad_add_fusion.place, s32[8]{0:T(128)S(1)} %copy-done.2, s32[48]{0:T(128)S(1)} %bitcast.13, bf16[768,4096]{1,0:T(8,128)(2,1)} %tokens.10, ...), custom_call_target="tpu_custom_call", output_to_operand_aliasing={{1}: (8, {})} | custom-call | flops 30000001024 | bytes 1 | tf_op jit(solution)/shard_map/pallas_call | solution.py:211
  48.9 0.0 collective-permute-done.12.refs_0_
  49.0 2.4 %shard_map.79 = (f32[6,64,128]{2,1,0:T(8,128)S(1)}, bf16[6,64,512]{2,1,0:T(8,128)(2,1)S(1)}) custom-call(s32[3]{0:T(128)S(1)} %pad_add_fusion.place, s32[8]{0:T(128)S(1)} %copy-done.2, s32[48]{0:T(128)S(1)} %bitcast.14, bf16[768,4096]{1,0:T(8,128)(2,1)} %tokens.10, ...), custom_call_target="tpu_custom_call", output_to_operand_aliasing={{1}: (6, {})} | custom-call | flops 1 | bytes 1 | tf_op jit(solution)/shard_map/pallas_call | solution.py:211
  51.3 0.0 copy-start.4
  51.4 0.2 collective-permute-start.16
  51.5 0.0 collective-permute-done.9
  51.5 0.0 collective-permute-done.10
  51.5 0.0 collective-permute-done.11
  51.5 0.3 maximum_add_fusion.base
  51.9 1.0 %collective-permute-done.16.far_sums = f32[6,64,128]{2,1,0:T(8,128)S(1)} collective-permute-done((f32[6,64,128]{2,1,0:T(8,128)S(1)}, f32[6,64,128]{2,1,0:T(8,128)S(1)}, u32[]{:S(2)}, u32[]{:S(2)}) %collective-permute-start.16) | collective-permute-done | bytes 196640 | tf_op jit(solution)/shard_map/ppermute | solution.py:300
  52.9 1.8 %shard_map.80 = bf16[768,512]{1,0:T(8,128)(2,1)} custom-call(s32[3]{0:T(128)S(1)} %pad_add_fusion.place, s32[48]{0:T(128)S(1)} %copy-done.4, f32[768,512]{1,0:T(8,128)S(1)} %maximum_add_fusion.base, f32[6,64,128]{2,1,0:T(8,128)S(1)} %get-tuple-element.53.sums, f32[6,64,128]{2,1,0:T(8,128)S(1)} %collective-permute-done.16.far_sums, ...), custom_call_target="tpu_custom_call" | custom-call | flops 1 | bytes 1 | tf_op jit(solution)/shard_map/pallas_call | solution.py:253
  (10 shorter events, 0.1 us)
Async XLA Ops:
  1.1 14.3 %collective-permute-start.2 = (bf16[64,4608]{1,0:T(8,128)(2,1)S(1)}, bf16[64,4608]{1,0:T(8,128)(2,1)S(1)}, u32[]{:S(2)}, u32[]{:S(2)}) collective-permute-start(bf16[64,4608]{1,0:T(8,128)(2,1)S(1)} %pad_maximum_fusion), channel_id=1, source_target_pairs={{0,2},{2,0},{4,6},{6,4},{8,10},{10,8},{12,14},{14,12},{1,3},{3,1},... | collective-permute-start | bytes 1769480 | tf_op jit(solution)/shard_map/ppermute | solution.py:294
  2.5 7.6 %collective-permute-start.1 = (bf16[64,2304]{1,0:T(8,128)(2,1)S(1)}, bf16[64,2304]{1,0:T(8,128)(2,1)S(1)}, u32[]{:S(2)}, u32[]{:S(2)}) collective-permute-start(bf16[64,2304]{1,0:T(8,128)(2,1)S(1)} %pad_maximum_fusion.1), channel_id=1, source_target_pairs={{0,4},{2,6},{4,8},{6,10},{8,12},{10,14},{12,0},{14,2},{1,5},{3,7},... | collective-permute-start | bytes 884744 | tf_op jit(solution)/shard_map/ppermute | solution.py:291
  3.9 15.2 %collective-permute-start = (bf16[64,2304]{1,0:T(8,128)(2,1)S(1)}, bf16[64,2304]{1,0:T(8,128)(2,1)S(1)}, u32[]{:S(2)}, u32[]{:S(2)}) collective-permute-start(bf16[64,2304]{1,0:T(8,128)(2,1)S(1)} %pad_maximum_fusion.1), channel_id=1, source_target_pairs={{0,12},{2,14},{4,0},{6,2},{8,4},{10,6},{12,8},{14,10},{1,13},{3,15... | collective-permute-start | bytes 884744 | tf_op jit(solution)/shard_map/ppermute | solution.py:291
  4.1 11.3 %copy-start = (bf16[1,64,4096]{2,1,0:T(8,128)(2,1)S(1)}, bf16[1,64,4096]{2,1,0:T(8,128)(2,1)}, u32[]{:S(2)}) copy-start(bf16[1,64,4096]{2,1,0:T(8,128)(2,1)} %param.9) | copy-start | bytes 1572868
  4.1 11.3 %copy-start.1 = (bf16[1,64,512]{2,1,0:T(8,128)(2,1)S(1)}, bf16[1,64,512]{2,1,0:T(8,128)(2,1)}, u32[]{:S(2)}) copy-start(bf16[1,64,512]{2,1,0:T(8,128)(2,1)} %param.10) | copy-start | bytes 196612
  4.1 11.3 %copy-start.2 = (s32[8]{0:T(128)S(1)}, s32[8]{0:T(128)}, u32[]{:S(2)}) copy-start(s32[8]{0:T(128)} %pool_index.9) | copy-start | bytes 100
  4.1 11.3 %copy-start.3 = (s32[48,1]{0,1:T(1,128)S(1)}, s32[48,1]{0,1:T(1,128)}, u32[]{:S(2)}) copy-start(s32[48,1]{0,1:T(1,128)} %param.12) | copy-start | bytes 580
  10.1 17.4 %collective-permute-start.4 = (bf16[64,2304]{1,0:T(8,128)(2,1)S(1)}, bf16[64,2304]{1,0:T(8,128)(2,1)S(1)}, u32[]{:S(2)}, u32[]{:S(2)}) collective-permute-start(bf16[64,2304]{1,0:T(8,128)(2,1)S(1)} %collective-permute-done.1.refs_3_), channel_id=1, source_target_pairs={{0,16},{16,0},{1,17},{17,1},{2,18},{18,2},{3,19},{19,3},{4,20},{20... | collective-permute-start | bytes 884744 | tf_op jit(solution)/shard_map/ppermute | solution.py:297
  10.4 19.1 %collective-permute-start.6 = (bf16[64,2304]{1,0:T(8,128)(2,1)S(1)}, bf16[64,2304]{1,0:T(8,128)(2,1)S(1)}, u32[]{:S(2)}, u32[]{:S(2)}) collective-permute-start(bf16[64,2304]{1,0:T(8,128)(2,1)S(1)} %collective-permute-done.1.refs_3_), channel_id=1, source_target_pairs={{0,2},{2,0},{4,6},{6,4},{8,10},{10,8},{12,14},{14,12},{1,3},{3,1},... | collective-permute-start | bytes 884744 | tf_op jit(solution)/shard_map/ppermute | solution.py:294
  19.0 17.0 %collective-permute-start.3 = (bf16[64,2304]{1,0:T(8,128)(2,1)S(1)}, bf16[64,2304]{1,0:T(8,128)(2,1)S(1)}, u32[]{:S(2)}, u32[]{:S(2)}) collective-permute-start(bf16[64,2304]{1,0:T(8,128)(2,1)S(1)} %collective-permute-done.refs_0_), channel_id=1, source_target_pairs={{0,16},{16,0},{1,17},{17,1},{2,18},{18,2},{3,19},{19,3},{4,20},{20... | collective-permute-start | bytes 884744 | tf_op jit(solution)/shard_map/ppermute | solution.py:297
  19.1 11.0 %collective-permute-start.7 = (bf16[64,2304]{1,0:T(8,128)(2,1)S(1)}, bf16[64,2304]{1,0:T(8,128)(2,1)S(1)}, u32[]{:S(2)}, u32[]{:S(2)}) collective-permute-start(bf16[64,2304]{1,0:T(8,128)(2,1)S(1)} %collective-permute-done.1.refs_3_), channel_id=1, source_target_pairs={{0,4},{2,6},{4,8},{6,10},{8,12},{10,14},{12,0},{14,2},{1,5},{3,7},... | collective-permute-start | bytes 884744 | tf_op jit(solution)/shard_map/ppermute | solution.py:291
  20.1 10.0 %collective-permute-start.8 = (bf16[64,2304]{1,0:T(8,128)(2,1)S(1)}, bf16[64,2304]{1,0:T(8,128)(2,1)S(1)}, u32[]{:S(2)}, u32[]{:S(2)}) collective-permute-start(bf16[64,2304]{1,0:T(8,128)(2,1)S(1)} %collective-permute-done.refs_0_), channel_id=1, source_target_pairs={{0,2},{2,0},{4,6},{6,4},{8,10},{10,8},{12,14},{14,12},{1,3},{3,1},... | collective-permute-start | bytes 884744 | tf_op jit(solution)/shard_map/ppermute | solution.py:294
  27.5 7.6 %collective-permute-start.5 = (bf16[64,2304]{1,0:T(8,128)(2,1)S(1)}, bf16[64,2304]{1,0:T(8,128)(2,1)S(1)}, u32[]{:S(2)}, u32[]{:S(2)}) collective-permute-start(bf16[64,2304]{1,0:T(8,128)(2,1)S(1)} %collective-permute-done.4.refs_1_), channel_id=1, source_target_pairs={{0,4},{2,6},{4,8},{6,10},{8,12},{10,14},{12,0},{14,2},{1,5},{3,7},... | collective-permute-start | bytes 884744 | tf_op jit(solution)/shard_map/ppermute | solution.py:291
  29.4 16.3 %collective-permute-start.13 = (bf16[64,2304]{1,0:T(8,128)(2,1)S(1)}, bf16[64,2304]{1,0:T(8,128)(2,1)S(1)}, u32[]{:S(2)}, u32[]{:S(2)}) collective-permute-start(bf16[64,2304]{1,0:T(8,128)(2,1)S(1)} %collective-permute-done.6.refs_2_), channel_id=1, source_target_pairs={{0,16},{16,0},{1,17},{17,1},{2,18},{18,2},{3,19},{19,3},{4,20},{20... | collective-permute-start | bytes 884744 | tf_op jit(solution)/shard_map/ppermute | solution.py:297
  30.1 15.7 %collective-permute-start.15 = (bf16[64,2304]{1,0:T(8,128)(2,1)S(1)}, bf16[64,2304]{1,0:T(8,128)(2,1)S(1)}, u32[]{:S(2)}, u32[]{:S(2)}) collective-permute-start(bf16[64,2304]{1,0:T(8,128)(2,1)S(1)} %collective-permute-done.7.refs_3_), channel_id=1, source_target_pairs={{0,2},{2,0},{4,6},{6,4},{8,10},{10,8},{12,14},{14,12},{1,3},{3,1},... | collective-permute-start | bytes 884744 | tf_op jit(solution)/shard_map/ppermute | solution.py:294
  30.7 15.6 %collective-permute-start.14 = (bf16[64,2304]{1,0:T(8,128)(2,1)S(1)}, bf16[64,2304]{1,0:T(8,128)(2,1)S(1)}, u32[]{:S(2)}, u32[]{:S(2)}) collective-permute-start(bf16[64,2304]{1,0:T(8,128)(2,1)S(1)} %collective-permute-done.8.refs_4_), channel_id=1, source_target_pairs={{0,16},{16,0},{1,17},{17,1},{2,18},{18,2},{3,19},{19,3},{4,20},{20... | collective-permute-start | bytes 884744 | tf_op jit(solution)/shard_map/ppermute | solution.py:297
  35.1 13.9 %collective-permute-start.12 = (bf16[64,2304]{1,0:T(8,128)(2,1)S(1)}, bf16[64,2304]{1,0:T(8,128)(2,1)S(1)}, u32[]{:S(2)}, u32[]{:S(2)}) collective-permute-start(bf16[64,2304]{1,0:T(8,128)(2,1)S(1)} %collective-permute-done.5.refs_1_), channel_id=1, source_target_pairs={{0,2},{2,0},{4,6},{6,4},{8,10},{10,8},{12,14},{14,12},{1,3},{3,1},... | collective-permute-start | bytes 884744 | tf_op jit(solution)/shard_map/ppermute | solution.py:294
  38.5 13.1 %collective-permute-start.9 = (f32[256,512]{1,0:T(8,128)S(1)}, f32[256,512]{1,0:T(8,128)S(1)}, u32[]{:S(2)}, u32[]{:S(2)}) collective-permute-start(f32[256,512]{1,0:T(8,128)S(1)} %get-tuple-element.43), channel_id=1, source_target_pairs={{0,1},{1,0},{2,3},{3,2},{4,5},{5,4},{6,7},{7,6},{8,9},{9,8},{10,11... | collective-permute-start | bytes 1572872 | tf_op jit(solution)/shard_map/ppermute | solution.py:300
  45.7 5.8 %collective-permute-start.10 = (f32[256,512]{1,0:T(8,128)S(1)}, f32[256,512]{1,0:T(8,128)S(1)}, u32[]{:S(2)}, u32[]{:S(2)}) collective-permute-start(f32[256,512]{1,0:T(8,128)S(1)} %get-tuple-element.45), channel_id=1, source_target_pairs={{0,1},{1,0},{2,3},{3,2},{4,5},{5,4},{6,7},{7,6},{8,9},{9,8},{10,11... | collective-permute-start | bytes 1572872 | tf_op jit(solution)/shard_map/ppermute | solution.py:300
  45.8 5.7 %collective-permute-start.11 = (f32[256,512]{1,0:T(8,128)S(1)}, f32[256,512]{1,0:T(8,128)S(1)}, u32[]{:S(2)}, u32[]{:S(2)}) collective-permute-start(f32[256,512]{1,0:T(8,128)S(1)} %get-tuple-element.47), channel_id=1, source_target_pairs={{0,1},{1,0},{2,3},{3,2},{4,5},{5,4},{6,7},{7,6},{8,9},{9,8},{10,11... | collective-permute-start | bytes 1572872 | tf_op jit(solution)/shard_map/ppermute | solution.py:300
  51.3 1.5 %copy-start.4 = (s32[48]{0:T(128)S(1)}, s32[48]{0:T(128)}, u32[]{:S(2)}) copy-start(s32[48]{0:T(128)} %live.1) | copy-start | bytes 580
  51.4 1.5 %collective-permute-start.16 = (f32[6,64,128]{2,1,0:T(8,128)S(1)}, f32[6,64,128]{2,1,0:T(8,128)S(1)}, u32[]{:S(2)}, u32[]{:S(2)}) collective-permute-start(f32[6,64,128]{2,1,0:T(8,128)S(1)} %get-tuple-element.53.sums), channel_id=1, source_target_pairs={{0,1},{1,0},{2,3},{3,2},{4,5},{5,4},{6,7},{7,6},{8,9},{9,8},{10,11... | collective-permute-start | bytes 589832 | tf_op jit(solution)/shard_map/ppermute | solution.py:300

commit v11 on v9

--- a/solution.py
+++ b/solution.py
@@ -9,7 +9,7 @@
 
 ADAPTER_RANK = 64
 BLK = 128
-FAR_PARTS = 3
+FAR_PARTS = 1
 SWAP = [(0, 1), (1, 0)]
 NT = (((1,), (1,)), ((), ()))
 TN = (((0,), (0,)), ((), ()))

time: 53.8 us -> 52.7 us (0.980)
  starting transfers between devices: 20.6 us -> 19.5 us
    ppermute x4 -> x2, starting transfers between devices: 1.13 us -> 0.62 us  [over_cores(): return lax.ppermute(array, 'tensor', SWAP)]
  transfers between devices with their start and end apart: 17 -> 15, of which waited for: 4 -> 4; matrix products, arithmetic and copies ran while one was open for 1% -> 1% of each run, Pallas kernels for 43% -> 44%
where the time goes in v11:
time: 52.7 us; the launch traced here: 52 us
  Pallas kernels  24.8 us (47%)
  starting transfers between devices  19.5 us (37%)
  waiting for transfers between devices  5.91 us (11%)
  other arithmetic  1.6 us (3%)
    pallas_call x2, Pallas kernels, base_sums(): pl.pallas_call(functools.partial(base_kernel, base_cuts(width), other), i...  11.8 us
    pallas_call x4, Pallas kernels, shrink_sums(): pl.pallas_call(functools.partial(shrink_kernel, pieces, count, len(prior)...  11.1 us
    ppermute x4, starting transfers between devices, ring(): return lax.ppermute(array, 'dp', pairs)  7.84 us
    ppermute x5, starting transfers between devices, over_y(): return lax.ppermute(array, 'dp', [(i, i ^ 1) for i in range(8)])  6.07 us
    ppermute x4, waiting for transfers between devices, ring(): return lax.ppermute(array, 'dp', pairs)  5.17 us
    ppermute x4, starting transfers between devices, over_x(): return lax.ppermute(array, 'groups', SWAP)  5.01 us
    pallas_call x1, Pallas kernels, final_keys(): pl.pallas_call(final_kernel, in_specs=[SMEM, SMEM] + [VMEM] * 4, out_spec...  1.84 us
    concatenate x1, other arithmetic, per_device_planes(): own = jnp.concatenate([down, up], axis=1)  1.12 us
  transfers between devices with their start and end apart: 15, of which 4 were waited for; matrix products, arithmetic and copies ran while one was open for 1% of the time, Pallas kernels for 44%

profile of v11, /device:TPU:0, one launch (start us, length us, event | category | flops | bytes accessed | tf_op | source)
XLA Modules:
  0.0 52.0 jit_solution(16169995560554319279)
XLA Ops:
  0.0 1.1 %pad_maximum_fusion = bf16[64,4608]{1,0:T(8,128)(2,1)S(1)} fusion(bf16[64,512]{1,0:T(8,128)(2,1)} %bitcast.8, bf16[64,4096]{1,0:T(8,128)(2,1)} %bitcast.6), kind=kLoop, calls=%fused_computation | loop fusion | flops 1179648 | bytes 1179648 | tf_op jit(solution)/shard_map/concatenate | solution.py:278
  1.1 3.0 %collective-permute-start.2 = (bf16[64,4608]{1,0:T(8,128)(2,1)S(1)}, bf16[64,4608]{1,0:T(8,128)(2,1)S(1)}, u32[]{:S(2)}, u32[]{:S(2)}) collective-permute-start(bf16[64,4608]{1,0:T(8,128)(2,1)S(1)} %pad_maximum_fusion), channel_id=1, source_target_pairs={{0,2},{2,0},{4,6},{6,4},{8,10},{10,8},{12,14},{14,12},{1,3},{3,1},... | collective-permute-start | bytes 1769480 | tf_op jit(solution)/shard_map/ppermute | solution.py:294
  4.2 1.6 %collective-permute-start.1 = (bf16[64,2304]{1,0:T(8,128)(2,1)S(1)}, bf16[64,2304]{1,0:T(8,128)(2,1)S(1)}, u32[]{:S(2)}, u32[]{:S(2)}) collective-permute-start(bf16[64,2304]{1,0:T(8,128)(2,1)S(1)} %pad_maximum_fusion.1), channel_id=1, source_target_pairs={{0,4},{2,6},{4,8},{6,10},{8,12},{10,14},{12,0},{14,2},{1,5},{3,7},... | collective-permute-start | bytes 884744 | tf_op jit(solution)/shard_map/ppermute | solution.py:291
  5.9 2.2 %collective-permute-start = (bf16[64,2304]{1,0:T(8,128)(2,1)S(1)}, bf16[64,2304]{1,0:T(8,128)(2,1)S(1)}, u32[]{:S(2)}, u32[]{:S(2)}) collective-permute-start(bf16[64,2304]{1,0:T(8,128)(2,1)S(1)} %pad_maximum_fusion.1), channel_id=1, source_target_pairs={{0,12},{2,14},{4,0},{6,2},{8,4},{10,6},{12,8},{14,10},{1,13},{3,15... | collective-permute-start | bytes 884744 | tf_op jit(solution)/shard_map/ppermute | solution.py:291
  8.1 0.1 pad_add_fusion.place
  8.2 5.9 %shard_map.73 = f32[768,512]{1,0:T(8,128)S(1)} custom-call(s32[3]{0:T(128)S(1)} %pad_add_fusion.place, bf16[768,4096]{1,0:T(8,128)(2,1)} %tokens.8, bf16[4096,1024]{1,0:T(8,128)(2,1)} %weight.3), custom_call_target="tpu_custom_call" | custom-call | flops 1 | bytes 1 | tf_op jit(solution)/shard_map/pallas_call | solution.py:85
  14.1 0.0 copy-start
  14.1 0.0 copy-start.1
  14.1 0.0 copy-start.2
  14.1 0.0 copy-start.3
  14.1 1.9 %collective-permute-done.1.refs_3_ = bf16[64,2304]{1,0:T(8,128)(2,1)S(1)} collective-permute-done((bf16[64,2304]{1,0:T(8,128)(2,1)S(1)}, bf16[64,2304]{1,0:T(8,128)(2,1)S(1)}, u32[]{:S(2)}, u32[]{:S(2)}) %collective-permute-start.1) | collective-permute-done | bytes 294944 | tf_op jit(solution)/shard_map/ppermute | solution.py:291
  16.1 1.5 %collective-permute-start.3 = (bf16[64,2304]{1,0:T(8,128)(2,1)S(1)}, bf16[64,2304]{1,0:T(8,128)(2,1)S(1)}, u32[]{:S(2)}, u32[]{:S(2)}) collective-permute-start(bf16[64,2304]{1,0:T(8,128)(2,1)S(1)} %collective-permute-done.1.refs_3_), channel_id=1, source_target_pairs={{0,16},{16,0},{1,17},{17,1},{2,18},{18,2},{3,19},{19,3},{4,20},{20... | collective-permute-start | bytes 884744 | tf_op jit(solution)/shard_map/ppermute | solution.py:297
  17.6 0.5 collective-permute-start.5
  18.1 2.3 %collective-permute-done.refs_4_ = bf16[64,2304]{1,0:T(8,128)(2,1)S(1)} collective-permute-done((bf16[64,2304]{1,0:T(8,128)(2,1)S(1)}, bf16[64,2304]{1,0:T(8,128)(2,1)S(1)}, u32[]{:S(2)}, u32[]{:S(2)}) %collective-permute-start) | collective-permute-done | bytes 294944 | tf_op jit(solution)/shard_map/ppermute | solution.py:291
  20.4 1.1 %collective-permute-start.6 = (bf16[64,2304]{1,0:T(8,128)(2,1)S(1)}, bf16[64,2304]{1,0:T(8,128)(2,1)S(1)}, u32[]{:S(2)}, u32[]{:S(2)}) collective-permute-start(bf16[64,2304]{1,0:T(8,128)(2,1)S(1)} %collective-permute-done.1.refs_3_), channel_id=1, source_target_pairs={{0,4},{2,6},{4,8},{6,10},{8,12},{10,14},{12,0},{14,2},{1,5},{3,7},... | collective-permute-start | bytes 884744 | tf_op jit(solution)/shard_map/ppermute | solution.py:291
  21.5 1.5 %collective-permute-start.7 = (bf16[64,2304]{1,0:T(8,128)(2,1)S(1)}, bf16[64,2304]{1,0:T(8,128)(2,1)S(1)}, u32[]{:S(2)}, u32[]{:S(2)}) collective-permute-start(bf16[64,2304]{1,0:T(8,128)(2,1)S(1)} %collective-permute-done.refs_4_), channel_id=1, source_target_pairs={{0,16},{16,0},{1,17},{17,1},{2,18},{18,2},{3,19},{19,3},{4,20},{20... | collective-permute-start | bytes 884744 | tf_op jit(solution)/shard_map/ppermute | solution.py:297
  23.0 0.0 collective-permute-done.2.refs_2_
  23.0 0.5 collective-permute-start.8
  23.5 5.9 %shard_map.74 = f32[768,512]{1,0:T(8,128)S(1)} custom-call(s32[3]{0:T(128)S(1)} %pad_add_fusion.place, bf16[768,4096]{1,0:T(8,128)(2,1)} %tokens.8, bf16[4096,1024]{1,0:T(8,128)(2,1)} %weight.3), custom_call_target="tpu_custom_call" | custom-call | flops 30000001024 | bytes 1 | tf_op jit(solution)/shard_map/pallas_call | solution.py:85
  29.4 0.0 collective-permute-done.3.refs_0_
  29.4 2.8 %collective-permute-start.4 = (bf16[64,2304]{1,0:T(8,128)(2,1)S(1)}, bf16[64,2304]{1,0:T(8,128)(2,1)S(1)}, u32[]{:S(2)}, u32[]{:S(2)}) collective-permute-start(bf16[64,2304]{1,0:T(8,128)(2,1)S(1)} %collective-permute-done.3.refs_0_), channel_id=1, source_target_pairs={{0,4},{2,6},{4,8},{6,10},{8,12},{10,14},{12,0},{14,2},{1,5},{3,7},... | collective-permute-start | bytes 884744 | tf_op jit(solution)/shard_map/ppermute | solution.py:291
  32.3 0.0 collective-permute-done.5.refs_1_
  32.3 1.5 %collective-permute-start.11 = (bf16[64,2304]{1,0:T(8,128)(2,1)S(1)}, bf16[64,2304]{1,0:T(8,128)(2,1)S(1)}, u32[]{:S(2)}, u32[]{:S(2)}) collective-permute-start(bf16[64,2304]{1,0:T(8,128)(2,1)S(1)} %collective-permute-done.5.refs_1_), channel_id=1, source_target_pairs={{0,16},{16,0},{1,17},{17,1},{2,18},{18,2},{3,19},{19,3},{4,20},{20... | collective-permute-start | bytes 884744 | tf_op jit(solution)/shard_map/ppermute | solution.py:297
  33.8 0.0 collective-permute-done.6.refs_2_
  33.8 0.0 collective-permute-done.8.refs_4_
  33.8 0.5 collective-permute-start.13
  34.3 0.5 %collective-permute-start.12 = (bf16[64,2304]{1,0:T(8,128)(2,1)S(1)}, bf16[64,2304]{1,0:T(8,128)(2,1)S(1)}, u32[]{:S(2)}, u32[]{:S(2)}) collective-permute-start(bf16[64,2304]{1,0:T(8,128)(2,1)S(1)} %collective-permute-done.8.refs_4_), channel_id=1, source_target_pairs={{0,16},{16,0},{1,17},{17,1},{2,18},{18,2},{3,19},{19,3},{4,20},{20... | collective-permute-start | bytes 884744 | tf_op jit(solution)/shard_map/ppermute | solution.py:297
  34.8 0.0 copy-done
  34.8 0.0 copy-done.1
  34.8 0.0 copy-done.3
  34.8 3.6 %shard_map.75 = (f32[6,64,128]{2,1,0:T(8,128)S(1)}, bf16[6,64,512]{2,1,0:T(8,128)(2,1)S(1)}) custom-call(s32[3]{0:T(128)S(1)} %pad_add_fusion.place, s32[8]{0:T(128)S(1)} %copy-done.2, s32[48]{0:T(128)S(1)} %bitcast.10, bf16[768,4096]{1,0:T(8,128)(2,1)} %tokens.8, bf16[64,4096]{1,0:T(8,128)(2,1)S(1)} %bitcast.7, bf16[64,512]{1,0:T(8,128)(2,1)S(1)} %bitcast.9, ...), custom_call_target="tpu_custom_call" | custom-call | flops 30000001024 | bytes 1 | tf_op jit(solution)/shard_map/pallas_call | solution.py:211
  38.4 0.9 %collective-permute-done.4.refs_0_ = bf16[64,2304]{1,0:T(8,128)(2,1)S(1)} collective-permute-done((bf16[64,2304]{1,0:T(8,128)(2,1)S(1)}, bf16[64,2304]{1,0:T(8,128)(2,1)S(1)}, u32[]{:S(2)}, u32[]{:S(2)}) %collective-permute-start.4) | collective-permute-done | bytes 294944 | tf_op jit(solution)/shard_map/ppermute | solution.py:291
  39.4 1.5 %collective-permute-start.10 = (bf16[64,2304]{1,0:T(8,128)(2,1)S(1)}, bf16[64,2304]{1,0:T(8,128)(2,1)S(1)}, u32[]{:S(2)}, u32[]{:S(2)}) collective-permute-start(bf16[64,2304]{1,0:T(8,128)(2,1)S(1)} %collective-permute-done.4.refs_0_), channel_id=1, source_target_pairs={{0,2},{2,0},{4,6},{6,4},{8,10},{10,8},{12,14},{14,12},{1,3},{3,1},... | collective-permute-start | bytes 884744 | tf_op jit(solution)/shard_map/ppermute | solution.py:294
  40.9 0.0 collective-permute-done.7.refs_3_
  40.9 3.6 %shard_map.76 = (f32[6,64,128]{2,1,0:T(8,128)S(1)}, bf16[6,64,512]{2,1,0:T(8,128)(2,1)S(1)}) custom-call(s32[3]{0:T(128)S(1)} %pad_add_fusion.place, s32[8]{0:T(128)S(1)} %copy-done.2, s32[48]{0:T(128)S(1)} %bitcast.11, bf16[768,4096]{1,0:T(8,128)(2,1)} %tokens.8, ...), custom_call_target="tpu_custom_call", output_to_operand_aliasing={{1}: (10, {})} | custom-call | flops 1 | bytes 1 | tf_op jit(solution)/shard_map/pallas_call | solution.py:211
  44.5 0.1 collective-permute-start.9
  44.6 0.0 collective-permute-done.11.refs_1_
  44.6 0.0 collective-permute-done.13.refs_3_
  44.6 0.0 collective-permute-done.12.refs_2_
  44.6 2.7 %shard_map.77 = (f32[6,64,128]{2,1,0:T(8,128)S(1)}, bf16[6,64,512]{2,1,0:T(8,128)(2,1)S(1)}) custom-call(s32[3]{0:T(128)S(1)} %pad_add_fusion.place, s32[8]{0:T(128)S(1)} %copy-done.2, s32[48]{0:T(128)S(1)} %bitcast.12, bf16[768,4096]{1,0:T(8,128)(2,1)} %tokens.8, ...), custom_call_target="tpu_custom_call", output_to_operand_aliasing={{1}: (9, {})} | custom-call | flops 30000001024 | bytes 1 | tf_op jit(solution)/shard_map/pallas_call | solution.py:211
  47.3 0.0 collective-permute-done.10.refs_0_
  47.3 1.2 %shard_map.78 = (f32[6,64,128]{2,1,0:T(8,128)S(1)}, bf16[6,64,512]{2,1,0:T(8,128)(2,1)S(1)}) custom-call(s32[3]{0:T(128)S(1)} %pad_add_fusion.place, s32[8]{0:T(128)S(1)} %copy-done.2, s32[48]{0:T(128)S(1)} %bitcast.13, bf16[768,4096]{1,0:T(8,128)(2,1)} %tokens.8, ...), custom_call_target="tpu_custom_call", output_to_operand_aliasing={{1}: (6, {})} | custom-call | flops 1 | bytes 1 | tf_op jit(solution)/shard_map/pallas_call | solution.py:211
  48.6 0.0 copy-start.4
  48.6 0.5 %collective-permute-start.14 = (f32[6,64,128]{2,1,0:T(8,128)S(1)}, f32[6,64,128]{2,1,0:T(8,128)S(1)}, u32[]{:S(2)}, u32[]{:S(2)}) collective-permute-start(f32[6,64,128]{2,1,0:T(8,128)S(1)} %get-tuple-element.39.sums), channel_id=1, source_target_pairs={{0,1},{1,0},{2,3},{3,2},{4,5},{5,4},{6,7},{7,6},{8,9},{9,8},{10,11... | collective-permute-start | bytes 589832 | tf_op jit(solution)/shard_map/ppermute | solution.py:300
  49.1 0.0 collective-permute-done.9
  49.1 0.3 add.3.base
  49.5 0.7 %collective-permute-done.14.far_sums = f32[6,64,128]{2,1,0:T(8,128)S(1)} collective-permute-done((f32[6,64,128]{2,1,0:T(8,128)S(1)}, f32[6,64,128]{2,1,0:T(8,128)S(1)}, u32[]{:S(2)}, u32[]{:S(2)}) %collective-permute-start.14) | collective-permute-done | bytes 196640 | tf_op jit(solution)/shard_map/ppermute | solution.py:300
  50.2 1.8 %shard_map.79 = bf16[768,512]{1,0:T(8,128)(2,1)} custom-call(s32[3]{0:T(128)S(1)} %pad_add_fusion.place, s32[48]{0:T(128)S(1)} %copy-done.4, f32[768,512]{1,0:T(8,128)S(1)} %add.3.base, f32[6,64,128]{2,1,0:T(8,128)S(1)} %get-tuple-element.39.sums, f32[6,64,128]{2,1,0:T(8,128)S(1)} %collective-permute-done.14.far_sums, ...), custom_call_target="tpu_custom_call" | custom-call | flops 1 | bytes 1 | tf_op jit(solution)/shard_map/pallas_call | solution.py:253
  (5 shorter events, 0.1 us)
Async XLA Ops:
  1.1 21.9 %collective-permute-start.2 = (bf16[64,4608]{1,0:T(8,128)(2,1)S(1)}, bf16[64,4608]{1,0:T(8,128)(2,1)S(1)}, u32[]{:S(2)}, u32[]{:S(2)}) collective-permute-start(bf16[64,4608]{1,0:T(8,128)(2,1)S(1)} %pad_maximum_fusion), channel_id=1, source_target_pairs={{0,2},{2,0},{4,6},{6,4},{8,10},{10,8},{12,14},{14,12},{1,3},{3,1},... | collective-permute-start | bytes 1769480 | tf_op jit(solution)/shard_map/ppermute | solution.py:294
  4.2 11.8 %collective-permute-start.1 = (bf16[64,2304]{1,0:T(8,128)(2,1)S(1)}, bf16[64,2304]{1,0:T(8,128)(2,1)S(1)}, u32[]{:S(2)}, u32[]{:S(2)}) collective-permute-start(bf16[64,2304]{1,0:T(8,128)(2,1)S(1)} %pad_maximum_fusion.1), channel_id=1, source_target_pairs={{0,4},{2,6},{4,8},{6,10},{8,12},{10,14},{12,0},{14,2},{1,5},{3,7},... | collective-permute-start | bytes 884744 | tf_op jit(solution)/shard_map/ppermute | solution.py:291
  5.9 14.5 %collective-permute-start = (bf16[64,2304]{1,0:T(8,128)(2,1)S(1)}, bf16[64,2304]{1,0:T(8,128)(2,1)S(1)}, u32[]{:S(2)}, u32[]{:S(2)}) collective-permute-start(bf16[64,2304]{1,0:T(8,128)(2,1)S(1)} %pad_maximum_fusion.1), channel_id=1, source_target_pairs={{0,12},{2,14},{4,0},{6,2},{8,4},{10,6},{12,8},{14,10},{1,13},{3,15... | collective-permute-start | bytes 884744 | tf_op jit(solution)/shard_map/ppermute | solution.py:291
  14.1 20.7 %copy-start = (bf16[1,64,4096]{2,1,0:T(8,128)(2,1)S(1)}, bf16[1,64,4096]{2,1,0:T(8,128)(2,1)}, u32[]{:S(2)}) copy-start(bf16[1,64,4096]{2,1,0:T(8,128)(2,1)} %param.9) | copy-start | bytes 1572868
  14.1 20.7 %copy-start.1 = (bf16[1,64,512]{2,1,0:T(8,128)(2,1)S(1)}, bf16[1,64,512]{2,1,0:T(8,128)(2,1)}, u32[]{:S(2)}) copy-start(bf16[1,64,512]{2,1,0:T(8,128)(2,1)} %param.10) | copy-start | bytes 196612
  14.1 20.7 %copy-start.2 = (s32[8]{0:T(128)S(1)}, s32[8]{0:T(128)}, u32[]{:S(2)}) copy-start(s32[8]{0:T(128)} %pool_index.7) | copy-start | bytes 100
  14.1 20.7 %copy-start.3 = (s32[48,1]{0,1:T(1,128)S(1)}, s32[48,1]{0,1:T(1,128)}, u32[]{:S(2)}) copy-start(s32[48,1]{0,1:T(1,128)} %param.12) | copy-start | bytes 580
  16.1 13.4 %collective-permute-start.3 = (bf16[64,2304]{1,0:T(8,128)(2,1)S(1)}, bf16[64,2304]{1,0:T(8,128)(2,1)S(1)}, u32[]{:S(2)}, u32[]{:S(2)}) collective-permute-start(bf16[64,2304]{1,0:T(8,128)(2,1)S(1)} %collective-permute-done.1.refs_3_), channel_id=1, source_target_pairs={{0,16},{16,0},{1,17},{17,1},{2,18},{18,2},{3,19},{19,3},{4,20},{20... | collective-permute-start | bytes 884744 | tf_op jit(solution)/shard_map/ppermute | solution.py:297
  17.6 14.7 %collective-permute-start.5 = (bf16[64,2304]{1,0:T(8,128)(2,1)S(1)}, bf16[64,2304]{1,0:T(8,128)(2,1)S(1)}, u32[]{:S(2)}, u32[]{:S(2)}) collective-permute-start(bf16[64,2304]{1,0:T(8,128)(2,1)S(1)} %collective-permute-done.1.refs_3_), channel_id=1, source_target_pairs={{0,2},{2,0},{4,6},{6,4},{8,10},{10,8},{12,14},{14,12},{1,3},{3,1},... | collective-permute-start | bytes 884744 | tf_op jit(solution)/shard_map/ppermute | solution.py:294
  20.4 13.4 %collective-permute-start.6 = (bf16[64,2304]{1,0:T(8,128)(2,1)S(1)}, bf16[64,2304]{1,0:T(8,128)(2,1)S(1)}, u32[]{:S(2)}, u32[]{:S(2)}) collective-permute-start(bf16[64,2304]{1,0:T(8,128)(2,1)S(1)} %collective-permute-done.1.refs_3_), channel_id=1, source_target_pairs={{0,4},{2,6},{4,8},{6,10},{8,12},{10,14},{12,0},{14,2},{1,5},{3,7},... | collective-permute-start | bytes 884744 | tf_op jit(solution)/shard_map/ppermute | solution.py:291
  21.5 19.4 %collective-permute-start.7 = (bf16[64,2304]{1,0:T(8,128)(2,1)S(1)}, bf16[64,2304]{1,0:T(8,128)(2,1)S(1)}, u32[]{:S(2)}, u32[]{:S(2)}) collective-permute-start(bf16[64,2304]{1,0:T(8,128)(2,1)S(1)} %collective-permute-done.refs_4_), channel_id=1, source_target_pairs={{0,16},{16,0},{1,17},{17,1},{2,18},{18,2},{3,19},{19,3},{4,20},{20... | collective-permute-start | bytes 884744 | tf_op jit(solution)/shard_map/ppermute | solution.py:297
  23.0 10.8 %collective-permute-start.8 = (bf16[64,2304]{1,0:T(8,128)(2,1)S(1)}, bf16[64,2304]{1,0:T(8,128)(2,1)S(1)}, u32[]{:S(2)}, u32[]{:S(2)}) collective-permute-start(bf16[64,2304]{1,0:T(8,128)(2,1)S(1)} %collective-permute-done.refs_4_), channel_id=1, source_target_pairs={{0,2},{2,0},{4,6},{6,4},{8,10},{10,8},{12,14},{14,12},{1,3},{3,1},... | collective-permute-start | bytes 884744 | tf_op jit(solution)/shard_map/ppermute | solution.py:294
  29.4 9.9 %collective-permute-start.4 = (bf16[64,2304]{1,0:T(8,128)(2,1)S(1)}, bf16[64,2304]{1,0:T(8,128)(2,1)S(1)}, u32[]{:S(2)}, u32[]{:S(2)}) collective-permute-start(bf16[64,2304]{1,0:T(8,128)(2,1)S(1)} %collective-permute-done.3.refs_0_), channel_id=1, source_target_pairs={{0,4},{2,6},{4,8},{6,10},{8,12},{10,14},{12,0},{14,2},{1,5},{3,7},... | collective-permute-start | bytes 884744 | tf_op jit(solution)/shard_map/ppermute | solution.py:291
  32.3 12.3 %collective-permute-start.11 = (bf16[64,2304]{1,0:T(8,128)(2,1)S(1)}, bf16[64,2304]{1,0:T(8,128)(2,1)S(1)}, u32[]{:S(2)}, u32[]{:S(2)}) collective-permute-start(bf16[64,2304]{1,0:T(8,128)(2,1)S(1)} %collective-permute-done.5.refs_1_), channel_id=1, source_target_pairs={{0,16},{16,0},{1,17},{17,1},{2,18},{18,2},{3,19},{19,3},{4,20},{20... | collective-permute-start | bytes 884744 | tf_op jit(solution)/shard_map/ppermute | solution.py:297
  33.8 10.8 %collective-permute-start.13 = (bf16[64,2304]{1,0:T(8,128)(2,1)S(1)}, bf16[64,2304]{1,0:T(8,128)(2,1)S(1)}, u32[]{:S(2)}, u32[]{:S(2)}) collective-permute-start(bf16[64,2304]{1,0:T(8,128)(2,1)S(1)} %collective-permute-done.6.refs_2_), channel_id=1, source_target_pairs={{0,2},{2,0},{4,6},{6,4},{8,10},{10,8},{12,14},{14,12},{1,3},{3,1},... | collective-permute-start | bytes 884744 | tf_op jit(solution)/shard_map/ppermute | solution.py:294
  34.3 10.3 %collective-permute-start.12 = (bf16[64,2304]{1,0:T(8,128)(2,1)S(1)}, bf16[64,2304]{1,0:T(8,128)(2,1)S(1)}, u32[]{:S(2)}, u32[]{:S(2)}) collective-permute-start(bf16[64,2304]{1,0:T(8,128)(2,1)S(1)} %collective-permute-done.8.refs_4_), channel_id=1, source_target_pairs={{0,16},{16,0},{1,17},{17,1},{2,18},{18,2},{3,19},{19,3},{4,20},{20... | collective-permute-start | bytes 884744 | tf_op jit(solution)/shard_map/ppermute | solution.py:297
  39.4 8.0 %collective-permute-start.10 = (bf16[64,2304]{1,0:T(8,128)(2,1)S(1)}, bf16[64,2304]{1,0:T(8,128)(2,1)S(1)}, u32[]{:S(2)}, u32[]{:S(2)}) collective-permute-start(bf16[64,2304]{1,0:T(8,128)(2,1)S(1)} %collective-permute-done.4.refs_0_), channel_id=1, source_target_pairs={{0,2},{2,0},{4,6},{6,4},{8,10},{10,8},{12,14},{14,12},{1,3},{3,1},... | collective-permute-start | bytes 884744 | tf_op jit(solution)/shard_map/ppermute | solution.py:294
  44.5 4.6 %collective-permute-start.9 = (f32[768,512]{1,0:T(8,128)S(1)}, f32[768,512]{1,0:T(8,128)S(1)}, u32[]{:S(2)}, u32[]{:S(2)}) collective-permute-start(f32[768,512]{1,0:T(8,128)S(1)} %shard_map.73), channel_id=1, source_target_pairs={{0,1},{1,0},{2,3},{3,2},{4,5},{5,4},{6,7},{7,6},{8,9},{9,8},{10,11... | collective-permute-start | bytes 4718600 | tf_op jit(solution)/shard_map/ppermute | solution.py:300
  48.6 1.6 %copy-start.4 = (s32[48]{0:T(128)S(1)}, s32[48]{0:T(128)}, u32[]{:S(2)}) copy-start(s32[48]{0:T(128)} %live.1) | copy-start | bytes 580
  48.6 1.6 %collective-permute-start.14 = (f32[6,64,128]{2,1,0:T(8,128)S(1)}, f32[6,64,128]{2,1,0:T(8,128)S(1)}, u32[]{:S(2)}, u32[]{:S(2)}) collective-permute-start(f32[6,64,128]{2,1,0:T(8,128)S(1)} %get-tuple-element.39.sums), channel_id=1, source_target_pairs={{0,1},{1,0},{2,3},{3,2},{4,5},{5,4},{6,7},{7,6},{8,9},{9,8},{10,11... | collective-permute-start | bytes 589832 | tf_op jit(solution)/shard_map/ppermute | solution.py:300
